TPU v7x, 32 devices: a whole 2x2x4 slice. The times are simulated.
32 devices in a mesh: seq: 8 (over y, x, core), head: 4 (over z).
Axes of the slice: x: 2, y: 2, z: 4, core: 2. Of those that a mesh axis runs over, the one named last changes fastest.
Arguments:
- byte_in: bfloat16 [1024, 8, 1024], P('seq'), may hold values from -6 to 6
- local_gain: float32 [1024], replicated, may hold values from 0.25 to 1.75
- local_qkv: bfloat16 [1024, 3, 1024], P(None, None, 'head'), may hold values from -0.1875 to 0.1875
- local_out: bfloat16 [1024, 1024], P('head'), may hold values from -0.1875 to 0.1875
- mlp_up: bfloat16 [1024, 4096], P(None, 'head'), may hold values from -0.1875 to 0.1875
- mlp_down: bfloat16 [4096, 1024], P('head'), may hold values from -0.09375 to 0.09375
- local_scale: float32 [8], P('head'), may hold values from 1 to 40
- patch_proj: bfloat16 [1024, 256], replicated, may hold values from -0.1875 to 0.1875
- global_gain: float32 [2048], replicated, may hold values from 0.25 to 1.75
- global_qkv: bfloat16 [2048, 3, 2048], P(None, None, 'head'), may hold values from -0.125 to 0.125
- global_out: bfloat16 [2048, 2048], P('head'), may hold values from -0.125 to 0.125
- global_scale: float32 [16], P('head'), may hold values from 1 to 40
- back_proj: bfloat16 [256, 1024], replicated, may hold values from -0.375 to 0.375
- owners: int32 [8, 16], replicated, may hold values from 0 to 7, as said below
Outputs:
- byte_out: bfloat16 [1024, 8, 1024], P('seq', 'head')
- global_state: bfloat16 [1024, 2048], P('seq', 'head')
Inputs may be any that keep to these rules, and one draw needn't show every extreme that they name: `owners`: row s names, for each of the 16 blocks of 8 patches of byte range s in order, its owner; each row names every owner exactly twice.
All inputs are finite; a program needn't handle non-finite values.
Results may differ from a plain program's by a relative error of at most 0.028.
The roundings to bfloat16 on the way count: a program that leaves them out, or rounds other values in their place, can miss the bound.
Values may be sent and summed in bfloat16 or wider, within the bound.
No kernel may reach another device: no remote copies, remote signals or barrier semaphores. Data moves between devices by JAX's collectives and lax.ppermute only.
A program may use at most 128 MiB of HBM per device.

v0:
```python
import math

import jax
import jax.numpy as jnp
from jax import lax
from jax.sharding import PartitionSpec as P

EPSILON = 1e-06
NEGATIVE = -1e30


def rms_norm(values, gain):
    mean_square = jnp.mean(values * values, axis=-1, keepdims=True)
    return values * lax.rsqrt(mean_square + EPSILON) * gain


def unit_heads(values, head_count):
    shaped = values.reshape(values.shape[0], head_count, -1)
    mean_square = jnp.mean(shaped * shaped, axis=-1, keepdims=True)
    return shaped * lax.rsqrt(mean_square + EPSILON)


def patch_attention(queries, key_rows, values, head_scale):
    patch_span = queries.shape[1]
    head_depth = queries.shape[-1]
    scores = jnp.einsum("pihd,pjhd->phij", queries, key_rows, preferred_element_type=jnp.float32)
    scores = scores * (head_scale[:, None, None] / math.sqrt(head_depth))
    causal = jnp.tril(jnp.ones((patch_span, patch_span), dtype=bool))
    scores = jnp.where(causal, scores, NEGATIVE)
    row_max = jnp.max(scores, axis=-1, keepdims=True)
    weights = jnp.where(causal, jnp.exp(scores - row_max), 0.0)
    weight_sum = jnp.sum(weights, axis=-1)
    summed = jnp.einsum(
        "phij,pjhd->pihd", weights.astype(jnp.bfloat16), values, preferred_element_type=jnp.float32
    )
    return (summed / jnp.transpose(weight_sum, (0, 2, 1))[..., None]).astype(jnp.bfloat16)


def route_plan(owners, source):
    listed = lax.dynamic_index_in_dim(owners, source, 0, keepdims=False)
    block_count = listed.shape[0]
    indices = jnp.arange(block_count, dtype=jnp.int32)
    earlier = (listed[None, :] == listed[:, None]) & (indices[None, :] < indices[:, None])
    rank_of = jnp.sum(earlier, axis=1)
    per_owner = block_count // owners.shape[0]
    slot_of = listed * per_owner + rank_of
    inverse = jnp.sum(jnp.where(slot_of[None, :] == indices[:, None], indices[None, :], 0), axis=1)
    return (slot_of, inverse)


def reorder_blocks(row_data, chosen_blocks):
    blocks = row_data.reshape(chosen_blocks.shape[0], -1, row_data.shape[-1])
    return jnp.take(blocks, chosen_blocks, axis=0).reshape(row_data.shape)


def owner_positions(owners, block_size):
    devices, block_count = owners.shape
    target = jnp.arange(devices, dtype=jnp.int32)
    indices = jnp.arange(block_count, dtype=jnp.int32)
    matches = owners[None, :, :] == target[:, None, None]
    first_block = jnp.min(jnp.where(matches, indices, block_count), axis=2)
    second_block = jnp.max(jnp.where(matches, indices, -1), axis=2)
    chosen_blocks = jnp.stack([first_block, second_block], axis=2)
    base_cells = (target[None, :, None] * block_count + chosen_blocks) * block_size
    positions = base_cells[..., None] + jnp.arange(block_size, dtype=jnp.int32)
    return positions.reshape(-1)


def attend_piece(carried, key_piece, queries, query_pos, key_table, head_scale):
    key_rows, value_rows = key_piece
    row_count = key_rows.shape[0]
    head_count = queries.shape[1]
    head_depth = queries.shape[2]

    def compute(running):
        running_max, running_sum, accumulated = running
        keys_three = key_rows.reshape(row_count, head_count, head_depth)
        values_three = value_rows.reshape(row_count, head_count, head_depth)
        scores = jnp.einsum("qhd,khd->qhk", queries, keys_three, preferred_element_type=jnp.float32)
        scores = scores * (head_scale[None, :, None] / math.sqrt(head_depth))
        visible = key_table[None, None, :] <= query_pos[:, None, None]
        scores = jnp.where(visible, scores, NEGATIVE)
        new_max = jnp.maximum(running_max, jnp.max(scores, axis=-1))
        weights = jnp.where(visible, jnp.exp(scores - new_max[..., None]), 0.0)
        new_sum = jnp.sum(weights, axis=-1)
        summed = jnp.einsum(
            "qhk,khd->qhd",
            weights.astype(jnp.bfloat16),
            values_three,
            preferred_element_type=jnp.float32,
        )
        return (new_max, new_sum, summed)

    def keep(running):
        return running

    return lax.cond(jnp.min(key_table) > jnp.max(query_pos), keep, compute, carried)


def on_device(
    byte_in,
    local_gain,
    local_qkv,
    local_out,
    mlp_up,
    mlp_down,
    local_scale,
    patch_proj,
    global_gain,
    global_qkv,
    global_out,
    global_scale,
    back_proj,
    owners,
):
    patches, patch_span, model_width = byte_in.shape
    head_index = lax.axis_index("head")
    own_count = patch_span // lax.axis_size("head")
    byte_rows = byte_in.reshape(-1, model_width).astype(jnp.float32)
    normed = rms_norm(byte_rows, local_gain).astype(jnp.bfloat16)
    head_part = local_qkv.shape[2]
    local_heads = local_scale.shape[0]
    projected = jnp.dot(
        normed, local_qkv.reshape(model_width, 3 * head_part), preferred_element_type=jnp.float32
    )
    queries = (
        unit_heads(projected[:, :head_part], local_heads)
        .astype(jnp.bfloat16)
        .reshape(patches, patch_span, local_heads, -1)
    )
    key_rows = (
        unit_heads(projected[:, head_part : 2 * head_part], local_heads)
        .astype(jnp.bfloat16)
        .reshape(patches, patch_span, local_heads, -1)
    )
    values = (
        projected[:, 2 * head_part :]
        .astype(jnp.bfloat16)
        .reshape(patches, patch_span, local_heads, -1)
    )
    attended = patch_attention(queries, key_rows, values, local_scale).reshape(-1, head_part)
    activated = jax.nn.gelu(
        jnp.dot(normed, mlp_up, preferred_element_type=jnp.float32), approximate=True
    ).astype(jnp.bfloat16)
    partial_sum = jnp.dot(attended, local_out, preferred_element_type=jnp.float32) + jnp.dot(
        activated, mlp_down, preferred_element_type=jnp.float32
    )
    shares = lax.psum_scatter(
        partial_sum.reshape(patches, patch_span, model_width),
        "head",
        scatter_dimension=1,
        tiled=True,
    )
    own_input = lax.dynamic_slice_in_dim(byte_in, head_index * own_count, own_count, 1).astype(
        jnp.float32
    )
    own_state = (own_input + shares).astype(jnp.bfloat16)
    own_patch = (
        jnp.dot(own_state.reshape(-1, model_width), patch_proj, preferred_element_type=jnp.float32)
        .reshape(patches, -1)
        .astype(jnp.bfloat16)
    )
    patch_in = lax.all_gather(own_patch, "head", axis=1, tiled=True)
    head_width = global_qkv.shape[2]
    head_group = global_scale.shape[0]
    gnormed = rms_norm(patch_in.astype(jnp.float32), global_gain).astype(jnp.bfloat16)
    global_mixed = jnp.dot(
        gnormed, global_qkv.reshape(-1, 3 * head_width), preferred_element_type=jnp.float32
    )
    global_query = (
        unit_heads(global_mixed[:, :head_width], head_group)
        .astype(jnp.bfloat16)
        .reshape(patches, head_width)
    )
    global_keys = (
        unit_heads(global_mixed[:, head_width : 2 * head_width], head_group)
        .astype(jnp.bfloat16)
        .reshape(patches, head_width)
    )
    global_values = global_mixed[:, 2 * head_width :].astype(jnp.bfloat16)
    residual = lax.dynamic_slice_in_dim(patch_in, head_index * head_width, head_width, 1)
    seq_index = lax.axis_index("seq")
    block_size = patches // owners.shape[1]
    slot_of, inverse = route_plan(owners, seq_index)
    routed_query, routed_keys, routed_values, routed_residual = (
        lax.all_to_all(
            reorder_blocks(global_query, inverse), "seq", split_axis=0, concat_axis=0, tiled=True
        ),
        lax.all_to_all(
            reorder_blocks(global_keys, inverse), "seq", split_axis=0, concat_axis=0, tiled=True
        ),
        lax.all_to_all(
            reorder_blocks(global_values, inverse), "seq", split_axis=0, concat_axis=0, tiled=True
        ),
        lax.all_to_all(
            reorder_blocks(residual, inverse), "seq", split_axis=0, concat_axis=0, tiled=True
        ),
    )
    key_table = owner_positions(owners, block_size)
    query_pos = lax.dynamic_slice_in_dim(key_table, seq_index * patches, patches)
    query_three = routed_query.reshape(patches, head_group, -1)
    head_depth = query_three.shape[-1]
    start_state = (
        jnp.full((patches, head_group), NEGATIVE, jnp.float32),
        jnp.zeros((patches, head_group), jnp.float32),
        jnp.zeros((patches, head_group, head_depth), jnp.float32),
    )
    final_max, final_sum, accumulated = attend_piece(
        start_state,
        (
            lax.all_gather(routed_keys, "seq", axis=0, tiled=True),
            lax.all_gather(routed_values, "seq", axis=0, tiled=True),
        ),
        query_three,
        query_pos,
        key_table,
        global_scale,
    )
    global_attended = (accumulated / final_sum[..., None]).astype(jnp.bfloat16).reshape(patches, -1)
    update = lax.psum_scatter(
        jnp.dot(global_attended, global_out, preferred_element_type=jnp.float32).astype(
            jnp.bfloat16
        ),
        "head",
        scatter_dimension=1,
        tiled=True,
    ).astype(jnp.float32)
    result = (update + routed_residual.astype(jnp.float32)).astype(jnp.bfloat16)
    returned = lax.all_to_all(result, "seq", split_axis=0, concat_axis=0, tiled=True)
    own_result = reorder_blocks(returned, slot_of)
    back_term = jnp.dot(
        own_result.reshape(-1, back_proj.shape[0]), back_proj, preferred_element_type=jnp.float32
    )
    byte_out = (
        (own_state.reshape(-1, model_width).astype(jnp.float32) + back_term)
        .reshape(patches, own_count, model_width)
        .astype(jnp.bfloat16)
    )
    return (byte_out, result)


def solution(mesh):
    placed = (
        P("seq", None, None),
        P(),
        P(None, None, "head"),
        P("head", None),
        P(None, "head"),
        P("head", None),
        P("head"),
        P(),
        P(),
        P(None, None, "head"),
        P("head", None),
        P("head"),
        P(),
        P(),
    )
    return jax.shard_map(
        on_device,
        mesh=mesh,
        in_specs=placed,
        out_specs=(P("seq", "head", None), P("seq", "head")),
        check_vma=False,
    )
```

profile of v0, /device:TPU:0, one launch (start us, length us, event | category | flops | bytes accessed | tf_op | source)
XLA Modules:
  0.0 281.0 jit_solution(17225748344498860086)
XLA Ops:
  7.2 2.2 fusion.18
  9.5 2.6 copy.101
  12.1 3.9 %fusion.37 = f32[1024,768]{0,1:T(8,128)S(1)} fusion(bf16[1024,768]{0,1:T(8,128)(2,1)} %bitcast.135, bf16[128,8,1024]{2,1,0:T(8,128)(2,1)} %param.18, f32[1024]{0:T(1024)S(1)} %copy-done.7, f32[128,8]{1,0:T(8,128)S(1)} %add_rsqrt_fusion.2), kind=kOutput, calls=%fused_computation.51 | convolution fusion | flops 1614807040 | bytes 6823936 | tf_op jit(solution)/shard_map/dot_general | solution.py:123
  18.9 2.6 copy.103
  22.8 2.3 fusion.63
  27.5 8.8 %fusion.32 = f32[1024,1024]{1,0:T(8,128)} fusion(bf16[1024,1024]{1,0:T(8,128)(2,1)S(1)} %copy-done, bf16[1024,1024]{1,0:T(8,128)(2,1)} %param.22, bf16[128,8,1024]{2,1,0:T(8,128)(2,1)} %param.18, f32[1024]{0:T(1024)S(1)} %copy-done.7, f32[1024]{0:T(1024)S(1)} %rsqrt.63), kind=kOutput, calls=%fused_computation.48 | convolution fusion | flops 4308598784 | bytes 10493952 | tf_op jit(solution)/shard_map/dot_general | solution.py:145
  36.3 5.4 %add_bitcast_fusion = f32[128,8,1024]{2,1,0:T(8,128)} fusion(f32[1024,1024]{1,0:T(8,128)} %fusion.32, bf16[256,1024]{1,0:T(8,128)(2,1)} %param.21, bf16[128,2,8,8]{3,2,1,0:T(8,128)(2,1)S(1)} %copy.108, bf16[1024,256]{1,0:T(8,128)(2,1)S(1)} %copy.102, f32[128,8,2]{1,2,0:T(2,128)S(1)} %copy.109), kind=kOutput, calls=%fused_computation.46 | convolution fusion | flops 542638080 | bytes 9478144 | tf_op jit(solution)/shard_map/dot_general | solution.py:145
  41.6 6.8 %copy.110 = f32[128,8,1024]{2,0,1:T(8,128)} copy(f32[128,8,1024]{2,1,0:T(8,128)} %add_bitcast_fusion) | data formatting | bytes 8388608 | tf_op jit(solution)/shard_map/reshape | solution.py:149
  48.5 8.8 %copy.113 = bf16[2048,3,512]{0,2,1:T(8,128)(2,1)} copy(bf16[2048,3,512]{2,0,1:T(8,128)(2,1)} %param.27) | data formatting | bytes 12582912 | tf_op args[9]
  57.7 2.2 constant_dynamic-slice_fusion.1
  60.0 68.1 %reduce-scatter.3.cloned.1.call-done = f32[128,2,1024]{2,0,1:T(8,128)} async-done(((f32[128,8,1024]{2,0,1:T(8,128)}), f32[128,2,1024]{2,0,1:T(8,128)}) %reduce-scatter.3.cloned.1.call-update) | async-done | bytes 1048592 | tf_op jit(solution)/shard_map/reduce_scatter | solution.py:148
  131.9 16.1 %all_gather.9 = bf16[128,2048]{1,0:T(8,128)(2,1)S(1)} all-gather(bf16[128,512]{1,0:T(8,128)(2,1)S(1)} %convert_element_type.115), channel_id=1, replica_groups=mesh['seq'=8,'head'=4] {'head'}, dimensions={1}, use_global_device_ids=true | all-gather | bytes 655360 | tf_op jit(solution)/shard_map/all_gather | solution.py:163
  148.1 5.0 %fusion.66 = f32[128,1536]{1,0:T(8,128)S(1)} fusion(bf16[2048,1536]{0,1:T(8,128)(2,1)} %bitcast.134, bf16[128,2048]{1,0:T(8,128)(2,1)S(1)} %all_gather.9, f32[2048]{0:T(1024)S(1)} %copy-done.4, f32[128]{0:T(128)S(1)} %add_rsqrt_fusion.5), kind=kOutput, calls=%fused_computation.84 | convolution fusion | flops 806354944 | bytes 7610880 | tf_op jit(solution)/shard_map/dot_general | solution.py:167
  154.6 1.7 mul.223
  158.5 1.7 mul.225
  160.2 1.7 mul.229
  164.0 1.8 mul.231
  165.8 1.8 fusion.76
  172.4 9.0 %all_to_all.51 = bf16[8,16,512]{2,1,0:T(8,128)(2,1)} all-to-all(bf16[8,16,512]{2,1,0:T(8,128)(2,1)S(1)} %bitcast.141), channel_id=1, replica_groups=mesh['seq'=8,'head'=4] {'seq'}, dimensions={0} | all-to-all | bytes 262144 | tf_op jit(solution)/shard_map/all_to_all | solution.py:189
  181.5 8.6 %all_to_all.52 = bf16[8,16,512]{2,1,0:T(8,128)(2,1)} all-to-all(bf16[8,16,512]{2,1,0:T(8,128)(2,1)S(1)} %bitcast.140), channel_id=1, replica_groups=mesh['seq'=8,'head'=4] {'seq'}, dimensions={0} | all-to-all | bytes 262144 | tf_op jit(solution)/shard_map/all_to_all | solution.py:192
  190.6 3.4 %all-to-all-start.1 = ((bf16[8,16,512]{2,1,0:T(8,128)(2,1)}), bf16[8,16,512]{2,1,0:T(8,128)(2,1)S(1)}, u32[]{:S(2)}, u32[]{:S(2)}) async-start(bf16[8,16,512]{2,1,0:T(8,128)(2,1)} %bitcast.24), calls=%async_computation.2 | async-start | bytes 262144 | tf_op jit(solution)/shard_map/all_to_all | solution.py:186
  197.0 2.5 all-to-all-done.1
  199.5 4.2 %all-gather.3.cloned.1.call-done = bf16[1024,512]{1,0:T(8,128)(2,1)} async-done(((bf16[128,512]{1,0:T(8,128)(2,1)}), bf16[1024,512]{1,0:T(8,128)(2,1)}) %all-gather.3.cloned.1.call-update) | async-done | bytes 1048592 | tf_op jit(solution)/shard_map/all_gather | solution.py:211
  203.6 25.4 %all-gather.5.cloned.1.call-done = bf16[1024,512]{1,0:T(8,128)(2,1)} async-done(((bf16[128,512]{1,0:T(8,128)(2,1)}), bf16[1024,512]{1,0:T(8,128)(2,1)}) %all-gather.5.cloned.1.call-update) | async-done | bytes 1048592 | tf_op jit(solution)/shard_map/all_gather | solution.py:212
  229.0 6.9 %conditional.1 = (f32[128,4]{0,1:T(4,128)S(1)}, f32[128,4,128]{0,2,1:T(8,128)S(1)}) conditional(s32[]{:T(128)} %convert_element_type.113, (s32[8,8,2,8]{3,2,1,0:T(2,128)S(1)}, s32[128]{0:T(128)S(1)}, bf16[1024,512]{1,0:T(8,128)(2,1)}, bf16[8,16,512]{2,1,0:T(8,128)(2,1)S(1)}, f32[4]{0:T(128)S(1)}, ...), branch_computations={%region_15.19_spmd, %region_18.20_spmd} | conditional | flops 275381760 | bytes 22700696 | solution.py:97
  229.4 1.8 fusion
  233.7 2.2 fusion.2
  235.9 2.9 %convolution_convert_fusion = bf16[128,2048]{1,0:T(8,128)(2,1)} fusion(bf16[128,512]{0,1:T(8,128)(2,1)S(1)} %bitcast.142, bf16[512,2048]{1,0:T(8,128)(2,1)} %param.28), kind=kOutput, calls=%fused_computation.47 | convolution fusion | flops 268697600 | bytes 2752512 | tf_op jit(solution)/shard_map/dot_general | solution.py:221
  238.9 8.1 %all_to_all.53 = bf16[8,16,512]{2,1,0:T(8,128)(2,1)S(1)} all-to-all(bf16[8,16,512]{2,1,0:T(8,128)(2,1)S(1)} %bitcast.139), channel_id=1, replica_groups=mesh['seq'=8,'head'=4] {'seq'}, dimensions={0} | all-to-all | bytes 262144 | tf_op jit(solution)/shard_map/all_to_all | solution.py:195
  246.9 13.7 %reduce-scatter.5.cloned.1.call-done = bf16[128,512]{1,0:T(8,128)(2,1)} async-done(((bf16[128,2048]{1,0:T(8,128)(2,1)}), bf16[128,512]{1,0:T(8,128)(2,1)}) %reduce-scatter.5.cloned.1.call-update) | async-done | bytes 131088 | tf_op jit(solution)/shard_map/reduce_scatter | solution.py:220
  262.3 3.6 %all-to-all-start.4 = ((bf16[8,16,512]{2,1,0:T(8,128)(2,1)}), bf16[8,16,512]{2,1,0:T(8,128)(2,1)S(1)}, u32[]{:S(2)}, u32[]{:S(2)}) async-start(bf16[8,16,512]{2,1,0:T(8,128)(2,1)} %bitcast.32), calls=%async_computation.6 | async-start | bytes 262144 | tf_op jit(solution)/shard_map/all_to_all | solution.py:229
  265.9 5.5 %all-to-all-done.4 = bf16[8,16,512]{2,1,0:T(8,128)(2,1)S(1)} async-done(((bf16[8,16,512]{2,1,0:T(8,128)(2,1)}), bf16[8,16,512]{2,1,0:T(8,128)(2,1)S(1)}, u32[]{:S(2)}, u32[]{:S(2)}) %all-to-all-start.4) | async-done | bytes 131104 | tf_op jit(solution)/shard_map/all_to_all | solution.py:229
  (97 shorter events, 31.2 us)
Async XLA Ops:
  7.2 20.3 %copy-start = (bf16[1024,1024]{1,0:T(8,128)(2,1)S(1)}, bf16[1024,1024]{1,0:T(8,128)(2,1)}, u32[]{:S(2)}) copy-start(bf16[1024,1024]{1,0:T(8,128)(2,1)} %param.23) | copy-start | bytes 6291460
  7.2 120.9 %reduce-scatter.3.cloned.1.call-start = ((), (), s32[]{:S(2)}) async-start(), calls=%async_computation.7 | async-start | bytes 5242880 | tf_op jit(solution)/shard_map/reduce_scatter | solution.py:148
  9.4 2.6 copy-start.7
  22.8 2.7 copy-start.8
  48.5 155.2 %all-gather.3.cloned.1.call-start = ((), (), s32[]{:S(2)}) async-start(), calls=%async_computation.8 | async-start | bytes 1179648 | tf_op jit(solution)/shard_map/all_gather | solution.py:211
  48.5 8.9 %copy-start.5 = (s32[8,16]{1,0:T(8,128)S(1)}, s32[8,16]{1,0:T(8,128)}, u32[]{:S(2)}) copy-start(s32[8,16]{1,0:T(8,128)} %param.31) | copy-start | bytes 1540
  130.0 18.1 %copy-start.4 = (f32[2048]{0:T(1024)S(1)}, f32[2048]{0:T(1024)}, u32[]{:S(2)}) copy-start(f32[2048]{0:T(1024)} %param.26) | copy-start | bytes 24580
  130.3 1.5 copy-start.1
  167.6 61.5 %copy-start.9 = (f32[4]{0:T(128)S(1)}, f32[4]{0:T(128)}, u32[]{:S(2)}) copy-start(f32[4]{0:T(128)} %param.29) | copy-start | bytes 52
  181.4 47.6 %all-gather.5.cloned.1.call-start = ((), (), s32[]{:S(2)}) async-start(), calls=%async_computation.9 | async-start | bytes 1179648 | tf_op jit(solution)/shard_map/all_gather | solution.py:212
  190.6 8.9 %all-to-all-start.1 = ((bf16[8,16,512]{2,1,0:T(8,128)(2,1)}), bf16[8,16,512]{2,1,0:T(8,128)(2,1)S(1)}, u32[]{:S(2)}, u32[]{:S(2)}) async-start(bf16[8,16,512]{2,1,0:T(8,128)(2,1)} %bitcast.24), calls=%async_computation.2 | async-start | bytes 262144 | tf_op jit(solution)/shard_map/all_to_all | solution.py:186
  194.0 66.7 %reduce-scatter.5.cloned.1.call-start = ((), (), s32[]{:S(2)}) async-start(), calls=%async_computation.10 | async-start | bytes 655360 | tf_op jit(solution)/shard_map/reduce_scatter | solution.py:220
  229.4 3.2 %copy-start.6 = (bf16[1024,512]{1,0:T(8,128)(2,1)S(1)}, bf16[1024,512]{1,0:T(8,128)(2,1)}, u32[]{:S(2)}) copy-start(bf16[1024,512]{1,0:T(8,128)(2,1)} %get-tuple-element.19) | copy-start | bytes 3145732 | tf_op jit(solution)/shard_map/cond
  231.2 1.4 copy-start.3
  235.9 36.2 %copy-start.2 = (bf16[256,1024]{1,0:T(8,128)(2,1)S(1)}, bf16[256,1024]{1,0:T(8,128)(2,1)}, u32[]{:S(2)}) copy-start(bf16[256,1024]{1,0:T(8,128)(2,1)} %copy-done.1) | copy-start | bytes 1572868
  262.3 9.1 %all-to-all-start.4 = ((bf16[8,16,512]{2,1,0:T(8,128)(2,1)}), bf16[8,16,512]{2,1,0:T(8,128)(2,1)S(1)}, u32[]{:S(2)}, u32[]{:S(2)}) async-start(bf16[8,16,512]{2,1,0:T(8,128)(2,1)} %bitcast.32), calls=%async_computation.6 | async-start | bytes 262144 | tf_op jit(solution)/shard_map/all_to_all | solution.py:229
Sparse Core Ops, SparseCore 0:
  48.6 79.4 reduce-scatter.2
  181.6 22.0 all-gather.2
  205.7 23.2 all-gather.4
  239.0 21.6 reduce-scatter.4
where the time goes:
time: 282 us; the launch traced here: 281 us
  waiting for transfers between devices  119 us (42%)
  local copies, waits for them, and re-layouts  47 us (17%)
  blocking collectives  41.7 us (15%)
  matrix products  33.9 us (12%)
  other arithmetic  16.3 us (6%)
  between operations  15.4 us (5%)
  starting transfers between devices  7.12 us (3%)
    reduce_scatter x1, waiting for transfers between devices, on_device(): lax.psum_scatter(partial_sum.reshape(patches, patch_span, model_width), '...  68.1 us
    all_gather x1, waiting for transfers between devices, on_device(): lax.all_gather(routed_values, 'seq', axis=0, tiled=True)  25.4 us
    all_gather x1, blocking collectives, on_device(): patch_in = lax.all_gather(own_patch, 'head', axis=1, tiled=True)  16.1 us
    reduce_scatter x1, waiting for transfers between devices, on_device(): lax.psum_scatter(jnp.dot(global_attended, global_out, preferred_element_t...  13.7 us
    unnamed x18, local copies, waits for them, and re-layouts  11.5 us
    all_to_all x1, blocking collectives, on_device(): lax.all_to_all(reorder_blocks(global_keys, inverse), 'seq', split_axis=0,...  8.98 us
    dot_general x1, matrix products, on_device(): jnp.dot(activated, mlp_down, preferred_element_type=jnp.float32)  8.8 us
    all_to_all x1, blocking collectives, on_device(): lax.all_to_all(reorder_blocks(global_values, inverse), 'seq', split_axis=...  8.59 us
  transfers between devices with their start and end apart: 6, of which 6 were waited for; matrix products, arithmetic and copies ran while one was open for 5% of the time, Pallas kernels for 0%

commit v1 on v0

v1 whole, which is shorter than its diff:
```python
import functools
import math

import jax
import jax.numpy as jnp
from jax import lax
from jax.experimental import pallas as pl
from jax.experimental.pallas import tpu as pltpu
from jax.sharding import PartitionSpec as P

EPSILON = 1e-06
NEGATIVE = -1e30
F32 = jnp.float32
BF16 = jnp.bfloat16
VMEM = pl.BlockSpec(memory_space=pltpu.VMEM)
SMEM = pl.BlockSpec(memory_space=pltpu.SMEM)


def dot(left, right):
    return jnp.dot(left, right, preferred_element_type=F32)


def dot_t(left, right):
    return lax.dot_general(left, right, (((1,), (1,)), ((), ())), preferred_element_type=F32)


def unit(values):
    return (values * lax.rsqrt(jnp.mean(values * values, axis=-1, keepdims=True) + EPSILON)).astype(BF16)


def gelu(values):
    inner = math.sqrt(2.0 / math.pi) * (values + 0.044715 * (values * values * values))
    return 0.5 * values * (1.0 + jnp.tanh(inner))


def local_kernel(
    span, own, me_ref, scale_ref, x_ref, gain_ref, qkv_ref, out_ref, up_ref, down_ref, proj_ref, part_ref, share_ref
):
    rows = x_ref.shape[0]
    group = rows // span
    at = lax.broadcasted_iota(jnp.int32, (rows, rows), 0)
    to = lax.broadcasted_iota(jnp.int32, (rows, rows), 1)
    order = (to == (at % group) * span + at // group).astype(F32).astype(BF16)
    x = dot(order, x_ref[...])
    normed = (
        x * lax.rsqrt(jnp.mean(x * x, axis=-1, keepdims=True) + EPSILON) * gain_ref[...]
    ).astype(BF16)
    query, key, value = (dot(normed, qkv_ref[i]) for i in range(3))
    seen = (at % group == to % group) & (to <= at)
    heads = scale_ref.shape[0]
    depth = query.shape[1] // heads
    attended = []
    for h in range(heads):
        cut = slice(h * depth, (h + 1) * depth)
        scores = dot_t(unit(query[:, cut]), unit(key[:, cut])) * (scale_ref[h] / math.sqrt(depth))
        scores = jnp.where(seen, scores, NEGATIVE)
        weights = jnp.exp(scores - jnp.max(scores, axis=-1, keepdims=True))
        total = jnp.sum(weights, axis=-1, keepdims=True)
        attended.append((dot(weights.astype(BF16), value[:, cut].astype(BF16)) / total).astype(BF16))
    act = gelu(dot(normed, up_ref[...])).astype(BF16)
    partial = dot(jnp.concatenate(attended, axis=1), out_ref[...]) + dot(act, down_ref[...])
    byte = lax.broadcasted_iota(jnp.int32, (rows, 1), 0) // group
    partial = (partial + jnp.where(byte // own == me_ref[0], x, 0.0)).astype(BF16)
    part_ref[...] = partial.reshape(part_ref.shape)
    share = dot(partial, proj_ref[...]).astype(BF16)
    width = share.shape[1]
    for b in range(span):
        share_ref[b // own, :, (b % own) * width : (b % own + 1) * width] = share[b * group : (b + 1) * group]


def local_part(me, scale, x, gain, qkv, out, up, down, proj, span, ways, group):
    rows, width = x.shape
    patches = rows // span
    own = span // ways
    once = lambda a: pl.BlockSpec(a.shape, lambda i: (0,) * a.ndim, pipeline_mode=pl.Buffered(1))
    return pl.pallas_call(
        functools.partial(local_kernel, span, own),
        grid=(patches // group,),
        in_specs=[SMEM, SMEM, pl.BlockSpec((group * span, width), lambda i: (i, 0))]
        + [once(a) for a in (gain, qkv, out, up, down, proj)],
        out_specs=(
            pl.BlockSpec((span, group, width), lambda i: (0, i, 0)),
            pl.BlockSpec((ways, group, own * proj.shape[1]), lambda i: (0, i, 0)),
        ),
        out_shape=(
            jax.ShapeDtypeStruct((span, patches, width), BF16),
            jax.ShapeDtypeStruct((ways, patches, own * proj.shape[1]), BF16),
        ),
        compiler_params=pltpu.CompilerParams(vmem_limit_bytes=48 * 2**20),
        name="local_part",
    )(me, scale, x, gain, qkv, out, up, down, proj)


def heads_kernel(kinds, depth, ids_ref, gain_ref, *refs):
    ways = gain_ref.shape[0]
    shares, weights, outs = refs[:ways], refs[ways : ways + len(kinds)], refs[ways + len(kinds) :]
    width = shares[0].shape[1]
    values = [s[...].astype(F32) for s in shares]
    square = sum(jnp.sum(v * v, axis=-1, keepdims=True) for v in values)
    factor = lax.rsqrt(square / (ways * width) + EPSILON)
    normed = [(v * factor * gain_ref[ids_ref[c]]).astype(BF16) for c, v in enumerate(values)]
    for kind, weight, out in zip(kinds, weights, outs):
        mixed = sum(
            dot(n, weight[0, pl.ds(pl.multiple_of(ids_ref[c] * width, width), width), :]) for c, n in enumerate(normed)
        )
        if kind < 2:
            for h in range(mixed.shape[1] // depth):
                out[:, h * depth : (h + 1) * depth] = unit(mixed[:, h * depth : (h + 1) * depth])
        else:
            out[...] = mixed.astype(BF16)


def global_heads(kinds, depth, ids, gain, shares, qkv):
    shape = jax.ShapeDtypeStruct((shares[0].shape[0], qkv.shape[2]), BF16)
    pick = lambda kind: pl.BlockSpec((1,) + qkv.shape[1:], lambda i: (kind, 0, 0), pipeline_mode=pl.Buffered(1))
    whole = lambda a: pl.BlockSpec(a.shape, lambda i: (0,) * a.ndim)
    return pl.pallas_call(
        functools.partial(heads_kernel, kinds, depth),
        grid=(1,),
        in_specs=[SMEM, whole(gain)] + [whole(s) for s in shares] + [pick(kind) for kind in kinds],
        out_specs=tuple(whole(shape) for _ in kinds),
        out_shape=tuple(shape for _ in kinds),
        compiler_params=pltpu.CompilerParams(vmem_limit_bytes=16 * 2**20),
        name="global_heads",
    )(ids, gain, *shares, *([qkv] * len(kinds)))


def attend_kernel(count, ids_ref, scale_ref, q_ref, *refs):
    keys, values, (proj_ref, out_ref) = refs[:count], refs[count : 2 * count], refs[2 * count :]
    rows = q_ref.shape[0]
    at = lax.broadcasted_iota(jnp.int32, (rows, rows), 0)
    to = lax.broadcasted_iota(jnp.int32, (rows, rows), 1)
    heads = scale_ref.shape[0]
    depth = q_ref.shape[1] // heads
    me = ids_ref[0]
    seen = [to + ids_ref[i] * rows <= at + me * rows for i in range(count)]
    attended = []
    for h in range(heads):
        cut = slice(h * depth, (h + 1) * depth)
        query = q_ref[:, cut]
        factor = scale_ref[h] / math.sqrt(depth)
        scores = [jnp.where(s, dot_t(query, k[:, cut]) * factor, NEGATIVE) for s, k in zip(seen, keys)]
        top = functools.reduce(jnp.maximum, [jnp.max(s, axis=-1, keepdims=True) for s in scores])
        weights = [jnp.exp(s - top) for s in scores]
        total = sum(jnp.sum(w, axis=-1, keepdims=True) for w in weights)
        summed = sum(dot(w.astype(BF16), v[:, cut]) for w, v in zip(weights, values))
        attended.append((summed / total).astype(BF16))
    update = dot(jnp.concatenate(attended, axis=1), proj_ref[...]).astype(BF16)
    width = out_ref.shape[2]
    for c in range(out_ref.shape[0]):
        out_ref[c] = update[:, c * width : (c + 1) * width]


def attend(ids, scale, query, keys, values, proj, ways):
    rows = query.shape[0]
    return pl.pallas_call(
        functools.partial(attend_kernel, len(keys)),
        in_specs=[SMEM, SMEM] + [VMEM] * (2 + 2 * len(keys)),
        out_specs=VMEM,
        out_shape=jax.ShapeDtypeStruct((ways, rows, proj.shape[1] // ways), BF16),
        compiler_params=pltpu.CompilerParams(vmem_limit_bytes=40 * 2**20),
        name="attend",
    )(ids, scale, query, *keys, *values, proj)


def result_kernel(count, order_ref, own_ref, *refs):
    pieces, (result_ref, routed_ref) = refs[:count], refs[count:]
    total = own_ref[...].astype(F32) + sum(p[...].astype(F32) for p in pieces)
    result = total.astype(BF16)
    result_ref[...] = result
    routed_ref[...] = dot(order_ref[...], result).astype(BF16)


def finish_result(order, residual, pieces):
    shape = jax.ShapeDtypeStruct(residual.shape, BF16)
    return pl.pallas_call(
        functools.partial(result_kernel, len(pieces)),
        in_specs=[VMEM] * (2 + len(pieces)),
        out_specs=(VMEM, VMEM),
        out_shape=(shape, shape),
        name="finish_result",
    )(order, residual, *pieces)


def bytes_kernel(count, result_ref, proj_ref, *refs):
    pieces, out_ref = refs[:count], refs[count]
    state = sum(p[...].astype(F32) for p in pieces).astype(BF16).astype(F32)
    rows = result_ref.shape[0]
    width = proj_ref.shape[0]
    own = state.shape[0] // rows
    mixed = [
        (state[b * rows : (b + 1) * rows] + dot(result_ref[:, b * width : (b + 1) * width], proj_ref[...])).astype(BF16)
        for b in range(own)
    ]
    at = lax.broadcasted_iota(jnp.int32, (rows * own, rows * own), 0)
    to = lax.broadcasted_iota(jnp.int32, (rows * own, rows * own), 1)
    order = (to == (at % own) * rows + at // own).astype(F32).astype(BF16)
    out_ref[...] = dot(order, jnp.concatenate(mixed, axis=0)).astype(BF16)


def finish_bytes(result, proj, pieces):
    return pl.pallas_call(
        functools.partial(bytes_kernel, len(pieces)),
        in_specs=[VMEM] * (2 + len(pieces)),
        out_specs=VMEM,
        out_shape=jax.ShapeDtypeStruct(pieces[0].shape, BF16),
        compiler_params=pltpu.CompilerParams(vmem_limit_bytes=32 * 2**20),
        name="finish_bytes",
    )(result, proj, *pieces)


def shift(value, axis, step):
    count = lax.axis_size(axis)
    return lax.ppermute(value, axis, [(i, (i + step) % count) for i in range(count)])


def scatter(chunks, axis):
    count = lax.axis_size(axis)
    me = lax.axis_index(axis)
    take = lambda step: lax.dynamic_index_in_dim(chunks, (me + step) % count, 0, keepdims=False)
    return [take(0)] + [shift(take(step), axis, step) for step in range(1, count)]


def gather(value, axis):
    return [value] + [shift(value, axis, step) for step in range(1, lax.axis_size(axis))]


def gather_chips(value, axis):
    count = lax.axis_size(axis)
    other = [(i, i ^ 1) for i in range(count)]
    pieces = [value] + [shift(value, axis, 2 * step) for step in range(1, count // 2)]
    return pieces + [lax.ppermute(p, axis, other) for p in pieces]


def chip_ids(axis):
    count = lax.axis_size(axis)
    me = lax.axis_index(axis)
    mine = (me - 2 * jnp.arange(count // 2, dtype=jnp.int32)) % count
    return jnp.concatenate([mine, mine ^ 1]).astype(jnp.int32)


def owner_order(owners, source, patches):
    listed = lax.dynamic_index_in_dim(owners, source, 0, keepdims=False)
    count = listed.shape[0]
    block = patches // count
    index = jnp.arange(count, dtype=jnp.int32)
    before = (listed[None, :] < listed[:, None]) | (
        (listed[None, :] == listed[:, None]) & (index[None, :] < index[:, None])
    )
    slot = jnp.sum(before, axis=1).astype(jnp.int32)
    row = jnp.arange(patches, dtype=jnp.int32)
    place = jnp.repeat(slot, block, total_repeat_length=patches) * block + row % block
    return (row[:, None] == place[None, :]).astype(BF16)


def on_device(
    byte_in,
    local_gain,
    local_qkv,
    local_out,
    mlp_up,
    mlp_down,
    local_scale,
    patch_proj,
    global_gain,
    global_qkv,
    global_out,
    global_scale,
    back_proj,
    owners,
):
    patches, span, width = byte_in.shape
    ways = lax.axis_size("head")
    own = span // ways
    me = lax.axis_index("head").astype(jnp.int32)
    seq = lax.axis_index("seq").astype(jnp.int32)
    depth = global_qkv.shape[2] // global_scale.shape[0]
    group = min(32, patches)

    part, share = local_part(
        me.reshape(1),
        local_scale,
        byte_in.reshape(-1, width),
        local_gain.reshape(1, -1),
        jnp.transpose(local_qkv, (1, 0, 2)),
        local_out,
        mlp_up,
        mlp_down,
        patch_proj,
        span,
        ways,
        group,
    )
    pieces = scatter(share, "head")
    residual = sum(p.astype(F32) for p in pieces).astype(BF16)
    shares = gather(residual, "head")
    ids = (me - jnp.arange(ways, dtype=jnp.int32)) % ways
    gain = global_gain.reshape(ways, 1, -1)
    qkv = jnp.transpose(global_qkv, (1, 0, 2))
    key, value = global_heads((1, 2), depth, ids, gain, shares, qkv)
    part, key, value = lax.optimization_barrier((part, key, value))
    (query,) = global_heads((0,), depth, ids, gain, shares, qkv)
    keys = gather_chips(key, "seq")
    values = gather_chips(value, "seq")
    bytes_pieces = scatter(part.reshape(ways, own * patches, width), "head")
    update = attend(chip_ids("seq"), global_scale, query, keys, values, global_out, ways)
    result, routed = finish_result(owner_order(owners, seq, patches), residual, scatter(update, "head"))
    global_state = lax.all_to_all(routed, "seq", split_axis=0, concat_axis=0, tiled=True)
    byte_out = finish_bytes(result, back_proj, bytes_pieces)
    return byte_out.reshape(patches, own, width), global_state


def solution(mesh):
    placed = (
        P("seq", None, None),
        P(),
        P(None, None, "head"),
        P("head", None),
        P(None, "head"),
        P("head", None),
        P("head"),
        P(),
        P(),
        P(None, None, "head"),
        P("head", None),
        P("head"),
        P(),
        P(),
    )
    return jax.shard_map(
        on_device,
        mesh=mesh,
        in_specs=placed,
        out_specs=(P("seq", "head", None), P("seq", "head")),
        check_vma=False,
    )
```

time: 282 us -> 148 us (0.52)
  waiting for transfers between devices: 119 us -> 58.7 us
  matrix products: 33.9 us -> 0 us
  local copies, waits for them, and re-layouts: 47 us -> 13.6 us
  blocking collectives: 41.7 us -> 8.81 us
  Pallas kernels: 0 us -> 23.6 us
  starting transfers between devices: 7.12 us -> 30.4 us
  between operations: 15.4 us -> 1.05 us
  other arithmetic: 16.3 us -> 11.1 us
    reduce_scatter x2 -> x0, waiting for transfers between devices: 81.8 us -> none  [the longest x1 68.1 us: on_device(): lax.psum_scatter(partial_sum.reshape(patches, patch_span, model_width), '...]
    ppermute x0 -> x26, waiting for transfers between devices: none -> 58.7 us  [the longest x18 58.7 us: shift(): lax.ppermute(value, axis, [(i, (i + step) % count) for i in range(count)])]
    dot_general x10 -> x0, matrix products: 33.9 us -> none  [the longest x1 8.8 us: on_device(): jnp.dot(activated, mlp_down, preferred_element_type=jnp.float32)]
    ppermute x0 -> x26, starting transfers between devices: none -> 30.4 us  [the longest x18 28.3 us: shift(): lax.ppermute(value, axis, [(i, (i + step) % count) for i in range(count)])]
    all_gather x2 -> x0, waiting for transfers between devices: 29.5 us -> none  [the longest x1 25.4 us: on_device(): lax.all_gather(routed_values, 'seq', axis=0, tiled=True)]
    pallas_call x0 -> x6, Pallas kernels: none -> 23.6 us  [the longest x1 15.2 us: local_part(): pl.pallas_call(functools.partial(local_kernel, span, own), grid=(patches...]
    all_to_all x3 -> x1, blocking collectives: 25.7 us -> 8.81 us  [on_device(): lax.all_to_all(routed, 'seq', split_axis=0, concat_axis=0, tiled=True)]
    all_gather x1 -> x0, blocking collectives: 16.1 us -> none  [on_device(): patch_in = lax.all_gather(own_patch, 'head', axis=1, tiled=True)]
  transfers between devices with their start and end apart: 6 -> 26, of which waited for: 6 -> 10; matrix products, arithmetic and copies ran while one was open for 5% -> 9% of each run, Pallas kernels for 0% -> 4%
where the time goes in v1:
time: 148 us; the launch traced here: 147 us
  waiting for transfers between devices  58.7 us (40%)
  starting transfers between devices  30.4 us (21%)
  Pallas kernels  23.6 us (16%)
  local copies, waits for them, and re-layouts  13.6 us (9%)
  other arithmetic  11.1 us (8%)
  blocking collectives  8.81 us (6%)
    ppermute x18, waiting for transfers between devices, shift(): lax.ppermute(value, axis, [(i, (i + step) % count) for i in range(count)])  58.7 us
    ppermute x18, starting transfers between devices, shift(): lax.ppermute(value, axis, [(i, (i + step) % count) for i in range(count)])  28.3 us
    pallas_call x1, Pallas kernels, local_part(): pl.pallas_call(functools.partial(local_kernel, span, own), grid=(patches...  15.2 us
    add x1, other arithmetic, owner_order(): jnp.repeat(slot, block, total_repeat_length=patches) * block + row % block  10 us
    unnamed x63, local copies, waits for them, and re-layouts  9.93 us
    all_to_all x1, blocking collectives, on_device(): lax.all_to_all(routed, 'seq', split_axis=0, concat_axis=0, tiled=True)  8.81 us
  transfers between devices with their start and end apart: 26, of which 10 were waited for; matrix products, arithmetic and copies ran while one was open for 9% of the time, Pallas kernels for 4%

profile of v1, /device:TPU:0, one launch (start us, length us, event | category | flops | bytes accessed | tf_op | source)
XLA Modules:
  0.0 147.2 jit_solution(18161906095450730557)
XLA Ops:
  0.7 1.4 copy-done.4
  5.5 15.2 %local_part.1 = (bf16[8,128,1024]{2,1,0:T(8,128)(2,1)S(1)}, bf16[4,128,512]{2,1,0:T(8,128)(2,1)S(1)}) custom-call(s32[1]{0:T(128)} %bitcast.17.me_ref, f32[2]{0:T(128)S(1)} %copy-done.11, bf16[1024,1024]{1,0:T(8,128)(2,1)} %bitcast.60, f32[1,1024]{1,0:T(1,128)S(1)} %bitcast.59, bf16[3,1024,256]{2,1,0:T(8,128)(2,1)S(1)} %bitcast.56, ...), custom_call_target="tpu_custom_call" | custom-call | tf_op jit(solution)/shard_map/local_part/pallas_call | solution.py:76
  20.8 3.1 %collective-permute-start = (bf16[128,512]{1,0:T(8,128)(2,1)S(1)}, bf16[128,512]{1,0:T(8,128)(2,1)S(1)}, u32[]{:S(2)}, u32[]{:S(2)}) collective-permute-start(bf16[128,512]{1,0:T(8,128)(2,1)S(1)} %get-tuple-element.40), channel_id=1, source_target_pairs={{0,1},{1,2},{2,3},{3,0},{4,5},{5,6},{6,7},{7,4},{8,9},{9,10},{10,1... | collective-permute-start | bytes 393224 | tf_op jit(solution)/shard_map/ppermute | solution.py:214
  23.8 2.6 %collective-permute-start.1 = (bf16[128,512]{1,0:T(8,128)(2,1)S(1)}, bf16[128,512]{1,0:T(8,128)(2,1)S(1)}, u32[]{:S(2)}, u32[]{:S(2)}) collective-permute-start(bf16[128,512]{1,0:T(8,128)(2,1)S(1)} %get-tuple-element.42), channel_id=1, source_target_pairs={{0,2},{1,3},{2,0},{3,1},{4,6},{5,7},{6,4},{7,5},{8,10},{9,11},{10,... | collective-permute-start | bytes 393224 | tf_op jit(solution)/shard_map/ppermute | solution.py:214
  26.4 1.3 collective-permute-start.2
  27.8 2.5 %collective-permute-done = bf16[128,512]{1,0:T(8,128)(2,1)S(1)} collective-permute-done((bf16[128,512]{1,0:T(8,128)(2,1)S(1)}, bf16[128,512]{1,0:T(8,128)(2,1)S(1)}, u32[]{:S(2)}, u32[]{:S(2)}) %collective-permute-start) | collective-permute-done | bytes 131104 | tf_op jit(solution)/shard_map/ppermute | solution.py:214
  30.3 4.8 %collective-permute-done.1 = bf16[128,512]{1,0:T(8,128)(2,1)S(1)} collective-permute-done((bf16[128,512]{1,0:T(8,128)(2,1)S(1)}, bf16[128,512]{1,0:T(8,128)(2,1)S(1)}, u32[]{:S(2)}, u32[]{:S(2)}) %collective-permute-start.1) | collective-permute-done | bytes 131104 | tf_op jit(solution)/shard_map/ppermute | solution.py:214
  35.2 3.3 %collective-permute-start.3 = (bf16[128,512]{1,0:T(8,128)(2,1)S(1)}, bf16[128,512]{1,0:T(8,128)(2,1)S(1)}, u32[]{:S(2)}, u32[]{:S(2)}) collective-permute-start(bf16[128,512]{1,0:T(8,128)(2,1)S(1)} %fusion.2.refs_0_.own_ref), channel_id=1, source_target_pairs={{0,1},{1,2},{2,3},{3,0},{4,5},{5,6},{6,7},{7,4},{8,9},{9,10},{10,1... | collective-permute-start | bytes 393224 | tf_op jit(solution)/shard_map/ppermute | solution.py:214
  38.5 1.6 %collective-permute-start.4 = (bf16[128,512]{1,0:T(8,128)(2,1)S(1)}, bf16[128,512]{1,0:T(8,128)(2,1)S(1)}, u32[]{:S(2)}, u32[]{:S(2)}) collective-permute-start(bf16[128,512]{1,0:T(8,128)(2,1)S(1)} %fusion.2.refs_0_.own_ref), channel_id=1, source_target_pairs={{0,2},{1,3},{2,0},{3,1},{4,6},{5,7},{6,4},{7,5},{8,10},{9,11},{10,... | collective-permute-start | bytes 393224 | tf_op jit(solution)/shard_map/ppermute | solution.py:214
  41.0 2.7 %collective-permute-done.3.refs_1_ = bf16[128,512]{1,0:T(8,128)(2,1)S(1)} collective-permute-done((bf16[128,512]{1,0:T(8,128)(2,1)S(1)}, bf16[128,512]{1,0:T(8,128)(2,1)S(1)}, u32[]{:S(2)}, u32[]{:S(2)}) %collective-permute-start.3) | collective-permute-done | bytes 131104 | tf_op jit(solution)/shard_map/ppermute | solution.py:214
  43.7 4.5 %collective-permute-done.4.refs_2_ = bf16[128,512]{1,0:T(8,128)(2,1)S(1)} collective-permute-done((bf16[128,512]{1,0:T(8,128)(2,1)S(1)}, bf16[128,512]{1,0:T(8,128)(2,1)S(1)}, u32[]{:S(2)}, u32[]{:S(2)}) %collective-permute-start.4) | collective-permute-done | bytes 131104 | tf_op jit(solution)/shard_map/ppermute | solution.py:214
  48.2 2.8 %copy-done.1 = bf16[2048,3,512]{2,0,1:T(8,128)(2,1)S(1)} copy-done((bf16[2048,3,512]{2,0,1:T(8,128)(2,1)S(1)}, bf16[2048,3,512]{2,0,1:T(8,128)(2,1)}, u32[]{:S(2)}) %copy-start.1) | copy-done | bytes 6291480
  51.0 1.4 global_heads.3
  52.5 1.5 %collective-permute-start.6 = (bf16[128,512]{1,0:T(8,128)(2,1)S(1)}, bf16[128,512]{1,0:T(8,128)(2,1)S(1)}, u32[]{:S(2)}, u32[]{:S(2)}) collective-permute-start(bf16[128,512]{1,0:T(8,128)(2,1)S(1)} %get-tuple-element.27.refs_0_), channel_id=1, source_target_pairs={{0,8},{4,12},{8,16},{12,20},{16,24},{20,28},{24,0},{28,4},{1,9},{5... | collective-permute-start | bytes 393224 | tf_op jit(solution)/shard_map/ppermute | solution.py:214
  54.0 1.5 %collective-permute-start.7 = (bf16[128,512]{1,0:T(8,128)(2,1)S(1)}, bf16[128,512]{1,0:T(8,128)(2,1)S(1)}, u32[]{:S(2)}, u32[]{:S(2)}) collective-permute-start(bf16[128,512]{1,0:T(8,128)(2,1)S(1)} %get-tuple-element.27.refs_0_), channel_id=1, source_target_pairs={{0,16},{4,20},{8,24},{12,28},{16,0},{20,4},{24,8},{28,12},{1,17},{... | collective-permute-start | bytes 393224 | tf_op jit(solution)/shard_map/ppermute | solution.py:214
  55.5 1.4 collective-permute-start.8
  58.3 1.5 %collective-permute-done.6.refs_1_ = bf16[128,512]{1,0:T(8,128)(2,1)S(1)} collective-permute-done((bf16[128,512]{1,0:T(8,128)(2,1)S(1)}, bf16[128,512]{1,0:T(8,128)(2,1)S(1)}, u32[]{:S(2)}, u32[]{:S(2)}) %collective-permute-start.6) | collective-permute-done | bytes 131104 | tf_op jit(solution)/shard_map/ppermute | solution.py:214
  59.8 1.5 %collective-permute-start.15 = (bf16[128,512]{1,0:T(8,128)(2,1)S(1)}, bf16[128,512]{1,0:T(8,128)(2,1)S(1)}, u32[]{:S(2)}, u32[]{:S(2)}) collective-permute-start(bf16[128,512]{1,0:T(8,128)(2,1)S(1)} %get-tuple-element.28.refs_8_), channel_id=1, source_target_pairs={{0,24},{4,28},{8,0},{12,4},{16,8},{20,12},{24,16},{28,20},{1,25},{... | collective-permute-start | bytes 393224 | tf_op jit(solution)/shard_map/ppermute | solution.py:214
  61.4 1.4 collective-permute-done.7.refs_2_
  63.2 2.2 %collective-permute-done.13.refs_9_ = bf16[128,512]{1,0:T(8,128)(2,1)S(1)} collective-permute-done((bf16[128,512]{1,0:T(8,128)(2,1)S(1)}, bf16[128,512]{1,0:T(8,128)(2,1)S(1)}, u32[]{:S(2)}, u32[]{:S(2)}) %collective-permute-start.13) | collective-permute-done | bytes 131104 | tf_op jit(solution)/shard_map/ppermute | solution.py:214
  66.2 1.3 global_heads.2.q_ref
  69.1 1.2 dynamic-slice_bitcast_fusion
  70.3 3.3 %collective-permute-start.23 = (bf16[256,1024]{1,0:T(8,128)(2,1)}, bf16[256,1024]{1,0:T(8,128)(2,1)S(1)}, u32[]{:S(2)}, u32[]{:S(2)}) collective-permute-start(bf16[256,1024]{1,0:T(8,128)(2,1)} %get-tuple-element.34), channel_id=1, source_target_pairs={{0,1},{1,2},{2,3},{3,0},{4,5},{5,6},{6,7},{7,4},{8,9},{9,10},{10,1... | collective-permute-start | bytes 1572872 | tf_op jit(solution)/shard_map/ppermute | solution.py:214
  73.6 2.0 %collective-permute-start.24 = (bf16[256,1024]{1,0:T(8,128)(2,1)}, bf16[256,1024]{1,0:T(8,128)(2,1)S(1)}, u32[]{:S(2)}, u32[]{:S(2)}) collective-permute-start(bf16[256,1024]{1,0:T(8,128)(2,1)} %get-tuple-element.33), channel_id=1, source_target_pairs={{0,2},{1,3},{2,0},{3,1},{4,6},{5,7},{6,4},{7,5},{8,10},{9,11},{10,... | collective-permute-start | bytes 1572872 | tf_op jit(solution)/shard_map/ppermute | solution.py:214
  76.3 2.9 %attend.1 = bf16[4,128,512]{2,1,0:T(8,128)(2,1)S(1)} custom-call(s32[8]{0:T(128)S(1)} %pad_add_fusion.ids_ref, f32[4]{0:T(128)S(1)} %copy-done.12, bf16[128,512]{1,0:T(8,128)(2,1)S(1)} %global_heads.2.q_ref, bf16[128,512]{1,0:T(8,128)(2,1)S(1)} %get-tuple-element.27.refs_0_, bf16[128,512]{1,0:T(8,128)(2,1)S(1)} %collective-permute-done.6.refs_1_, ...), custom_call_target="tpu_custom_call" | custom-call | tf_op jit(solution)/shard_map/attend/pallas_call | solution.py:156
  79.9 1.6 %collective-permute-start.20 = (bf16[128,512]{1,0:T(8,128)(2,1)S(1)}, bf16[128,512]{1,0:T(8,128)(2,1)S(1)}, u32[]{:S(2)}, u32[]{:S(2)}) collective-permute-start(bf16[128,512]{1,0:T(8,128)(2,1)S(1)} %get-tuple-element.38), channel_id=1, source_target_pairs={{0,1},{1,2},{2,3},{3,0},{4,5},{5,6},{6,7},{7,4},{8,9},{9,10},{10,1... | collective-permute-start | bytes 393224 | tf_op jit(solution)/shard_map/ppermute | solution.py:214
  81.6 10.0 %fusion.6 = s32[128]{0:T(128)S(1)} fusion(pred[128]{0:T(512)(128)(4,1)S(1)} %copy-done.16, pred[128]{0:T(512)(128)(4,1)S(1)} %copy-done.17, pred[128]{0:T(512)(128)(4,1)S(1)} %copy-done.18, pred[128]{0:T(512)(128)(4,1)S(1)} %copy-done.19, pred[128]{0:T(512)(128)(4,1)S(1)} %copy-done.20, pred[128]{0:T(512)(128)(4,1)S(1)} %copy-done.21, ...), kind=kLoop, calls=%fused_computation.29 | loop fusion | flops 2944 | bytes 2496 | tf_op jit(solution)/shard_map/add | solution.py:252
  92.7 20.7 %collective-permute-done.20.refs_1_ = bf16[128,512]{1,0:T(8,128)(2,1)S(1)} collective-permute-done((bf16[128,512]{1,0:T(8,128)(2,1)S(1)}, bf16[128,512]{1,0:T(8,128)(2,1)S(1)}, u32[]{:S(2)}, u32[]{:S(2)}) %collective-permute-start.20) | collective-permute-done | bytes 131104 | tf_op jit(solution)/shard_map/ppermute | solution.py:214
  114.1 15.6 %collective-permute-done.21.refs_2_ = bf16[128,512]{1,0:T(8,128)(2,1)S(1)} collective-permute-done((bf16[128,512]{1,0:T(8,128)(2,1)S(1)}, bf16[128,512]{1,0:T(8,128)(2,1)S(1)}, u32[]{:S(2)}, u32[]{:S(2)}) %collective-permute-start.21) | collective-permute-done | bytes 131104 | tf_op jit(solution)/shard_map/ppermute | solution.py:214
  129.7 2.7 %collective-permute-done.22.refs_3_ = bf16[128,512]{1,0:T(8,128)(2,1)S(1)} collective-permute-done((bf16[128,512]{1,0:T(8,128)(2,1)S(1)}, bf16[128,512]{1,0:T(8,128)(2,1)S(1)}, u32[]{:S(2)}, u32[]{:S(2)}) %collective-permute-start.22) | collective-permute-done | bytes 131104 | tf_op jit(solution)/shard_map/ppermute | solution.py:214
  133.0 2.1 %finish_result.1 = (bf16[128,512]{1,0:T(8,128)(2,1)}, bf16[128,512]{1,0:T(8,128)(2,1)}) custom-call(bf16[128,128]{1,0:T(8,128)(2,1)} %fusion.3.order_ref, bf16[128,512]{1,0:T(8,128)(2,1)} %copy-done.2, bf16[128,512]{1,0:T(8,128)(2,1)} %get-tuple-element.39.refs_0_, bf16[128,512]{1,0:T(8,128)(2,1)} %copy-done.13, bf16[128,512]{1,0:T(8,128)(2,1)} %copy-done.14, ...), custom_call_target="tpu_custom_call" | custom-call | tf_op jit(solution)/shard_map/finish_result/pallas_call | solution.py:176
  135.1 8.8 %all_to_all.12 = bf16[8,16,512]{2,1,0:T(8,128)(2,1)S(1)} all-to-all(bf16[8,16,512]{2,1,0:T(8,128)(2,1)} %bitcast.62), channel_id=1, replica_groups=mesh['seq'=8,'head'=4] {'seq'}, dimensions={0} | all-to-all | bytes 262144 | tf_op jit(solution)/shard_map/all_to_all | solution.py:308
  (103 shorter events, 15.6 us)
Async XLA Ops:
  0.6 56.9 %copy-start = (s32[8,16]{1,0:T(8,128)S(1)}, s32[8,16]{1,0:T(8,128)}, u32[]{:S(2)}) copy-start(s32[8,16]{1,0:T(8,128)} %param.29) | copy-start | bytes 1540
  5.5 42.7 %copy-start.9 = (f32[2048]{0:T(1024)S(1)}, f32[2048]{0:T(1024)}, u32[]{:S(2)}) copy-start(f32[2048]{0:T(1024)} %param.24) | copy-start | bytes 24580
  20.8 9.5 %collective-permute-start = (bf16[128,512]{1,0:T(8,128)(2,1)S(1)}, bf16[128,512]{1,0:T(8,128)(2,1)S(1)}, u32[]{:S(2)}, u32[]{:S(2)}) collective-permute-start(bf16[128,512]{1,0:T(8,128)(2,1)S(1)} %get-tuple-element.40), channel_id=1, source_target_pairs={{0,1},{1,2},{2,3},{3,0},{4,5},{5,6},{6,7},{7,4},{8,9},{9,10},{10,1... | collective-permute-start | bytes 393224 | tf_op jit(solution)/shard_map/ppermute | solution.py:214
  23.8 11.2 %collective-permute-start.1 = (bf16[128,512]{1,0:T(8,128)(2,1)S(1)}, bf16[128,512]{1,0:T(8,128)(2,1)S(1)}, u32[]{:S(2)}, u32[]{:S(2)}) collective-permute-start(bf16[128,512]{1,0:T(8,128)(2,1)S(1)} %get-tuple-element.42), channel_id=1, source_target_pairs={{0,2},{1,3},{2,0},{3,1},{4,6},{5,7},{6,4},{7,5},{8,10},{9,11},{10,... | collective-permute-start | bytes 393224 | tf_op jit(solution)/shard_map/ppermute | solution.py:214
  26.4 8.6 %collective-permute-start.2 = (bf16[128,512]{1,0:T(8,128)(2,1)S(1)}, bf16[128,512]{1,0:T(8,128)(2,1)S(1)}, u32[]{:S(2)}, u32[]{:S(2)}) collective-permute-start(bf16[128,512]{1,0:T(8,128)(2,1)S(1)} %get-tuple-element.41), channel_id=1, source_target_pairs={{0,3},{1,0},{2,1},{3,2},{4,7},{5,4},{6,5},{7,6},{8,11},{9,8},{10,9... | collective-permute-start | bytes 393224 | tf_op jit(solution)/shard_map/ppermute | solution.py:214
  35.2 31.1 %copy-start.2 = (bf16[128,512]{1,0:T(8,128)(2,1)}, bf16[128,512]{1,0:T(8,128)(2,1)S(1)}, u32[]{:S(2)}) copy-start(bf16[128,512]{1,0:T(8,128)(2,1)S(1)} %fusion.2.refs_0_.own_ref) | copy-start | bytes 393220
  35.2 8.5 %collective-permute-start.3 = (bf16[128,512]{1,0:T(8,128)(2,1)S(1)}, bf16[128,512]{1,0:T(8,128)(2,1)S(1)}, u32[]{:S(2)}, u32[]{:S(2)}) collective-permute-start(bf16[128,512]{1,0:T(8,128)(2,1)S(1)} %fusion.2.refs_0_.own_ref), channel_id=1, source_target_pairs={{0,1},{1,2},{2,3},{3,0},{4,5},{5,6},{6,7},{7,4},{8,9},{9,10},{10,1... | collective-permute-start | bytes 393224 | tf_op jit(solution)/shard_map/ppermute | solution.py:214
  38.5 9.7 %collective-permute-start.4 = (bf16[128,512]{1,0:T(8,128)(2,1)S(1)}, bf16[128,512]{1,0:T(8,128)(2,1)S(1)}, u32[]{:S(2)}, u32[]{:S(2)}) collective-permute-start(bf16[128,512]{1,0:T(8,128)(2,1)S(1)} %fusion.2.refs_0_.own_ref), channel_id=1, source_target_pairs={{0,2},{1,3},{2,0},{3,1},{4,6},{5,7},{6,4},{7,5},{8,10},{9,11},{10,... | collective-permute-start | bytes 393224 | tf_op jit(solution)/shard_map/ppermute | solution.py:214
  40.1 8.1 %collective-permute-start.5 = (bf16[128,512]{1,0:T(8,128)(2,1)S(1)}, bf16[128,512]{1,0:T(8,128)(2,1)S(1)}, u32[]{:S(2)}, u32[]{:S(2)}) collective-permute-start(bf16[128,512]{1,0:T(8,128)(2,1)S(1)} %fusion.2.refs_0_.own_ref), channel_id=1, source_target_pairs={{0,3},{1,0},{2,1},{3,2},{4,7},{5,4},{6,5},{7,6},{8,11},{9,8},{10,9... | collective-permute-start | bytes 393224 | tf_op jit(solution)/shard_map/ppermute | solution.py:214
  52.5 7.3 %collective-permute-start.6 = (bf16[128,512]{1,0:T(8,128)(2,1)S(1)}, bf16[128,512]{1,0:T(8,128)(2,1)S(1)}, u32[]{:S(2)}, u32[]{:S(2)}) collective-permute-start(bf16[128,512]{1,0:T(8,128)(2,1)S(1)} %get-tuple-element.27.refs_0_), channel_id=1, source_target_pairs={{0,8},{4,12},{8,16},{12,20},{16,24},{20,28},{24,0},{28,4},{1,9},{5... | collective-permute-start | bytes 393224 | tf_op jit(solution)/shard_map/ppermute | solution.py:214
  54.0 8.7 %collective-permute-start.7 = (bf16[128,512]{1,0:T(8,128)(2,1)S(1)}, bf16[128,512]{1,0:T(8,128)(2,1)S(1)}, u32[]{:S(2)}, u32[]{:S(2)}) collective-permute-start(bf16[128,512]{1,0:T(8,128)(2,1)S(1)} %get-tuple-element.27.refs_0_), channel_id=1, source_target_pairs={{0,16},{4,20},{8,24},{12,28},{16,0},{20,4},{24,8},{28,12},{1,17},{... | collective-permute-start | bytes 393224 | tf_op jit(solution)/shard_map/ppermute | solution.py:214
  55.5 7.2 %collective-permute-start.8 = (bf16[128,512]{1,0:T(8,128)(2,1)S(1)}, bf16[128,512]{1,0:T(8,128)(2,1)S(1)}, u32[]{:S(2)}, u32[]{:S(2)}) collective-permute-start(bf16[128,512]{1,0:T(8,128)(2,1)S(1)} %get-tuple-element.27.refs_0_), channel_id=1, source_target_pairs={{0,24},{4,28},{8,0},{12,4},{16,8},{20,12},{24,16},{28,20},{1,25},{... | collective-permute-start | bytes 393224 | tf_op jit(solution)/shard_map/ppermute | solution.py:214
  57.0 8.5 %collective-permute-start.13 = (bf16[128,512]{1,0:T(8,128)(2,1)S(1)}, bf16[128,512]{1,0:T(8,128)(2,1)S(1)}, u32[]{:S(2)}, u32[]{:S(2)}) collective-permute-start(bf16[128,512]{1,0:T(8,128)(2,1)S(1)} %get-tuple-element.28.refs_8_), channel_id=1, source_target_pairs={{0,8},{4,12},{8,16},{12,20},{16,24},{20,28},{24,0},{28,4},{1,9},{5... | collective-permute-start | bytes 393224 | tf_op jit(solution)/shard_map/ppermute | solution.py:214
  57.8 9.7 %collective-permute-start.14 = (bf16[128,512]{1,0:T(8,128)(2,1)S(1)}, bf16[128,512]{1,0:T(8,128)(2,1)S(1)}, u32[]{:S(2)}, u32[]{:S(2)}) collective-permute-start(bf16[128,512]{1,0:T(8,128)(2,1)S(1)} %get-tuple-element.28.refs_8_), channel_id=1, source_target_pairs={{0,16},{4,20},{8,24},{12,28},{16,0},{20,4},{24,8},{28,12},{1,17},{... | collective-permute-start | bytes 393224 | tf_op jit(solution)/shard_map/ppermute | solution.py:214
  59.8 8.3 %collective-permute-start.15 = (bf16[128,512]{1,0:T(8,128)(2,1)S(1)}, bf16[128,512]{1,0:T(8,128)(2,1)S(1)}, u32[]{:S(2)}, u32[]{:S(2)}) collective-permute-start(bf16[128,512]{1,0:T(8,128)(2,1)S(1)} %get-tuple-element.28.refs_8_), channel_id=1, source_target_pairs={{0,24},{4,28},{8,0},{12,4},{16,8},{20,12},{24,16},{28,20},{1,25},{... | collective-permute-start | bytes 393224 | tf_op jit(solution)/shard_map/ppermute | solution.py:214
  62.7 5.4 %collective-permute-start.16 = (bf16[128,512]{1,0:T(8,128)(2,1)S(1)}, bf16[128,512]{1,0:T(8,128)(2,1)S(1)}, u32[]{:S(2)}, u32[]{:S(2)}) collective-permute-start(bf16[128,512]{1,0:T(8,128)(2,1)S(1)} %get-tuple-element.28.refs_8_), channel_id=1, source_target_pairs={{0,4},{4,0},{8,12},{12,8},{16,20},{20,16},{24,28},{28,24},{1,5},{5... | collective-permute-start | bytes 393224 | tf_op jit(solution)/shard_map/ppermute | solution.py:232
  62.7 5.9 %collective-permute-start.9 = (bf16[128,512]{1,0:T(8,128)(2,1)S(1)}, bf16[128,512]{1,0:T(8,128)(2,1)S(1)}, u32[]{:S(2)}, u32[]{:S(2)}) collective-permute-start(bf16[128,512]{1,0:T(8,128)(2,1)S(1)} %get-tuple-element.27.refs_0_), channel_id=1, source_target_pairs={{0,4},{4,0},{8,12},{12,8},{16,20},{20,16},{24,28},{28,24},{1,5},{5... | collective-permute-start | bytes 393224 | tf_op jit(solution)/shard_map/ppermute | solution.py:232
  65.4 3.2 %collective-permute-start.10 = (bf16[128,512]{1,0:T(8,128)(2,1)S(1)}, bf16[128,512]{1,0:T(8,128)(2,1)S(1)}, u32[]{:S(2)}, u32[]{:S(2)}) collective-permute-start(bf16[128,512]{1,0:T(8,128)(2,1)S(1)} %collective-permute-done.6.refs_1_), channel_id=1, source_target_pairs={{0,4},{4,0},{8,12},{12,8},{16,20},{20,16},{24,28},{28,24},{1,5},{5... | collective-permute-start | bytes 393224 | tf_op jit(solution)/shard_map/ppermute | solution.py:232
  67.5 2.8 %collective-permute-start.11 = (bf16[128,512]{1,0:T(8,128)(2,1)S(1)}, bf16[128,512]{1,0:T(8,128)(2,1)S(1)}, u32[]{:S(2)}, u32[]{:S(2)}) collective-permute-start(bf16[128,512]{1,0:T(8,128)(2,1)S(1)} %collective-permute-done.7.refs_2_), channel_id=1, source_target_pairs={{0,4},{4,0},{8,12},{12,8},{16,20},{20,16},{24,28},{28,24},{1,5},{5... | collective-permute-start | bytes 393224 | tf_op jit(solution)/shard_map/ppermute | solution.py:232
  68.1 5.5 %collective-permute-start.12 = (bf16[128,512]{1,0:T(8,128)(2,1)S(1)}, bf16[128,512]{1,0:T(8,128)(2,1)S(1)}, u32[]{:S(2)}, u32[]{:S(2)}) collective-permute-start(bf16[128,512]{1,0:T(8,128)(2,1)S(1)} %collective-permute-done.8.refs_3_), channel_id=1, source_target_pairs={{0,4},{4,0},{8,12},{12,8},{16,20},{20,16},{24,28},{28,24},{1,5},{5... | collective-permute-start | bytes 393224 | tf_op jit(solution)/shard_map/ppermute | solution.py:232
  68.2 7.4 %collective-permute-start.17 = (bf16[128,512]{1,0:T(8,128)(2,1)S(1)}, bf16[128,512]{1,0:T(8,128)(2,1)S(1)}, u32[]{:S(2)}, u32[]{:S(2)}) collective-permute-start(bf16[128,512]{1,0:T(8,128)(2,1)S(1)} %collective-permute-done.13.refs_9_), channel_id=1, source_target_pairs={{0,4},{4,0},{8,12},{12,8},{16,20},{20,16},{24,28},{28,24},{1,5},{5... | collective-permute-start | bytes 393224 | tf_op jit(solution)/shard_map/ppermute | solution.py:232
  68.6 7.7 %collective-permute-start.18 = (bf16[128,512]{1,0:T(8,128)(2,1)S(1)}, bf16[128,512]{1,0:T(8,128)(2,1)S(1)}, u32[]{:S(2)}, u32[]{:S(2)}) collective-permute-start(bf16[128,512]{1,0:T(8,128)(2,1)S(1)} %collective-permute-done.14.refs_10_), channel_id=1, source_target_pairs={{0,4},{4,0},{8,12},{12,8},{16,20},{20,16},{24,28},{28,24},{1,5},{5... | collective-permute-start | bytes 393224 | tf_op jit(solution)/shard_map/ppermute | solution.py:232
  68.7 7.6 %collective-permute-start.19 = (bf16[128,512]{1,0:T(8,128)(2,1)S(1)}, bf16[128,512]{1,0:T(8,128)(2,1)S(1)}, u32[]{:S(2)}, u32[]{:S(2)}) collective-permute-start(bf16[128,512]{1,0:T(8,128)(2,1)S(1)} %collective-permute-done.15.refs_11_), channel_id=1, source_target_pairs={{0,4},{4,0},{8,12},{12,8},{16,20},{20,16},{24,28},{28,24},{1,5},{5... | collective-permute-start | bytes 393224 | tf_op jit(solution)/shard_map/ppermute | solution.py:232
  69.1 7.1 %copy-start.12 = (f32[4]{0:T(128)S(1)}, f32[4]{0:T(128)}, u32[]{:S(2)}) copy-start(f32[4]{0:T(128)} %scale_ref.3) | copy-start | bytes 52
  70.3 73.6 %collective-permute-start.23 = (bf16[256,1024]{1,0:T(8,128)(2,1)}, bf16[256,1024]{1,0:T(8,128)(2,1)S(1)}, u32[]{:S(2)}, u32[]{:S(2)}) collective-permute-start(bf16[256,1024]{1,0:T(8,128)(2,1)} %get-tuple-element.34), channel_id=1, source_target_pairs={{0,1},{1,2},{2,3},{3,0},{4,5},{5,6},{6,7},{7,4},{8,9},{9,10},{10,1... | collective-permute-start | bytes 1572872 | tf_op jit(solution)/shard_map/ppermute | solution.py:214
  73.6 70.3 %collective-permute-start.24 = (bf16[256,1024]{1,0:T(8,128)(2,1)}, bf16[256,1024]{1,0:T(8,128)(2,1)S(1)}, u32[]{:S(2)}, u32[]{:S(2)}) collective-permute-start(bf16[256,1024]{1,0:T(8,128)(2,1)} %get-tuple-element.33), channel_id=1, source_target_pairs={{0,2},{1,3},{2,0},{3,1},{4,6},{5,7},{6,4},{7,5},{8,10},{9,11},{10,... | collective-permute-start | bytes 1572872 | tf_op jit(solution)/shard_map/ppermute | solution.py:214
  75.7 68.2 %collective-permute-start.25 = (bf16[256,1024]{1,0:T(8,128)(2,1)}, bf16[256,1024]{1,0:T(8,128)(2,1)S(1)}, u32[]{:S(2)}, u32[]{:S(2)}) collective-permute-start(bf16[256,1024]{1,0:T(8,128)(2,1)} %get-tuple-element.32), channel_id=1, source_target_pairs={{0,3},{1,0},{2,1},{3,2},{4,7},{5,4},{6,5},{7,6},{8,11},{9,8},{10,9... | collective-permute-start | bytes 1572872 | tf_op jit(solution)/shard_map/ppermute | solution.py:214
  79.2 64.7 %copy-start.7 = (bf16[256,1024]{1,0:T(8,128)(2,1)S(1)}, bf16[256,1024]{1,0:T(8,128)(2,1)}, u32[]{:S(2)}) copy-start(bf16[256,1024]{1,0:T(8,128)(2,1)} %proj_ref.3) | copy-start | bytes 1572868
  79.9 33.5 %collective-permute-start.20 = (bf16[128,512]{1,0:T(8,128)(2,1)S(1)}, bf16[128,512]{1,0:T(8,128)(2,1)S(1)}, u32[]{:S(2)}, u32[]{:S(2)}) collective-permute-start(bf16[128,512]{1,0:T(8,128)(2,1)S(1)} %get-tuple-element.38), channel_id=1, source_target_pairs={{0,1},{1,2},{2,3},{3,0},{4,5},{5,6},{6,7},{7,4},{8,9},{9,10},{10,1... | collective-permute-start | bytes 393224 | tf_op jit(solution)/shard_map/ppermute | solution.py:214
  91.7 38.0 %collective-permute-start.21 = (bf16[128,512]{1,0:T(8,128)(2,1)S(1)}, bf16[128,512]{1,0:T(8,128)(2,1)S(1)}, u32[]{:S(2)}, u32[]{:S(2)}) collective-permute-start(bf16[128,512]{1,0:T(8,128)(2,1)S(1)} %get-tuple-element.37), channel_id=1, source_target_pairs={{0,2},{1,3},{2,0},{3,1},{4,6},{5,7},{6,4},{7,5},{8,10},{9,11},{10,... | collective-permute-start | bytes 393224 | tf_op jit(solution)/shard_map/ppermute | solution.py:214
  113.4 19.0 %copy-start.13 = (bf16[128,512]{1,0:T(8,128)(2,1)}, bf16[128,512]{1,0:T(8,128)(2,1)S(1)}, u32[]{:S(2)}) copy-start(bf16[128,512]{1,0:T(8,128)(2,1)S(1)} %collective-permute-done.20.refs_1_) | copy-start | bytes 393220
  113.4 19.0 %collective-permute-start.22 = (bf16[128,512]{1,0:T(8,128)(2,1)S(1)}, bf16[128,512]{1,0:T(8,128)(2,1)S(1)}, u32[]{:S(2)}, u32[]{:S(2)}) collective-permute-start(bf16[128,512]{1,0:T(8,128)(2,1)S(1)} %get-tuple-element.36), channel_id=1, source_target_pairs={{0,3},{1,0},{2,1},{3,2},{4,7},{5,4},{6,5},{7,6},{8,11},{9,8},{10,9... | collective-permute-start | bytes 393224 | tf_op jit(solution)/shard_map/ppermute | solution.py:214
  (25 other events, 107.7 us)

commit v2 on v1

--- a/solution.py
+++ b/solution.py
@@ -13,6 +13,7 @@
 F32 = jnp.float32
 BF16 = jnp.bfloat16
 VMEM = pl.BlockSpec(memory_space=pltpu.VMEM)
+HBM = pl.BlockSpec(memory_space=pltpu.HBM)
 SMEM = pl.BlockSpec(memory_space=pltpu.SMEM)
 
 
@@ -33,9 +34,23 @@
     return 0.5 * values * (1.0 + jnp.tanh(inner))
 
 
-def local_kernel(
-    span, own, me_ref, scale_ref, x_ref, gain_ref, qkv_ref, out_ref, up_ref, down_ref, proj_ref, part_ref, share_ref
-):
+def local_kernel(span, own, me_ref, scale_ref, x_ref, gain_ref, *refs):
+    sources, (part_ref, share_ref), held, sems = refs[:5], refs[5:7], refs[7:12], refs[12]
+    copies = [pltpu.make_async_copy(s, h, sems.at[i]) for i, (s, h) in enumerate(zip(sources, held))]
+    first = pl.program_id(0) == 0
+
+    @pl.when(first)
+    def _():
+        for copy in copies:
+            copy.start()
+
+    def arrived(i):
+        @pl.when(first)
+        def _():
+            copies[i].wait()
+
+        return held[i]
+
     rows = x_ref.shape[0]
     group = rows // span
     at = lax.broadcasted_iota(jnp.int32, (rows, rows), 0)
@@ -45,6 +60,7 @@
     normed = (
         x * lax.rsqrt(jnp.mean(x * x, axis=-1, keepdims=True) + EPSILON) * gain_ref[...]
     ).astype(BF16)
+    qkv_ref = arrived(0)
     query, key, value = (dot(normed, qkv_ref[i]) for i in range(3))
     seen = (at % group == to % group) & (to <= at)
     heads = scale_ref.shape[0]
@@ -57,12 +73,12 @@
         weights = jnp.exp(scores - jnp.max(scores, axis=-1, keepdims=True))
         total = jnp.sum(weights, axis=-1, keepdims=True)
         attended.append((dot(weights.astype(BF16), value[:, cut].astype(BF16)) / total).astype(BF16))
-    act = gelu(dot(normed, up_ref[...])).astype(BF16)
-    partial = dot(jnp.concatenate(attended, axis=1), out_ref[...]) + dot(act, down_ref[...])
+    act = gelu(dot(normed, arrived(1)[...])).astype(BF16)
+    partial = dot(jnp.concatenate(attended, axis=1), arrived(2)[...]) + dot(act, arrived(3)[...])
     byte = lax.broadcasted_iota(jnp.int32, (rows, 1), 0) // group
     partial = (partial + jnp.where(byte // own == me_ref[0], x, 0.0)).astype(BF16)
     part_ref[...] = partial.reshape(part_ref.shape)
-    share = dot(partial, proj_ref[...]).astype(BF16)
+    share = dot(partial, arrived(4)[...]).astype(BF16)
     width = share.shape[1]
     for b in range(span):
         share_ref[b // own, :, (b % own) * width : (b % own + 1) * width] = share[b * group : (b + 1) * group]
@@ -72,12 +88,13 @@
     rows, width = x.shape
     patches = rows // span
     own = span // ways
-    once = lambda a: pl.BlockSpec(a.shape, lambda i: (0,) * a.ndim, pipeline_mode=pl.Buffered(1))
+    weights = (qkv, up, out, down, proj)
     return pl.pallas_call(
         functools.partial(local_kernel, span, own),
         grid=(patches // group,),
         in_specs=[SMEM, SMEM, pl.BlockSpec((group * span, width), lambda i: (i, 0))]
-        + [once(a) for a in (gain, qkv, out, up, down, proj)],
+        + [pl.BlockSpec(gain.shape, lambda i: (0, 0))]
+        + [HBM] * len(weights),
         out_specs=(
             pl.BlockSpec((span, group, width), lambda i: (0, i, 0)),
             pl.BlockSpec((ways, group, own * proj.shape[1]), lambda i: (0, i, 0)),
@@ -86,52 +103,52 @@
             jax.ShapeDtypeStruct((span, patches, width), BF16),
             jax.ShapeDtypeStruct((ways, patches, own * proj.shape[1]), BF16),
         ),
-        compiler_params=pltpu.CompilerParams(vmem_limit_bytes=48 * 2**20),
+        scratch_shapes=[pltpu.VMEM(w.shape, w.dtype) for w in weights] + [pltpu.SemaphoreType.DMA((len(weights),))],
+        compiler_params=pltpu.CompilerParams(vmem_limit_bytes=36 * 2**20),
         name="local_part",
-    )(me, scale, x, gain, qkv, out, up, down, proj)
+    )(me, scale, x, gain, *weights)
 
 
 def heads_kernel(kinds, depth, ids_ref, gain_ref, *refs):
     ways = gain_ref.shape[0]
-    shares, weights, outs = refs[:ways], refs[ways : ways + len(kinds)], refs[ways + len(kinds) :]
+    shares, weights, out = refs[:ways], refs[ways : ways + len(kinds)], refs[-1]
     width = shares[0].shape[1]
     values = [s[...].astype(F32) for s in shares]
     square = sum(jnp.sum(v * v, axis=-1, keepdims=True) for v in values)
     factor = lax.rsqrt(square / (ways * width) + EPSILON)
     normed = [(v * factor * gain_ref[ids_ref[c]]).astype(BF16) for c, v in enumerate(values)]
-    for kind, weight, out in zip(kinds, weights, outs):
+    for i, (kind, weight) in enumerate(zip(kinds, weights)):
         mixed = sum(
             dot(n, weight[0, pl.ds(pl.multiple_of(ids_ref[c] * width, width), width), :]) for c, n in enumerate(normed)
         )
+        size = mixed.shape[1]
         if kind < 2:
-            for h in range(mixed.shape[1] // depth):
-                out[:, h * depth : (h + 1) * depth] = unit(mixed[:, h * depth : (h + 1) * depth])
-        else:
-            out[...] = mixed.astype(BF16)
+            mixed = jnp.concatenate([unit(mixed[:, c : c + depth]) for c in range(0, size, depth)], axis=1)
+        out[:, i * size : (i + 1) * size] = mixed.astype(BF16)
 
 
 def global_heads(kinds, depth, ids, gain, shares, qkv):
-    shape = jax.ShapeDtypeStruct((shares[0].shape[0], qkv.shape[2]), BF16)
+    shape = jax.ShapeDtypeStruct((shares[0].shape[0], len(kinds) * qkv.shape[2]), BF16)
     pick = lambda kind: pl.BlockSpec((1,) + qkv.shape[1:], lambda i: (kind, 0, 0), pipeline_mode=pl.Buffered(1))
     whole = lambda a: pl.BlockSpec(a.shape, lambda i: (0,) * a.ndim)
     return pl.pallas_call(
         functools.partial(heads_kernel, kinds, depth),
         grid=(1,),
         in_specs=[SMEM, whole(gain)] + [whole(s) for s in shares] + [pick(kind) for kind in kinds],
-        out_specs=tuple(whole(shape) for _ in kinds),
-        out_shape=tuple(shape for _ in kinds),
+        out_specs=whole(shape),
+        out_shape=shape,
         compiler_params=pltpu.CompilerParams(vmem_limit_bytes=16 * 2**20),
         name="global_heads",
     )(ids, gain, *shares, *([qkv] * len(kinds)))
 
 
 def attend_kernel(count, ids_ref, scale_ref, q_ref, *refs):
-    keys, values, (proj_ref, out_ref) = refs[:count], refs[count : 2 * count], refs[2 * count :]
-    rows = q_ref.shape[0]
+    pieces, (proj_ref, out_ref) = refs[:count], refs[count:]
+    rows, size = q_ref.shape
     at = lax.broadcasted_iota(jnp.int32, (rows, rows), 0)
     to = lax.broadcasted_iota(jnp.int32, (rows, rows), 1)
     heads = scale_ref.shape[0]
-    depth = q_ref.shape[1] // heads
+    depth = size // heads
     me = ids_ref[0]
     seen = [to + ids_ref[i] * rows <= at + me * rows for i in range(count)]
     attended = []
@@ -139,11 +156,12 @@
         cut = slice(h * depth, (h + 1) * depth)
         query = q_ref[:, cut]
         factor = scale_ref[h] / math.sqrt(depth)
-        scores = [jnp.where(s, dot_t(query, k[:, cut]) * factor, NEGATIVE) for s, k in zip(seen, keys)]
+        scores = [jnp.where(s, dot_t(query, p[:, cut]) * factor, NEGATIVE) for s, p in zip(seen, pieces)]
         top = functools.reduce(jnp.maximum, [jnp.max(s, axis=-1, keepdims=True) for s in scores])
         weights = [jnp.exp(s - top) for s in scores]
         total = sum(jnp.sum(w, axis=-1, keepdims=True) for w in weights)
-        summed = sum(dot(w.astype(BF16), v[:, cut]) for w, v in zip(weights, values))
+        cut = slice(size + h * depth, size + (h + 1) * depth)
+        summed = sum(dot(w.astype(BF16), p[:, cut]) for w, p in zip(weights, pieces))
         attended.append((summed / total).astype(BF16))
     update = dot(jnp.concatenate(attended, axis=1), proj_ref[...]).astype(BF16)
     width = out_ref.shape[2]
@@ -151,16 +169,16 @@
         out_ref[c] = update[:, c * width : (c + 1) * width]
 
 
-def attend(ids, scale, query, keys, values, proj, ways):
+def attend(ids, scale, query, pieces, proj, ways):
     rows = query.shape[0]
     return pl.pallas_call(
-        functools.partial(attend_kernel, len(keys)),
-        in_specs=[SMEM, SMEM] + [VMEM] * (2 + 2 * len(keys)),
+        functools.partial(attend_kernel, len(pieces)),
+        in_specs=[SMEM, SMEM] + [VMEM] * (2 + len(pieces)),
         out_specs=VMEM,
         out_shape=jax.ShapeDtypeStruct((ways, rows, proj.shape[1] // ways), BF16),
         compiler_params=pltpu.CompilerParams(vmem_limit_bytes=40 * 2**20),
         name="attend",
-    )(ids, scale, query, *keys, *values, proj)
+    )(ids, scale, query, *pieces, proj)
 
 
 def result_kernel(count, order_ref, own_ref, *refs):
@@ -182,9 +200,12 @@
     )(order, residual, *pieces)
 
 
-def bytes_kernel(count, result_ref, proj_ref, *refs):
+def bytes_kernel(count, kept_ref, result_ref, proj_ref, *refs):
     pieces, out_ref = refs[:count], refs[count]
-    state = sum(p[...].astype(F32) for p in pieces).astype(BF16).astype(F32)
+    state = pieces[0][...].astype(F32)
+    for i, p in enumerate(pieces[1:], 1):
+        state += jnp.where(kept_ref[i] != 0, p[...].astype(F32), 0.0)
+    state = state.astype(BF16).astype(F32)
     rows = result_ref.shape[0]
     width = proj_ref.shape[0]
     own = state.shape[0] // rows
@@ -198,15 +219,15 @@
     out_ref[...] = dot(order, jnp.concatenate(mixed, axis=0)).astype(BF16)
 
 
-def finish_bytes(result, proj, pieces):
+def finish_bytes(kept, result, proj, pieces):
     return pl.pallas_call(
         functools.partial(bytes_kernel, len(pieces)),
-        in_specs=[VMEM] * (2 + len(pieces)),
+        in_specs=[SMEM] + [VMEM] * (2 + len(pieces)),
         out_specs=VMEM,
         out_shape=jax.ShapeDtypeStruct(pieces[0].shape, BF16),
         compiler_params=pltpu.CompilerParams(vmem_limit_bytes=32 * 2**20),
         name="finish_bytes",
-    )(result, proj, *pieces)
+    )(kept, result, proj, *pieces)
 
 
 def shift(value, axis, step):
@@ -219,6 +240,28 @@
     me = lax.axis_index(axis)
     take = lambda step: lax.dynamic_index_in_dim(chunks, (me + step) % count, 0, keepdims=False)
     return [take(0)] + [shift(take(step), axis, step) for step in range(1, count)]
+
+
+class Relay:
+    def __init__(self, chunks, axis):
+        self.chunks, self.axis = chunks, axis
+        self.me = me = lax.axis_index(axis)
+        self.outer = (me == 0) | (me == 3)
+        take = self.take
+        self.own = take(me)
+        far = jnp.where(self.outer, 3 - me, me ^ 1)
+        self.swapped = lax.ppermute(take(far), axis, [(0, 1), (1, 0), (2, 3), (3, 2)])
+        self.middle = lax.ppermute(take(jnp.where(self.outer, me, 3 - me)), axis, [(1, 2), (2, 1)])
+
+    def take(self, index):
+        return lax.dynamic_index_in_dim(self.chunks, index, 0, keepdims=False)
+
+    def rest(self):
+        me, outer = self.me, self.outer
+        inward = lax.ppermute(self.take(me ^ 1), self.axis, [(0, 1), (3, 2)])
+        sent = self.take(me ^ 2).astype(F32) + jnp.where(outer, 0.0, self.swapped.astype(F32))
+        crossed = lax.ppermute(sent.astype(BF16), self.axis, [(0, 2), (2, 0), (1, 3), (3, 1)])
+        return [self.own, self.swapped, self.middle, inward, crossed]
 
 
 def gather(value, axis):
@@ -249,7 +292,8 @@
     )
     slot = jnp.sum(before, axis=1).astype(jnp.int32)
     row = jnp.arange(patches, dtype=jnp.int32)
-    place = jnp.repeat(slot, block, total_repeat_length=patches) * block + row % block
+    spread = jnp.sum(jnp.where(row[:, None] // block == index[None, :], slot[None, :], 0), axis=1).astype(jnp.int32)
+    place = spread * block + row % block
     return (row[:, None] == place[None, :]).astype(BF16)
 
 
@@ -297,16 +341,24 @@
     ids = (me - jnp.arange(ways, dtype=jnp.int32)) % ways
     gain = global_gain.reshape(ways, 1, -1)
     qkv = jnp.transpose(global_qkv, (1, 0, 2))
-    key, value = global_heads((1, 2), depth, ids, gain, shares, qkv)
-    part, key, value = lax.optimization_barrier((part, key, value))
-    (query,) = global_heads((0,), depth, ids, gain, shares, qkv)
-    keys = gather_chips(key, "seq")
-    values = gather_chips(value, "seq")
-    bytes_pieces = scatter(part.reshape(ways, own * patches, width), "head")
-    update = attend(chip_ids("seq"), global_scale, query, keys, values, global_out, ways)
+    keyed = global_heads((1, 2), depth, ids, gain, shares, qkv)
+    part, keyed = lax.optimization_barrier((part, keyed))
+    chunks = part.reshape(ways, own * patches, width)
+    if ways == 4:
+        relay = Relay(chunks, "head")
+        relay.swapped, shares = lax.optimization_barrier((relay.swapped, shares))
+        outer = relay.outer.astype(jnp.int32)
+        kept = jnp.stack([1 + 0 * outer, outer, 1 - outer, 1 - outer, 1 + 0 * outer])
+    query = global_heads((0,), depth, ids, gain, shares, qkv)
+    update = attend(chip_ids("seq"), global_scale, query, gather_chips(keyed, "seq"), global_out, ways)
+    if ways == 4:
+        bytes_pieces = relay.rest()
+    else:
+        bytes_pieces = scatter(chunks, "head")
+        kept = jnp.ones((ways,), jnp.int32)
     result, routed = finish_result(owner_order(owners, seq, patches), residual, scatter(update, "head"))
     global_state = lax.all_to_all(routed, "seq", split_axis=0, concat_axis=0, tiled=True)
-    byte_out = finish_bytes(result, back_proj, bytes_pieces)
+    byte_out = finish_bytes(kept, result, back_proj, bytes_pieces)
     return byte_out.reshape(patches, own, width), global_state
 
 

time: 148 us -> 147 us (level)
  local copies, waits for them, and re-layouts: 13.6 us -> 23.3 us
  blocking collectives: 8.81 us -> 0 us
  other arithmetic: 11.1 us -> 3.15 us
  Pallas kernels: 23.6 us -> 27.7 us
  starting transfers between devices: 30.4 us -> 33.4 us
    unnamed x63 -> x57, local copies, waits for them, and re-layouts: 9.93 us -> 20.2 us
    add x1, other arithmetic: 10 us -> 0.01 us  [owner_order(): place = spread * block + row % block]
    ppermute x0 -> x4, starting transfers between devices: none -> 9.36 us  [the longest x1 4.59 us: rest(): inward = lax.ppermute(self.take(me ^ 1), self.axis, [(0, 1), (3, 2)])]
    all_to_all x1 -> x0, blocking collectives: 8.81 us -> none  [on_device(): lax.all_to_all(routed, 'seq', split_axis=0, concat_axis=0, tiled=True)]
    ppermute x18 -> x12, starting transfers between devices: 28.3 us -> 20.2 us  [shift(): lax.ppermute(value, axis, [(i, (i + step) % count) for i in range(count)])]
    ppermute x18 -> x12, waiting for transfers between devices: 58.7 us -> 52.7 us  [shift(): lax.ppermute(value, axis, [(i, (i + step) % count) for i in range(count)])]
    all_to_all x0 -> x1, waiting for transfers between devices: none -> 5.37 us  [on_device(): lax.all_to_all(routed, 'seq', split_axis=0, concat_axis=0, tiled=True)]
    all_to_all x0 -> x1, starting transfers between devices: none -> 3.37 us  [on_device(): lax.all_to_all(routed, 'seq', split_axis=0, concat_axis=0, tiled=True)]
  transfers between devices with their start and end apart: 26 -> 21, of which waited for: 10 -> 11; matrix products, arithmetic and copies ran while one was open for 9% -> 3% of each run, Pallas kernels for 4% -> 5%
where the time goes in v2:
time: 147 us; the launch traced here: 146 us
  waiting for transfers between devices  58.1 us (40%)
  starting transfers between devices  33.4 us (23%)
  Pallas kernels  27.7 us (19%)
  local copies, waits for them, and re-layouts  23.3 us (16%)
  other arithmetic  3.15 us (2%)
    ppermute x12, waiting for transfers between devices, shift(): lax.ppermute(value, axis, [(i, (i + step) % count) for i in range(count)])  52.7 us
    unnamed x57, local copies, waits for them, and re-layouts  20.2 us
    ppermute x12, starting transfers between devices, shift(): lax.ppermute(value, axis, [(i, (i + step) % count) for i in range(count)])  20.2 us
    pallas_call x1, Pallas kernels, local_part(): pl.pallas_call(functools.partial(local_kernel, span, own), grid=(patches...  17.1 us
    all_to_all x1, waiting for transfers between devices, on_device(): lax.all_to_all(routed, 'seq', split_axis=0, concat_axis=0, tiled=True)  5.37 us
    ppermute x1, starting transfers between devices, rest(): inward = lax.ppermute(self.take(me ^ 1), self.axis, [(0, 1), (3, 2)])  4.59 us
    pallas_call x1, Pallas kernels, attend(): pl.pallas_call(functools.partial(attend_kernel, len(pieces)), in_specs=[S...  3.81 us
    all_to_all x1, starting transfers between devices, on_device(): lax.all_to_all(routed, 'seq', split_axis=0, concat_axis=0, tiled=True)  3.37 us
  transfers between devices with their start and end apart: 21, of which 11 were waited for; matrix products, arithmetic and copies ran while one was open for 3% of the time, Pallas kernels for 5%

profile of v2, /device:TPU:0, one launch (start us, length us, event | category | flops | bytes accessed | tf_op | source)
XLA Modules:
  0.0 146.5 jit_solution(9754941829485083220)
XLA Ops:
  0.7 1.6 %copy-done.5 = bf16[128,8,1024]{2,1,0:T(8,128)(2,1)S(1)} copy-done((bf16[128,8,1024]{2,1,0:T(8,128)(2,1)S(1)}, bf16[128,8,1024]{2,1,0:T(8,128)(2,1)}, u32[]{:S(2)}) %copy-start.5) | copy-done | bytes 2097176
  2.3 1.6 %copy-done.6 = bf16[1024,1024]{1,0:T(8,128)(2,1)S(1)} copy-done((bf16[1024,1024]{1,0:T(8,128)(2,1)S(1)}, bf16[1024,1024]{1,0:T(8,128)(2,1)}, u32[]{:S(2)}) %copy-start.6) | copy-done | bytes 2097176
  3.9 1.6 %copy-done.7 = bf16[1024,1024]{1,0:T(8,128)(2,1)S(1)} copy-done((bf16[1024,1024]{1,0:T(8,128)(2,1)S(1)}, bf16[1024,1024]{1,0:T(8,128)(2,1)}, u32[]{:S(2)}) %copy-start.7) | copy-done | bytes 2097176
  5.5 1.4 copy-done.8
  10.3 17.1 %local_part.1 = (bf16[8,128,1024]{2,1,0:T(8,128)(2,1)S(1)}, bf16[4,128,512]{2,1,0:T(8,128)(2,1)S(1)}) custom-call(s32[1]{0:T(128)} %bitcast.3.me_ref, f32[2]{0:T(128)S(1)} %copy-done.21, bf16[1024,1024]{1,0:T(8,128)(2,1)S(1)} %bitcast.46, f32[1,1024]{1,0:T(1,128)S(1)} %bitcast.50, bf16[3,1024,256]{2,1,0:T(8,128)(2,1)S(1)} %bitcast.47, ...), custom_call_target="tpu_custom_call" | custom-call | tf_op jit(solution)/shard_map/local_part/pallas_call | solution.py:92
  27.5 3.1 %collective-permute-start = (bf16[128,512]{1,0:T(8,128)(2,1)S(1)}, bf16[128,512]{1,0:T(8,128)(2,1)S(1)}, u32[]{:S(2)}, u32[]{:S(2)}) collective-permute-start(bf16[128,512]{1,0:T(8,128)(2,1)S(1)} %get-tuple-element.32), channel_id=1, source_target_pairs={{0,1},{1,2},{2,3},{3,0},{4,5},{5,6},{6,7},{7,4},{8,9},{9,10},{10,1... | collective-permute-start | bytes 393224 | tf_op jit(solution)/shard_map/ppermute | solution.py:235
  30.5 2.6 %collective-permute-start.1 = (bf16[128,512]{1,0:T(8,128)(2,1)S(1)}, bf16[128,512]{1,0:T(8,128)(2,1)S(1)}, u32[]{:S(2)}, u32[]{:S(2)}) collective-permute-start(bf16[128,512]{1,0:T(8,128)(2,1)S(1)} %get-tuple-element.34), channel_id=1, source_target_pairs={{0,2},{1,3},{2,0},{3,1},{4,6},{5,7},{6,4},{7,5},{8,10},{9,11},{10,... | collective-permute-start | bytes 393224 | tf_op jit(solution)/shard_map/ppermute | solution.py:235
  34.5 2.5 %collective-permute-done = bf16[128,512]{1,0:T(8,128)(2,1)S(1)} collective-permute-done((bf16[128,512]{1,0:T(8,128)(2,1)S(1)}, bf16[128,512]{1,0:T(8,128)(2,1)S(1)}, u32[]{:S(2)}, u32[]{:S(2)}) %collective-permute-start) | collective-permute-done | bytes 131104 | tf_op jit(solution)/shard_map/ppermute | solution.py:235
  37.0 4.8 %collective-permute-done.1 = bf16[128,512]{1,0:T(8,128)(2,1)S(1)} collective-permute-done((bf16[128,512]{1,0:T(8,128)(2,1)S(1)}, bf16[128,512]{1,0:T(8,128)(2,1)S(1)}, u32[]{:S(2)}, u32[]{:S(2)}) %collective-permute-start.1) | collective-permute-done | bytes 131104 | tf_op jit(solution)/shard_map/ppermute | solution.py:235
  41.9 3.3 %collective-permute-start.3 = (bf16[128,512]{1,0:T(8,128)(2,1)S(1)}, bf16[128,512]{1,0:T(8,128)(2,1)S(1)}, u32[]{:S(2)}, u32[]{:S(2)}) collective-permute-start(bf16[128,512]{1,0:T(8,128)(2,1)S(1)} %fusion.3.refs_0_.own_ref), channel_id=1, source_target_pairs={{0,1},{1,2},{2,3},{3,0},{4,5},{5,6},{6,7},{7,4},{8,9},{9,10},{10,1... | collective-permute-start | bytes 393224 | tf_op jit(solution)/shard_map/ppermute | solution.py:235
  45.2 1.6 %collective-permute-start.4 = (bf16[128,512]{1,0:T(8,128)(2,1)S(1)}, bf16[128,512]{1,0:T(8,128)(2,1)S(1)}, u32[]{:S(2)}, u32[]{:S(2)}) collective-permute-start(bf16[128,512]{1,0:T(8,128)(2,1)S(1)} %fusion.3.refs_0_.own_ref), channel_id=1, source_target_pairs={{0,2},{1,3},{2,0},{3,1},{4,6},{5,7},{6,4},{7,5},{8,10},{9,11},{10,... | collective-permute-start | bytes 393224 | tf_op jit(solution)/shard_map/ppermute | solution.py:235
  47.6 2.7 %collective-permute-done.3.refs_1_ = bf16[128,512]{1,0:T(8,128)(2,1)S(1)} collective-permute-done((bf16[128,512]{1,0:T(8,128)(2,1)S(1)}, bf16[128,512]{1,0:T(8,128)(2,1)S(1)}, u32[]{:S(2)}, u32[]{:S(2)}) %collective-permute-start.3) | collective-permute-done | bytes 131104 | tf_op jit(solution)/shard_map/ppermute | solution.py:235
  50.4 4.5 %collective-permute-done.4.refs_2_ = bf16[128,512]{1,0:T(8,128)(2,1)S(1)} collective-permute-done((bf16[128,512]{1,0:T(8,128)(2,1)S(1)}, bf16[128,512]{1,0:T(8,128)(2,1)S(1)}, u32[]{:S(2)}, u32[]{:S(2)}) %collective-permute-start.4) | collective-permute-done | bytes 131104 | tf_op jit(solution)/shard_map/ppermute | solution.py:235
  54.9 2.9 %copy-done.1 = bf16[2048,3,512]{2,0,1:T(8,128)(2,1)S(1)} copy-done((bf16[2048,3,512]{2,0,1:T(8,128)(2,1)S(1)}, bf16[2048,3,512]{2,0,1:T(8,128)(2,1)}, u32[]{:S(2)}) %copy-start.1) | copy-done | bytes 6291480
  57.8 1.4 global_heads.2.refs_0_
  60.5 3.2 %collective-permute-start.6 = (bf16[256,1024]{1,0:T(8,128)(2,1)}, bf16[256,1024]{1,0:T(8,128)(2,1)S(1)}, u32[]{:S(2)}, u32[]{:S(2)}) collective-permute-start(bf16[256,1024]{1,0:T(8,128)(2,1)} %get-tuple-element.27), channel_id=1, source_target_pairs={{0,1},{1,0},{2,3},{3,2},{4,5},{5,4},{6,7},{7,6},{8,9},{9,8},{10,11... | collective-permute-start | bytes 1572872 | tf_op jit(solution)/shard_map/ppermute | solution.py:253
  63.7 1.5 %collective-permute-start.7 = (bf16[128,1024]{1,0:T(8,128)(2,1)S(1)}, bf16[128,1024]{1,0:T(8,128)(2,1)}, u32[]{:S(2)}, u32[]{:S(2)}) collective-permute-start(bf16[128,1024]{1,0:T(8,128)(2,1)S(1)} %global_heads.2.refs_0_), channel_id=1, source_target_pairs={{0,8},{4,12},{8,16},{12,20},{16,24},{20,28},{24,0},{28,4},{1,9},{5... | collective-permute-start | bytes 786440 | tf_op jit(solution)/shard_map/ppermute | solution.py:235
  65.2 1.5 %collective-permute-start.8 = (bf16[128,1024]{1,0:T(8,128)(2,1)S(1)}, bf16[128,1024]{1,0:T(8,128)(2,1)}, u32[]{:S(2)}, u32[]{:S(2)}) collective-permute-start(bf16[128,1024]{1,0:T(8,128)(2,1)S(1)} %global_heads.2.refs_0_), channel_id=1, source_target_pairs={{0,16},{4,20},{8,24},{12,28},{16,0},{20,4},{24,8},{28,12},{1,17},{... | collective-permute-start | bytes 786440 | tf_op jit(solution)/shard_map/ppermute | solution.py:235
  66.7 1.4 collective-permute-start.9
  69.0 5.0 %collective-permute-done.7.refs_1_ = bf16[128,1024]{1,0:T(8,128)(2,1)} collective-permute-done((bf16[128,1024]{1,0:T(8,128)(2,1)S(1)}, bf16[128,1024]{1,0:T(8,128)(2,1)}, u32[]{:S(2)}, u32[]{:S(2)}) %collective-permute-start.7) | collective-permute-done | bytes 262176 | tf_op jit(solution)/shard_map/ppermute | solution.py:235
  74.0 4.3 %collective-permute-done.8.refs_2_ = bf16[128,1024]{1,0:T(8,128)(2,1)} collective-permute-done((bf16[128,1024]{1,0:T(8,128)(2,1)S(1)}, bf16[128,1024]{1,0:T(8,128)(2,1)}, u32[]{:S(2)}, u32[]{:S(2)}) %collective-permute-start.8) | collective-permute-done | bytes 262176 | tf_op jit(solution)/shard_map/ppermute | solution.py:235
  79.4 1.5 %collective-permute-start.17 = (bf16[256,1024]{1,0:T(8,128)(2,1)}, bf16[256,1024]{1,0:T(8,128)(2,1)}, u32[]{:S(2)}, u32[]{:S(2)}) collective-permute-start(bf16[256,1024]{1,0:T(8,128)(2,1)} %get-tuple-element.25), channel_id=1, source_target_pairs={{1,2},{2,1},{5,6},{6,5},{9,10},{10,9},{13,14},{14,13},{17,18},{18,... | collective-permute-start | bytes 1572872 | tf_op jit(solution)/shard_map/ppermute | solution.py:254
  80.9 2.8 %copy-done.2 = bf16[2048,3,512]{2,0,1:T(8,128)(2,1)S(1)} copy-done((bf16[2048,3,512]{2,0,1:T(8,128)(2,1)S(1)}, bf16[2048,3,512]{2,0,1:T(8,128)(2,1)}, u32[]{:S(2)}) %copy-start.2) | copy-done | bytes 6291480
  88.7 4.6 %collective-permute-start.18 = (bf16[256,1024]{1,0:T(8,128)(2,1)}, bf16[256,1024]{1,0:T(8,128)(2,1)S(1)}, u32[]{:S(2)}, u32[]{:S(2)}) collective-permute-start(bf16[256,1024]{1,0:T(8,128)(2,1)} %get-tuple-element.24), channel_id=1, source_target_pairs={{0,1},{3,2},{4,5},{7,6},{8,9},{11,10},{12,13},{15,14},{16,17},{19,... | collective-permute-start | bytes 1572872 | tf_op jit(solution)/shard_map/ppermute | solution.py:261
  93.4 3.8 %attend.1 = bf16[4,128,512]{2,1,0:T(8,128)(2,1)S(1)} custom-call(s32[8]{0:T(128)S(1)} %copy-done.23, f32[4]{0:T(128)S(1)} %copy-done.22, bf16[128,512]{1,0:T(8,128)(2,1)S(1)} %global_heads.3.q_ref, bf16[128,1024]{1,0:T(8,128)(2,1)S(1)} %global_heads.2.refs_0_, bf16[128,1024]{1,0:T(8,128)(2,1)} %collective-permute-done.7.refs_1_, ...), custom_call_target="tpu_custom_call" | custom-call | tf_op jit(solution)/shard_map/attend/pallas_call | solution.py:174
  97.9 1.6 %collective-permute-start.14 = (bf16[128,512]{1,0:T(8,128)(2,1)S(1)}, bf16[128,512]{1,0:T(8,128)(2,1)S(1)}, u32[]{:S(2)}, u32[]{:S(2)}) collective-permute-start(bf16[128,512]{1,0:T(8,128)(2,1)S(1)} %get-tuple-element.30), channel_id=1, source_target_pairs={{0,1},{1,2},{2,3},{3,0},{4,5},{5,6},{6,7},{7,4},{8,9},{9,10},{10,1... | collective-permute-start | bytes 393224 | tf_op jit(solution)/shard_map/ppermute | solution.py:235
  100.9 20.6 %collective-permute-done.14.refs_1_ = bf16[128,512]{1,0:T(8,128)(2,1)S(1)} collective-permute-done((bf16[128,512]{1,0:T(8,128)(2,1)S(1)}, bf16[128,512]{1,0:T(8,128)(2,1)S(1)}, u32[]{:S(2)}, u32[]{:S(2)}) %collective-permute-start.14) | collective-permute-done | bytes 131104 | tf_op jit(solution)/shard_map/ppermute | solution.py:235
  122.1 6.8 %collective-permute-done.15.refs_2_ = bf16[128,512]{1,0:T(8,128)(2,1)S(1)} collective-permute-done((bf16[128,512]{1,0:T(8,128)(2,1)S(1)}, bf16[128,512]{1,0:T(8,128)(2,1)S(1)}, u32[]{:S(2)}, u32[]{:S(2)}) %collective-permute-start.15) | collective-permute-done | bytes 131104 | tf_op jit(solution)/shard_map/ppermute | solution.py:235
  131.0 2.1 %finish_result.1 = (bf16[128,512]{1,0:T(8,128)(2,1)}, bf16[128,512]{1,0:T(8,128)(2,1)}) custom-call(bf16[128,128]{1,0:T(8,128)(2,1)} %fusion.4.order_ref, bf16[128,512]{1,0:T(8,128)(2,1)} %copy-done.3, bf16[128,512]{1,0:T(8,128)(2,1)} %get-tuple-element.31.refs_0_, bf16[128,512]{1,0:T(8,128)(2,1)} %copy-done.24, bf16[128,512]{1,0:T(8,128)(2,1)} %copy-done.25, ...), custom_call_target="tpu_custom_call" | custom-call | tf_op jit(solution)/shard_map/finish_result/pallas_call | solution.py:194
  133.1 3.4 %all-to-all-start = ((bf16[8,16,512]{2,1,0:T(8,128)(2,1)}), bf16[8,16,512]{2,1,0:T(8,128)(2,1)S(1)}, u32[]{:S(2)}, u32[]{:S(2)}) async-start(bf16[8,16,512]{2,1,0:T(8,128)(2,1)} %bitcast.52), calls=%async_computation | async-start | bytes 262144 | tf_op jit(solution)/shard_map/all_to_all | solution.py:360
  136.5 5.4 %all-to-all-done = bf16[8,16,512]{2,1,0:T(8,128)(2,1)S(1)} async-done(((bf16[8,16,512]{2,1,0:T(8,128)(2,1)}), bf16[8,16,512]{2,1,0:T(8,128)(2,1)S(1)}, u32[]{:S(2)}, u32[]{:S(2)}) %all-to-all-start) | async-done | bytes 131104 | tf_op jit(solution)/shard_map/all_to_all | solution.py:360
  142.8 2.0 %finish_bytes.1 = bf16[256,1024]{1,0:T(8,128)(2,1)S(1)} custom-call(s32[5]{0:T(128)S(1)} %stack.12.kept_ref, bf16[128,512]{1,0:T(8,128)(2,1)S(1)} %copy-done.18, bf16[256,1024]{1,0:T(8,128)(2,1)S(1)} %copy-done.17, bf16[256,1024]{1,0:T(8,128)(2,1)S(1)} %get-tuple-element.26.refs_0_, bf16[256,1024]{1,0:T(8,128)(2,1)S(1)} %collective-permute-done.6.refs_1_, ...), custom_call_target="tpu_custom_call" | custom-call | tf_op jit(solution)/shard_map/finish_bytes/pallas_call | solution.py:223
  (89 shorter events, 21.3 us)
Async XLA Ops:
  0.6 67.6 %copy-start = (s32[8,16]{1,0:T(8,128)S(1)}, s32[8,16]{1,0:T(8,128)}, u32[]{:S(2)}) copy-start(s32[8,16]{1,0:T(8,128)} %param.27) | copy-start | bytes 1540
  10.3 44.6 %copy-start.19 = (f32[2048]{0:T(1024)S(1)}, f32[2048]{0:T(1024)}, u32[]{:S(2)}) copy-start(f32[2048]{0:T(1024)} %param.22) | copy-start | bytes 24580
  27.5 9.5 %collective-permute-start = (bf16[128,512]{1,0:T(8,128)(2,1)S(1)}, bf16[128,512]{1,0:T(8,128)(2,1)S(1)}, u32[]{:S(2)}, u32[]{:S(2)}) collective-permute-start(bf16[128,512]{1,0:T(8,128)(2,1)S(1)} %get-tuple-element.32), channel_id=1, source_target_pairs={{0,1},{1,2},{2,3},{3,0},{4,5},{5,6},{6,7},{7,4},{8,9},{9,10},{10,1... | collective-permute-start | bytes 393224 | tf_op jit(solution)/shard_map/ppermute | solution.py:235
  30.5 11.2 %collective-permute-start.1 = (bf16[128,512]{1,0:T(8,128)(2,1)S(1)}, bf16[128,512]{1,0:T(8,128)(2,1)S(1)}, u32[]{:S(2)}, u32[]{:S(2)}) collective-permute-start(bf16[128,512]{1,0:T(8,128)(2,1)S(1)} %get-tuple-element.34), channel_id=1, source_target_pairs={{0,2},{1,3},{2,0},{3,1},{4,6},{5,7},{6,4},{7,5},{8,10},{9,11},{10,... | collective-permute-start | bytes 393224 | tf_op jit(solution)/shard_map/ppermute | solution.py:235
  33.1 8.6 %collective-permute-start.2 = (bf16[128,512]{1,0:T(8,128)(2,1)S(1)}, bf16[128,512]{1,0:T(8,128)(2,1)S(1)}, u32[]{:S(2)}, u32[]{:S(2)}) collective-permute-start(bf16[128,512]{1,0:T(8,128)(2,1)S(1)} %get-tuple-element.33), channel_id=1, source_target_pairs={{0,3},{1,0},{2,1},{3,2},{4,7},{5,4},{6,5},{7,6},{8,11},{9,8},{10,9... | collective-permute-start | bytes 393224 | tf_op jit(solution)/shard_map/ppermute | solution.py:235
  41.8 39.0 %copy-start.3 = (bf16[128,512]{1,0:T(8,128)(2,1)}, bf16[128,512]{1,0:T(8,128)(2,1)S(1)}, u32[]{:S(2)}) copy-start(bf16[128,512]{1,0:T(8,128)(2,1)S(1)} %fusion.3.refs_0_.own_ref) | copy-start | bytes 393220
  41.9 8.5 %collective-permute-start.3 = (bf16[128,512]{1,0:T(8,128)(2,1)S(1)}, bf16[128,512]{1,0:T(8,128)(2,1)S(1)}, u32[]{:S(2)}, u32[]{:S(2)}) collective-permute-start(bf16[128,512]{1,0:T(8,128)(2,1)S(1)} %fusion.3.refs_0_.own_ref), channel_id=1, source_target_pairs={{0,1},{1,2},{2,3},{3,0},{4,5},{5,6},{6,7},{7,4},{8,9},{9,10},{10,1... | collective-permute-start | bytes 393224 | tf_op jit(solution)/shard_map/ppermute | solution.py:235
  45.2 9.7 %collective-permute-start.4 = (bf16[128,512]{1,0:T(8,128)(2,1)S(1)}, bf16[128,512]{1,0:T(8,128)(2,1)S(1)}, u32[]{:S(2)}, u32[]{:S(2)}) collective-permute-start(bf16[128,512]{1,0:T(8,128)(2,1)S(1)} %fusion.3.refs_0_.own_ref), channel_id=1, source_target_pairs={{0,2},{1,3},{2,0},{3,1},{4,6},{5,7},{6,4},{7,5},{8,10},{9,11},{10,... | collective-permute-start | bytes 393224 | tf_op jit(solution)/shard_map/ppermute | solution.py:235
  46.8 8.1 %collective-permute-start.5 = (bf16[128,512]{1,0:T(8,128)(2,1)S(1)}, bf16[128,512]{1,0:T(8,128)(2,1)S(1)}, u32[]{:S(2)}, u32[]{:S(2)}) collective-permute-start(bf16[128,512]{1,0:T(8,128)(2,1)S(1)} %fusion.3.refs_0_.own_ref), channel_id=1, source_target_pairs={{0,3},{1,0},{2,1},{3,2},{4,7},{5,4},{6,5},{7,6},{8,11},{9,8},{10,9... | collective-permute-start | bytes 393224 | tf_op jit(solution)/shard_map/ppermute | solution.py:235
  50.4 8.9 %copy-start.9 = (bf16[128,512]{1,0:T(8,128)(2,1)}, bf16[128,512]{1,0:T(8,128)(2,1)S(1)}, u32[]{:S(2)}) copy-start(bf16[128,512]{1,0:T(8,128)(2,1)S(1)} %collective-permute-done.3.refs_1_) | copy-start | bytes 393220
  54.9 4.4 %copy-start.13 = (bf16[128,512]{1,0:T(8,128)(2,1)}, bf16[128,512]{1,0:T(8,128)(2,1)S(1)}, u32[]{:S(2)}) copy-start(bf16[128,512]{1,0:T(8,128)(2,1)S(1)} %collective-permute-done.5.refs_3_) | copy-start | bytes 393220
  60.5 18.9 %collective-permute-start.6 = (bf16[256,1024]{1,0:T(8,128)(2,1)}, bf16[256,1024]{1,0:T(8,128)(2,1)S(1)}, u32[]{:S(2)}, u32[]{:S(2)}) collective-permute-start(bf16[256,1024]{1,0:T(8,128)(2,1)} %get-tuple-element.27), channel_id=1, source_target_pairs={{0,1},{1,0},{2,3},{3,2},{4,5},{5,4},{6,7},{7,6},{8,9},{9,8},{10,11... | collective-permute-start | bytes 1572872 | tf_op jit(solution)/shard_map/ppermute | solution.py:253
  63.7 10.3 %collective-permute-start.7 = (bf16[128,1024]{1,0:T(8,128)(2,1)S(1)}, bf16[128,1024]{1,0:T(8,128)(2,1)}, u32[]{:S(2)}, u32[]{:S(2)}) collective-permute-start(bf16[128,1024]{1,0:T(8,128)(2,1)S(1)} %global_heads.2.refs_0_), channel_id=1, source_target_pairs={{0,8},{4,12},{8,16},{12,20},{16,24},{20,28},{24,0},{28,4},{1,9},{5... | collective-permute-start | bytes 786440 | tf_op jit(solution)/shard_map/ppermute | solution.py:235
  65.2 13.1 %collective-permute-start.8 = (bf16[128,1024]{1,0:T(8,128)(2,1)S(1)}, bf16[128,1024]{1,0:T(8,128)(2,1)}, u32[]{:S(2)}, u32[]{:S(2)}) collective-permute-start(bf16[128,1024]{1,0:T(8,128)(2,1)S(1)} %global_heads.2.refs_0_), channel_id=1, source_target_pairs={{0,16},{4,20},{8,24},{12,28},{16,0},{20,4},{24,8},{28,12},{1,17},{... | collective-permute-start | bytes 786440 | tf_op jit(solution)/shard_map/ppermute | solution.py:235
  66.7 11.7 %collective-permute-start.9 = (bf16[128,1024]{1,0:T(8,128)(2,1)S(1)}, bf16[128,1024]{1,0:T(8,128)(2,1)}, u32[]{:S(2)}, u32[]{:S(2)}) collective-permute-start(bf16[128,1024]{1,0:T(8,128)(2,1)S(1)} %global_heads.2.refs_0_), channel_id=1, source_target_pairs={{0,24},{4,28},{8,0},{12,4},{16,8},{20,12},{24,16},{28,20},{1,25},{... | collective-permute-start | bytes 786440 | tf_op jit(solution)/shard_map/ppermute | solution.py:235
  69.0 19.7 %collective-permute-start.10 = (bf16[128,1024]{1,0:T(8,128)(2,1)S(1)}, bf16[128,1024]{1,0:T(8,128)(2,1)}, u32[]{:S(2)}, u32[]{:S(2)}) collective-permute-start(bf16[128,1024]{1,0:T(8,128)(2,1)S(1)} %global_heads.2.refs_0_), channel_id=1, source_target_pairs={{0,4},{4,0},{8,12},{12,8},{16,20},{20,16},{24,28},{28,24},{1,5},{5... | collective-permute-start | bytes 786440 | tf_op jit(solution)/shard_map/ppermute | solution.py:275
  74.0 19.3 %collective-permute-start.11 = (bf16[128,1024]{1,0:T(8,128)(2,1)}, bf16[128,1024]{1,0:T(8,128)(2,1)}, u32[]{:S(2)}, u32[]{:S(2)}) collective-permute-start(bf16[128,1024]{1,0:T(8,128)(2,1)} %collective-permute-done.7.refs_1_), channel_id=1, source_target_pairs={{0,4},{4,0},{8,12},{12,8},{16,20},{20,16},{24,28},{28,24},{1,5},{5... | collective-permute-start | bytes 786440 | tf_op jit(solution)/shard_map/ppermute | solution.py:275
  78.3 15.1 %collective-permute-start.12 = (bf16[128,1024]{1,0:T(8,128)(2,1)}, bf16[128,1024]{1,0:T(8,128)(2,1)}, u32[]{:S(2)}, u32[]{:S(2)}) collective-permute-start(bf16[128,1024]{1,0:T(8,128)(2,1)} %collective-permute-done.8.refs_2_), channel_id=1, source_target_pairs={{0,4},{4,0},{8,12},{12,8},{16,20},{20,16},{24,28},{28,24},{1,5},{5... | collective-permute-start | bytes 786440 | tf_op jit(solution)/shard_map/ppermute | solution.py:275
  78.4 15.0 %collective-permute-start.13 = (bf16[128,1024]{1,0:T(8,128)(2,1)}, bf16[128,1024]{1,0:T(8,128)(2,1)}, u32[]{:S(2)}, u32[]{:S(2)}) collective-permute-start(bf16[128,1024]{1,0:T(8,128)(2,1)} %collective-permute-done.9.refs_3_), channel_id=1, source_target_pairs={{0,4},{4,0},{8,12},{12,8},{16,20},{20,16},{24,28},{28,24},{1,5},{5... | collective-permute-start | bytes 786440 | tf_op jit(solution)/shard_map/ppermute | solution.py:275
  79.4 62.5 %collective-permute-start.17 = (bf16[256,1024]{1,0:T(8,128)(2,1)}, bf16[256,1024]{1,0:T(8,128)(2,1)}, u32[]{:S(2)}, u32[]{:S(2)}) collective-permute-start(bf16[256,1024]{1,0:T(8,128)(2,1)} %get-tuple-element.25), channel_id=1, source_target_pairs={{1,2},{2,1},{5,6},{6,5},{9,10},{10,9},{13,14},{14,13},{17,18},{18,... | collective-permute-start | bytes 1572872 | tf_op jit(solution)/shard_map/ppermute | solution.py:254
  86.4 7.0 %copy-start.4 = (bf16[512,2048]{1,0:T(8,128)(2,1)S(1)}, bf16[512,2048]{1,0:T(8,128)(2,1)}, u32[]{:S(2)}) copy-start(bf16[512,2048]{1,0:T(8,128)(2,1)} %refs_8_.1) | copy-start | bytes 6291460
  86.4 7.0 %copy-start.22 = (f32[4]{0:T(128)S(1)}, f32[4]{0:T(128)}, u32[]{:S(2)}) copy-start(f32[4]{0:T(128)} %scale_ref.3) | copy-start | bytes 52
  86.4 7.0 %copy-start.23 = (s32[8]{0:T(128)S(1)}, s32[8]{0:T(128)}, u32[]{:S(2)}) copy-start(s32[8]{0:T(128)} %pad_add_fusion.ids_ref) | copy-start | bytes 100
  88.7 10.9 %copy-start.27 = (s32[128]{0:T(128)S(1)}, s32[128]{0:T(128)}, u32[]{:S(2)}) copy-start(s32[128]{0:T(128)} %select_reduce_fusion) | copy-start | bytes 1540
  88.7 53.2 %collective-permute-start.18 = (bf16[256,1024]{1,0:T(8,128)(2,1)}, bf16[256,1024]{1,0:T(8,128)(2,1)S(1)}, u32[]{:S(2)}, u32[]{:S(2)}) collective-permute-start(bf16[256,1024]{1,0:T(8,128)(2,1)} %get-tuple-element.24), channel_id=1, source_target_pairs={{0,1},{3,2},{4,5},{7,6},{8,9},{11,10},{12,13},{15,14},{16,17},{19,... | collective-permute-start | bytes 1572872 | tf_op jit(solution)/shard_map/ppermute | solution.py:261
  93.3 48.6 %collective-permute-start.19 = (bf16[256,1024]{1,0:T(8,128)(2,1)}, bf16[256,1024]{1,0:T(8,128)(2,1)S(1)}, u32[]{:S(2)}, u32[]{:S(2)}) collective-permute-start(bf16[256,1024]{1,0:T(8,128)(2,1)} %fusion), channel_id=1, source_target_pairs={{0,2},{2,0},{1,3},{3,1},{4,6},{6,4},{5,7},{7,5},{8,10},{10,8},{9,1... | collective-permute-start | bytes 1572872 | tf_op jit(solution)/shard_map/ppermute | solution.py:263
  97.2 44.7 %copy-start.17 = (bf16[256,1024]{1,0:T(8,128)(2,1)S(1)}, bf16[256,1024]{1,0:T(8,128)(2,1)}, u32[]{:S(2)}) copy-start(bf16[256,1024]{1,0:T(8,128)(2,1)} %proj_ref.1) | copy-start | bytes 1572868
  97.9 23.5 %collective-permute-start.14 = (bf16[128,512]{1,0:T(8,128)(2,1)S(1)}, bf16[128,512]{1,0:T(8,128)(2,1)S(1)}, u32[]{:S(2)}, u32[]{:S(2)}) collective-permute-start(bf16[128,512]{1,0:T(8,128)(2,1)S(1)} %get-tuple-element.30), channel_id=1, source_target_pairs={{0,1},{1,2},{2,3},{3,0},{4,5},{5,6},{6,7},{7,4},{8,9},{9,10},{10,1... | collective-permute-start | bytes 393224 | tf_op jit(solution)/shard_map/ppermute | solution.py:235
  99.6 29.4 %collective-permute-start.15 = (bf16[128,512]{1,0:T(8,128)(2,1)S(1)}, bf16[128,512]{1,0:T(8,128)(2,1)S(1)}, u32[]{:S(2)}, u32[]{:S(2)}) collective-permute-start(bf16[128,512]{1,0:T(8,128)(2,1)S(1)} %get-tuple-element.29), channel_id=1, source_target_pairs={{0,2},{1,3},{2,0},{3,1},{4,6},{5,7},{6,4},{7,5},{8,10},{9,11},{10,... | collective-permute-start | bytes 393224 | tf_op jit(solution)/shard_map/ppermute | solution.py:235
  121.5 8.9 %copy-start.24 = (bf16[128,512]{1,0:T(8,128)(2,1)}, bf16[128,512]{1,0:T(8,128)(2,1)S(1)}, u32[]{:S(2)}) copy-start(bf16[128,512]{1,0:T(8,128)(2,1)S(1)} %collective-permute-done.14.refs_1_) | copy-start | bytes 393220
  121.5 8.9 %collective-permute-start.16 = (bf16[128,512]{1,0:T(8,128)(2,1)S(1)}, bf16[128,512]{1,0:T(8,128)(2,1)S(1)}, u32[]{:S(2)}, u32[]{:S(2)}) collective-permute-start(bf16[128,512]{1,0:T(8,128)(2,1)S(1)} %get-tuple-element.28), channel_id=1, source_target_pairs={{0,3},{1,0},{2,1},{3,2},{4,7},{5,4},{6,5},{7,6},{8,11},{9,8},{10,9... | collective-permute-start | bytes 393224 | tf_op jit(solution)/shard_map/ppermute | solution.py:235
  133.1 8.8 %all-to-all-start = ((bf16[8,16,512]{2,1,0:T(8,128)(2,1)}), bf16[8,16,512]{2,1,0:T(8,128)(2,1)S(1)}, u32[]{:S(2)}, u32[]{:S(2)}) async-start(bf16[8,16,512]{2,1,0:T(8,128)(2,1)} %bitcast.52), calls=%async_computation | async-start | bytes 262144 | tf_op jit(solution)/shard_map/all_to_all | solution.py:360
  (17 other events, 25.3 us)

commit v3 on v1

v3 whole, which is shorter than its diff:
```python
import functools
import math

import jax
import jax.numpy as jnp
from jax import lax
from jax.experimental import pallas as pl
from jax.experimental.pallas import tpu as pltpu
from jax.sharding import PartitionSpec as P

EPSILON = 1e-06
NEGATIVE = -1e30
F32 = jnp.float32
BF16 = jnp.bfloat16
VMEM = pl.BlockSpec(memory_space=pltpu.VMEM)
HBM = pl.BlockSpec(memory_space=pltpu.HBM)
SMEM = pl.BlockSpec(memory_space=pltpu.SMEM)


def dot(left, right):
    return jnp.dot(left, right, preferred_element_type=F32)


def dot_t(left, right):
    return lax.dot_general(left, right, (((1,), (1,)), ((), ())), preferred_element_type=F32)


def unit(values):
    return (values * lax.rsqrt(jnp.mean(values * values, axis=-1, keepdims=True) + EPSILON)).astype(BF16)


def gelu(values):
    inner = math.sqrt(2.0 / math.pi) * (values + 0.044715 * (values * values * values))
    return 0.5 * values * (1.0 + jnp.tanh(inner))


def local_kernel(span, piece, step, me_ref, scale_ref, slots_ref, gain_ref, x_hbm, *refs):
    ways = slots_ref.shape[1]
    sources, parts, shares = refs[:5], refs[5 : 5 + ways], refs[5 + ways : 5 + 2 * ways]
    x_ref, part_ref, share_ref = refs[5 + 2 * ways : 8 + 2 * ways]
    held, (in_sem, x_sem, part_sem, share_sem) = refs[8 + 2 * ways : 13 + 2 * ways], refs[13 + 2 * ways :]
    patches = share_ref.shape[1]
    width = x_ref.shape[1]
    own = span // ways
    rows = piece * span
    pieces = patches // piece
    loads = [pltpu.make_async_copy(s, h, in_sem.at[i]) for i, (s, h) in enumerate(zip(sources, held))]
    cuts = [slice(i * rows, (i + 1) * rows) for i in range(pieces)]
    x_loads = [pltpu.make_async_copy(x_hbm.at[pl.ds(c.start, rows)], x_ref.at[pl.ds(c.start, rows)], x_sem.at[i]) for i, c in enumerate(cuts)]
    x_loads[0].start()
    loads[0].start()
    for copy in x_loads[1:] + loads[1:]:
        copy.start()
    qkv_ref, up_ref, out_ref, down_ref, proj_ref = held
    at = lax.broadcasted_iota(jnp.int32, (rows, rows), 0)
    to = lax.broadcasted_iota(jnp.int32, (rows, rows), 1)
    order = (to == (at % piece) * span + at // piece).astype(F32).astype(BF16)
    kept = lax.broadcasted_iota(jnp.int32, (rows, 1), 0) // piece // own == me_ref[0]
    xs, normed = [], []
    for i, cut in enumerate(cuts):
        x_loads[i].wait()
        x = dot(order, x_ref[cut])
        xs.append(jnp.where(kept, x, 0.0).astype(BF16))
        factor = lax.rsqrt(jnp.mean(x * x, axis=-1, keepdims=True) + EPSILON)
        normed.append((x * factor * gain_ref[...]).astype(BF16))
    xs, normed = jnp.concatenate(xs, axis=0), jnp.concatenate(normed, axis=0)
    loads[0].wait()
    query, key, value = (dot(normed, qkv_ref[i]) for i in range(3))
    seen = (at % piece == to % piece) & (to <= at)
    heads = scale_ref.shape[0]
    depth = query.shape[1] // heads
    attended = []
    for cut in cuts:
        columns = []
        for h in range(heads):
            head = slice(h * depth, (h + 1) * depth)
            scores = dot_t(unit(query[cut, head]), unit(key[cut, head])) * (scale_ref[h] / math.sqrt(depth))
            scores = jnp.where(seen, scores, NEGATIVE)
            weights = jnp.exp(scores - jnp.max(scores, axis=-1, keepdims=True))
            total = jnp.sum(weights, axis=-1, keepdims=True)
            columns.append((dot(weights.astype(BF16), value[cut, head].astype(BF16)) / total).astype(BF16))
        attended.append(jnp.concatenate(columns, axis=1))
    attended = jnp.concatenate(attended, axis=0)
    loads[1].wait()
    act = gelu(dot(normed, up_ref[...])).astype(BF16)
    for copy in loads[2:]:
        copy.wait()
    share = 0.0
    stores = []
    for c in range(0, width, step):
        columns = slice(c, c + step)
        partial = dot(attended, out_ref[:, columns]) + dot(act, down_ref[:, columns])
        partial = (partial + xs[:, columns].astype(F32)).astype(BF16)
        for i, cut in enumerate(cuts):
            for b in range(span):
                put = (b % own) * patches + i * piece
                part_ref[b // own, put : put + piece, columns] = partial[cut][b * piece : (b + 1) * piece]
        for slot, part in enumerate(parts):
            source = part_ref.at[slots_ref[0, slot], :, pl.ds(c, step)]
            stores.append(pltpu.make_async_copy(source, part.at[:, pl.ds(c, step)], part_sem.at[len(stores)]))
            stores[-1].start()
        share += dot(partial, proj_ref[columns])
    share = share.astype(BF16)
    size = share.shape[1]
    for i, cut in enumerate(cuts):
        for b in range(span):
            put = slice((b % own) * size, (b % own + 1) * size)
            share_ref[b // own, i * piece : (i + 1) * piece, put] = share[cut][b * piece : (b + 1) * piece]
    for slot, out in enumerate(shares):
        stores.append(pltpu.make_async_copy(share_ref.at[slots_ref[1, slot]], out, share_sem.at[slot]))
        stores[-1].start()
    for copy in stores:
        copy.wait()


def local_part(me, scale, slots, x, gain, qkv, out, up, down, proj, span):
    rows, width = x.shape
    patches = rows // span
    ways = slots.shape[1]
    own = span // ways
    weights = (qkv, up, out, down, proj)
    piece = math.gcd(patches, 32)
    step = math.gcd(width, 256)
    part = (own * patches, width)
    share = (patches, own * proj.shape[1])
    outs = pl.pallas_call(
        functools.partial(local_kernel, span, piece, step),
        in_specs=[SMEM, SMEM, SMEM, VMEM] + [HBM] * (1 + len(weights)),
        out_specs=[HBM] * (2 * ways),
        out_shape=[jax.ShapeDtypeStruct(part, BF16)] * ways + [jax.ShapeDtypeStruct(share, BF16)] * ways,
        scratch_shapes=[pltpu.VMEM(x.shape, BF16), pltpu.VMEM((ways, *part), BF16), pltpu.VMEM((ways, *share), BF16)]
        + [pltpu.VMEM(w.shape, w.dtype) for w in weights]
        + [
            pltpu.SemaphoreType.DMA((len(weights),)),
            pltpu.SemaphoreType.DMA((patches // piece,)),
            pltpu.SemaphoreType.DMA((ways * (width // step),)),
            pltpu.SemaphoreType.DMA((ways,)),
        ],
        compiler_params=pltpu.CompilerParams(vmem_limit_bytes=60 * 2**20),
        name="local_part",
    )(me, scale, slots, gain, x, *weights)
    return outs[:ways], outs[ways:]


def fetch_kernel(source, held, sems):
    parts = source.shape[0]
    copies = [pltpu.make_async_copy(source.at[i], held.at[i], sems.at[i]) for i in range(parts)]
    for copy in copies:
        copy.start()
    for copy in copies:
        copy.wait()


def fetch(weight):
    return pl.pallas_call(
        fetch_kernel,
        in_specs=[HBM],
        out_specs=VMEM,
        out_shape=pltpu.VMEM(weight.shape, weight.dtype),
        scratch_shapes=[pltpu.SemaphoreType.DMA((weight.shape[0],))],
        compiler_params=pltpu.CompilerParams(vmem_limit_bytes=50 * 2**20),
        name="fetch",
    )(weight)


def heads_kernel(depth, ids_ref, gain_ref, *refs):
    ways = gain_ref.shape[0]
    shares, (weight, query_ref, keyed_ref) = refs[:ways], refs[ways:]
    width = shares[0].shape[1]
    values = [s[...].astype(F32) for s in shares]
    square = sum(jnp.sum(v * v, axis=-1, keepdims=True) for v in values)
    factor = lax.rsqrt(square / (ways * width) + EPSILON)
    normed = [(v * factor * gain_ref[ids_ref[c]]).astype(BF16) for c, v in enumerate(values)]
    for kind in range(3):
        mixed = sum(
            dot(n, weight[kind, pl.ds(pl.multiple_of(ids_ref[c] * width, width), width), :])
            for c, n in enumerate(normed)
        )
        size = mixed.shape[1]
        if kind < 2:
            mixed = jnp.concatenate([unit(mixed[:, c : c + depth]) for c in range(0, size, depth)], axis=1)
        if kind == 0:
            query_ref[...] = mixed
        else:
            keyed_ref[:, (kind - 1) * size : kind * size] = mixed.astype(BF16)


def global_heads(depth, ids, gain, shares, qkv):
    rows, size = shares[0].shape[0], qkv.shape[2]
    return pl.pallas_call(
        functools.partial(heads_kernel, depth),
        in_specs=[SMEM] + [VMEM] * (2 + len(shares)),
        out_specs=(VMEM, VMEM),
        out_shape=(jax.ShapeDtypeStruct((rows, size), BF16), jax.ShapeDtypeStruct((rows, 2 * size), BF16)),
        compiler_params=pltpu.CompilerParams(vmem_limit_bytes=8 * 2**20),
        name="global_heads",
    )(ids, gain, *shares, qkv)


def attend_kernel(count, slots_ref, ids_ref, scale_ref, q_ref, *refs):
    pieces, proj_ref, outs = refs[:count], refs[count], refs[count + 1 :]
    rows, size = q_ref.shape
    at = lax.broadcasted_iota(jnp.int32, (rows, rows), 0)
    to = lax.broadcasted_iota(jnp.int32, (rows, rows), 1)
    heads = scale_ref.shape[0]
    depth = size // heads
    me = ids_ref[0]
    seen = [to + ids_ref[i] * rows <= at + me * rows for i in range(count)]
    attended = []
    for h in range(heads):
        cut = slice(h * depth, (h + 1) * depth)
        query = q_ref[:, cut]
        factor = scale_ref[h] / math.sqrt(depth)
        scores = [jnp.where(s, dot_t(query, p[:, cut]) * factor, NEGATIVE) for s, p in zip(seen, pieces)]
        top = functools.reduce(jnp.maximum, [jnp.max(s, axis=-1, keepdims=True) for s in scores])
        weights = [jnp.exp(s - top) for s in scores]
        total = sum(jnp.sum(w, axis=-1, keepdims=True) for w in weights)
        cut = slice(size + h * depth, size + (h + 1) * depth)
        summed = sum(dot(w.astype(BF16), p[:, cut]) for w, p in zip(weights, pieces))
        attended.append((summed / total).astype(BF16))
    attended = jnp.concatenate(attended, axis=1)
    for slot, out in enumerate(outs):
        width = out.shape[1]
        out[...] = dot(attended, proj_ref[:, pl.ds(pl.multiple_of(slots_ref[slot] * width, width), width)]).astype(BF16)


def attend(slots, ids, scale, query, pieces, proj):
    rows, ways = query.shape[0], slots.shape[0]
    return pl.pallas_call(
        functools.partial(attend_kernel, len(pieces)),
        in_specs=[SMEM, SMEM, SMEM] + [VMEM] * (2 + len(pieces)),
        out_specs=[VMEM] * ways,
        out_shape=[jax.ShapeDtypeStruct((rows, proj.shape[1] // ways), BF16)] * ways,
        compiler_params=pltpu.CompilerParams(vmem_limit_bytes=16 * 2**20),
        name="attend",
    )(slots, ids, scale, query, *pieces, proj)


def result_kernel(count, order_ref, own_ref, *refs):
    pieces, (result_ref, routed_ref) = refs[:count], refs[count:]
    total = own_ref[...].astype(F32) + sum(p[...].astype(F32) for p in pieces)
    result = total.astype(BF16)
    result_ref[...] = result
    routed_ref[...] = dot(order_ref[...], result).astype(BF16)


def finish_result(order, residual, pieces):
    shape = jax.ShapeDtypeStruct(residual.shape, BF16)
    return pl.pallas_call(
        functools.partial(result_kernel, len(pieces)),
        in_specs=[VMEM] * (2 + len(pieces)),
        out_specs=(VMEM, VMEM),
        out_shape=(shape, shape),
        compiler_params=pltpu.CompilerParams(vmem_limit_bytes=4 * 2**20),
        name="finish_result",
    )(order, residual, *pieces)


def bytes_kernel(count, kept_ref, result_ref, proj_ref, *refs):
    pieces, out_ref = refs[:count], refs[count]
    state = pieces[0][...].astype(F32)
    for i, p in enumerate(pieces[1:], 1):
        state += jnp.where(kept_ref[i] != 0, p[...].astype(F32), 0.0)
    state = state.astype(BF16).astype(F32)
    rows = result_ref.shape[0]
    width = proj_ref.shape[0]
    own = state.shape[0] // rows
    mixed = [
        (state[b * rows : (b + 1) * rows] + dot(result_ref[:, b * width : (b + 1) * width], proj_ref[...])).astype(BF16)
        for b in range(own)
    ]
    at = lax.broadcasted_iota(jnp.int32, (rows * own, rows * own), 0)
    to = lax.broadcasted_iota(jnp.int32, (rows * own, rows * own), 1)
    order = (to == (at % own) * rows + at // own).astype(F32).astype(BF16)
    out_ref[...] = dot(order, jnp.concatenate(mixed, axis=0)).astype(BF16)


def finish_bytes(kept, result, proj, pieces):
    return pl.pallas_call(
        functools.partial(bytes_kernel, len(pieces)),
        in_specs=[SMEM] + [VMEM] * (2 + len(pieces)),
        out_specs=VMEM,
        out_shape=jax.ShapeDtypeStruct(pieces[0].shape, BF16),
        compiler_params=pltpu.CompilerParams(vmem_limit_bytes=16 * 2**20),
        name="finish_bytes",
    )(kept, result, proj, *pieces)


def shift(value, axis, step):
    count = lax.axis_size(axis)
    return lax.ppermute(value, axis, [(i, (i + step) % count) for i in range(count)])


def scatter(chunks, axis):
    return [chunks[0]] + [shift(chunk, axis, step) for step, chunk in enumerate(chunks[1:], 1)]


def shift_slots(axis):
    count = lax.axis_size(axis)
    return ((lax.axis_index(axis) + jnp.arange(count)) % count).astype(jnp.int32)


def relay_slots(axis):
    me = lax.axis_index(axis)
    outer = (me == 0) | (me == 3)
    beside, across = me ^ 1, 3 - me
    return jnp.stack([me, jnp.where(outer, across, beside), jnp.where(outer, beside, across), me ^ 2]).astype(jnp.int32)


def relay_first(chunks, axis):
    swapped = lax.ppermute(chunks[1], axis, [(0, 1), (1, 0), (2, 3), (3, 2)])
    middle = lax.ppermute(chunks[2], axis, [(1, 2), (2, 1)])
    return swapped, middle


def relay_rest(chunks, swapped, middle, axis):
    me = lax.axis_index(axis)
    outer = (me == 0) | (me == 3)
    sent = (chunks[3].astype(F32) + jnp.where(outer, 0.0, swapped.astype(F32))).astype(BF16)
    inward = lax.ppermute(chunks[2], axis, [(0, 1), (3, 2)])
    crossed = lax.ppermute(sent, axis, [(0, 2), (2, 0), (1, 3), (3, 1)])
    outer = outer.astype(jnp.int32)
    return jnp.stack([1 + 0 * outer, outer, 1 - outer, 1 - outer, 1 + 0 * outer]), [chunks[0], swapped, middle, inward, crossed]


def gather(value, axis):
    return [value] + [shift(value, axis, step) for step in range(1, lax.axis_size(axis))]


def gather_chips(value, axis):
    count = lax.axis_size(axis)
    other = [(i, i ^ 1) for i in range(count)]
    pieces = [value] + [shift(value, axis, 2 * step) for step in range(1, count // 2)]
    return pieces + [lax.ppermute(p, axis, other) for p in pieces]


def chip_ids(axis):
    count = lax.axis_size(axis)
    me = lax.axis_index(axis)
    mine = (me - 2 * jnp.arange(count // 2, dtype=jnp.int32)) % count
    return jnp.concatenate([mine, mine ^ 1]).astype(jnp.int32)


def owner_order(owners, source, patches):
    listed = lax.dynamic_index_in_dim(owners, source, 0, keepdims=False)
    count = listed.shape[0]
    block = patches // count
    index = jnp.arange(count, dtype=jnp.int32)
    before = (listed[None, :] < listed[:, None]) | (
        (listed[None, :] == listed[:, None]) & (index[None, :] < index[:, None])
    )
    slot = jnp.sum(before, axis=1).astype(jnp.int32)
    row = jnp.arange(patches, dtype=jnp.int32)
    spread = jnp.sum(jnp.where(row[:, None] // block == index[None, :], slot[None, :], 0), axis=1).astype(jnp.int32)
    place = spread * block + row % block
    return (row[:, None] == place[None, :]).astype(BF16)


def on_device(
    byte_in,
    local_gain,
    local_qkv,
    local_out,
    mlp_up,
    mlp_down,
    local_scale,
    patch_proj,
    global_gain,
    global_qkv,
    global_out,
    global_scale,
    back_proj,
    owners,
):
    patches, span, width = byte_in.shape
    ways = lax.axis_size("head")
    own = span // ways
    me = lax.axis_index("head").astype(jnp.int32)
    seq = lax.axis_index("seq").astype(jnp.int32)
    depth = global_qkv.shape[2] // global_scale.shape[0]

    line = ways == 4
    slots = jnp.stack([relay_slots("head") if line else shift_slots("head"), shift_slots("head")])
    parts, chunks = local_part(
        me.reshape(1),
        local_scale,
        slots,
        byte_in.reshape(-1, width),
        local_gain.reshape(1, -1),
        jnp.transpose(local_qkv, (1, 0, 2)),
        local_out,
        mlp_up,
        mlp_down,
        patch_proj,
        span,
    )
    residual = sum(p.astype(F32) for p in scatter(chunks, "head")).astype(BF16)
    weight, residual = lax.optimization_barrier((jnp.transpose(global_qkv, (1, 0, 2)), residual))
    shares = gather(residual, "head")
    ids = (me - jnp.arange(ways, dtype=jnp.int32)) % ways
    query, keyed = global_heads(depth, ids, global_gain.reshape(ways, 1, -1), shares, fetch(weight))
    parts, keyed = lax.optimization_barrier((parts, keyed))
    if line:
        swapped, middle = relay_first(parts, "head")
        query, swapped, middle = lax.optimization_barrier((query, swapped, middle))
        kept, parts = relay_rest(parts, swapped, middle, "head")
    else:
        kept, parts = jnp.ones((ways,), jnp.int32), scatter(parts, "head")
    update = attend(slots[1], chip_ids("seq"), global_scale, query, gather_chips(keyed, "seq"), global_out)
    result, routed = finish_result(owner_order(owners, seq, patches), residual, scatter(update, "head"))
    global_state = lax.all_to_all(routed, "seq", split_axis=0, concat_axis=0, tiled=True)
    byte_out = finish_bytes(kept, result, back_proj, parts)
    return byte_out.reshape(patches, own, width), global_state


def solution(mesh):
    placed = (
        P("seq", None, None),
        P(),
        P(None, None, "head"),
        P("head", None),
        P(None, "head"),
        P("head", None),
        P("head"),
        P(),
        P(),
        P(None, None, "head"),
        P("head", None),
        P("head"),
        P(),
        P(),
    )
    return jax.shard_map(
        on_device,
        mesh=mesh,
        in_specs=placed,
        out_specs=(P("seq", "head", None), P("seq", "head")),
        check_vma=False,
    )
```

time: 148 us -> 123 us (0.83)
  local copies, waits for them, and re-layouts: 13.6 us -> 1.79 us
  blocking collectives: 8.81 us -> 0 us
  other arithmetic: 11.1 us -> 3.06 us
  starting transfers between devices: 30.4 us -> 35.5 us
  waiting for transfers between devices: 58.7 us -> 54.2 us
  Pallas kernels: 23.6 us -> 27.8 us
    ppermute x18 -> x12, waiting for transfers between devices: 58.7 us -> 48.2 us  [shift(): lax.ppermute(value, axis, [(i, (i + step) % count) for i in range(count)])]
    add x1, other arithmetic: 10 us -> 0.01 us  [owner_order(): place = spread * block + row % block]
    unnamed x63 -> x17, local copies, waits for them, and re-layouts: 9.93 us -> 0.7 us
    ppermute x0 -> x4, starting transfers between devices: none -> 8.94 us  [the longest x1 4.93 us: relay_rest(): inward = lax.ppermute(chunks[2], axis, [(0, 1), (3, 2)])]
    all_to_all x1 -> x0, blocking collectives: 8.81 us -> none  [on_device(): lax.all_to_all(routed, 'seq', split_axis=0, concat_axis=0, tiled=True)]
    ppermute x18 -> x12, starting transfers between devices: 28.3 us -> 22.5 us  [shift(): lax.ppermute(value, axis, [(i, (i + step) % count) for i in range(count)])]
    all_to_all x0 -> x1, waiting for transfers between devices: none -> 5.37 us  [on_device(): lax.all_to_all(routed, 'seq', split_axis=0, concat_axis=0, tiled=True)]
    pallas_call x5, Pallas kernels: 21.5 us -> 26.8 us  [the longest x1 17.4 us: local_part(): pl.pallas_call(functools.partial(local_kernel, span, piece, step), in_spe...]
  transfers between devices with their start and end apart: 26 -> 21, of which waited for: 10 -> 10; matrix products, arithmetic and copies ran while one was open for 9% -> 1% of each run, Pallas kernels for 4% -> 5%
where the time goes in v3:
time: 123 us
  waiting for transfers between devices  54.2 us (44%)
  starting transfers between devices  35.5 us (29%)
  Pallas kernels  27.8 us (23%)
  other arithmetic  3.06 us (2%)
  local copies, waits for them, and re-layouts  1.79 us (1%)
    ppermute x12, waiting for transfers between devices, shift(): lax.ppermute(value, axis, [(i, (i + step) % count) for i in range(count)])  48.2 us
    ppermute x12, starting transfers between devices, shift(): lax.ppermute(value, axis, [(i, (i + step) % count) for i in range(count)])  22.5 us
    pallas_call x1, Pallas kernels, local_part(): pl.pallas_call(functools.partial(local_kernel, span, piece, step), in_spe...  17.4 us
    all_to_all x1, waiting for transfers between devices, on_device(): lax.all_to_all(routed, 'seq', split_axis=0, concat_axis=0, tiled=True)  5.37 us
    ppermute x1, starting transfers between devices, relay_rest(): inward = lax.ppermute(chunks[2], axis, [(0, 1), (3, 2)])  4.93 us
    all_to_all x1, starting transfers between devices, on_device(): lax.all_to_all(routed, 'seq', split_axis=0, concat_axis=0, tiled=True)  3.37 us
    ppermute x1, starting transfers between devices, relay_first(): swapped = lax.ppermute(chunks[1], axis, [(0, 1), (1, 0), (2, 3), (3, 2)])  3.32 us
    pallas_call x1, Pallas kernels, attend(): pl.pallas_call(functools.partial(attend_kernel, len(pieces)), in_specs=[S...  2.94 us
  transfers between devices with their start and end apart: 21, of which 10 were waited for; matrix products, arithmetic and copies ran while one was open for 1% of the time, Pallas kernels for 5%

profile of v3, /device:TPU:0, one launch (start us, length us, event | category | flops | bytes accessed | tf_op | source)
XLA Modules:
  0.0 123.2 jit_solution(11500861187625338904)
XLA Ops:
  1.3 17.4 %local_part.1 = (bf16[256,1024]{1,0:T(8,128)(2,1)}, bf16[256,1024]{1,0:T(8,128)(2,1)}, bf16[256,1024]{1,0:T(8,128)(2,1)}, bf16[256,1024]{1,0:T(8,128)(2,1)}, bf1...) custom-call(s32[1]{0:T(128)} %bitcast.4.me_ref, ...), custom_call_target="tpu_custom_call" | custom-call | tf_op jit(solution)/shard_map/local_part/pallas_call | solution.py:126
  18.7 3.1 %collective-permute-start = (bf16[128,512]{1,0:T(8,128)(2,1)}, bf16[128,512]{1,0:T(8,128)(2,1)S(1)}, u32[]{:S(2)}, u32[]{:S(2)}) collective-permute-start(bf16[128,512]{1,0:T(8,128)(2,1)} %get-tuple-element.29), channel_id=1, source_target_pairs={{0,1},{1,2},{2,3},{3,0},{4,5},{5,6},{6,7},{7,4},{8,9},{9,10},{10,1... | collective-permute-start | bytes 393224 | tf_op jit(solution)/shard_map/ppermute | solution.py:291
  21.8 2.6 %collective-permute-start.1 = (bf16[128,512]{1,0:T(8,128)(2,1)}, bf16[128,512]{1,0:T(8,128)(2,1)S(1)}, u32[]{:S(2)}, u32[]{:S(2)}) collective-permute-start(bf16[128,512]{1,0:T(8,128)(2,1)} %get-tuple-element.30), channel_id=1, source_target_pairs={{0,2},{1,3},{2,0},{3,1},{4,6},{5,7},{6,4},{7,5},{8,10},{9,11},{10,... | collective-permute-start | bytes 393224 | tf_op jit(solution)/shard_map/ppermute | solution.py:291
  24.4 1.4 %collective-permute-start.2 = (bf16[128,512]{1,0:T(8,128)(2,1)}, bf16[128,512]{1,0:T(8,128)(2,1)S(1)}, u32[]{:S(2)}, u32[]{:S(2)}) collective-permute-start(bf16[128,512]{1,0:T(8,128)(2,1)} %get-tuple-element.31), channel_id=1, source_target_pairs={{0,3},{1,0},{2,1},{3,2},{4,7},{5,4},{6,5},{7,6},{8,11},{9,8},{10,9... | collective-permute-start | bytes 393224 | tf_op jit(solution)/shard_map/ppermute | solution.py:291
  25.8 2.7 %collective-permute-done = bf16[128,512]{1,0:T(8,128)(2,1)S(1)} collective-permute-done((bf16[128,512]{1,0:T(8,128)(2,1)}, bf16[128,512]{1,0:T(8,128)(2,1)S(1)}, u32[]{:S(2)}, u32[]{:S(2)}) %collective-permute-start) | collective-permute-done | bytes 131104 | tf_op jit(solution)/shard_map/ppermute | solution.py:291
  28.5 4.8 %collective-permute-done.1 = bf16[128,512]{1,0:T(8,128)(2,1)S(1)} collective-permute-done((bf16[128,512]{1,0:T(8,128)(2,1)}, bf16[128,512]{1,0:T(8,128)(2,1)S(1)}, u32[]{:S(2)}, u32[]{:S(2)}) %collective-permute-start.1) | collective-permute-done | bytes 131104 | tf_op jit(solution)/shard_map/ppermute | solution.py:291
  33.2 1.0 add_convert_fusion.1.refs_0_.own_ref
  34.2 3.3 %collective-permute-start.3 = (bf16[128,512]{1,0:T(8,128)(2,1)S(1)}, bf16[128,512]{1,0:T(8,128)(2,1)S(1)}, u32[]{:S(2)}, u32[]{:S(2)}) collective-permute-start(bf16[128,512]{1,0:T(8,128)(2,1)S(1)} %add_convert_fusion.1.refs_0_.own_ref), channel_id=1, source_target_pairs={{0,1},{1,2},{2,3},{3,0},{4,5},{5,6},{6,7},{7,4},{8,9},{9,10},{10,1... | collective-permute-start | bytes 393224 | tf_op jit(solution)/shard_map/ppermute | solution.py:291
  37.5 1.6 %collective-permute-start.4 = (bf16[128,512]{1,0:T(8,128)(2,1)S(1)}, bf16[128,512]{1,0:T(8,128)(2,1)S(1)}, u32[]{:S(2)}, u32[]{:S(2)}) collective-permute-start(bf16[128,512]{1,0:T(8,128)(2,1)S(1)} %add_convert_fusion.1.refs_0_.own_ref), channel_id=1, source_target_pairs={{0,2},{1,3},{2,0},{3,1},{4,6},{5,7},{6,4},{7,5},{8,10},{9,11},{10,... | collective-permute-start | bytes 393224 | tf_op jit(solution)/shard_map/ppermute | solution.py:291
  39.2 0.8 collective-permute-start.5
  40.0 2.9 %fetch.1.refs_4_ = bf16[3,2048,512]{2,1,0:T(8,128)(2,1)S(1)} custom-call(bf16[3,2048,512]{2,1,0:T(8,128)(2,1)} %bitcast.18), custom_call_target="tpu_custom_call" | custom-call | tf_op jit(solution)/shard_map/fetch/pallas_call | solution.py:155
  42.9 4.3 %collective-permute-done.4.refs_2_ = bf16[128,512]{1,0:T(8,128)(2,1)S(1)} collective-permute-done((bf16[128,512]{1,0:T(8,128)(2,1)S(1)}, bf16[128,512]{1,0:T(8,128)(2,1)S(1)}, u32[]{:S(2)}, u32[]{:S(2)}) %collective-permute-start.4) | collective-permute-done | bytes 131104 | tf_op jit(solution)/shard_map/ppermute | solution.py:291
  47.3 1.7 %global_heads.1 = (bf16[128,512]{1,0:T(8,128)(2,1)S(1)}, bf16[128,1024]{1,0:T(8,128)(2,1)S(1)}) custom-call(s32[4]{0:T(128)S(1)} %and_select_fusion.ids_ref, f32[4,1,512]{2,1,0:T(1,128)S(1)} %bitcast.17, bf16[128,512]{1,0:T(8,128)(2,1)S(1)} %add_convert_fusion.1.refs_0_.own_ref, bf16[128,512]{1,0:T(8,128)(2,1)S(1)} %collective-permute-done.3.refs_1_, ...), custom_call_target="tpu_custom_call" | custom-call | tf_op jit(solution)/shard_map/global_heads/pallas_call | solution.py:190
  49.0 3.3 %collective-permute-start.6 = (bf16[256,1024]{1,0:T(8,128)(2,1)S(1)}, bf16[256,1024]{1,0:T(8,128)(2,1)S(1)}, u32[]{:S(2)}, u32[]{:S(2)}) collective-permute-start(bf16[256,1024]{1,0:T(8,128)(2,1)S(1)} %copy-done.7), channel_id=1, source_target_pairs={{0,1},{1,0},{2,3},{3,2},{4,5},{5,4},{6,7},{7,6},{8,9},{9,8},{10,11... | collective-permute-start | bytes 1572872 | tf_op jit(solution)/shard_map/ppermute | solution.py:311
  53.1 1.5 %collective-permute-start.8 = (bf16[128,1024]{1,0:T(8,128)(2,1)S(1)}, bf16[128,1024]{1,0:T(8,128)(2,1)S(1)}, u32[]{:S(2)}, u32[]{:S(2)}) collective-permute-start(bf16[128,1024]{1,0:T(8,128)(2,1)S(1)} %get-tuple-element.43.refs_0_), channel_id=1, source_target_pairs={{0,8},{4,12},{8,16},{12,20},{16,24},{20,28},{24,0},{28,4},{1,9},{5... | collective-permute-start | bytes 786440 | tf_op jit(solution)/shard_map/ppermute | solution.py:291
  54.6 1.5 %collective-permute-start.9 = (bf16[128,1024]{1,0:T(8,128)(2,1)S(1)}, bf16[128,1024]{1,0:T(8,128)(2,1)S(1)}, u32[]{:S(2)}, u32[]{:S(2)}) collective-permute-start(bf16[128,1024]{1,0:T(8,128)(2,1)S(1)} %get-tuple-element.43.refs_0_), channel_id=1, source_target_pairs={{0,16},{4,20},{8,24},{12,28},{16,0},{20,4},{24,8},{28,12},{1,17},{... | collective-permute-start | bytes 786440 | tf_op jit(solution)/shard_map/ppermute | solution.py:291
  56.1 1.4 %collective-permute-start.10 = (bf16[128,1024]{1,0:T(8,128)(2,1)S(1)}, bf16[128,1024]{1,0:T(8,128)(2,1)S(1)}, u32[]{:S(2)}, u32[]{:S(2)}) collective-permute-start(bf16[128,1024]{1,0:T(8,128)(2,1)S(1)} %get-tuple-element.43.refs_0_), channel_id=1, source_target_pairs={{0,24},{4,28},{8,0},{12,4},{16,8},{20,12},{24,16},{28,20},{1,25},{... | collective-permute-start | bytes 786440 | tf_op jit(solution)/shard_map/ppermute | solution.py:291
  57.8 5.4 %collective-permute-done.8.refs_1_ = bf16[128,1024]{1,0:T(8,128)(2,1)S(1)} collective-permute-done((bf16[128,1024]{1,0:T(8,128)(2,1)S(1)}, bf16[128,1024]{1,0:T(8,128)(2,1)S(1)}, u32[]{:S(2)}, u32[]{:S(2)}) %collective-permute-start.8) | collective-permute-done | bytes 262176 | tf_op jit(solution)/shard_map/ppermute | solution.py:291
  63.3 4.3 %collective-permute-done.9.refs_2_ = bf16[128,1024]{1,0:T(8,128)(2,1)S(1)} collective-permute-done((bf16[128,1024]{1,0:T(8,128)(2,1)S(1)}, bf16[128,1024]{1,0:T(8,128)(2,1)S(1)}, u32[]{:S(2)}, u32[]{:S(2)}) %collective-permute-start.9) | collective-permute-done | bytes 262176 | tf_op jit(solution)/shard_map/ppermute | solution.py:291
  67.6 4.9 %collective-permute-start.18 = (bf16[256,1024]{1,0:T(8,128)(2,1)}, bf16[256,1024]{1,0:T(8,128)(2,1)S(1)}, u32[]{:S(2)}, u32[]{:S(2)}) collective-permute-start(bf16[256,1024]{1,0:T(8,128)(2,1)} %get-tuple-element.41), channel_id=1, source_target_pairs={{0,1},{3,2},{4,5},{7,6},{8,9},{11,10},{12,13},{15,14},{16,17},{19,... | collective-permute-start | bytes 1572872 | tf_op jit(solution)/shard_map/ppermute | solution.py:320
  73.2 1.0 add_convert_fusion
  74.9 2.9 %attend.1 = (bf16[128,512]{1,0:T(8,128)(2,1)S(1)}, bf16[128,512]{1,0:T(8,128)(2,1)S(1)}, bf16[128,512]{1,0:T(8,128)(2,1)S(1)}, bf16[128,512]{1,0:T(8,128)(2,1)S(1)}) custom-call(s32[4]{0:T(128)S(1)} %and_select_fusion.2.slots_ref, s32[8]{0:T(128)S(1)} %pad_add_fusion.1.ids_ref, f32[4]{0:T(128)S(1)} %copy-done.5, ...), custom_call_target="tpu_custom_call" | custom-call | tf_op jit(solution)/shard_map/attend/pallas_call | solution.py:229
  77.8 1.4 %collective-permute-start.15 = (bf16[128,512]{1,0:T(8,128)(2,1)S(1)}, bf16[128,512]{1,0:T(8,128)(2,1)S(1)}, u32[]{:S(2)}, u32[]{:S(2)}) collective-permute-start(bf16[128,512]{1,0:T(8,128)(2,1)S(1)} %get-tuple-element.45), channel_id=1, source_target_pairs={{0,1},{1,2},{2,3},{3,0},{4,5},{5,6},{6,7},{7,4},{8,9},{9,10},{10,1... | collective-permute-start | bytes 393224 | tf_op jit(solution)/shard_map/ppermute | solution.py:291
  79.2 1.1 collective-permute-start.16
  80.3 2.8 %collective-permute-start.17 = (bf16[128,512]{1,0:T(8,128)(2,1)S(1)}, bf16[128,512]{1,0:T(8,128)(2,1)S(1)}, u32[]{:S(2)}, u32[]{:S(2)}) collective-permute-start(bf16[128,512]{1,0:T(8,128)(2,1)S(1)} %get-tuple-element.47), channel_id=1, source_target_pairs={{0,3},{1,0},{2,1},{3,2},{4,7},{5,4},{6,5},{7,6},{8,11},{9,8},{10,9... | collective-permute-start | bytes 393224 | tf_op jit(solution)/shard_map/ppermute | solution.py:291
  83.1 17.8 %collective-permute-done.15.refs_1_ = bf16[128,512]{1,0:T(8,128)(2,1)S(1)} collective-permute-done((bf16[128,512]{1,0:T(8,128)(2,1)S(1)}, bf16[128,512]{1,0:T(8,128)(2,1)S(1)}, u32[]{:S(2)}, u32[]{:S(2)}) %collective-permute-start.15) | collective-permute-done | bytes 131104 | tf_op jit(solution)/shard_map/ppermute | solution.py:291
  100.9 8.8 %collective-permute-done.16.refs_2_ = bf16[128,512]{1,0:T(8,128)(2,1)S(1)} collective-permute-done((bf16[128,512]{1,0:T(8,128)(2,1)S(1)}, bf16[128,512]{1,0:T(8,128)(2,1)S(1)}, u32[]{:S(2)}, u32[]{:S(2)}) %collective-permute-start.16) | collective-permute-done | bytes 131104 | tf_op jit(solution)/shard_map/ppermute | solution.py:291
  109.8 0.9 finish_result.1
  110.7 3.4 %all-to-all-start = ((bf16[8,16,512]{2,1,0:T(8,128)(2,1)}), bf16[8,16,512]{2,1,0:T(8,128)(2,1)S(1)}, u32[]{:S(2)}, u32[]{:S(2)}) async-start(bf16[8,16,512]{2,1,0:T(8,128)(2,1)} %bitcast.13), calls=%async_computation | async-start | bytes 262144 | tf_op jit(solution)/shard_map/all_to_all | solution.py:411
  114.1 5.4 %all-to-all-done = bf16[8,16,512]{2,1,0:T(8,128)(2,1)S(1)} async-done(((bf16[8,16,512]{2,1,0:T(8,128)(2,1)}), bf16[8,16,512]{2,1,0:T(8,128)(2,1)S(1)}, u32[]{:S(2)}, u32[]{:S(2)}) %all-to-all-start) | async-done | bytes 131104 | tf_op jit(solution)/shard_map/all_to_all | solution.py:411
  119.5 2.0 %finish_bytes.1 = bf16[256,1024]{1,0:T(8,128)(2,1)S(1)} custom-call(s32[5]{0:T(128)S(1)} %stack.32.kept_ref, bf16[128,512]{1,0:T(8,128)(2,1)S(1)} %get-tuple-element.48.result_ref, bf16[256,1024]{1,0:T(8,128)(2,1)S(1)} %copy-done.2, bf16[256,1024]{1,0:T(8,128)(2,1)S(1)} %copy-done.3, bf16[256,1024]{1,0:T(8,128)(2,1)S(1)} %collective-permute-done.6.refs_1_, ...), custom_call_target="tpu_custom_call" | custom-call | tf_op jit(solution)/shard_map/finish_bytes/pallas_call | solution.py:279
  121.5 1.0 reshape.118
  (50 shorter events, 3.9 us)
Async XLA Ops:
  0.6 56.9 %copy-start = (s32[8,16]{1,0:T(8,128)S(1)}, s32[8,16]{1,0:T(8,128)}, u32[]{:S(2)}) copy-start(s32[8,16]{1,0:T(8,128)} %param.27) | copy-start | bytes 1540
  18.7 9.7 %collective-permute-start = (bf16[128,512]{1,0:T(8,128)(2,1)}, bf16[128,512]{1,0:T(8,128)(2,1)S(1)}, u32[]{:S(2)}, u32[]{:S(2)}) collective-permute-start(bf16[128,512]{1,0:T(8,128)(2,1)} %get-tuple-element.29), channel_id=1, source_target_pairs={{0,1},{1,2},{2,3},{3,0},{4,5},{5,6},{6,7},{7,4},{8,9},{9,10},{10,1... | collective-permute-start | bytes 393224 | tf_op jit(solution)/shard_map/ppermute | solution.py:291
  21.8 11.4 %collective-permute-start.1 = (bf16[128,512]{1,0:T(8,128)(2,1)}, bf16[128,512]{1,0:T(8,128)(2,1)S(1)}, u32[]{:S(2)}, u32[]{:S(2)}) collective-permute-start(bf16[128,512]{1,0:T(8,128)(2,1)} %get-tuple-element.30), channel_id=1, source_target_pairs={{0,2},{1,3},{2,0},{3,1},{4,6},{5,7},{6,4},{7,5},{8,10},{9,11},{10,... | collective-permute-start | bytes 393224 | tf_op jit(solution)/shard_map/ppermute | solution.py:291
  24.4 8.9 %collective-permute-start.2 = (bf16[128,512]{1,0:T(8,128)(2,1)}, bf16[128,512]{1,0:T(8,128)(2,1)S(1)}, u32[]{:S(2)}, u32[]{:S(2)}) collective-permute-start(bf16[128,512]{1,0:T(8,128)(2,1)} %get-tuple-element.31), channel_id=1, source_target_pairs={{0,3},{1,0},{2,1},{3,2},{4,7},{5,4},{6,5},{7,6},{8,11},{9,8},{10,9... | collective-permute-start | bytes 393224 | tf_op jit(solution)/shard_map/ppermute | solution.py:291
  34.2 8.7 %collective-permute-start.3 = (bf16[128,512]{1,0:T(8,128)(2,1)S(1)}, bf16[128,512]{1,0:T(8,128)(2,1)S(1)}, u32[]{:S(2)}, u32[]{:S(2)}) collective-permute-start(bf16[128,512]{1,0:T(8,128)(2,1)S(1)} %add_convert_fusion.1.refs_0_.own_ref), channel_id=1, source_target_pairs={{0,1},{1,2},{2,3},{3,0},{4,5},{5,6},{6,7},{7,4},{8,9},{9,10},{10,1... | collective-permute-start | bytes 393224 | tf_op jit(solution)/shard_map/ppermute | solution.py:291
  37.5 9.7 %collective-permute-start.4 = (bf16[128,512]{1,0:T(8,128)(2,1)S(1)}, bf16[128,512]{1,0:T(8,128)(2,1)S(1)}, u32[]{:S(2)}, u32[]{:S(2)}) collective-permute-start(bf16[128,512]{1,0:T(8,128)(2,1)S(1)} %add_convert_fusion.1.refs_0_.own_ref), channel_id=1, source_target_pairs={{0,2},{1,3},{2,0},{3,1},{4,6},{5,7},{6,4},{7,5},{8,10},{9,11},{10,... | collective-permute-start | bytes 393224 | tf_op jit(solution)/shard_map/ppermute | solution.py:291
  39.2 8.1 %collective-permute-start.5 = (bf16[128,512]{1,0:T(8,128)(2,1)S(1)}, bf16[128,512]{1,0:T(8,128)(2,1)S(1)}, u32[]{:S(2)}, u32[]{:S(2)}) collective-permute-start(bf16[128,512]{1,0:T(8,128)(2,1)S(1)} %add_convert_fusion.1.refs_0_.own_ref), channel_id=1, source_target_pairs={{0,3},{1,0},{2,1},{3,2},{4,7},{5,4},{6,5},{7,6},{8,11},{9,8},{10,9... | collective-permute-start | bytes 393224 | tf_op jit(solution)/shard_map/ppermute | solution.py:291
  40.0 7.3 %copy-start.4 = (f32[2048]{0:T(1024)S(1)}, f32[2048]{0:T(1024)}, u32[]{:S(2)}) copy-start(f32[2048]{0:T(1024)} %param.22) | copy-start | bytes 24580
  47.3 1.7 %copy-start.7 = (bf16[256,1024]{1,0:T(8,128)(2,1)S(1)}, bf16[256,1024]{1,0:T(8,128)(2,1)}, u32[]{:S(2)}) copy-start(bf16[256,1024]{1,0:T(8,128)(2,1)} %get-tuple-element.40) | copy-start | bytes 1572868
  47.3 25.9 %copy-start.6 = (bf16[256,1024]{1,0:T(8,128)(2,1)S(1)}, bf16[256,1024]{1,0:T(8,128)(2,1)}, u32[]{:S(2)}) copy-start(bf16[256,1024]{1,0:T(8,128)(2,1)} %get-tuple-element.52) | copy-start | bytes 1572868
  47.3 27.6 %copy-start.1 = (bf16[512,2048]{1,0:T(8,128)(2,1)S(1)}, bf16[512,2048]{1,0:T(8,128)(2,1)}, u32[]{:S(2)}) copy-start(bf16[512,2048]{1,0:T(8,128)(2,1)} %refs_8_.1) | copy-start | bytes 6291460
  47.3 27.6 %copy-start.5 = (f32[4]{0:T(128)S(1)}, f32[4]{0:T(128)}, u32[]{:S(2)}) copy-start(f32[4]{0:T(128)} %scale_ref.3) | copy-start | bytes 52
  49.0 23.6 %collective-permute-start.6 = (bf16[256,1024]{1,0:T(8,128)(2,1)S(1)}, bf16[256,1024]{1,0:T(8,128)(2,1)S(1)}, u32[]{:S(2)}, u32[]{:S(2)}) collective-permute-start(bf16[256,1024]{1,0:T(8,128)(2,1)S(1)} %copy-done.7), channel_id=1, source_target_pairs={{0,1},{1,0},{2,3},{3,2},{4,5},{5,4},{6,7},{7,6},{8,9},{9,8},{10,11... | collective-permute-start | bytes 1572872 | tf_op jit(solution)/shard_map/ppermute | solution.py:311
  52.3 20.8 %collective-permute-start.7 = (bf16[256,1024]{1,0:T(8,128)(2,1)}, bf16[256,1024]{1,0:T(8,128)(2,1)S(1)}, u32[]{:S(2)}, u32[]{:S(2)}) collective-permute-start(bf16[256,1024]{1,0:T(8,128)(2,1)} %get-tuple-element.41), channel_id=1, source_target_pairs={{1,2},{2,1},{5,6},{6,5},{9,10},{10,9},{13,14},{14,13},{17,18},{18,... | collective-permute-start | bytes 1572872 | tf_op jit(solution)/shard_map/ppermute | solution.py:312
  53.1 10.2 %collective-permute-start.8 = (bf16[128,1024]{1,0:T(8,128)(2,1)S(1)}, bf16[128,1024]{1,0:T(8,128)(2,1)S(1)}, u32[]{:S(2)}, u32[]{:S(2)}) collective-permute-start(bf16[128,1024]{1,0:T(8,128)(2,1)S(1)} %get-tuple-element.43.refs_0_), channel_id=1, source_target_pairs={{0,8},{4,12},{8,16},{12,20},{16,24},{20,28},{24,0},{28,4},{1,9},{5... | collective-permute-start | bytes 786440 | tf_op jit(solution)/shard_map/ppermute | solution.py:291
  54.6 13.0 %collective-permute-start.9 = (bf16[128,1024]{1,0:T(8,128)(2,1)S(1)}, bf16[128,1024]{1,0:T(8,128)(2,1)S(1)}, u32[]{:S(2)}, u32[]{:S(2)}) collective-permute-start(bf16[128,1024]{1,0:T(8,128)(2,1)S(1)} %get-tuple-element.43.refs_0_), channel_id=1, source_target_pairs={{0,16},{4,20},{8,24},{12,28},{16,0},{20,4},{24,8},{28,12},{1,17},{... | collective-permute-start | bytes 786440 | tf_op jit(solution)/shard_map/ppermute | solution.py:291
  56.1 16.4 %collective-permute-start.10 = (bf16[128,1024]{1,0:T(8,128)(2,1)S(1)}, bf16[128,1024]{1,0:T(8,128)(2,1)S(1)}, u32[]{:S(2)}, u32[]{:S(2)}) collective-permute-start(bf16[128,1024]{1,0:T(8,128)(2,1)S(1)} %get-tuple-element.43.refs_0_), channel_id=1, source_target_pairs={{0,24},{4,28},{8,0},{12,4},{16,8},{20,12},{24,16},{28,20},{1,25},{... | collective-permute-start | bytes 786440 | tf_op jit(solution)/shard_map/ppermute | solution.py:291
  63.3 10.9 %collective-permute-start.11 = (bf16[128,1024]{1,0:T(8,128)(2,1)S(1)}, bf16[128,1024]{1,0:T(8,128)(2,1)S(1)}, u32[]{:S(2)}, u32[]{:S(2)}) collective-permute-start(bf16[128,1024]{1,0:T(8,128)(2,1)S(1)} %get-tuple-element.43.refs_0_), channel_id=1, source_target_pairs={{0,4},{4,0},{8,12},{12,8},{16,20},{20,16},{24,28},{28,24},{1,5},{5... | collective-permute-start | bytes 786440 | tf_op jit(solution)/shard_map/ppermute | solution.py:334
  67.6 51.9 %collective-permute-start.18 = (bf16[256,1024]{1,0:T(8,128)(2,1)}, bf16[256,1024]{1,0:T(8,128)(2,1)S(1)}, u32[]{:S(2)}, u32[]{:S(2)}) collective-permute-start(bf16[256,1024]{1,0:T(8,128)(2,1)} %get-tuple-element.41), channel_id=1, source_target_pairs={{0,1},{3,2},{4,5},{7,6},{8,9},{11,10},{12,13},{15,14},{16,17},{19,... | collective-permute-start | bytes 1572872 | tf_op jit(solution)/shard_map/ppermute | solution.py:320
  72.5 1.7 %collective-permute-start.12 = (bf16[128,1024]{1,0:T(8,128)(2,1)S(1)}, bf16[128,1024]{1,0:T(8,128)(2,1)S(1)}, u32[]{:S(2)}, u32[]{:S(2)}) collective-permute-start(bf16[128,1024]{1,0:T(8,128)(2,1)S(1)} %collective-permute-done.8.refs_1_), channel_id=1, source_target_pairs={{0,4},{4,0},{8,12},{12,8},{16,20},{20,16},{24,28},{28,24},{1,5},{5... | collective-permute-start | bytes 786440 | tf_op jit(solution)/shard_map/ppermute | solution.py:334
  72.6 1.9 %collective-permute-start.13 = (bf16[128,1024]{1,0:T(8,128)(2,1)S(1)}, bf16[128,1024]{1,0:T(8,128)(2,1)S(1)}, u32[]{:S(2)}, u32[]{:S(2)}) collective-permute-start(bf16[128,1024]{1,0:T(8,128)(2,1)S(1)} %collective-permute-done.9.refs_2_), channel_id=1, source_target_pairs={{0,4},{4,0},{8,12},{12,8},{16,20},{20,16},{24,28},{28,24},{1,5},{5... | collective-permute-start | bytes 786440 | tf_op jit(solution)/shard_map/ppermute | solution.py:334
  73.1 1.8 %collective-permute-start.14 = (bf16[128,1024]{1,0:T(8,128)(2,1)S(1)}, bf16[128,1024]{1,0:T(8,128)(2,1)S(1)}, u32[]{:S(2)}, u32[]{:S(2)}) collective-permute-start(bf16[128,1024]{1,0:T(8,128)(2,1)S(1)} %collective-permute-done.10.refs_3_), channel_id=1, source_target_pairs={{0,4},{4,0},{8,12},{12,8},{16,20},{20,16},{24,28},{28,24},{1,5},{5... | collective-permute-start | bytes 786440 | tf_op jit(solution)/shard_map/ppermute | solution.py:334
  74.2 45.3 %collective-permute-start.19 = (bf16[256,1024]{1,0:T(8,128)(2,1)}, bf16[256,1024]{1,0:T(8,128)(2,1)}, u32[]{:S(2)}, u32[]{:S(2)}) collective-permute-start(bf16[256,1024]{1,0:T(8,128)(2,1)} %add_convert_fusion), channel_id=1, source_target_pairs={{0,2},{2,0},{1,3},{3,1},{4,6},{6,4},{5,7},{7,5},{8,10},{10,8},{9,1... | collective-permute-start | bytes 1572872 | tf_op jit(solution)/shard_map/ppermute | solution.py:321
  74.2 45.3 %copy-start.2 = (bf16[256,1024]{1,0:T(8,128)(2,1)S(1)}, bf16[256,1024]{1,0:T(8,128)(2,1)}, u32[]{:S(2)}) copy-start(bf16[256,1024]{1,0:T(8,128)(2,1)} %proj_ref.1) | copy-start | bytes 1572868
  74.2 45.3 %copy-start.3 = (bf16[256,1024]{1,0:T(8,128)(2,1)S(1)}, bf16[256,1024]{1,0:T(8,128)(2,1)}, u32[]{:S(2)}) copy-start(bf16[256,1024]{1,0:T(8,128)(2,1)} %get-tuple-element.49.refs_0_) | copy-start | bytes 1572868
  77.8 23.1 %collective-permute-start.15 = (bf16[128,512]{1,0:T(8,128)(2,1)S(1)}, bf16[128,512]{1,0:T(8,128)(2,1)S(1)}, u32[]{:S(2)}, u32[]{:S(2)}) collective-permute-start(bf16[128,512]{1,0:T(8,128)(2,1)S(1)} %get-tuple-element.45), channel_id=1, source_target_pairs={{0,1},{1,2},{2,3},{3,0},{4,5},{5,6},{6,7},{7,4},{8,9},{9,10},{10,1... | collective-permute-start | bytes 393224 | tf_op jit(solution)/shard_map/ppermute | solution.py:291
  79.2 30.6 %collective-permute-start.16 = (bf16[128,512]{1,0:T(8,128)(2,1)S(1)}, bf16[128,512]{1,0:T(8,128)(2,1)S(1)}, u32[]{:S(2)}, u32[]{:S(2)}) collective-permute-start(bf16[128,512]{1,0:T(8,128)(2,1)S(1)} %get-tuple-element.46), channel_id=1, source_target_pairs={{0,2},{1,3},{2,0},{3,1},{4,6},{5,7},{6,4},{7,5},{8,10},{9,11},{10,... | collective-permute-start | bytes 393224 | tf_op jit(solution)/shard_map/ppermute | solution.py:291
  80.3 29.5 %collective-permute-start.17 = (bf16[128,512]{1,0:T(8,128)(2,1)S(1)}, bf16[128,512]{1,0:T(8,128)(2,1)S(1)}, u32[]{:S(2)}, u32[]{:S(2)}) collective-permute-start(bf16[128,512]{1,0:T(8,128)(2,1)S(1)} %get-tuple-element.47), channel_id=1, source_target_pairs={{0,3},{1,0},{2,1},{3,2},{4,7},{5,4},{6,5},{7,6},{8,11},{9,8},{10,9... | collective-permute-start | bytes 393224 | tf_op jit(solution)/shard_map/ppermute | solution.py:291
  110.7 8.8 %all-to-all-start = ((bf16[8,16,512]{2,1,0:T(8,128)(2,1)}), bf16[8,16,512]{2,1,0:T(8,128)(2,1)S(1)}, u32[]{:S(2)}, u32[]{:S(2)}) async-start(bf16[8,16,512]{2,1,0:T(8,128)(2,1)} %bitcast.13), calls=%async_computation | async-start | bytes 262144 | tf_op jit(solution)/shard_map/all_to_all | solution.py:411

commit v4 on v3

--- a/solution.py
+++ b/solution.py
@@ -38,7 +38,7 @@
     ways = slots_ref.shape[1]
     sources, parts, shares = refs[:5], refs[5 : 5 + ways], refs[5 + ways : 5 + 2 * ways]
     x_ref, part_ref, share_ref = refs[5 + 2 * ways : 8 + 2 * ways]
-    held, (in_sem, x_sem, part_sem, share_sem) = refs[8 + 2 * ways : 13 + 2 * ways], refs[13 + 2 * ways :]
+    held, (in_sem, x_sem, part_sem) = refs[8 + 2 * ways : 13 + 2 * ways], refs[13 + 2 * ways :]
     patches = share_ref.shape[1]
     width = x_ref.shape[1]
     own = span // ways
@@ -47,9 +47,7 @@
     loads = [pltpu.make_async_copy(s, h, in_sem.at[i]) for i, (s, h) in enumerate(zip(sources, held))]
     cuts = [slice(i * rows, (i + 1) * rows) for i in range(pieces)]
     x_loads = [pltpu.make_async_copy(x_hbm.at[pl.ds(c.start, rows)], x_ref.at[pl.ds(c.start, rows)], x_sem.at[i]) for i, c in enumerate(cuts)]
-    x_loads[0].start()
-    loads[0].start()
-    for copy in x_loads[1:] + loads[1:]:
+    for copy in x_loads + loads:
         copy.start()
     qkv_ref, up_ref, out_ref, down_ref, proj_ref = held
     at = lax.broadcasted_iota(jnp.int32, (rows, rows), 0)
@@ -57,14 +55,14 @@
     order = (to == (at % piece) * span + at // piece).astype(F32).astype(BF16)
     kept = lax.broadcasted_iota(jnp.int32, (rows, 1), 0) // piece // own == me_ref[0]
     xs, normed = [], []
+    for copy in x_loads + loads:
+        copy.wait()
     for i, cut in enumerate(cuts):
-        x_loads[i].wait()
         x = dot(order, x_ref[cut])
         xs.append(jnp.where(kept, x, 0.0).astype(BF16))
         factor = lax.rsqrt(jnp.mean(x * x, axis=-1, keepdims=True) + EPSILON)
         normed.append((x * factor * gain_ref[...]).astype(BF16))
     xs, normed = jnp.concatenate(xs, axis=0), jnp.concatenate(normed, axis=0)
-    loads[0].wait()
     query, key, value = (dot(normed, qkv_ref[i]) for i in range(3))
     seen = (at % piece == to % piece) & (to <= at)
     heads = scale_ref.shape[0]
@@ -81,15 +79,13 @@
             columns.append((dot(weights.astype(BF16), value[cut, head].astype(BF16)) / total).astype(BF16))
         attended.append(jnp.concatenate(columns, axis=1))
     attended = jnp.concatenate(attended, axis=0)
-    loads[1].wait()
     act = gelu(dot(normed, up_ref[...])).astype(BF16)
-    for copy in loads[2:]:
-        copy.wait()
+    mixed = jnp.concatenate([attended, act], axis=1)
     share = 0.0
     stores = []
     for c in range(0, width, step):
         columns = slice(c, c + step)
-        partial = dot(attended, out_ref[:, columns]) + dot(act, down_ref[:, columns])
+        partial = dot(mixed, jnp.concatenate([out_ref[:, columns], down_ref[:, columns]], axis=0))
         partial = (partial + xs[:, columns].astype(F32)).astype(BF16)
         for i, cut in enumerate(cuts):
             for b in range(span):
@@ -107,8 +103,7 @@
             put = slice((b % own) * size, (b % own + 1) * size)
             share_ref[b // own, i * piece : (i + 1) * piece, put] = share[cut][b * piece : (b + 1) * piece]
     for slot, out in enumerate(shares):
-        stores.append(pltpu.make_async_copy(share_ref.at[slots_ref[1, slot]], out, share_sem.at[slot]))
-        stores[-1].start()
+        out[...] = share_ref[slots_ref[1, slot]]
     for copy in stores:
         copy.wait()
 
@@ -120,21 +115,20 @@
     own = span // ways
     weights = (qkv, up, out, down, proj)
     piece = math.gcd(patches, 32)
-    step = math.gcd(width, 256)
+    step = math.gcd(width, 1024)
     part = (own * patches, width)
     share = (patches, own * proj.shape[1])
     outs = pl.pallas_call(
         functools.partial(local_kernel, span, piece, step),
         in_specs=[SMEM, SMEM, SMEM, VMEM] + [HBM] * (1 + len(weights)),
-        out_specs=[HBM] * (2 * ways),
-        out_shape=[jax.ShapeDtypeStruct(part, BF16)] * ways + [jax.ShapeDtypeStruct(share, BF16)] * ways,
+        out_specs=[HBM] * ways + [VMEM] * ways,
+        out_shape=[jax.ShapeDtypeStruct(part, BF16)] * ways + [pltpu.VMEM(share, BF16)] * ways,
         scratch_shapes=[pltpu.VMEM(x.shape, BF16), pltpu.VMEM((ways, *part), BF16), pltpu.VMEM((ways, *share), BF16)]
         + [pltpu.VMEM(w.shape, w.dtype) for w in weights]
         + [
             pltpu.SemaphoreType.DMA((len(weights),)),
             pltpu.SemaphoreType.DMA((patches // piece,)),
             pltpu.SemaphoreType.DMA((ways * (width // step),)),
-            pltpu.SemaphoreType.DMA((ways,)),
         ],
         compiler_params=pltpu.CompilerParams(vmem_limit_bytes=60 * 2**20),
         name="local_part",
@@ -163,77 +157,102 @@
     )(weight)
 
 
-def heads_kernel(depth, ids_ref, gain_ref, *refs):
+def heads_kernel(depth, core_ref, ids_ref, gain_ref, *refs):
     ways = gain_ref.shape[0]
-    shares, (weight, query_ref, keyed_ref) = refs[:ways], refs[ways:]
+    shares, weight, outs = refs[:ways], refs[ways], refs[ways + 1 :]
     width = shares[0].shape[1]
     values = [s[...].astype(F32) for s in shares]
     square = sum(jnp.sum(v * v, axis=-1, keepdims=True) for v in values)
     factor = lax.rsqrt(square / (ways * width) + EPSILON)
     normed = [(v * factor * gain_ref[ids_ref[c]]).astype(BF16) for c, v in enumerate(values)]
+    size = outs[0].shape[1] // 3
     for kind in range(3):
-        mixed = sum(
-            dot(n, weight[kind, pl.ds(pl.multiple_of(ids_ref[c] * width, width), width), :])
-            for c, n in enumerate(normed)
-        )
-        size = mixed.shape[1]
-        if kind < 2:
-            mixed = jnp.concatenate([unit(mixed[:, c : c + depth]) for c in range(0, size, depth)], axis=1)
-        if kind == 0:
-            query_ref[...] = mixed
-        else:
-            keyed_ref[:, (kind - 1) * size : kind * size] = mixed.astype(BF16)
-
-
-def global_heads(depth, ids, gain, shares, qkv):
-    rows, size = shares[0].shape[0], qkv.shape[2]
+        for i, out in ((1, outs[1]), (0, outs[0])):
+            columns = pl.ds(pl.multiple_of((core_ref[0] ^ i) * size, size), size)
+            mixed = sum(
+                dot(n, weight[kind, pl.ds(pl.multiple_of(ids_ref[c] * width, width), width), columns])
+                for c, n in enumerate(normed)
+            )
+            if kind < 2:
+                mixed = jnp.concatenate([unit(mixed[:, c : c + depth]) for c in range(0, size, depth)], axis=1)
+            out[:, kind * size : (kind + 1) * size] = mixed.astype(BF16)
+
+
+def global_heads(depth, core, ids, gain, shares, qkv):
+    shape = jax.ShapeDtypeStruct((shares[0].shape[0], 3 * qkv.shape[2] // 2), BF16)
     return pl.pallas_call(
         functools.partial(heads_kernel, depth),
-        in_specs=[SMEM] + [VMEM] * (2 + len(shares)),
+        in_specs=[SMEM, SMEM] + [VMEM] * (2 + len(shares)),
         out_specs=(VMEM, VMEM),
-        out_shape=(jax.ShapeDtypeStruct((rows, size), BF16), jax.ShapeDtypeStruct((rows, 2 * size), BF16)),
+        out_shape=(shape, shape),
         compiler_params=pltpu.CompilerParams(vmem_limit_bytes=8 * 2**20),
         name="global_heads",
-    )(ids, gain, *shares, qkv)
-
-
-def attend_kernel(count, slots_ref, ids_ref, scale_ref, q_ref, *refs):
-    pieces, proj_ref, outs = refs[:count], refs[count], refs[count + 1 :]
-    rows, size = q_ref.shape
-    at = lax.broadcasted_iota(jnp.int32, (rows, rows), 0)
-    to = lax.broadcasted_iota(jnp.int32, (rows, rows), 1)
-    heads = scale_ref.shape[0]
-    depth = size // heads
-    me = ids_ref[0]
-    seen = [to + ids_ref[i] * rows <= at + me * rows for i in range(count)]
-    attended = []
+    )(core, ids, gain, *shares, qkv)
+
+
+def attend_kernel(depth, me_ref, ids_ref, scale_ref, kept_ref, given_ref, *refs):
+    pieces, (own_ref, other_ref) = refs[:-2], refs[-2:]
+    rows = kept_ref.shape[0]
+    size = own_ref.shape[1]
+    heads = size // depth
+    me = me_ref[0]
+
+    def places(index, shape, axis):
+        row = lax.broadcasted_iota(jnp.int32, shape, axis)
+        return jnp.where(row < rows, index * rows + row, (index ^ 1) * rows + row - rows)
+
+    at = places(me, (2 * rows, 1), 0)
+    seen = [places(i, (1, 2 * rows), 1) <= at for i in [me] + [ids_ref[p + 1] for p in range(len(pieces))]]
+    own = jnp.concatenate([kept_ref[...], given_ref[...]], axis=0)
+    query = own[:, :size]
+    pieces = [own[:, size:]] + [p[...] for p in pieces]
     for h in range(heads):
         cut = slice(h * depth, (h + 1) * depth)
-        query = q_ref[:, cut]
-        factor = scale_ref[h] / math.sqrt(depth)
-        scores = [jnp.where(s, dot_t(query, p[:, cut]) * factor, NEGATIVE) for s, p in zip(seen, pieces)]
+        factor = scale_ref[(me % 2) * heads + h] / math.sqrt(depth)
+        scores = [jnp.where(s, dot_t(query[:, cut], p[:, cut]) * factor, NEGATIVE) for s, p in zip(seen, pieces)]
         top = functools.reduce(jnp.maximum, [jnp.max(s, axis=-1, keepdims=True) for s in scores])
         weights = [jnp.exp(s - top) for s in scores]
         total = sum(jnp.sum(w, axis=-1, keepdims=True) for w in weights)
-        cut = slice(size + h * depth, size + (h + 1) * depth)
-        summed = sum(dot(w.astype(BF16), p[:, cut]) for w, p in zip(weights, pieces))
-        attended.append((summed / total).astype(BF16))
-    attended = jnp.concatenate(attended, axis=1)
+        values = slice(size + h * depth, size + (h + 1) * depth)
+        summed = sum(dot(w.astype(BF16), p[:, values]) for w, p in zip(weights, pieces))
+        attended = (summed / total).astype(BF16)
+        own_ref[:, cut] = attended[:rows]
+        other_ref[:, cut] = attended[rows:]
+
+
+def attend(depth, me, ids, scale, kept, given, pieces):
+    rows = kept.shape[0]
+    shape = jax.ShapeDtypeStruct((rows, kept.shape[1] // 3), BF16)
+    return pl.pallas_call(
+        functools.partial(attend_kernel, depth),
+        in_specs=[SMEM, SMEM, SMEM] + [VMEM] * (2 + len(pieces)),
+        out_specs=(VMEM, VMEM),
+        out_shape=(shape, shape),
+        compiler_params=pltpu.CompilerParams(vmem_limit_bytes=20 * 2**20),
+        name="attend",
+    )(me, ids, scale, kept, given, *pieces)
+
+
+def project_kernel(core_ref, slots_ref, own_ref, other_ref, proj_ref, *outs):
+    size = own_ref.shape[1]
+    own_rows = pl.ds(pl.multiple_of(core_ref[0] * size, size), size)
+    other_rows = pl.ds(pl.multiple_of((core_ref[0] ^ 1) * size, size), size)
     for slot, out in enumerate(outs):
         width = out.shape[1]
-        out[...] = dot(attended, proj_ref[:, pl.ds(pl.multiple_of(slots_ref[slot] * width, width), width)]).astype(BF16)
-
-
-def attend(slots, ids, scale, query, pieces, proj):
-    rows, ways = query.shape[0], slots.shape[0]
-    return pl.pallas_call(
-        functools.partial(attend_kernel, len(pieces)),
-        in_specs=[SMEM, SMEM, SMEM] + [VMEM] * (2 + len(pieces)),
+        columns = pl.ds(pl.multiple_of(slots_ref[slot] * width, width), width)
+        out[...] = (dot(own_ref[...], proj_ref[own_rows, columns]) + dot(other_ref[...], proj_ref[other_rows, columns])).astype(BF16)
+
+
+def project(core, slots, own, other, proj):
+    ways = slots.shape[0]
+    return pl.pallas_call(
+        project_kernel,
+        in_specs=[SMEM, SMEM] + [VMEM] * 3,
         out_specs=[VMEM] * ways,
-        out_shape=[jax.ShapeDtypeStruct((rows, proj.shape[1] // ways), BF16)] * ways,
-        compiler_params=pltpu.CompilerParams(vmem_limit_bytes=16 * 2**20),
-        name="attend",
-    )(slots, ids, scale, query, *pieces, proj)
+        out_shape=[jax.ShapeDtypeStruct((own.shape[0], proj.shape[1] // ways), BF16)] * ways,
+        compiler_params=pltpu.CompilerParams(vmem_limit_bytes=6 * 2**20),
+        name="project",
+    )(core, slots, own, other, proj)
 
 
 def result_kernel(count, order_ref, own_ref, *refs):
@@ -313,13 +332,17 @@
     return swapped, middle
 
 
-def relay_rest(chunks, swapped, middle, axis):
+def relay_sum(chunks, swapped, axis):
     me = lax.axis_index(axis)
-    outer = (me == 0) | (me == 3)
-    sent = (chunks[3].astype(F32) + jnp.where(outer, 0.0, swapped.astype(F32))).astype(BF16)
+    relayed = jnp.where((me == 0) | (me == 3), 0.0, swapped.astype(F32))
+    return (chunks[3].astype(F32) + relayed).astype(BF16)
+
+
+def relay_rest(chunks, swapped, middle, sent, axis):
     inward = lax.ppermute(chunks[2], axis, [(0, 1), (3, 2)])
     crossed = lax.ppermute(sent, axis, [(0, 2), (2, 0), (1, 3), (3, 1)])
-    outer = outer.astype(jnp.int32)
+    me = lax.axis_index(axis)
+    outer = ((me == 0) | (me == 3)).astype(jnp.int32)
     return jnp.stack([1 + 0 * outer, outer, 1 - outer, 1 - outer, 1 + 0 * outer]), [chunks[0], swapped, middle, inward, crossed]
 
 
@@ -327,18 +350,13 @@
     return [value] + [shift(value, axis, step) for step in range(1, lax.axis_size(axis))]
 
 
-def gather_chips(value, axis):
+def swap_cores(value, axis):
+    return lax.ppermute(value, axis, [(i, i ^ 1) for i in range(lax.axis_size(axis))])
+
+
+def twin_ids(axis):
     count = lax.axis_size(axis)
-    other = [(i, i ^ 1) for i in range(count)]
-    pieces = [value] + [shift(value, axis, 2 * step) for step in range(1, count // 2)]
-    return pieces + [lax.ppermute(p, axis, other) for p in pieces]
-
-
-def chip_ids(axis):
-    count = lax.axis_size(axis)
-    me = lax.axis_index(axis)
-    mine = (me - 2 * jnp.arange(count // 2, dtype=jnp.int32)) % count
-    return jnp.concatenate([mine, mine ^ 1]).astype(jnp.int32)
+    return ((lax.axis_index(axis) - 2 * jnp.arange(count // 2)) % count).astype(jnp.int32)
 
 
 def owner_order(owners, source, patches):
@@ -398,18 +416,26 @@
     weight, residual = lax.optimization_barrier((jnp.transpose(global_qkv, (1, 0, 2)), residual))
     shares = gather(residual, "head")
     ids = (me - jnp.arange(ways, dtype=jnp.int32)) % ways
-    query, keyed = global_heads(depth, ids, global_gain.reshape(ways, 1, -1), shares, fetch(weight))
-    parts, keyed = lax.optimization_barrier((parts, keyed))
+    core = (seq % 2).reshape(1)
+    kept, given = global_heads(depth, core, ids, global_gain.reshape(ways, 1, -1), shares, fetch(weight))
+    received = swap_cores(given, "seq")
+    parts, received = lax.optimization_barrier((parts, received))
+    half = kept.shape[1] // 3
+    keyed = jnp.concatenate([kept[:, half:], received[:, half:]], axis=0)
+    pieces = [shift(keyed, "seq", 2 * step) for step in range(1, lax.axis_size("seq") // 2)]
     if line:
         swapped, middle = relay_first(parts, "head")
-        query, swapped, middle = lax.optimization_barrier((query, swapped, middle))
-        kept, parts = relay_rest(parts, swapped, middle, "head")
+        sent = relay_sum(parts, swapped, "head")
+        kept, sent, middle = lax.optimization_barrier((kept, sent, middle))
+        counted, parts = relay_rest(parts, swapped, middle, sent, "head")
     else:
-        kept, parts = jnp.ones((ways,), jnp.int32), scatter(parts, "head")
-    update = attend(slots[1], chip_ids("seq"), global_scale, query, gather_chips(keyed, "seq"), global_out)
-    result, routed = finish_result(owner_order(owners, seq, patches), residual, scatter(update, "head"))
+        counted, parts = jnp.ones((ways,), jnp.int32), scatter(parts, "head")
+    own_heads, other_heads = attend(depth, seq.reshape(1), twin_ids("seq"), global_scale, kept, received, pieces)
+    update = project(core, slots[1], own_heads, swap_cores(other_heads, "seq"), global_out)
+    updates, parts = lax.optimization_barrier((scatter(update, "head"), parts))
+    result, routed = finish_result(owner_order(owners, seq, patches), residual, updates)
     global_state = lax.all_to_all(routed, "seq", split_axis=0, concat_axis=0, tiled=True)
-    byte_out = finish_bytes(kept, result, back_proj, parts)
+    byte_out = finish_bytes(counted, result, back_proj, parts)
     return byte_out.reshape(patches, own, width), global_state
 
 

time: 123 us -> 117 us (0.951)
  waiting for transfers between devices: 54.2 us -> 46.9 us
  local copies, waits for them, and re-layouts: 1.79 us -> 7.57 us
  Pallas kernels: 27.8 us -> 25.1 us
  starting transfers between devices: 35.5 us -> 34 us
    ppermute x12, waiting for transfers between devices: 48.2 us -> 36.1 us  [shift(): lax.ppermute(value, axis, [(i, (i + step) % count) for i in range(count)])]
    ppermute x1, waiting for transfers between devices: 0.01 us -> 7.77 us  [relay_first(): swapped = lax.ppermute(chunks[1], axis, [(0, 1), (1, 0), (2, 3), (3, 2)])]
    unnamed x17 -> x25, local copies, waits for them, and re-layouts: 0.7 us -> 6.47 us
    all_to_all x1, waiting for transfers between devices: 5.37 us -> 0.01 us  [on_device(): lax.all_to_all(routed, 'seq', split_axis=0, concat_axis=0, tiled=True)]
    ppermute x4 -> x2, waiting for transfers between devices: 0.62 us -> 2.64 us  [swap_cores(): lax.ppermute(value, axis, [(i, i ^ 1) for i in range(lax.axis_size(axis))])]
    pallas_call x1, Pallas kernels: 17.4 us -> 15.4 us  [local_part(): pl.pallas_call(functools.partial(local_kernel, span, piece, step), in_spe...]
    pallas_call x2 -> x3, Pallas kernels: 4.61 us -> 4.42 us  [the longest x1 1.72 us: attend(): pl.pallas_call(functools.partial(attend_kernel, depth), in_specs=[SMEM, S...]
  transfers between devices with their start and end apart: 21 -> 19, of which waited for: 10 -> 9; matrix products, arithmetic and copies ran while one was open for 1% -> 2% of each run, Pallas kernels for 5% -> 6%
where the time goes in v4:
time: 117 us
  waiting for transfers between devices  46.9 us (40%)
  starting transfers between devices  34 us (29%)
  Pallas kernels  25.1 us (21%)
  local copies, waits for them, and re-layouts  7.57 us (6%)
  other arithmetic  2.33 us (2%)
    ppermute x12, waiting for transfers between devices, shift(): lax.ppermute(value, axis, [(i, (i + step) % count) for i in range(count)])  36.1 us
    ppermute x12, starting transfers between devices, shift(): lax.ppermute(value, axis, [(i, (i + step) % count) for i in range(count)])  21.8 us
    pallas_call x1, Pallas kernels, local_part(): pl.pallas_call(functools.partial(local_kernel, span, piece, step), in_spe...  15.4 us
    ppermute x1, waiting for transfers between devices, relay_first(): swapped = lax.ppermute(chunks[1], axis, [(0, 1), (1, 0), (2, 3), (3, 2)])  7.77 us
    unnamed x25, local copies, waits for them, and re-layouts  6.47 us
    ppermute x1, starting transfers between devices, relay_rest(): inward = lax.ppermute(chunks[2], axis, [(0, 1), (3, 2)])  3.85 us
    all_to_all x1, starting transfers between devices, on_device(): lax.all_to_all(routed, 'seq', split_axis=0, concat_axis=0, tiled=True)  3.73 us
    ppermute x1, starting transfers between devices, relay_first(): swapped = lax.ppermute(chunks[1], axis, [(0, 1), (1, 0), (2, 3), (3, 2)])  3.28 us
  transfers between devices with their start and end apart: 19, of which 9 were waited for; matrix products, arithmetic and copies ran while one was open for 2% of the time, Pallas kernels for 6%

profile of v4, /device:TPU:0, one launch (start us, length us, event | category | flops | bytes accessed | tf_op | source)
XLA Modules:
  0.0 116.8 jit_solution(3690683784270509567)
XLA Ops:
  1.3 15.4 %local_part.1 = (bf16[256,1024]{1,0:T(8,128)(2,1)}, bf16[256,1024]{1,0:T(8,128)(2,1)}, bf16[256,1024]{1,0:T(8,128)(2,1)}, bf16[256,1024]{1,0:T(8,128)(2,1)}, bf1...) custom-call(s32[1]{0:T(128)} %bitcast.4.me_ref, ...), custom_call_target="tpu_custom_call" | custom-call | tf_op jit(solution)/shard_map/local_part/pallas_call | solution.py:121
  16.8 3.1 %collective-permute-start = (bf16[128,512]{1,0:T(8,128)(2,1)S(1)}, bf16[128,512]{1,0:T(8,128)(2,1)S(1)}, u32[]{:S(2)}, u32[]{:S(2)}) collective-permute-start(bf16[128,512]{1,0:T(8,128)(2,1)S(1)} %get-tuple-element.40), channel_id=1, source_target_pairs={{0,1},{1,2},{2,3},{3,0},{4,5},{5,6},{6,7},{7,4},{8,9},{9,10},{10,1... | collective-permute-start | bytes 393224 | tf_op jit(solution)/shard_map/ppermute | solution.py:310
  19.8 2.6 %collective-permute-start.1 = (bf16[128,512]{1,0:T(8,128)(2,1)S(1)}, bf16[128,512]{1,0:T(8,128)(2,1)S(1)}, u32[]{:S(2)}, u32[]{:S(2)}) collective-permute-start(bf16[128,512]{1,0:T(8,128)(2,1)S(1)} %get-tuple-element.41), channel_id=1, source_target_pairs={{0,2},{1,3},{2,0},{3,1},{4,6},{5,7},{6,4},{7,5},{8,10},{9,11},{10,... | collective-permute-start | bytes 393224 | tf_op jit(solution)/shard_map/ppermute | solution.py:310
  22.4 1.3 %collective-permute-start.2 = (bf16[128,512]{1,0:T(8,128)(2,1)S(1)}, bf16[128,512]{1,0:T(8,128)(2,1)S(1)}, u32[]{:S(2)}, u32[]{:S(2)}) collective-permute-start(bf16[128,512]{1,0:T(8,128)(2,1)S(1)} %get-tuple-element.42), channel_id=1, source_target_pairs={{0,3},{1,0},{2,1},{3,2},{4,7},{5,4},{6,5},{7,6},{8,11},{9,8},{10,9... | collective-permute-start | bytes 393224 | tf_op jit(solution)/shard_map/ppermute | solution.py:310
  23.8 2.5 %collective-permute-done = bf16[128,512]{1,0:T(8,128)(2,1)S(1)} collective-permute-done((bf16[128,512]{1,0:T(8,128)(2,1)S(1)}, bf16[128,512]{1,0:T(8,128)(2,1)S(1)}, u32[]{:S(2)}, u32[]{:S(2)}) %collective-permute-start) | collective-permute-done | bytes 131104 | tf_op jit(solution)/shard_map/ppermute | solution.py:310
  26.3 4.8 %collective-permute-done.1 = bf16[128,512]{1,0:T(8,128)(2,1)S(1)} collective-permute-done((bf16[128,512]{1,0:T(8,128)(2,1)S(1)}, bf16[128,512]{1,0:T(8,128)(2,1)S(1)}, u32[]{:S(2)}, u32[]{:S(2)}) %collective-permute-start.1) | collective-permute-done | bytes 131104 | tf_op jit(solution)/shard_map/ppermute | solution.py:310
  31.2 3.3 %collective-permute-start.3 = (bf16[128,512]{1,0:T(8,128)(2,1)S(1)}, bf16[128,512]{1,0:T(8,128)(2,1)S(1)}, u32[]{:S(2)}, u32[]{:S(2)}) collective-permute-start(bf16[128,512]{1,0:T(8,128)(2,1)S(1)} %add_convert_fusion.1.refs_0_.own_ref), channel_id=1, source_target_pairs={{0,1},{1,2},{2,3},{3,0},{4,5},{5,6},{6,7},{7,4},{8,9},{9,10},{10,1... | collective-permute-start | bytes 393224 | tf_op jit(solution)/shard_map/ppermute | solution.py:310
  34.5 1.6 %collective-permute-start.4 = (bf16[128,512]{1,0:T(8,128)(2,1)S(1)}, bf16[128,512]{1,0:T(8,128)(2,1)S(1)}, u32[]{:S(2)}, u32[]{:S(2)}) collective-permute-start(bf16[128,512]{1,0:T(8,128)(2,1)S(1)} %add_convert_fusion.1.refs_0_.own_ref), channel_id=1, source_target_pairs={{0,2},{1,3},{2,0},{3,1},{4,6},{5,7},{6,4},{7,5},{8,10},{9,11},{10,... | collective-permute-start | bytes 393224 | tf_op jit(solution)/shard_map/ppermute | solution.py:310
  36.9 2.9 %fetch.1.refs_4_ = bf16[3,2048,512]{2,1,0:T(8,128)(2,1)S(1)} custom-call(bf16[3,2048,512]{2,1,0:T(8,128)(2,1)} %bitcast.20), custom_call_target="tpu_custom_call" | custom-call | tf_op jit(solution)/shard_map/fetch/pallas_call | solution.py:149
  39.9 4.4 %collective-permute-done.4.refs_2_ = bf16[128,512]{1,0:T(8,128)(2,1)S(1)} collective-permute-done((bf16[128,512]{1,0:T(8,128)(2,1)S(1)}, bf16[128,512]{1,0:T(8,128)(2,1)S(1)}, u32[]{:S(2)}, u32[]{:S(2)}) %collective-permute-start.4) | collective-permute-done | bytes 131104 | tf_op jit(solution)/shard_map/ppermute | solution.py:310
  44.2 1.7 %global_heads.1 = (bf16[128,768]{1,0:T(8,128)(2,1)S(1)}, bf16[128,768]{1,0:T(8,128)(2,1)S(1)}) custom-call(s32[1]{0:T(128)} %bitcast.12.core_ref, s32[4]{0:T(128)S(1)} %and_select_fusion.ids_ref, f32[4,1,512]{2,1,0:T(1,128)S(1)} %bitcast.19, bf16[128,512]{1,0:T(8,128)(2,1)S(1)} %add_convert_fusion.1.refs_0_.own_ref, ...), custom_call_target="tpu_custom_call" | custom-call | tf_op jit(solution)/shard_map/global_heads/pallas_call | solution.py:183
  46.0 1.4 %collective-permute-done.6.given_ref = bf16[128,768]{1,0:T(8,128)(2,1)S(1)} collective-permute-done((bf16[128,768]{1,0:T(8,128)(2,1)S(1)}, bf16[128,768]{1,0:T(8,128)(2,1)S(1)}, u32[]{:S(2)}, u32[]{:S(2)}) %collective-permute-start.6) | collective-permute-done | bytes 196640 | tf_op jit(solution)/shard_map/ppermute | solution.py:354
  47.5 3.3 %collective-permute-start.7 = (bf16[256,1024]{1,0:T(8,128)(2,1)}, bf16[256,1024]{1,0:T(8,128)(2,1)S(1)}, u32[]{:S(2)}, u32[]{:S(2)}) collective-permute-start(bf16[256,1024]{1,0:T(8,128)(2,1)} %get-tuple-element.52), channel_id=1, source_target_pairs={{0,1},{1,0},{2,3},{3,2},{4,5},{5,4},{6,7},{7,6},{8,9},{9,8},{10,11... | collective-permute-start | bytes 1572872 | tf_op jit(solution)/shard_map/ppermute | solution.py:330
  51.8 1.6 %collective-permute-start.10 = (bf16[256,512]{1,0:T(8,128)(2,1)S(1)}, bf16[256,512]{1,0:T(8,128)(2,1)S(1)}, u32[]{:S(2)}, u32[]{:S(2)}) collective-permute-start(bf16[256,512]{1,0:T(8,128)(2,1)S(1)} %pad_maximum_fusion), channel_id=1, source_target_pairs={{0,16},{4,20},{8,24},{12,28},{16,0},{20,4},{24,8},{28,12},{1,17},{... | collective-permute-start | bytes 786440 | tf_op jit(solution)/shard_map/ppermute | solution.py:310
  53.4 1.4 %collective-permute-start.11 = (bf16[256,512]{1,0:T(8,128)(2,1)S(1)}, bf16[256,512]{1,0:T(8,128)(2,1)S(1)}, u32[]{:S(2)}, u32[]{:S(2)}) collective-permute-start(bf16[256,512]{1,0:T(8,128)(2,1)S(1)} %pad_maximum_fusion), channel_id=1, source_target_pairs={{0,24},{4,28},{8,0},{12,4},{16,8},{20,12},{24,16},{28,20},{1,25},{... | collective-permute-start | bytes 786440 | tf_op jit(solution)/shard_map/ppermute | solution.py:310
  55.4 7.8 %collective-permute-done.7.refs_1_ = bf16[256,1024]{1,0:T(8,128)(2,1)S(1)} collective-permute-done((bf16[256,1024]{1,0:T(8,128)(2,1)}, bf16[256,1024]{1,0:T(8,128)(2,1)S(1)}, u32[]{:S(2)}, u32[]{:S(2)}) %collective-permute-start.7) | collective-permute-done | bytes 524320 | tf_op jit(solution)/shard_map/ppermute | solution.py:330
  63.2 3.8 %collective-permute-start.16 = (bf16[256,1024]{1,0:T(8,128)(2,1)}, bf16[256,1024]{1,0:T(8,128)(2,1)S(1)}, u32[]{:S(2)}, u32[]{:S(2)}) collective-permute-start(bf16[256,1024]{1,0:T(8,128)(2,1)} %get-tuple-element.53), channel_id=1, source_target_pairs={{0,1},{3,2},{4,5},{7,6},{8,9},{11,10},{12,13},{15,14},{16,17},{19,... | collective-permute-start | bytes 1572872 | tf_op jit(solution)/shard_map/ppermute | solution.py:342
  67.0 1.3 %add_convert_fusion = bf16[256,1024]{1,0:T(8,128)(2,1)S(1)} fusion(bf16[256,1024]{1,0:T(8,128)(2,1)S(1)} %collective-permute-done.7.refs_1_, bf16[256,1024]{1,0:T(8,128)(2,1)} %get-tuple-element.51, pred[]{:T(512)S(6)} %or.8), kind=kLoop, calls=%fused_computation | loop fusion | flops 1310720 | bytes 1572865 | tf_op jit(solution)/shard_map/convert_element_type | solution.py:338
  69.6 1.7 %attend.1 = (bf16[128,256]{1,0:T(8,128)(2,1)S(1)}, bf16[128,256]{1,0:T(8,128)(2,1)S(1)}) custom-call(s32[1]{0:T(128)} %bitcast.13.me_ref, s32[4]{0:T(128)S(1)} %and_select_fusion.1.ids_ref, f32[4]{0:T(128)S(1)} %copy-done.11, bf16[128,768]{1,0:T(8,128)(2,1)S(1)} %get-tuple-element.54.kept_ref, bf16[128,768]{1,0:T(8,128)(2,1)S(1)} %collective-permute-done.6.given_ref, ...), custom_call_target="tpu_custom_call" | custom-call | tf_op jit(solution)/shard_map/attend/pallas_call | solution.py:226
  71.4 1.2 %collective-permute-done.12.other_ref = bf16[128,256]{1,0:T(8,128)(2,1)S(1)} collective-permute-done((bf16[128,256]{1,0:T(8,128)(2,1)S(1)}, bf16[128,256]{1,0:T(8,128)(2,1)S(1)}, u32[]{:S(2)}, u32[]{:S(2)}) %collective-permute-start.12) | collective-permute-done | bytes 65568 | tf_op jit(solution)/shard_map/ppermute | solution.py:354
  72.7 1.0 project.1
  73.7 1.9 %collective-permute-start.13 = (bf16[128,512]{1,0:T(8,128)(2,1)S(1)}, bf16[128,512]{1,0:T(8,128)(2,1)S(1)}, u32[]{:S(2)}, u32[]{:S(2)}) collective-permute-start(bf16[128,512]{1,0:T(8,128)(2,1)S(1)} %get-tuple-element.59), channel_id=1, source_target_pairs={{0,1},{1,2},{2,3},{3,0},{4,5},{5,6},{6,7},{7,4},{8,9},{9,10},{10,1... | collective-permute-start | bytes 393224 | tf_op jit(solution)/shard_map/ppermute | solution.py:310
  76.3 2.8 %collective-permute-start.15 = (bf16[128,512]{1,0:T(8,128)(2,1)S(1)}, bf16[128,512]{1,0:T(8,128)(2,1)S(1)}, u32[]{:S(2)}, u32[]{:S(2)}) collective-permute-start(bf16[128,512]{1,0:T(8,128)(2,1)S(1)} %get-tuple-element.61), channel_id=1, source_target_pairs={{0,3},{1,0},{2,1},{3,2},{4,7},{5,4},{6,5},{7,6},{8,11},{9,8},{10,9... | collective-permute-start | bytes 393224 | tf_op jit(solution)/shard_map/ppermute | solution.py:310
  79.5 16.2 %collective-permute-done.13.refs_1_ = bf16[128,512]{1,0:T(8,128)(2,1)S(1)} collective-permute-done((bf16[128,512]{1,0:T(8,128)(2,1)S(1)}, bf16[128,512]{1,0:T(8,128)(2,1)S(1)}, u32[]{:S(2)}, u32[]{:S(2)}) %collective-permute-start.13) | collective-permute-done | bytes 131104 | tf_op jit(solution)/shard_map/ppermute | solution.py:310
  95.7 8.2 %collective-permute-done.14.refs_2_ = bf16[128,512]{1,0:T(8,128)(2,1)S(1)} collective-permute-done((bf16[128,512]{1,0:T(8,128)(2,1)S(1)}, bf16[128,512]{1,0:T(8,128)(2,1)S(1)}, u32[]{:S(2)}, u32[]{:S(2)}) %collective-permute-start.14) | collective-permute-done | bytes 131104 | tf_op jit(solution)/shard_map/ppermute | solution.py:310
  105.7 3.7 %all-to-all-start = ((bf16[8,16,512]{2,1,0:T(8,128)(2,1)}), bf16[8,16,512]{2,1,0:T(8,128)(2,1)S(1)}, u32[]{:S(2)}, u32[]{:S(2)}) async-start(bf16[8,16,512]{2,1,0:T(8,128)(2,1)} %bitcast.15), calls=%async_computation | async-start | bytes 262144 | tf_op jit(solution)/shard_map/all_to_all | solution.py:437
  109.5 1.0 copy-done.3
  110.5 1.0 copy-done.5
  111.6 1.0 copy-done.7
  112.6 1.0 copy-done.9
  113.6 1.5 %finish_bytes.1 = bf16[256,1024]{1,0:T(8,128)(2,1)S(1)} custom-call(s32[5]{0:T(128)S(1)} %stack.32.kept_ref, bf16[128,512]{1,0:T(8,128)(2,1)S(1)} %get-tuple-element.69.result_ref, bf16[256,1024]{1,0:T(8,128)(2,1)S(1)} %copy-done.2, bf16[256,1024]{1,0:T(8,128)(2,1)S(1)} %copy-done.3, bf16[256,1024]{1,0:T(8,128)(2,1)S(1)} %collective-permute-done.7.refs_1_, ...), custom_call_target="tpu_custom_call" | custom-call | tf_op jit(solution)/shard_map/finish_bytes/pallas_call | solution.py:298
  115.1 1.0 reshape.126
  (57 shorter events, 8.1 us)
Async XLA Ops:
  0.6 50.1 %copy-start = (s32[8,16]{1,0:T(8,128)S(1)}, s32[8,16]{1,0:T(8,128)}, u32[]{:S(2)}) copy-start(s32[8,16]{1,0:T(8,128)} %param.27) | copy-start | bytes 1540
  16.8 9.5 %collective-permute-start = (bf16[128,512]{1,0:T(8,128)(2,1)S(1)}, bf16[128,512]{1,0:T(8,128)(2,1)S(1)}, u32[]{:S(2)}, u32[]{:S(2)}) collective-permute-start(bf16[128,512]{1,0:T(8,128)(2,1)S(1)} %get-tuple-element.40), channel_id=1, source_target_pairs={{0,1},{1,2},{2,3},{3,0},{4,5},{5,6},{6,7},{7,4},{8,9},{9,10},{10,1... | collective-permute-start | bytes 393224 | tf_op jit(solution)/shard_map/ppermute | solution.py:310
  19.8 11.2 %collective-permute-start.1 = (bf16[128,512]{1,0:T(8,128)(2,1)S(1)}, bf16[128,512]{1,0:T(8,128)(2,1)S(1)}, u32[]{:S(2)}, u32[]{:S(2)}) collective-permute-start(bf16[128,512]{1,0:T(8,128)(2,1)S(1)} %get-tuple-element.41), channel_id=1, source_target_pairs={{0,2},{1,3},{2,0},{3,1},{4,6},{5,7},{6,4},{7,5},{8,10},{9,11},{10,... | collective-permute-start | bytes 393224 | tf_op jit(solution)/shard_map/ppermute | solution.py:310
  22.4 8.6 %collective-permute-start.2 = (bf16[128,512]{1,0:T(8,128)(2,1)S(1)}, bf16[128,512]{1,0:T(8,128)(2,1)S(1)}, u32[]{:S(2)}, u32[]{:S(2)}) collective-permute-start(bf16[128,512]{1,0:T(8,128)(2,1)S(1)} %get-tuple-element.42), channel_id=1, source_target_pairs={{0,3},{1,0},{2,1},{3,2},{4,7},{5,4},{6,5},{7,6},{8,11},{9,8},{10,9... | collective-permute-start | bytes 393224 | tf_op jit(solution)/shard_map/ppermute | solution.py:310
  31.2 8.7 %collective-permute-start.3 = (bf16[128,512]{1,0:T(8,128)(2,1)S(1)}, bf16[128,512]{1,0:T(8,128)(2,1)S(1)}, u32[]{:S(2)}, u32[]{:S(2)}) collective-permute-start(bf16[128,512]{1,0:T(8,128)(2,1)S(1)} %add_convert_fusion.1.refs_0_.own_ref), channel_id=1, source_target_pairs={{0,1},{1,2},{2,3},{3,0},{4,5},{5,6},{6,7},{7,4},{8,9},{9,10},{10,1... | collective-permute-start | bytes 393224 | tf_op jit(solution)/shard_map/ppermute | solution.py:310
  34.5 9.7 %collective-permute-start.4 = (bf16[128,512]{1,0:T(8,128)(2,1)S(1)}, bf16[128,512]{1,0:T(8,128)(2,1)S(1)}, u32[]{:S(2)}, u32[]{:S(2)}) collective-permute-start(bf16[128,512]{1,0:T(8,128)(2,1)S(1)} %add_convert_fusion.1.refs_0_.own_ref), channel_id=1, source_target_pairs={{0,2},{1,3},{2,0},{3,1},{4,6},{5,7},{6,4},{7,5},{8,10},{9,11},{10,... | collective-permute-start | bytes 393224 | tf_op jit(solution)/shard_map/ppermute | solution.py:310
  36.1 8.1 %collective-permute-start.5 = (bf16[128,512]{1,0:T(8,128)(2,1)S(1)}, bf16[128,512]{1,0:T(8,128)(2,1)S(1)}, u32[]{:S(2)}, u32[]{:S(2)}) collective-permute-start(bf16[128,512]{1,0:T(8,128)(2,1)S(1)} %add_convert_fusion.1.refs_0_.own_ref), channel_id=1, source_target_pairs={{0,3},{1,0},{2,1},{3,2},{4,7},{5,4},{6,5},{7,6},{8,11},{9,8},{10,9... | collective-permute-start | bytes 393224 | tf_op jit(solution)/shard_map/ppermute | solution.py:310
  36.9 7.3 %copy-start.10 = (f32[2048]{0:T(1024)S(1)}, f32[2048]{0:T(1024)}, u32[]{:S(2)}) copy-start(f32[2048]{0:T(1024)} %param.22) | copy-start | bytes 24580
  45.9 23.7 %copy-start.11 = (f32[4]{0:T(128)S(1)}, f32[4]{0:T(128)}, u32[]{:S(2)}) copy-start(f32[4]{0:T(128)} %scale_ref.3) | copy-start | bytes 52
  45.9 26.7 %copy-start.1 = (bf16[512,2048]{1,0:T(8,128)(2,1)S(1)}, bf16[512,2048]{1,0:T(8,128)(2,1)}, u32[]{:S(2)}) copy-start(bf16[512,2048]{1,0:T(8,128)(2,1)} %proj_ref.2) | copy-start | bytes 6291460
  45.9 1.5 %collective-permute-start.6 = (bf16[128,768]{1,0:T(8,128)(2,1)S(1)}, bf16[128,768]{1,0:T(8,128)(2,1)S(1)}, u32[]{:S(2)}, u32[]{:S(2)}) collective-permute-start(bf16[128,768]{1,0:T(8,128)(2,1)S(1)} %get-tuple-element.50), channel_id=1, source_target_pairs={{0,4},{4,0},{8,12},{12,8},{16,20},{20,16},{24,28},{28,24},{1,5},{5... | collective-permute-start | bytes 589832 | tf_op jit(solution)/shard_map/ppermute | solution.py:354
  47.5 15.7 %collective-permute-start.7 = (bf16[256,1024]{1,0:T(8,128)(2,1)}, bf16[256,1024]{1,0:T(8,128)(2,1)S(1)}, u32[]{:S(2)}, u32[]{:S(2)}) collective-permute-start(bf16[256,1024]{1,0:T(8,128)(2,1)} %get-tuple-element.52), channel_id=1, source_target_pairs={{0,1},{1,0},{2,3},{3,2},{4,5},{5,4},{6,7},{7,6},{8,9},{9,8},{10,11... | collective-permute-start | bytes 1572872 | tf_op jit(solution)/shard_map/ppermute | solution.py:330
  50.9 17.4 %collective-permute-start.8 = (bf16[256,1024]{1,0:T(8,128)(2,1)}, bf16[256,1024]{1,0:T(8,128)(2,1)S(1)}, u32[]{:S(2)}, u32[]{:S(2)}) collective-permute-start(bf16[256,1024]{1,0:T(8,128)(2,1)} %get-tuple-element.53), channel_id=1, source_target_pairs={{1,2},{2,1},{5,6},{6,5},{9,10},{10,9},{13,14},{14,13},{17,18},{18,... | collective-permute-start | bytes 1572872 | tf_op jit(solution)/shard_map/ppermute | solution.py:331
  51.8 17.8 %collective-permute-start.10 = (bf16[256,512]{1,0:T(8,128)(2,1)S(1)}, bf16[256,512]{1,0:T(8,128)(2,1)S(1)}, u32[]{:S(2)}, u32[]{:S(2)}) collective-permute-start(bf16[256,512]{1,0:T(8,128)(2,1)S(1)} %pad_maximum_fusion), channel_id=1, source_target_pairs={{0,16},{4,20},{8,24},{12,28},{16,0},{20,4},{24,8},{28,12},{1,17},{... | collective-permute-start | bytes 786440 | tf_op jit(solution)/shard_map/ppermute | solution.py:310
  53.4 16.2 %collective-permute-start.11 = (bf16[256,512]{1,0:T(8,128)(2,1)S(1)}, bf16[256,512]{1,0:T(8,128)(2,1)S(1)}, u32[]{:S(2)}, u32[]{:S(2)}) collective-permute-start(bf16[256,512]{1,0:T(8,128)(2,1)S(1)} %pad_maximum_fusion), channel_id=1, source_target_pairs={{0,24},{4,28},{8,0},{12,4},{16,8},{20,12},{24,16},{28,20},{1,25},{... | collective-permute-start | bytes 786440 | tf_op jit(solution)/shard_map/ppermute | solution.py:310
  54.8 14.8 %collective-permute-start.9 = (bf16[256,512]{1,0:T(8,128)(2,1)S(1)}, bf16[256,512]{1,0:T(8,128)(2,1)S(1)}, u32[]{:S(2)}, u32[]{:S(2)}) collective-permute-start(bf16[256,512]{1,0:T(8,128)(2,1)S(1)} %pad_maximum_fusion), channel_id=1, source_target_pairs={{0,8},{4,12},{8,16},{12,20},{16,24},{20,28},{24,0},{28,4},{1,9},{5... | collective-permute-start | bytes 786440 | tf_op jit(solution)/shard_map/ppermute | solution.py:310
  63.2 16.3 %collective-permute-start.16 = (bf16[256,1024]{1,0:T(8,128)(2,1)}, bf16[256,1024]{1,0:T(8,128)(2,1)S(1)}, u32[]{:S(2)}, u32[]{:S(2)}) collective-permute-start(bf16[256,1024]{1,0:T(8,128)(2,1)} %get-tuple-element.53), channel_id=1, source_target_pairs={{0,1},{3,2},{4,5},{7,6},{8,9},{11,10},{12,13},{15,14},{16,17},{19,... | collective-permute-start | bytes 1572872 | tf_op jit(solution)/shard_map/ppermute | solution.py:342
  68.3 0.8 copy-start.4
  69.1 34.8 %collective-permute-start.17 = (bf16[256,1024]{1,0:T(8,128)(2,1)S(1)}, bf16[256,1024]{1,0:T(8,128)(2,1)S(1)}, u32[]{:S(2)}, u32[]{:S(2)}) collective-permute-start(bf16[256,1024]{1,0:T(8,128)(2,1)S(1)} %add_convert_fusion), channel_id=1, source_target_pairs={{0,2},{2,0},{1,3},{3,1},{4,6},{6,4},{5,7},{7,5},{8,10},{10,8},{9,1... | collective-permute-start | bytes 1572872 | tf_op jit(solution)/shard_map/ppermute | solution.py:343
  71.3 38.1 %copy-start.2 = (bf16[256,1024]{1,0:T(8,128)(2,1)S(1)}, bf16[256,1024]{1,0:T(8,128)(2,1)}, u32[]{:S(2)}) copy-start(bf16[256,1024]{1,0:T(8,128)(2,1)} %proj_ref.3) | copy-start | bytes 1572868
  71.3 1.3 %collective-permute-start.12 = (bf16[128,256]{1,0:T(8,128)(2,1)S(1)}, bf16[128,256]{1,0:T(8,128)(2,1)S(1)}, u32[]{:S(2)}, u32[]{:S(2)}) collective-permute-start(bf16[128,256]{1,0:T(8,128)(2,1)S(1)} %get-tuple-element.57), channel_id=1, source_target_pairs={{0,4},{4,0},{8,12},{12,8},{16,20},{20,16},{24,28},{28,24},{1,5},{5... | collective-permute-start | bytes 196616 | tf_op jit(solution)/shard_map/ppermute | solution.py:354
  73.7 22.1 %collective-permute-start.13 = (bf16[128,512]{1,0:T(8,128)(2,1)S(1)}, bf16[128,512]{1,0:T(8,128)(2,1)S(1)}, u32[]{:S(2)}, u32[]{:S(2)}) collective-permute-start(bf16[128,512]{1,0:T(8,128)(2,1)S(1)} %get-tuple-element.59), channel_id=1, source_target_pairs={{0,1},{1,2},{2,3},{3,0},{4,5},{5,6},{6,7},{7,4},{8,9},{9,10},{10,1... | collective-permute-start | bytes 393224 | tf_op jit(solution)/shard_map/ppermute | solution.py:310
  75.6 28.3 %collective-permute-start.14 = (bf16[128,512]{1,0:T(8,128)(2,1)S(1)}, bf16[128,512]{1,0:T(8,128)(2,1)S(1)}, u32[]{:S(2)}, u32[]{:S(2)}) collective-permute-start(bf16[128,512]{1,0:T(8,128)(2,1)S(1)} %get-tuple-element.60), channel_id=1, source_target_pairs={{0,2},{1,3},{2,0},{3,1},{4,6},{5,7},{6,4},{7,5},{8,10},{9,11},{10,... | collective-permute-start | bytes 393224 | tf_op jit(solution)/shard_map/ppermute | solution.py:310
  76.3 27.7 %collective-permute-start.15 = (bf16[128,512]{1,0:T(8,128)(2,1)S(1)}, bf16[128,512]{1,0:T(8,128)(2,1)S(1)}, u32[]{:S(2)}, u32[]{:S(2)}) collective-permute-start(bf16[128,512]{1,0:T(8,128)(2,1)S(1)} %get-tuple-element.61), channel_id=1, source_target_pairs={{0,3},{1,0},{2,1},{3,2},{4,7},{5,4},{6,5},{7,6},{8,11},{9,8},{10,9... | collective-permute-start | bytes 393224 | tf_op jit(solution)/shard_map/ppermute | solution.py:310
  79.5 26.2 %copy-start.6 = (bf16[256,1024]{1,0:T(8,128)(2,1)}, bf16[256,1024]{1,0:T(8,128)(2,1)S(1)}, u32[]{:S(2)}) copy-start(bf16[256,1024]{1,0:T(8,128)(2,1)S(1)} %collective-permute-done.16.refs_3_) | copy-start | bytes 1572868
  103.9 0.8 copy-start.8
  105.7 10.5 %all-to-all-start = ((bf16[8,16,512]{2,1,0:T(8,128)(2,1)}), bf16[8,16,512]{2,1,0:T(8,128)(2,1)S(1)}, u32[]{:S(2)}, u32[]{:S(2)}) async-start(bf16[8,16,512]{2,1,0:T(8,128)(2,1)} %bitcast.15), calls=%async_computation | async-start | bytes 262144 | tf_op jit(solution)/shard_map/all_to_all | solution.py:437
  109.5 1.0 copy-start.3
  110.5 1.0 copy-start.5
  111.6 1.0 copy-start.7
  112.6 1.0 copy-start.9

commit v5 on v4

--- a/solution.py
+++ b/solution.py
@@ -275,34 +275,38 @@
     )(order, residual, *pieces)
 
 
-def bytes_kernel(count, kept_ref, result_ref, proj_ref, *refs):
-    pieces, out_ref = refs[:count], refs[count]
-    state = pieces[0][...].astype(F32)
-    for i, p in enumerate(pieces[1:], 1):
-        state += jnp.where(kept_ref[i] != 0, p[...].astype(F32), 0.0)
-    state = state.astype(BF16).astype(F32)
+def bytes_kernel(count, counted_ref, result_ref, proj_ref, *refs):
+    sources, out_ref, held, sems = refs[:count], refs[count], refs[count + 1], refs[count + 2]
+    copies = [pltpu.make_async_copy(p, held.at[i], sems.at[i]) for i, p in enumerate(sources)]
+    for copy in copies:
+        copy.start()
     rows = result_ref.shape[0]
     width = proj_ref.shape[0]
-    own = state.shape[0] // rows
-    mixed = [
-        (state[b * rows : (b + 1) * rows] + dot(result_ref[:, b * width : (b + 1) * width], proj_ref[...])).astype(BF16)
-        for b in range(own)
-    ]
+    own = out_ref.shape[0] // rows
+    back = jnp.concatenate([dot(result_ref[:, b * width : (b + 1) * width], proj_ref[...]) for b in range(own)], axis=0)
     at = lax.broadcasted_iota(jnp.int32, (rows * own, rows * own), 0)
     to = lax.broadcasted_iota(jnp.int32, (rows * own, rows * own), 1)
     order = (to == (at % own) * rows + at // own).astype(F32).astype(BF16)
-    out_ref[...] = dot(order, jnp.concatenate(mixed, axis=0)).astype(BF16)
-
-
-def finish_bytes(kept, result, proj, pieces):
+    for copy in copies:
+        copy.wait()
+    state = held[0].astype(F32)
+    for i in range(1, count):
+        state += jnp.where(counted_ref[i] != 0, held[i].astype(F32), 0.0)
+    state = state.astype(BF16).astype(F32)
+    out_ref[...] = dot(order, (state + back).astype(BF16)).astype(BF16)
+
+
+def finish_bytes(counted, result, proj, pieces):
+    shape = pieces[0].shape
     return pl.pallas_call(
         functools.partial(bytes_kernel, len(pieces)),
-        in_specs=[SMEM] + [VMEM] * (2 + len(pieces)),
+        in_specs=[SMEM, VMEM, VMEM] + [pl.BlockSpec(memory_space=pl.ANY)] * len(pieces),
         out_specs=VMEM,
-        out_shape=jax.ShapeDtypeStruct(pieces[0].shape, BF16),
+        out_shape=jax.ShapeDtypeStruct(shape, BF16),
+        scratch_shapes=[pltpu.VMEM((len(pieces), *shape), BF16), pltpu.SemaphoreType.DMA((len(pieces),))],
         compiler_params=pltpu.CompilerParams(vmem_limit_bytes=16 * 2**20),
         name="finish_bytes",
-    )(kept, result, proj, *pieces)
+    )(counted, result, proj, *pieces)
 
 
 def shift(value, axis, step):
@@ -412,21 +416,23 @@
         patch_proj,
         span,
     )
-    residual = sum(p.astype(F32) for p in scatter(chunks, "head")).astype(BF16)
+    chunks = scatter(chunks, "head")
+    if line:
+        swapped, middle = relay_first(parts, "head")
+        chunks, swapped, middle = lax.optimization_barrier((chunks, swapped, middle))
+        sent = relay_sum(parts, swapped, "head")
+    residual = sum(p.astype(F32) for p in chunks).astype(BF16)
     weight, residual = lax.optimization_barrier((jnp.transpose(global_qkv, (1, 0, 2)), residual))
     shares = gather(residual, "head")
     ids = (me - jnp.arange(ways, dtype=jnp.int32)) % ways
     core = (seq % 2).reshape(1)
     kept, given = global_heads(depth, core, ids, global_gain.reshape(ways, 1, -1), shares, fetch(weight))
     received = swap_cores(given, "seq")
-    parts, received = lax.optimization_barrier((parts, received))
     half = kept.shape[1] // 3
     keyed = jnp.concatenate([kept[:, half:], received[:, half:]], axis=0)
     pieces = [shift(keyed, "seq", 2 * step) for step in range(1, lax.axis_size("seq") // 2)]
     if line:
-        swapped, middle = relay_first(parts, "head")
-        sent = relay_sum(parts, swapped, "head")
-        kept, sent, middle = lax.optimization_barrier((kept, sent, middle))
+        parts, sent, received = lax.optimization_barrier((parts, sent, received))
         counted, parts = relay_rest(parts, swapped, middle, sent, "head")
     else:
         counted, parts = jnp.ones((ways,), jnp.int32), scatter(parts, "head")

time: 117 us -> 117 us (level)
  local copies, waits for them, and re-layouts: 7.57 us -> 2.84 us
  waiting for transfers between devices: 46.9 us -> 51.6 us
    ppermute x12, waiting for transfers between devices: 36.1 us -> 47.5 us  [shift(): lax.ppermute(value, axis, [(i, (i + step) % count) for i in range(count)])]
    ppermute x1, waiting for transfers between devices: 7.77 us -> 0.01 us  [relay_first(): swapped = lax.ppermute(chunks[1], axis, [(0, 1), (1, 0), (2, 3), (3, 2)])]
    unnamed x25 -> x21, local copies, waits for them, and re-layouts: 6.47 us -> 1.74 us
    all_to_all x1, waiting for transfers between devices: 0.01 us -> 1.54 us  [on_device(): lax.all_to_all(routed, 'seq', split_axis=0, concat_axis=0, tiled=True)]
    ppermute x1, starting transfers between devices: 3.85 us -> 5.32 us  [relay_rest(): inward = lax.ppermute(chunks[2], axis, [(0, 1), (3, 2)])]
  transfers between devices with their start and end apart: 19 -> 19, of which waited for: 9 -> 12; matrix products, arithmetic and copies ran while one was open for 2% -> 1% of each run, Pallas kernels for 6% -> 6%
where the time goes in v5:
time: 117 us; the launch traced here: 116 us
  waiting for transfers between devices  51.6 us (44%)
  starting transfers between devices  34.1 us (29%)
  Pallas kernels  25.5 us (22%)
  local copies, waits for them, and re-layouts  2.84 us (2%)
  other arithmetic  1.27 us (1%)
    ppermute x12, waiting for transfers between devices, shift(): lax.ppermute(value, axis, [(i, (i + step) % count) for i in range(count)])  47.5 us
    ppermute x12, starting transfers between devices, shift(): lax.ppermute(value, axis, [(i, (i + step) % count) for i in range(count)])  21.1 us
    pallas_call x1, Pallas kernels, local_part(): pl.pallas_call(functools.partial(local_kernel, span, piece, step), in_spe...  15.4 us
    ppermute x1, starting transfers between devices, relay_rest(): inward = lax.ppermute(chunks[2], axis, [(0, 1), (3, 2)])  5.32 us
    all_to_all x1, starting transfers between devices, on_device(): lax.all_to_all(routed, 'seq', split_axis=0, concat_axis=0, tiled=True)  3.66 us
    ppermute x1, starting transfers between devices, relay_first(): swapped = lax.ppermute(chunks[1], axis, [(0, 1), (1, 0), (2, 3), (3, 2)])  3.09 us
    pallas_call x1, Pallas kernels, fetch(): pl.pallas_call(fetch_kernel, in_specs=[HBM], out_specs=VMEM, out_shape=pl...  2.9 us
    ppermute x2, waiting for transfers between devices, swap_cores(): lax.ppermute(value, axis, [(i, i ^ 1) for i in range(lax.axis_size(axis))])  2.54 us
  transfers between devices with their start and end apart: 19, of which 12 were waited for; matrix products, arithmetic and copies ran while one was open for 1% of the time, Pallas kernels for 6%

profile of v5, /device:TPU:0, one launch (start us, length us, event | category | flops | bytes accessed | tf_op | source)
XLA Modules:
  0.0 116.2 jit_solution(5911638195626886107)
XLA Ops:
  1.3 15.4 %local_part.1 = (bf16[256,1024]{1,0:T(8,128)(2,1)}, bf16[256,1024]{1,0:T(8,128)(2,1)}, bf16[256,1024]{1,0:T(8,128)(2,1)}, bf16[256,1024]{1,0:T(8,128)(2,1)}, bf1...) custom-call(s32[1]{0:T(128)} %bitcast.4.me_ref, ...), custom_call_target="tpu_custom_call" | custom-call | tf_op jit(solution)/shard_map/local_part/pallas_call | solution.py:121
  16.8 3.1 %collective-permute-start.3 = (bf16[256,1024]{1,0:T(8,128)(2,1)}, bf16[256,1024]{1,0:T(8,128)(2,1)S(1)}, u32[]{:S(2)}, u32[]{:S(2)}) collective-permute-start(bf16[256,1024]{1,0:T(8,128)(2,1)} %get-tuple-element.45), channel_id=1, source_target_pairs={{0,1},{1,0},{2,3},{3,2},{4,5},{5,4},{6,7},{7,6},{8,9},{9,8},{10,11... | collective-permute-start | bytes 1572872 | tf_op jit(solution)/shard_map/ppermute | solution.py:334
  20.6 4.4 %collective-permute-start = (bf16[128,512]{1,0:T(8,128)(2,1)S(1)}, bf16[128,512]{1,0:T(8,128)(2,1)S(1)}, u32[]{:S(2)}, u32[]{:S(2)}) collective-permute-start(bf16[128,512]{1,0:T(8,128)(2,1)S(1)} %get-tuple-element.42), channel_id=1, source_target_pairs={{0,1},{1,2},{2,3},{3,0},{4,5},{5,6},{6,7},{7,4},{8,9},{9,10},{10,1... | collective-permute-start | bytes 393224 | tf_op jit(solution)/shard_map/ppermute | solution.py:314
  25.0 2.4 %collective-permute-start.2 = (bf16[128,512]{1,0:T(8,128)(2,1)S(1)}, bf16[128,512]{1,0:T(8,128)(2,1)S(1)}, u32[]{:S(2)}, u32[]{:S(2)}) collective-permute-start(bf16[128,512]{1,0:T(8,128)(2,1)S(1)} %get-tuple-element.44), channel_id=1, source_target_pairs={{0,3},{1,0},{2,1},{3,2},{4,7},{5,4},{6,5},{7,6},{8,11},{9,8},{10,9... | collective-permute-start | bytes 393224 | tf_op jit(solution)/shard_map/ppermute | solution.py:314
  27.4 10.8 %collective-permute-done = bf16[128,512]{1,0:T(8,128)(2,1)S(1)} collective-permute-done((bf16[128,512]{1,0:T(8,128)(2,1)S(1)}, bf16[128,512]{1,0:T(8,128)(2,1)S(1)}, u32[]{:S(2)}, u32[]{:S(2)}) %collective-permute-start) | collective-permute-done | bytes 131104 | tf_op jit(solution)/shard_map/ppermute | solution.py:314
  38.2 7.5 %collective-permute-done.1 = bf16[128,512]{1,0:T(8,128)(2,1)S(1)} collective-permute-done((bf16[128,512]{1,0:T(8,128)(2,1)S(1)}, bf16[128,512]{1,0:T(8,128)(2,1)S(1)}, u32[]{:S(2)}, u32[]{:S(2)}) %collective-permute-start.1) | collective-permute-done | bytes 131104 | tf_op jit(solution)/shard_map/ppermute | solution.py:314
  45.9 2.3 %collective-permute-start.5 = (bf16[128,512]{1,0:T(8,128)(2,1)S(1)}, bf16[128,512]{1,0:T(8,128)(2,1)S(1)}, u32[]{:S(2)}, u32[]{:S(2)}) collective-permute-start(bf16[128,512]{1,0:T(8,128)(2,1)S(1)} %add_convert_fusion.1.refs_0_.own_ref), channel_id=1, source_target_pairs={{0,1},{1,2},{2,3},{3,0},{4,5},{5,6},{6,7},{7,4},{8,9},{9,10},{10,1... | collective-permute-start | bytes 393224 | tf_op jit(solution)/shard_map/ppermute | solution.py:314
  48.1 2.6 %collective-permute-start.6 = (bf16[128,512]{1,0:T(8,128)(2,1)S(1)}, bf16[128,512]{1,0:T(8,128)(2,1)S(1)}, u32[]{:S(2)}, u32[]{:S(2)}) collective-permute-start(bf16[128,512]{1,0:T(8,128)(2,1)S(1)} %add_convert_fusion.1.refs_0_.own_ref), channel_id=1, source_target_pairs={{0,2},{1,3},{2,0},{3,1},{4,6},{5,7},{6,4},{7,5},{8,10},{9,11},{10,... | collective-permute-start | bytes 393224 | tf_op jit(solution)/shard_map/ppermute | solution.py:314
  51.0 2.9 %fetch.1.refs_4_ = bf16[3,2048,512]{2,1,0:T(8,128)(2,1)S(1)} custom-call(bf16[3,2048,512]{2,1,0:T(8,128)(2,1)} %bitcast.20), custom_call_target="tpu_custom_call" | custom-call | tf_op jit(solution)/shard_map/fetch/pallas_call | solution.py:149
  53.9 0.8 collective-permute-done.5.refs_1_
  54.7 3.3 %collective-permute-done.6.refs_2_ = bf16[128,512]{1,0:T(8,128)(2,1)S(1)} collective-permute-done((bf16[128,512]{1,0:T(8,128)(2,1)S(1)}, bf16[128,512]{1,0:T(8,128)(2,1)S(1)}, u32[]{:S(2)}, u32[]{:S(2)}) %collective-permute-start.6) | collective-permute-done | bytes 131104 | tf_op jit(solution)/shard_map/ppermute | solution.py:314
  58.1 1.7 %global_heads.1 = (bf16[128,768]{1,0:T(8,128)(2,1)S(1)}, bf16[128,768]{1,0:T(8,128)(2,1)S(1)}) custom-call(s32[1]{0:T(128)} %bitcast.12.core_ref, s32[4]{0:T(128)S(1)} %and_select_fusion.ids_ref, f32[4,1,512]{2,1,0:T(1,128)S(1)} %bitcast.19, bf16[128,512]{1,0:T(8,128)(2,1)S(1)} %add_convert_fusion.1.refs_0_.own_ref, ...), custom_call_target="tpu_custom_call" | custom-call | tf_op jit(solution)/shard_map/global_heads/pallas_call | solution.py:183
  60.0 1.3 %collective-permute-done.8.given_ref = bf16[128,768]{1,0:T(8,128)(2,1)S(1)} collective-permute-done((bf16[128,768]{1,0:T(8,128)(2,1)S(1)}, bf16[128,768]{1,0:T(8,128)(2,1)S(1)}, u32[]{:S(2)}, u32[]{:S(2)}) %collective-permute-start.8) | collective-permute-done | bytes 196640 | tf_op jit(solution)/shard_map/ppermute | solution.py:358
  61.4 1.6 %collective-permute-start.10 = (bf16[256,512]{1,0:T(8,128)(2,1)S(1)}, bf16[256,512]{1,0:T(8,128)(2,1)S(1)}, u32[]{:S(2)}, u32[]{:S(2)}) collective-permute-start(bf16[256,512]{1,0:T(8,128)(2,1)S(1)} %pad_maximum_fusion), channel_id=1, source_target_pairs={{0,16},{4,20},{8,24},{12,28},{16,0},{20,4},{24,8},{28,12},{1,17},{... | collective-permute-start | bytes 786440 | tf_op jit(solution)/shard_map/ppermute | solution.py:314
  63.0 1.4 %collective-permute-start.11 = (bf16[256,512]{1,0:T(8,128)(2,1)S(1)}, bf16[256,512]{1,0:T(8,128)(2,1)S(1)}, u32[]{:S(2)}, u32[]{:S(2)}) collective-permute-start(bf16[256,512]{1,0:T(8,128)(2,1)S(1)} %pad_maximum_fusion), channel_id=1, source_target_pairs={{0,24},{4,28},{8,0},{12,4},{16,8},{20,12},{24,16},{28,20},{1,25},{... | collective-permute-start | bytes 786440 | tf_op jit(solution)/shard_map/ppermute | solution.py:314
  65.2 5.3 %collective-permute-start.16 = (bf16[256,1024]{1,0:T(8,128)(2,1)S(1)}, bf16[256,1024]{1,0:T(8,128)(2,1)S(1)}, u32[]{:S(2)}, u32[]{:S(2)}) collective-permute-start(bf16[256,1024]{1,0:T(8,128)(2,1)S(1)} %copy-done.9), channel_id=1, source_target_pairs={{0,1},{3,2},{4,5},{7,6},{8,9},{11,10},{12,13},{15,14},{16,17},{19,... | collective-permute-start | bytes 1572872 | tf_op jit(solution)/shard_map/ppermute | solution.py:346
  70.6 1.5 %collective-permute-done.11.refs_2_ = bf16[256,512]{1,0:T(8,128)(2,1)S(1)} collective-permute-done((bf16[256,512]{1,0:T(8,128)(2,1)S(1)}, bf16[256,512]{1,0:T(8,128)(2,1)S(1)}, u32[]{:S(2)}, u32[]{:S(2)}) %collective-permute-start.11) | collective-permute-done | bytes 262176 | tf_op jit(solution)/shard_map/ppermute | solution.py:314
  72.2 4.4 %collective-permute-done.9.refs_0_ = bf16[256,512]{1,0:T(8,128)(2,1)S(1)} collective-permute-done((bf16[256,512]{1,0:T(8,128)(2,1)S(1)}, bf16[256,512]{1,0:T(8,128)(2,1)S(1)}, u32[]{:S(2)}, u32[]{:S(2)}) %collective-permute-start.9) | collective-permute-done | bytes 262176 | tf_op jit(solution)/shard_map/ppermute | solution.py:314
  76.6 1.7 %attend.1 = (bf16[128,256]{1,0:T(8,128)(2,1)S(1)}, bf16[128,256]{1,0:T(8,128)(2,1)S(1)}) custom-call(s32[1]{0:T(128)} %bitcast.13.me_ref, s32[4]{0:T(128)S(1)} %and_select_fusion.1.ids_ref, f32[4]{0:T(128)S(1)} %copy-done.7, bf16[128,768]{1,0:T(8,128)(2,1)S(1)} %get-tuple-element.53.kept_ref, bf16[128,768]{1,0:T(8,128)(2,1)S(1)} %collective-permute-done.8.given_ref, ...), custom_call_target="tpu_custom_call" | custom-call | tf_op jit(solution)/shard_map/attend/pallas_call | solution.py:226
  78.4 1.2 %collective-permute-done.12.other_ref = bf16[128,256]{1,0:T(8,128)(2,1)S(1)} collective-permute-done((bf16[128,256]{1,0:T(8,128)(2,1)S(1)}, bf16[128,256]{1,0:T(8,128)(2,1)S(1)}, u32[]{:S(2)}, u32[]{:S(2)}) %collective-permute-start.12) | collective-permute-done | bytes 65568 | tf_op jit(solution)/shard_map/ppermute | solution.py:358
  79.6 1.0 project.1
  80.7 3.2 %collective-permute-start.13 = (bf16[128,512]{1,0:T(8,128)(2,1)S(1)}, bf16[128,512]{1,0:T(8,128)(2,1)S(1)}, u32[]{:S(2)}, u32[]{:S(2)}) collective-permute-start(bf16[128,512]{1,0:T(8,128)(2,1)S(1)} %get-tuple-element.62), channel_id=1, source_target_pairs={{0,1},{1,2},{2,3},{3,0},{4,5},{5,6},{6,7},{7,4},{8,9},{9,10},{10,1... | collective-permute-start | bytes 393224 | tf_op jit(solution)/shard_map/ppermute | solution.py:314
  83.9 1.2 %collective-permute-start.14 = (bf16[128,512]{1,0:T(8,128)(2,1)S(1)}, bf16[128,512]{1,0:T(8,128)(2,1)S(1)}, u32[]{:S(2)}, u32[]{:S(2)}) collective-permute-start(bf16[128,512]{1,0:T(8,128)(2,1)S(1)} %get-tuple-element.63), channel_id=1, source_target_pairs={{0,2},{1,3},{2,0},{3,1},{4,6},{5,7},{6,4},{7,5},{8,10},{9,11},{10,... | collective-permute-start | bytes 393224 | tf_op jit(solution)/shard_map/ppermute | solution.py:314
  85.1 1.2 %collective-permute-start.15 = (bf16[128,512]{1,0:T(8,128)(2,1)S(1)}, bf16[128,512]{1,0:T(8,128)(2,1)S(1)}, u32[]{:S(2)}, u32[]{:S(2)}) collective-permute-start(bf16[128,512]{1,0:T(8,128)(2,1)S(1)} %get-tuple-element.64), channel_id=1, source_target_pairs={{0,3},{1,0},{2,1},{3,2},{4,7},{5,4},{6,5},{7,6},{8,11},{9,8},{10,9... | collective-permute-start | bytes 393224 | tf_op jit(solution)/shard_map/ppermute | solution.py:314
  86.4 11.3 %collective-permute-done.13.refs_1_ = bf16[128,512]{1,0:T(8,128)(2,1)S(1)} collective-permute-done((bf16[128,512]{1,0:T(8,128)(2,1)S(1)}, bf16[128,512]{1,0:T(8,128)(2,1)S(1)}, u32[]{:S(2)}, u32[]{:S(2)}) %collective-permute-start.13) | collective-permute-done | bytes 131104 | tf_op jit(solution)/shard_map/ppermute | solution.py:314
  97.7 7.7 %collective-permute-done.14.refs_2_ = bf16[128,512]{1,0:T(8,128)(2,1)S(1)} collective-permute-done((bf16[128,512]{1,0:T(8,128)(2,1)S(1)}, bf16[128,512]{1,0:T(8,128)(2,1)S(1)}, u32[]{:S(2)}, u32[]{:S(2)}) %collective-permute-start.14) | collective-permute-done | bytes 131104 | tf_op jit(solution)/shard_map/ppermute | solution.py:314
  105.4 0.9 finish_result.1
  106.4 3.7 %all-to-all-start = ((bf16[8,16,512]{2,1,0:T(8,128)(2,1)}), bf16[8,16,512]{2,1,0:T(8,128)(2,1)S(1)}, u32[]{:S(2)}, u32[]{:S(2)}) async-start(bf16[8,16,512]{2,1,0:T(8,128)(2,1)} %bitcast.15), calls=%async_computation | async-start | bytes 262144 | tf_op jit(solution)/shard_map/all_to_all | solution.py:443
  110.1 1.0 copy-done.5
  111.2 1.9 %finish_bytes.1 = bf16[256,1024]{1,0:T(8,128)(2,1)S(1)} custom-call(s32[5]{0:T(128)S(1)} %stack.32.counted_ref, bf16[128,512]{1,0:T(8,128)(2,1)S(1)} %get-tuple-element.73.result_ref, bf16[256,1024]{1,0:T(8,128)(2,1)S(1)} %copy-done.2, bf16[256,1024]{1,0:T(8,128)(2,1)S(1)} %copy-done.3, bf16[256,1024]{1,0:T(8,128)(2,1)S(1)} %collective-permute-done.3.refs_1_, ...), custom_call_target="tpu_custom_call" | custom-call | tf_op jit(solution)/shard_map/finish_bytes/pallas_call | solution.py:301
  113.0 1.0 reshape.126
  114.0 1.5 %all-to-all-done = bf16[8,16,512]{2,1,0:T(8,128)(2,1)S(1)} async-done(((bf16[8,16,512]{2,1,0:T(8,128)(2,1)}), bf16[8,16,512]{2,1,0:T(8,128)(2,1)S(1)}, u32[]{:S(2)}, u32[]{:S(2)}) %all-to-all-start) | async-done | bytes 131104 | tf_op jit(solution)/shard_map/all_to_all | solution.py:443
  (53 shorter events, 3.7 us)
Async XLA Ops:
  0.6 50.2 %copy-start = (s32[8,16]{1,0:T(8,128)S(1)}, s32[8,16]{1,0:T(8,128)}, u32[]{:S(2)}) copy-start(s32[8,16]{1,0:T(8,128)} %param.27) | copy-start | bytes 1540
  16.8 29.0 %collective-permute-start.3 = (bf16[256,1024]{1,0:T(8,128)(2,1)}, bf16[256,1024]{1,0:T(8,128)(2,1)S(1)}, u32[]{:S(2)}, u32[]{:S(2)}) collective-permute-start(bf16[256,1024]{1,0:T(8,128)(2,1)} %get-tuple-element.45), channel_id=1, source_target_pairs={{0,1},{1,0},{2,3},{3,2},{4,5},{5,4},{6,7},{7,6},{8,9},{9,8},{10,11... | collective-permute-start | bytes 1572872 | tf_op jit(solution)/shard_map/ppermute | solution.py:334
  19.9 25.9 %collective-permute-start.4 = (bf16[256,1024]{1,0:T(8,128)(2,1)}, bf16[256,1024]{1,0:T(8,128)(2,1)S(1)}, u32[]{:S(2)}, u32[]{:S(2)}) collective-permute-start(bf16[256,1024]{1,0:T(8,128)(2,1)} %get-tuple-element.67), channel_id=1, source_target_pairs={{1,2},{2,1},{5,6},{6,5},{9,10},{10,9},{13,14},{14,13},{17,18},{18,... | collective-permute-start | bytes 1572872 | tf_op jit(solution)/shard_map/ppermute | solution.py:335
  20.6 17.7 %collective-permute-start = (bf16[128,512]{1,0:T(8,128)(2,1)S(1)}, bf16[128,512]{1,0:T(8,128)(2,1)S(1)}, u32[]{:S(2)}, u32[]{:S(2)}) collective-permute-start(bf16[128,512]{1,0:T(8,128)(2,1)S(1)} %get-tuple-element.42), channel_id=1, source_target_pairs={{0,1},{1,2},{2,3},{3,0},{4,5},{5,6},{6,7},{7,4},{8,9},{9,10},{10,1... | collective-permute-start | bytes 393224 | tf_op jit(solution)/shard_map/ppermute | solution.py:314
  25.0 20.8 %collective-permute-start.1 = (bf16[128,512]{1,0:T(8,128)(2,1)S(1)}, bf16[128,512]{1,0:T(8,128)(2,1)S(1)}, u32[]{:S(2)}, u32[]{:S(2)}) collective-permute-start(bf16[128,512]{1,0:T(8,128)(2,1)S(1)} %get-tuple-element.43), channel_id=1, source_target_pairs={{0,2},{1,3},{2,0},{3,1},{4,6},{5,7},{6,4},{7,5},{8,10},{9,11},{10,... | collective-permute-start | bytes 393224 | tf_op jit(solution)/shard_map/ppermute | solution.py:314
  25.0 20.8 %collective-permute-start.2 = (bf16[128,512]{1,0:T(8,128)(2,1)S(1)}, bf16[128,512]{1,0:T(8,128)(2,1)S(1)}, u32[]{:S(2)}, u32[]{:S(2)}) collective-permute-start(bf16[128,512]{1,0:T(8,128)(2,1)S(1)} %get-tuple-element.44), channel_id=1, source_target_pairs={{0,3},{1,0},{2,1},{3,2},{4,7},{5,4},{6,5},{7,6},{8,11},{9,8},{10,9... | collective-permute-start | bytes 393224 | tf_op jit(solution)/shard_map/ppermute | solution.py:314
  45.9 8.9 %collective-permute-start.5 = (bf16[128,512]{1,0:T(8,128)(2,1)S(1)}, bf16[128,512]{1,0:T(8,128)(2,1)S(1)}, u32[]{:S(2)}, u32[]{:S(2)}) collective-permute-start(bf16[128,512]{1,0:T(8,128)(2,1)S(1)} %add_convert_fusion.1.refs_0_.own_ref), channel_id=1, source_target_pairs={{0,1},{1,2},{2,3},{3,0},{4,5},{5,6},{6,7},{7,4},{8,9},{9,10},{10,1... | collective-permute-start | bytes 393224 | tf_op jit(solution)/shard_map/ppermute | solution.py:314
  48.1 9.9 %collective-permute-start.6 = (bf16[128,512]{1,0:T(8,128)(2,1)S(1)}, bf16[128,512]{1,0:T(8,128)(2,1)S(1)}, u32[]{:S(2)}, u32[]{:S(2)}) collective-permute-start(bf16[128,512]{1,0:T(8,128)(2,1)S(1)} %add_convert_fusion.1.refs_0_.own_ref), channel_id=1, source_target_pairs={{0,2},{1,3},{2,0},{3,1},{4,6},{5,7},{6,4},{7,5},{8,10},{9,11},{10,... | collective-permute-start | bytes 393224 | tf_op jit(solution)/shard_map/ppermute | solution.py:314
  50.8 7.3 %collective-permute-start.7 = (bf16[128,512]{1,0:T(8,128)(2,1)S(1)}, bf16[128,512]{1,0:T(8,128)(2,1)S(1)}, u32[]{:S(2)}, u32[]{:S(2)}) collective-permute-start(bf16[128,512]{1,0:T(8,128)(2,1)S(1)} %add_convert_fusion.1.refs_0_.own_ref), channel_id=1, source_target_pairs={{0,3},{1,0},{2,1},{3,2},{4,7},{5,4},{6,5},{7,6},{8,11},{9,8},{10,9... | collective-permute-start | bytes 393224 | tf_op jit(solution)/shard_map/ppermute | solution.py:314
  51.0 7.1 %copy-start.6 = (f32[2048]{0:T(1024)S(1)}, f32[2048]{0:T(1024)}, u32[]{:S(2)}) copy-start(f32[2048]{0:T(1024)} %param.22) | copy-start | bytes 24580
  58.1 6.9 %copy-start.8 = (bf16[256,1024]{1,0:T(8,128)(2,1)S(1)}, bf16[256,1024]{1,0:T(8,128)(2,1)}, u32[]{:S(2)}) copy-start(bf16[256,1024]{1,0:T(8,128)(2,1)} %get-tuple-element.55) | copy-start | bytes 1572868
  59.8 5.4 %copy-start.9 = (bf16[256,1024]{1,0:T(8,128)(2,1)S(1)}, bf16[256,1024]{1,0:T(8,128)(2,1)}, u32[]{:S(2)}) copy-start(bf16[256,1024]{1,0:T(8,128)(2,1)} %get-tuple-element.67) | copy-start | bytes 1572868
  59.8 16.8 %copy-start.7 = (f32[4]{0:T(128)S(1)}, f32[4]{0:T(128)}, u32[]{:S(2)}) copy-start(f32[4]{0:T(128)} %scale_ref.3) | copy-start | bytes 52
  59.8 19.8 %copy-start.1 = (bf16[512,2048]{1,0:T(8,128)(2,1)S(1)}, bf16[512,2048]{1,0:T(8,128)(2,1)}, u32[]{:S(2)}) copy-start(bf16[512,2048]{1,0:T(8,128)(2,1)} %proj_ref.2) | copy-start | bytes 6291460
  59.8 1.5 %collective-permute-start.8 = (bf16[128,768]{1,0:T(8,128)(2,1)S(1)}, bf16[128,768]{1,0:T(8,128)(2,1)S(1)}, u32[]{:S(2)}, u32[]{:S(2)}) collective-permute-start(bf16[128,768]{1,0:T(8,128)(2,1)S(1)} %get-tuple-element.57), channel_id=1, source_target_pairs={{0,4},{4,0},{8,12},{12,8},{16,20},{20,16},{24,28},{28,24},{1,5},{5... | collective-permute-start | bytes 589832 | tf_op jit(solution)/shard_map/ppermute | solution.py:358
  61.4 9.3 %collective-permute-start.10 = (bf16[256,512]{1,0:T(8,128)(2,1)S(1)}, bf16[256,512]{1,0:T(8,128)(2,1)S(1)}, u32[]{:S(2)}, u32[]{:S(2)}) collective-permute-start(bf16[256,512]{1,0:T(8,128)(2,1)S(1)} %pad_maximum_fusion), channel_id=1, source_target_pairs={{0,16},{4,20},{8,24},{12,28},{16,0},{20,4},{24,8},{28,12},{1,17},{... | collective-permute-start | bytes 786440 | tf_op jit(solution)/shard_map/ppermute | solution.py:314
  63.0 9.2 %collective-permute-start.11 = (bf16[256,512]{1,0:T(8,128)(2,1)S(1)}, bf16[256,512]{1,0:T(8,128)(2,1)S(1)}, u32[]{:S(2)}, u32[]{:S(2)}) collective-permute-start(bf16[256,512]{1,0:T(8,128)(2,1)S(1)} %pad_maximum_fusion), channel_id=1, source_target_pairs={{0,24},{4,28},{8,0},{12,4},{16,8},{20,12},{24,16},{28,20},{1,25},{... | collective-permute-start | bytes 786440 | tf_op jit(solution)/shard_map/ppermute | solution.py:314
  64.4 12.2 %collective-permute-start.9 = (bf16[256,512]{1,0:T(8,128)(2,1)S(1)}, bf16[256,512]{1,0:T(8,128)(2,1)S(1)}, u32[]{:S(2)}, u32[]{:S(2)}) collective-permute-start(bf16[256,512]{1,0:T(8,128)(2,1)S(1)} %pad_maximum_fusion), channel_id=1, source_target_pairs={{0,8},{4,12},{8,16},{12,20},{16,24},{20,28},{24,0},{28,4},{1,9},{5... | collective-permute-start | bytes 786440 | tf_op jit(solution)/shard_map/ppermute | solution.py:314
  65.2 40.2 %collective-permute-start.16 = (bf16[256,1024]{1,0:T(8,128)(2,1)S(1)}, bf16[256,1024]{1,0:T(8,128)(2,1)S(1)}, u32[]{:S(2)}, u32[]{:S(2)}) collective-permute-start(bf16[256,1024]{1,0:T(8,128)(2,1)S(1)} %copy-done.9), channel_id=1, source_target_pairs={{0,1},{3,2},{4,5},{7,6},{8,9},{11,10},{12,13},{15,14},{16,17},{19,... | collective-permute-start | bytes 1572872 | tf_op jit(solution)/shard_map/ppermute | solution.py:346
  70.5 34.9 %collective-permute-start.17 = (bf16[256,1024]{1,0:T(8,128)(2,1)S(1)}, bf16[256,1024]{1,0:T(8,128)(2,1)S(1)}, u32[]{:S(2)}, u32[]{:S(2)}) collective-permute-start(bf16[256,1024]{1,0:T(8,128)(2,1)S(1)} %add_convert_fusion), channel_id=1, source_target_pairs={{0,2},{2,0},{1,3},{3,1},{4,6},{6,4},{5,7},{7,5},{8,10},{10,8},{9,1... | collective-permute-start | bytes 1572872 | tf_op jit(solution)/shard_map/ppermute | solution.py:347
  76.6 33.5 %copy-start.2 = (bf16[256,1024]{1,0:T(8,128)(2,1)S(1)}, bf16[256,1024]{1,0:T(8,128)(2,1)}, u32[]{:S(2)}) copy-start(bf16[256,1024]{1,0:T(8,128)(2,1)} %proj_ref.3) | copy-start | bytes 1572868
  76.6 33.5 %copy-start.3 = (bf16[256,1024]{1,0:T(8,128)(2,1)S(1)}, bf16[256,1024]{1,0:T(8,128)(2,1)}, u32[]{:S(2)}) copy-start(bf16[256,1024]{1,0:T(8,128)(2,1)} %get-tuple-element.74.refs_0_) | copy-start | bytes 1572868
  78.3 1.3 %collective-permute-start.12 = (bf16[128,256]{1,0:T(8,128)(2,1)S(1)}, bf16[128,256]{1,0:T(8,128)(2,1)S(1)}, u32[]{:S(2)}, u32[]{:S(2)}) collective-permute-start(bf16[128,256]{1,0:T(8,128)(2,1)S(1)} %get-tuple-element.60), channel_id=1, source_target_pairs={{0,4},{4,0},{8,12},{12,8},{16,20},{20,16},{24,28},{28,24},{1,5},{5... | collective-permute-start | bytes 196616 | tf_op jit(solution)/shard_map/ppermute | solution.py:358
  80.7 17.0 %collective-permute-start.13 = (bf16[128,512]{1,0:T(8,128)(2,1)S(1)}, bf16[128,512]{1,0:T(8,128)(2,1)S(1)}, u32[]{:S(2)}, u32[]{:S(2)}) collective-permute-start(bf16[128,512]{1,0:T(8,128)(2,1)S(1)} %get-tuple-element.62), channel_id=1, source_target_pairs={{0,1},{1,2},{2,3},{3,0},{4,5},{5,6},{6,7},{7,4},{8,9},{9,10},{10,1... | collective-permute-start | bytes 393224 | tf_op jit(solution)/shard_map/ppermute | solution.py:314
  83.9 21.5 %collective-permute-start.14 = (bf16[128,512]{1,0:T(8,128)(2,1)S(1)}, bf16[128,512]{1,0:T(8,128)(2,1)S(1)}, u32[]{:S(2)}, u32[]{:S(2)}) collective-permute-start(bf16[128,512]{1,0:T(8,128)(2,1)S(1)} %get-tuple-element.63), channel_id=1, source_target_pairs={{0,2},{1,3},{2,0},{3,1},{4,6},{5,7},{6,4},{7,5},{8,10},{9,11},{10,... | collective-permute-start | bytes 393224 | tf_op jit(solution)/shard_map/ppermute | solution.py:314
  85.1 20.3 %collective-permute-start.15 = (bf16[128,512]{1,0:T(8,128)(2,1)S(1)}, bf16[128,512]{1,0:T(8,128)(2,1)S(1)}, u32[]{:S(2)}, u32[]{:S(2)}) collective-permute-start(bf16[128,512]{1,0:T(8,128)(2,1)S(1)} %get-tuple-element.64), channel_id=1, source_target_pairs={{0,3},{1,0},{2,1},{3,2},{4,7},{5,4},{6,5},{7,6},{8,11},{9,8},{10,9... | collective-permute-start | bytes 393224 | tf_op jit(solution)/shard_map/ppermute | solution.py:314
  105.4 0.9 copy-start.4
  106.4 9.2 %all-to-all-start = ((bf16[8,16,512]{2,1,0:T(8,128)(2,1)}), bf16[8,16,512]{2,1,0:T(8,128)(2,1)S(1)}, u32[]{:S(2)}, u32[]{:S(2)}) async-start(bf16[8,16,512]{2,1,0:T(8,128)(2,1)} %bitcast.15), calls=%async_computation | async-start | bytes 262144 | tf_op jit(solution)/shard_map/all_to_all | solution.py:443
  110.1 1.0 copy-start.5

commit v6 on v5

--- a/solution.py
+++ b/solution.py
@@ -275,9 +275,15 @@
     )(order, residual, *pieces)
 
 
-def bytes_kernel(count, counted_ref, result_ref, proj_ref, *refs):
-    sources, out_ref, held, sems = refs[:count], refs[count], refs[count + 1], refs[count + 2]
-    copies = [pltpu.make_async_copy(p, held.at[i], sems.at[i]) for i, p in enumerate(sources)]
+def bytes_kernel(cuts, counted_ref, result_ref, proj_ref, *refs):
+    sources, (out_ref, held, sems) = refs[: sum(cuts)], refs[sum(cuts) :]
+    count = len(cuts)
+    copies = []
+    for i, cut in enumerate(cuts):
+        rows = held.shape[1] // cut
+        for c in range(cut):
+            at = len(copies)
+            copies.append(pltpu.make_async_copy(sources[at], held.at[i, pl.ds(c * rows, rows)], sems.at[at]))
     for copy in copies:
         copy.start()
     rows = result_ref.shape[0]
@@ -297,16 +303,17 @@
 
 
 def finish_bytes(counted, result, proj, pieces):
-    shape = pieces[0].shape
-    return pl.pallas_call(
-        functools.partial(bytes_kernel, len(pieces)),
-        in_specs=[SMEM, VMEM, VMEM] + [pl.BlockSpec(memory_space=pl.ANY)] * len(pieces),
+    shape = pieces[0][0].shape
+    flat = [part for piece in pieces for part in piece]
+    return pl.pallas_call(
+        functools.partial(bytes_kernel, tuple(len(piece) for piece in pieces)),
+        in_specs=[SMEM, VMEM, VMEM] + [pl.BlockSpec(memory_space=pl.ANY)] * len(flat),
         out_specs=VMEM,
         out_shape=jax.ShapeDtypeStruct(shape, BF16),
-        scratch_shapes=[pltpu.VMEM((len(pieces), *shape), BF16), pltpu.SemaphoreType.DMA((len(pieces),))],
+        scratch_shapes=[pltpu.VMEM((len(pieces), *shape), BF16), pltpu.SemaphoreType.DMA((len(flat),))],
         compiler_params=pltpu.CompilerParams(vmem_limit_bytes=16 * 2**20),
         name="finish_bytes",
-    )(counted, result, proj, *pieces)
+    )(counted, result, proj, *flat)
 
 
 def shift(value, axis, step):
@@ -342,12 +349,18 @@
     return (chunks[3].astype(F32) + relayed).astype(BF16)
 
 
-def relay_rest(chunks, swapped, middle, sent, axis):
-    inward = lax.ppermute(chunks[2], axis, [(0, 1), (3, 2)])
-    crossed = lax.ppermute(sent, axis, [(0, 2), (2, 0), (1, 3), (3, 1)])
+def relay_inward(chunks, axis):
+    return lax.ppermute(chunks[2], axis, [(0, 1), (3, 2)])
+
+
+def relay_cross(sent, axis):
+    return lax.ppermute(sent, axis, [(0, 2), (2, 0), (1, 3), (3, 1)])
+
+
+def relay_counted(axis):
     me = lax.axis_index(axis)
     outer = ((me == 0) | (me == 3)).astype(jnp.int32)
-    return jnp.stack([1 + 0 * outer, outer, 1 - outer, 1 - outer, 1 + 0 * outer]), [chunks[0], swapped, middle, inward, crossed]
+    return jnp.stack([1 + 0 * outer, outer, 1 - outer, 1 - outer, 1 + 0 * outer])
 
 
 def gather(value, axis):
@@ -416,32 +429,37 @@
         patch_proj,
         span,
     )
-    chunks = scatter(chunks, "head")
-    if line:
-        swapped, middle = relay_first(parts, "head")
-        chunks, swapped, middle = lax.optimization_barrier((chunks, swapped, middle))
-        sent = relay_sum(parts, swapped, "head")
-    residual = sum(p.astype(F32) for p in chunks).astype(BF16)
+    residual = sum(p.astype(F32) for p in scatter(chunks, "head")).astype(BF16)
     weight, residual = lax.optimization_barrier((jnp.transpose(global_qkv, (1, 0, 2)), residual))
     shares = gather(residual, "head")
     ids = (me - jnp.arange(ways, dtype=jnp.int32)) % ways
     core = (seq % 2).reshape(1)
     kept, given = global_heads(depth, core, ids, global_gain.reshape(ways, 1, -1), shares, fetch(weight))
     received = swap_cores(given, "seq")
+    parts, received = lax.optimization_barrier((parts, received))
     half = kept.shape[1] // 3
     keyed = jnp.concatenate([kept[:, half:], received[:, half:]], axis=0)
     pieces = [shift(keyed, "seq", 2 * step) for step in range(1, lax.axis_size("seq") // 2)]
     if line:
-        parts, sent, received = lax.optimization_barrier((parts, sent, received))
-        counted, parts = relay_rest(parts, swapped, middle, sent, "head")
-    else:
-        counted, parts = jnp.ones((ways,), jnp.int32), scatter(parts, "head")
+        swapped, middle = relay_first(parts, "head")
+        sent = relay_sum(parts, swapped, "head")
+        cut = sent.shape[0] // 2
+        early, late = sent[:cut], sent[cut:]
+        kept, early, middle = lax.optimization_barrier((kept, early, middle))
+        early = relay_cross(early, "head")
     own_heads, other_heads = attend(depth, seq.reshape(1), twin_ids("seq"), global_scale, kept, received, pieces)
     update = project(core, slots[1], own_heads, swap_cores(other_heads, "seq"), global_out)
-    updates, parts = lax.optimization_barrier((scatter(update, "head"), parts))
+    updates = scatter(update, "head")
+    if line:
+        updates, early, parts, late = lax.optimization_barrier((updates, early, parts, late))
+        counted = relay_counted("head")
+        byte_pieces = [(parts[0],), (swapped,), (middle,), (relay_inward(parts, "head"),), (early, relay_cross(late, "head"))]
+    else:
+        counted = jnp.ones((ways,), jnp.int32)
+        byte_pieces = [(part,) for part in scatter(parts, "head")]
     result, routed = finish_result(owner_order(owners, seq, patches), residual, updates)
     global_state = lax.all_to_all(routed, "seq", split_axis=0, concat_axis=0, tiled=True)
-    byte_out = finish_bytes(counted, result, back_proj, parts)
+    byte_out = finish_bytes(counted, result, back_proj, byte_pieces)
     return byte_out.reshape(patches, own, width), global_state
 
 

time: 117 us -> 122 us (1.043)
  starting transfers between devices: 34.1 us -> 37.2 us
  local copies, waits for them, and re-layouts: 2.84 us -> 5.13 us
    ppermute x12, waiting for transfers between devices: 47.5 us -> 30.5 us  [shift(): lax.ppermute(value, axis, [(i, (i + step) % count) for i in range(count)])]
    ppermute x1, waiting for transfers between devices: 0.01 us -> 7.5 us  [relay_first(): swapped = lax.ppermute(chunks[1], axis, [(0, 1), (1, 0), (2, 3), (3, 2)])]
    ppermute x2 -> x3, waiting for transfers between devices: 0.01 us -> 6.53 us  [the longest x2 6.52 us: relay_cross(): return lax.ppermute(sent, axis, [(0, 2), (2, 0), (1, 3), (3, 1)])]
    all_to_all x1, waiting for transfers between devices: 1.54 us -> 5.45 us  [on_device(): lax.all_to_all(routed, 'seq', split_axis=0, concat_axis=0, tiled=True)]
    ppermute x2 -> x3, starting transfers between devices: 5.39 us -> 8.43 us  [the longest x1 5.04 us: relay_inward(): return lax.ppermute(chunks[2], axis, [(0, 1), (3, 2)])]
    unnamed x21, local copies, waits for them, and re-layouts: 1.74 us -> 3.27 us
  transfers between devices with their start and end apart: 19 -> 20, of which waited for: 12 -> 10; matrix products, arithmetic and copies ran while one was open for 1% -> 1% of each run, Pallas kernels for 6% -> 4%
where the time goes in v6:
time: 122 us; the launch traced here: 121 us
  waiting for transfers between devices  51.4 us (42%)
  starting transfers between devices  37.2 us (30%)
  Pallas kernels  25.5 us (21%)
  local copies, waits for them, and re-layouts  5.13 us (4%)
  other arithmetic  1.27 us (1%)
    ppermute x12, waiting for transfers between devices, shift(): lax.ppermute(value, axis, [(i, (i + step) % count) for i in range(count)])  30.5 us
    ppermute x12, starting transfers between devices, shift(): lax.ppermute(value, axis, [(i, (i + step) % count) for i in range(count)])  20.5 us
    pallas_call x1, Pallas kernels, local_part(): pl.pallas_call(functools.partial(local_kernel, span, piece, step), in_spe...  15.4 us
    ppermute x1, waiting for transfers between devices, relay_first(): swapped = lax.ppermute(chunks[1], axis, [(0, 1), (1, 0), (2, 3), (3, 2)])  7.5 us
    ppermute x2, waiting for transfers between devices, relay_cross(): return lax.ppermute(sent, axis, [(0, 2), (2, 0), (1, 3), (3, 1)])  6.52 us
    all_to_all x1, waiting for transfers between devices, on_device(): lax.all_to_all(routed, 'seq', split_axis=0, concat_axis=0, tiled=True)  5.45 us
    ppermute x1, starting transfers between devices, relay_inward(): return lax.ppermute(chunks[2], axis, [(0, 1), (3, 2)])  5.04 us
    all_to_all x1, starting transfers between devices, on_device(): lax.all_to_all(routed, 'seq', split_axis=0, concat_axis=0, tiled=True)  4 us
  transfers between devices with their start and end apart: 20, of which 10 were waited for; matrix products, arithmetic and copies ran while one was open for 1% of the time, Pallas kernels for 4%

profile of v6, /device:TPU:0, one launch (start us, length us, event | category | flops | bytes accessed | tf_op | source)
XLA Modules:
  0.0 121.4 jit_solution(8845536688282443654)
XLA Ops:
  1.3 15.4 %local_part.1 = (bf16[256,1024]{1,0:T(8,128)(2,1)}, bf16[256,1024]{1,0:T(8,128)(2,1)}, bf16[256,1024]{1,0:T(8,128)(2,1)}, bf16[256,1024]{1,0:T(8,128)(2,1)}, bf1...) custom-call(s32[1]{0:T(128)} %bitcast.4.me_ref, ...), custom_call_target="tpu_custom_call" | custom-call | tf_op jit(solution)/shard_map/local_part/pallas_call | solution.py:121
  16.8 3.1 %collective-permute-start = (bf16[128,512]{1,0:T(8,128)(2,1)S(1)}, bf16[128,512]{1,0:T(8,128)(2,1)S(1)}, u32[]{:S(2)}, u32[]{:S(2)}) collective-permute-start(bf16[128,512]{1,0:T(8,128)(2,1)S(1)} %get-tuple-element.39), channel_id=1, source_target_pairs={{0,1},{1,2},{2,3},{3,0},{4,5},{5,6},{6,7},{7,4},{8,9},{9,10},{10,1... | collective-permute-start | bytes 393224 | tf_op jit(solution)/shard_map/ppermute | solution.py:321
  19.8 2.6 %collective-permute-start.1 = (bf16[128,512]{1,0:T(8,128)(2,1)S(1)}, bf16[128,512]{1,0:T(8,128)(2,1)S(1)}, u32[]{:S(2)}, u32[]{:S(2)}) collective-permute-start(bf16[128,512]{1,0:T(8,128)(2,1)S(1)} %get-tuple-element.40), channel_id=1, source_target_pairs={{0,2},{1,3},{2,0},{3,1},{4,6},{5,7},{6,4},{7,5},{8,10},{9,11},{10,... | collective-permute-start | bytes 393224 | tf_op jit(solution)/shard_map/ppermute | solution.py:321
  22.4 1.3 %collective-permute-start.2 = (bf16[128,512]{1,0:T(8,128)(2,1)S(1)}, bf16[128,512]{1,0:T(8,128)(2,1)S(1)}, u32[]{:S(2)}, u32[]{:S(2)}) collective-permute-start(bf16[128,512]{1,0:T(8,128)(2,1)S(1)} %get-tuple-element.41), channel_id=1, source_target_pairs={{0,3},{1,0},{2,1},{3,2},{4,7},{5,4},{6,5},{7,6},{8,11},{9,8},{10,9... | collective-permute-start | bytes 393224 | tf_op jit(solution)/shard_map/ppermute | solution.py:321
  23.8 2.5 %collective-permute-done = bf16[128,512]{1,0:T(8,128)(2,1)S(1)} collective-permute-done((bf16[128,512]{1,0:T(8,128)(2,1)S(1)}, bf16[128,512]{1,0:T(8,128)(2,1)S(1)}, u32[]{:S(2)}, u32[]{:S(2)}) %collective-permute-start) | collective-permute-done | bytes 131104 | tf_op jit(solution)/shard_map/ppermute | solution.py:321
  26.3 4.8 %collective-permute-done.1 = bf16[128,512]{1,0:T(8,128)(2,1)S(1)} collective-permute-done((bf16[128,512]{1,0:T(8,128)(2,1)S(1)}, bf16[128,512]{1,0:T(8,128)(2,1)S(1)}, u32[]{:S(2)}, u32[]{:S(2)}) %collective-permute-start.1) | collective-permute-done | bytes 131104 | tf_op jit(solution)/shard_map/ppermute | solution.py:321
  31.2 3.3 %collective-permute-start.3 = (bf16[128,512]{1,0:T(8,128)(2,1)S(1)}, bf16[128,512]{1,0:T(8,128)(2,1)S(1)}, u32[]{:S(2)}, u32[]{:S(2)}) collective-permute-start(bf16[128,512]{1,0:T(8,128)(2,1)S(1)} %add_convert_fusion.1.refs_0_.own_ref), channel_id=1, source_target_pairs={{0,1},{1,2},{2,3},{3,0},{4,5},{5,6},{6,7},{7,4},{8,9},{9,10},{10,1... | collective-permute-start | bytes 393224 | tf_op jit(solution)/shard_map/ppermute | solution.py:321
  34.5 1.6 %collective-permute-start.4 = (bf16[128,512]{1,0:T(8,128)(2,1)S(1)}, bf16[128,512]{1,0:T(8,128)(2,1)S(1)}, u32[]{:S(2)}, u32[]{:S(2)}) collective-permute-start(bf16[128,512]{1,0:T(8,128)(2,1)S(1)} %add_convert_fusion.1.refs_0_.own_ref), channel_id=1, source_target_pairs={{0,2},{1,3},{2,0},{3,1},{4,6},{5,7},{6,4},{7,5},{8,10},{9,11},{10,... | collective-permute-start | bytes 393224 | tf_op jit(solution)/shard_map/ppermute | solution.py:321
  36.9 2.9 %fetch.1.refs_4_ = bf16[3,2048,512]{2,1,0:T(8,128)(2,1)S(1)} custom-call(bf16[3,2048,512]{2,1,0:T(8,128)(2,1)} %bitcast.20), custom_call_target="tpu_custom_call" | custom-call | tf_op jit(solution)/shard_map/fetch/pallas_call | solution.py:149
  39.9 4.4 %collective-permute-done.4.refs_2_ = bf16[128,512]{1,0:T(8,128)(2,1)S(1)} collective-permute-done((bf16[128,512]{1,0:T(8,128)(2,1)S(1)}, bf16[128,512]{1,0:T(8,128)(2,1)S(1)}, u32[]{:S(2)}, u32[]{:S(2)}) %collective-permute-start.4) | collective-permute-done | bytes 131104 | tf_op jit(solution)/shard_map/ppermute | solution.py:321
  44.2 1.7 %global_heads.1 = (bf16[128,768]{1,0:T(8,128)(2,1)S(1)}, bf16[128,768]{1,0:T(8,128)(2,1)S(1)}) custom-call(s32[1]{0:T(128)} %bitcast.12.core_ref, s32[4]{0:T(128)S(1)} %and_select_fusion.ids_ref, f32[4,1,512]{2,1,0:T(1,128)S(1)} %bitcast.19, bf16[128,512]{1,0:T(8,128)(2,1)S(1)} %add_convert_fusion.1.refs_0_.own_ref, ...), custom_call_target="tpu_custom_call" | custom-call | tf_op jit(solution)/shard_map/global_heads/pallas_call | solution.py:183
  46.0 1.4 %collective-permute-done.6.given_ref = bf16[128,768]{1,0:T(8,128)(2,1)S(1)} collective-permute-done((bf16[128,768]{1,0:T(8,128)(2,1)S(1)}, bf16[128,768]{1,0:T(8,128)(2,1)S(1)}, u32[]{:S(2)}, u32[]{:S(2)}) %collective-permute-start.6) | collective-permute-done | bytes 196640 | tf_op jit(solution)/shard_map/ppermute | solution.py:371
  47.5 3.3 %collective-permute-start.7 = (bf16[256,1024]{1,0:T(8,128)(2,1)S(1)}, bf16[256,1024]{1,0:T(8,128)(2,1)S(1)}, u32[]{:S(2)}, u32[]{:S(2)}) collective-permute-start(bf16[256,1024]{1,0:T(8,128)(2,1)S(1)} %copy-done.9), channel_id=1, source_target_pairs={{0,1},{1,0},{2,3},{3,2},{4,5},{5,4},{6,7},{7,6},{8,9},{9,8},{10,11... | collective-permute-start | bytes 1572872 | tf_op jit(solution)/shard_map/ppermute | solution.py:341
  51.9 1.6 %collective-permute-start.10 = (bf16[256,512]{1,0:T(8,128)(2,1)S(1)}, bf16[256,512]{1,0:T(8,128)(2,1)S(1)}, u32[]{:S(2)}, u32[]{:S(2)}) collective-permute-start(bf16[256,512]{1,0:T(8,128)(2,1)S(1)} %pad_maximum_fusion), channel_id=1, source_target_pairs={{0,16},{4,20},{8,24},{12,28},{16,0},{20,4},{24,8},{28,12},{1,17},{... | collective-permute-start | bytes 786440 | tf_op jit(solution)/shard_map/ppermute | solution.py:321
  53.4 1.4 %collective-permute-start.11 = (bf16[256,512]{1,0:T(8,128)(2,1)S(1)}, bf16[256,512]{1,0:T(8,128)(2,1)S(1)}, u32[]{:S(2)}, u32[]{:S(2)}) collective-permute-start(bf16[256,512]{1,0:T(8,128)(2,1)S(1)} %pad_maximum_fusion), channel_id=1, source_target_pairs={{0,24},{4,28},{8,0},{12,4},{16,8},{20,12},{24,16},{28,20},{1,25},{... | collective-permute-start | bytes 786440 | tf_op jit(solution)/shard_map/ppermute | solution.py:321
  55.5 7.5 %collective-permute-done.7.refs_1_ = bf16[256,1024]{1,0:T(8,128)(2,1)S(1)} collective-permute-done((bf16[256,1024]{1,0:T(8,128)(2,1)S(1)}, bf16[256,1024]{1,0:T(8,128)(2,1)S(1)}, u32[]{:S(2)}, u32[]{:S(2)}) %collective-permute-start.7) | collective-permute-done | bytes 524320 | tf_op jit(solution)/shard_map/ppermute | solution.py:341
  63.9 2.9 %collective-permute-done.9.refs_0_ = bf16[256,512]{1,0:T(8,128)(2,1)S(1)} collective-permute-done((bf16[256,512]{1,0:T(8,128)(2,1)S(1)}, bf16[256,512]{1,0:T(8,128)(2,1)S(1)}, u32[]{:S(2)}, u32[]{:S(2)}) %collective-permute-start.9) | collective-permute-done | bytes 262176 | tf_op jit(solution)/shard_map/ppermute | solution.py:321
  66.8 1.7 %attend.1 = (bf16[128,256]{1,0:T(8,128)(2,1)S(1)}, bf16[128,256]{1,0:T(8,128)(2,1)S(1)}) custom-call(s32[1]{0:T(128)} %bitcast.13.me_ref, s32[4]{0:T(128)S(1)} %and_select_fusion.1.ids_ref, f32[4]{0:T(128)S(1)} %copy-done.7, bf16[128,768]{1,0:T(8,128)(2,1)S(1)} %get-tuple-element.53.kept_ref, bf16[128,768]{1,0:T(8,128)(2,1)S(1)} %collective-permute-done.6.given_ref, ...), custom_call_target="tpu_custom_call" | custom-call | tf_op jit(solution)/shard_map/attend/pallas_call | solution.py:226
  68.6 3.3 %collective-permute-start.16 = (bf16[128,1024]{1,0:T(8,128)(2,1)S(1)}, bf16[128,1024]{1,0:T(8,128)(2,1)S(1)}, u32[]{:S(2)}, u32[]{:S(2)}) collective-permute-start(bf16[128,1024]{1,0:T(8,128)(2,1)S(1)} %get-tuple-element.61), channel_id=1, source_target_pairs={{0,2},{2,0},{1,3},{3,1},{4,6},{6,4},{5,7},{7,5},{8,10},{10,8},{9,1... | collective-permute-start | bytes 786440 | tf_op jit(solution)/shard_map/ppermute | solution.py:357
  71.9 1.0 project.1
  72.9 1.5 %collective-permute-start.13 = (bf16[128,512]{1,0:T(8,128)(2,1)S(1)}, bf16[128,512]{1,0:T(8,128)(2,1)S(1)}, u32[]{:S(2)}, u32[]{:S(2)}) collective-permute-start(bf16[128,512]{1,0:T(8,128)(2,1)S(1)} %get-tuple-element.58), channel_id=1, source_target_pairs={{0,1},{1,2},{2,3},{3,0},{4,5},{5,6},{6,7},{7,4},{8,9},{9,10},{10,1... | collective-permute-start | bytes 393224 | tf_op jit(solution)/shard_map/ppermute | solution.py:321
  74.4 1.8 %collective-permute-start.14 = (bf16[128,512]{1,0:T(8,128)(2,1)S(1)}, bf16[128,512]{1,0:T(8,128)(2,1)S(1)}, u32[]{:S(2)}, u32[]{:S(2)}) collective-permute-start(bf16[128,512]{1,0:T(8,128)(2,1)S(1)} %get-tuple-element.59), channel_id=1, source_target_pairs={{0,2},{1,3},{2,0},{3,1},{4,6},{5,7},{6,4},{7,5},{8,10},{9,11},{10,... | collective-permute-start | bytes 393224 | tf_op jit(solution)/shard_map/ppermute | solution.py:321
  77.2 7.4 %collective-permute-done.13.refs_1_ = bf16[128,512]{1,0:T(8,128)(2,1)S(1)} collective-permute-done((bf16[128,512]{1,0:T(8,128)(2,1)S(1)}, bf16[128,512]{1,0:T(8,128)(2,1)S(1)}, u32[]{:S(2)}, u32[]{:S(2)}) %collective-permute-start.13) | collective-permute-done | bytes 131104 | tf_op jit(solution)/shard_map/ppermute | solution.py:321
  84.6 8.6 %collective-permute-done.14.refs_2_ = bf16[128,512]{1,0:T(8,128)(2,1)S(1)} collective-permute-done((bf16[128,512]{1,0:T(8,128)(2,1)S(1)}, bf16[128,512]{1,0:T(8,128)(2,1)S(1)}, u32[]{:S(2)}, u32[]{:S(2)}) %collective-permute-start.14) | collective-permute-done | bytes 131104 | tf_op jit(solution)/shard_map/ppermute | solution.py:321
  93.1 5.0 %collective-permute-start.17 = (bf16[256,1024]{1,0:T(8,128)(2,1)}, bf16[256,1024]{1,0:T(8,128)(2,1)S(1)}, u32[]{:S(2)}, u32[]{:S(2)}) collective-permute-start(bf16[256,1024]{1,0:T(8,128)(2,1)} %get-tuple-element.70), channel_id=1, source_target_pairs={{0,1},{3,2},{4,5},{7,6},{8,9},{11,10},{12,13},{15,14},{16,17},{19,... | collective-permute-start | bytes 1572872 | tf_op jit(solution)/shard_map/ppermute | solution.py:353
  99.2 4.0 %all-to-all-start = ((bf16[8,16,512]{2,1,0:T(8,128)(2,1)}), bf16[8,16,512]{2,1,0:T(8,128)(2,1)}, u32[]{:S(2)}, u32[]{:S(2)}) async-start(bf16[8,16,512]{2,1,0:T(8,128)(2,1)} %bitcast.15), calls=%async_computation | async-start | bytes 262144 | tf_op jit(solution)/shard_map/all_to_all | solution.py:461
  103.3 5.4 %all-to-all-done = bf16[8,16,512]{2,1,0:T(8,128)(2,1)} async-done(((bf16[8,16,512]{2,1,0:T(8,128)(2,1)}), bf16[8,16,512]{2,1,0:T(8,128)(2,1)}, u32[]{:S(2)}, u32[]{:S(2)}) %all-to-all-start) | async-done | bytes 131104 | tf_op jit(solution)/shard_map/all_to_all | solution.py:461
  108.7 6.5 %collective-permute-done.18.refs_5_ = bf16[128,1024]{1,0:T(8,128)(2,1)S(1)} collective-permute-done((bf16[128,1024]{1,0:T(8,128)(2,1)}, bf16[128,1024]{1,0:T(8,128)(2,1)S(1)}, u32[]{:S(2)}, u32[]{:S(2)}) %collective-permute-start.18) | collective-permute-done | bytes 262176 | tf_op jit(solution)/shard_map/ppermute | solution.py:357
  116.0 0.9 copy-done.5
  116.9 1.9 %finish_bytes.1 = bf16[256,1024]{1,0:T(8,128)(2,1)S(1)} custom-call(s32[5]{0:T(128)S(1)} %stack.32.counted_ref, bf16[128,512]{1,0:T(8,128)(2,1)S(1)} %get-tuple-element.67.result_ref, bf16[256,1024]{1,0:T(8,128)(2,1)S(1)} %copy-done.2, bf16[256,1024]{1,0:T(8,128)(2,1)S(1)} %copy-done.3, bf16[256,1024]{1,0:T(8,128)(2,1)S(1)} %collective-permute-done.7.refs_1_, ...), custom_call_target="tpu_custom_call" | custom-call | tf_op jit(solution)/shard_map/finish_bytes/pallas_call | solution.py:308
  118.8 1.0 reshape.126
  119.8 1.6 %copy.17 = bf16[128,512]{1,0:T(8,128)(2,1)} copy(bf16[128,512]{1,0:T(8,128)(2,1)} %bitcast.16) | data formatting | bytes 262144
  (56 shorter events, 7.1 us)
Async XLA Ops:
  0.6 50.1 %copy-start = (s32[8,16]{1,0:T(8,128)S(1)}, s32[8,16]{1,0:T(8,128)}, u32[]{:S(2)}) copy-start(s32[8,16]{1,0:T(8,128)} %param.27) | copy-start | bytes 1540
  16.8 9.5 %collective-permute-start = (bf16[128,512]{1,0:T(8,128)(2,1)S(1)}, bf16[128,512]{1,0:T(8,128)(2,1)S(1)}, u32[]{:S(2)}, u32[]{:S(2)}) collective-permute-start(bf16[128,512]{1,0:T(8,128)(2,1)S(1)} %get-tuple-element.39), channel_id=1, source_target_pairs={{0,1},{1,2},{2,3},{3,0},{4,5},{5,6},{6,7},{7,4},{8,9},{9,10},{10,1... | collective-permute-start | bytes 393224 | tf_op jit(solution)/shard_map/ppermute | solution.py:321
  19.8 11.2 %collective-permute-start.1 = (bf16[128,512]{1,0:T(8,128)(2,1)S(1)}, bf16[128,512]{1,0:T(8,128)(2,1)S(1)}, u32[]{:S(2)}, u32[]{:S(2)}) collective-permute-start(bf16[128,512]{1,0:T(8,128)(2,1)S(1)} %get-tuple-element.40), channel_id=1, source_target_pairs={{0,2},{1,3},{2,0},{3,1},{4,6},{5,7},{6,4},{7,5},{8,10},{9,11},{10,... | collective-permute-start | bytes 393224 | tf_op jit(solution)/shard_map/ppermute | solution.py:321
  22.4 8.6 %collective-permute-start.2 = (bf16[128,512]{1,0:T(8,128)(2,1)S(1)}, bf16[128,512]{1,0:T(8,128)(2,1)S(1)}, u32[]{:S(2)}, u32[]{:S(2)}) collective-permute-start(bf16[128,512]{1,0:T(8,128)(2,1)S(1)} %get-tuple-element.41), channel_id=1, source_target_pairs={{0,3},{1,0},{2,1},{3,2},{4,7},{5,4},{6,5},{7,6},{8,11},{9,8},{10,9... | collective-permute-start | bytes 393224 | tf_op jit(solution)/shard_map/ppermute | solution.py:321
  31.2 8.7 %collective-permute-start.3 = (bf16[128,512]{1,0:T(8,128)(2,1)S(1)}, bf16[128,512]{1,0:T(8,128)(2,1)S(1)}, u32[]{:S(2)}, u32[]{:S(2)}) collective-permute-start(bf16[128,512]{1,0:T(8,128)(2,1)S(1)} %add_convert_fusion.1.refs_0_.own_ref), channel_id=1, source_target_pairs={{0,1},{1,2},{2,3},{3,0},{4,5},{5,6},{6,7},{7,4},{8,9},{9,10},{10,1... | collective-permute-start | bytes 393224 | tf_op jit(solution)/shard_map/ppermute | solution.py:321
  34.5 9.7 %collective-permute-start.4 = (bf16[128,512]{1,0:T(8,128)(2,1)S(1)}, bf16[128,512]{1,0:T(8,128)(2,1)S(1)}, u32[]{:S(2)}, u32[]{:S(2)}) collective-permute-start(bf16[128,512]{1,0:T(8,128)(2,1)S(1)} %add_convert_fusion.1.refs_0_.own_ref), channel_id=1, source_target_pairs={{0,2},{1,3},{2,0},{3,1},{4,6},{5,7},{6,4},{7,5},{8,10},{9,11},{10,... | collective-permute-start | bytes 393224 | tf_op jit(solution)/shard_map/ppermute | solution.py:321
  36.1 8.1 %collective-permute-start.5 = (bf16[128,512]{1,0:T(8,128)(2,1)S(1)}, bf16[128,512]{1,0:T(8,128)(2,1)S(1)}, u32[]{:S(2)}, u32[]{:S(2)}) collective-permute-start(bf16[128,512]{1,0:T(8,128)(2,1)S(1)} %add_convert_fusion.1.refs_0_.own_ref), channel_id=1, source_target_pairs={{0,3},{1,0},{2,1},{3,2},{4,7},{5,4},{6,5},{7,6},{8,11},{9,8},{10,9... | collective-permute-start | bytes 393224 | tf_op jit(solution)/shard_map/ppermute | solution.py:321
  36.9 7.3 %copy-start.6 = (f32[2048]{0:T(1024)S(1)}, f32[2048]{0:T(1024)}, u32[]{:S(2)}) copy-start(f32[2048]{0:T(1024)} %param.22) | copy-start | bytes 24580
  44.2 3.2 %copy-start.9 = (bf16[256,1024]{1,0:T(8,128)(2,1)S(1)}, bf16[256,1024]{1,0:T(8,128)(2,1)}, u32[]{:S(2)}) copy-start(bf16[256,1024]{1,0:T(8,128)(2,1)} %get-tuple-element.51) | copy-start | bytes 1572868
  44.2 18.7 %copy-start.8 = (bf16[256,1024]{1,0:T(8,128)(2,1)S(1)}, bf16[256,1024]{1,0:T(8,128)(2,1)}, u32[]{:S(2)}) copy-start(bf16[256,1024]{1,0:T(8,128)(2,1)} %get-tuple-element.50) | copy-start | bytes 1572868
  45.9 20.9 %copy-start.7 = (f32[4]{0:T(128)S(1)}, f32[4]{0:T(128)}, u32[]{:S(2)}) copy-start(f32[4]{0:T(128)} %scale_ref.3) | copy-start | bytes 52
  45.9 1.5 %collective-permute-start.6 = (bf16[128,768]{1,0:T(8,128)(2,1)S(1)}, bf16[128,768]{1,0:T(8,128)(2,1)S(1)}, u32[]{:S(2)}, u32[]{:S(2)}) collective-permute-start(bf16[128,768]{1,0:T(8,128)(2,1)S(1)} %get-tuple-element.49), channel_id=1, source_target_pairs={{0,4},{4,0},{8,12},{12,8},{16,20},{20,16},{24,28},{28,24},{1,5},{5... | collective-permute-start | bytes 589832 | tf_op jit(solution)/shard_map/ppermute | solution.py:371
  47.5 15.5 %collective-permute-start.7 = (bf16[256,1024]{1,0:T(8,128)(2,1)S(1)}, bf16[256,1024]{1,0:T(8,128)(2,1)S(1)}, u32[]{:S(2)}, u32[]{:S(2)}) collective-permute-start(bf16[256,1024]{1,0:T(8,128)(2,1)S(1)} %copy-done.9), channel_id=1, source_target_pairs={{0,1},{1,0},{2,3},{3,2},{4,5},{5,4},{6,7},{7,6},{8,9},{9,8},{10,11... | collective-permute-start | bytes 1572872 | tf_op jit(solution)/shard_map/ppermute | solution.py:341
  51.0 21.0 %copy-start.1 = (bf16[512,2048]{1,0:T(8,128)(2,1)S(1)}, bf16[512,2048]{1,0:T(8,128)(2,1)}, u32[]{:S(2)}) copy-start(bf16[512,2048]{1,0:T(8,128)(2,1)} %proj_ref.2) | copy-start | bytes 6291460
  51.0 12.9 %collective-permute-start.8 = (bf16[256,1024]{1,0:T(8,128)(2,1)}, bf16[256,1024]{1,0:T(8,128)(2,1)S(1)}, u32[]{:S(2)}, u32[]{:S(2)}) collective-permute-start(bf16[256,1024]{1,0:T(8,128)(2,1)} %get-tuple-element.70), channel_id=1, source_target_pairs={{1,2},{2,1},{5,6},{6,5},{9,10},{10,9},{13,14},{14,13},{17,18},{18,... | collective-permute-start | bytes 1572872 | tf_op jit(solution)/shard_map/ppermute | solution.py:342
  51.9 12.1 %collective-permute-start.10 = (bf16[256,512]{1,0:T(8,128)(2,1)S(1)}, bf16[256,512]{1,0:T(8,128)(2,1)S(1)}, u32[]{:S(2)}, u32[]{:S(2)}) collective-permute-start(bf16[256,512]{1,0:T(8,128)(2,1)S(1)} %pad_maximum_fusion), channel_id=1, source_target_pairs={{0,16},{4,20},{8,24},{12,28},{16,0},{20,4},{24,8},{28,12},{1,17},{... | collective-permute-start | bytes 786440 | tf_op jit(solution)/shard_map/ppermute | solution.py:321
  53.4 10.5 %collective-permute-start.11 = (bf16[256,512]{1,0:T(8,128)(2,1)S(1)}, bf16[256,512]{1,0:T(8,128)(2,1)S(1)}, u32[]{:S(2)}, u32[]{:S(2)}) collective-permute-start(bf16[256,512]{1,0:T(8,128)(2,1)S(1)} %pad_maximum_fusion), channel_id=1, source_target_pairs={{0,24},{4,28},{8,0},{12,4},{16,8},{20,12},{24,16},{28,20},{1,25},{... | collective-permute-start | bytes 786440 | tf_op jit(solution)/shard_map/ppermute | solution.py:321
  54.9 11.9 %collective-permute-start.9 = (bf16[256,512]{1,0:T(8,128)(2,1)S(1)}, bf16[256,512]{1,0:T(8,128)(2,1)S(1)}, u32[]{:S(2)}, u32[]{:S(2)}) collective-permute-start(bf16[256,512]{1,0:T(8,128)(2,1)S(1)} %pad_maximum_fusion), channel_id=1, source_target_pairs={{0,8},{4,12},{8,16},{12,20},{16,24},{20,28},{24,0},{28,4},{1,9},{5... | collective-permute-start | bytes 786440 | tf_op jit(solution)/shard_map/ppermute | solution.py:321
  66.8 49.2 %copy-start.2 = (bf16[256,1024]{1,0:T(8,128)(2,1)S(1)}, bf16[256,1024]{1,0:T(8,128)(2,1)}, u32[]{:S(2)}) copy-start(bf16[256,1024]{1,0:T(8,128)(2,1)} %proj_ref.3) | copy-start | bytes 1572868
  66.8 49.2 %copy-start.3 = (bf16[256,1024]{1,0:T(8,128)(2,1)S(1)}, bf16[256,1024]{1,0:T(8,128)(2,1)}, u32[]{:S(2)}) copy-start(bf16[256,1024]{1,0:T(8,128)(2,1)} %get-tuple-element.68.refs_0_) | copy-start | bytes 1572868
  68.5 3.4 %collective-permute-start.12 = (bf16[128,256]{1,0:T(8,128)(2,1)S(1)}, bf16[128,256]{1,0:T(8,128)(2,1)S(1)}, u32[]{:S(2)}, u32[]{:S(2)}) collective-permute-start(bf16[128,256]{1,0:T(8,128)(2,1)S(1)} %get-tuple-element.56), channel_id=1, source_target_pairs={{0,4},{4,0},{8,12},{12,8},{16,20},{20,16},{24,28},{28,24},{1,5},{5... | collective-permute-start | bytes 196616 | tf_op jit(solution)/shard_map/ppermute | solution.py:371
  68.6 24.5 %collective-permute-start.16 = (bf16[128,1024]{1,0:T(8,128)(2,1)S(1)}, bf16[128,1024]{1,0:T(8,128)(2,1)S(1)}, u32[]{:S(2)}, u32[]{:S(2)}) collective-permute-start(bf16[128,1024]{1,0:T(8,128)(2,1)S(1)} %get-tuple-element.61), channel_id=1, source_target_pairs={{0,2},{2,0},{1,3},{3,1},{4,6},{6,4},{5,7},{7,5},{8,10},{10,8},{9,1... | collective-permute-start | bytes 786440 | tf_op jit(solution)/shard_map/ppermute | solution.py:357
  72.9 11.6 %collective-permute-start.13 = (bf16[128,512]{1,0:T(8,128)(2,1)S(1)}, bf16[128,512]{1,0:T(8,128)(2,1)S(1)}, u32[]{:S(2)}, u32[]{:S(2)}) collective-permute-start(bf16[128,512]{1,0:T(8,128)(2,1)S(1)} %get-tuple-element.58), channel_id=1, source_target_pairs={{0,1},{1,2},{2,3},{3,0},{4,5},{5,6},{6,7},{7,4},{8,9},{9,10},{10,1... | collective-permute-start | bytes 393224 | tf_op jit(solution)/shard_map/ppermute | solution.py:321
  74.4 18.7 %collective-permute-start.14 = (bf16[128,512]{1,0:T(8,128)(2,1)S(1)}, bf16[128,512]{1,0:T(8,128)(2,1)S(1)}, u32[]{:S(2)}, u32[]{:S(2)}) collective-permute-start(bf16[128,512]{1,0:T(8,128)(2,1)S(1)} %get-tuple-element.59), channel_id=1, source_target_pairs={{0,2},{1,3},{2,0},{3,1},{4,6},{5,7},{6,4},{7,5},{8,10},{9,11},{10,... | collective-permute-start | bytes 393224 | tf_op jit(solution)/shard_map/ppermute | solution.py:321
  76.2 16.9 %collective-permute-start.15 = (bf16[128,512]{1,0:T(8,128)(2,1)S(1)}, bf16[128,512]{1,0:T(8,128)(2,1)S(1)}, u32[]{:S(2)}, u32[]{:S(2)}) collective-permute-start(bf16[128,512]{1,0:T(8,128)(2,1)S(1)} %get-tuple-element.60), channel_id=1, source_target_pairs={{0,3},{1,0},{2,1},{3,2},{4,7},{5,4},{6,5},{7,6},{8,11},{9,8},{10,9... | collective-permute-start | bytes 393224 | tf_op jit(solution)/shard_map/ppermute | solution.py:321
  93.1 22.8 %collective-permute-start.17 = (bf16[256,1024]{1,0:T(8,128)(2,1)}, bf16[256,1024]{1,0:T(8,128)(2,1)S(1)}, u32[]{:S(2)}, u32[]{:S(2)}) collective-permute-start(bf16[256,1024]{1,0:T(8,128)(2,1)} %get-tuple-element.70), channel_id=1, source_target_pairs={{0,1},{3,2},{4,5},{7,6},{8,9},{11,10},{12,13},{15,14},{16,17},{19,... | collective-permute-start | bytes 1572872 | tf_op jit(solution)/shard_map/ppermute | solution.py:353
  98.2 17.1 %collective-permute-start.18 = (bf16[128,1024]{1,0:T(8,128)(2,1)}, bf16[128,1024]{1,0:T(8,128)(2,1)S(1)}, u32[]{:S(2)}, u32[]{:S(2)}) collective-permute-start(bf16[128,1024]{1,0:T(8,128)(2,1)} %get-tuple-element.72), channel_id=1, source_target_pairs={{0,2},{2,0},{1,3},{3,1},{4,6},{6,4},{5,7},{7,5},{8,10},{10,8},{9,1... | collective-permute-start | bytes 786440 | tf_op jit(solution)/shard_map/ppermute | solution.py:357
  99.2 9.5 %all-to-all-start = ((bf16[8,16,512]{2,1,0:T(8,128)(2,1)}), bf16[8,16,512]{2,1,0:T(8,128)(2,1)}, u32[]{:S(2)}, u32[]{:S(2)}) async-start(bf16[8,16,512]{2,1,0:T(8,128)(2,1)} %bitcast.15), calls=%async_computation | async-start | bytes 262144 | tf_op jit(solution)/shard_map/all_to_all | solution.py:461
  115.3 0.7 copy-start.4
  116.0 1.0 copy-start.5

commit v7 on v5

--- a/solution.py
+++ b/solution.py
@@ -12,6 +12,7 @@
 NEGATIVE = -1e30
 F32 = jnp.float32
 BF16 = jnp.bfloat16
+BRIEF = pl.CostEstimate(flops=1, bytes_accessed=1, transcendentals=0)
 VMEM = pl.BlockSpec(memory_space=pltpu.VMEM)
 HBM = pl.BlockSpec(memory_space=pltpu.HBM)
 SMEM = pl.BlockSpec(memory_space=pltpu.SMEM)
@@ -35,7 +36,7 @@
 
 
 def local_kernel(span, piece, step, me_ref, scale_ref, slots_ref, gain_ref, x_hbm, *refs):
-    ways = slots_ref.shape[1]
+    ways = slots_ref.shape[0]
     sources, parts, shares = refs[:5], refs[5 : 5 + ways], refs[5 + ways : 5 + 2 * ways]
     x_ref, part_ref, share_ref = refs[5 + 2 * ways : 8 + 2 * ways]
     held, (in_sem, x_sem, part_sem) = refs[8 + 2 * ways : 13 + 2 * ways], refs[13 + 2 * ways :]
@@ -92,7 +93,7 @@
                 put = (b % own) * patches + i * piece
                 part_ref[b // own, put : put + piece, columns] = partial[cut][b * piece : (b + 1) * piece]
         for slot, part in enumerate(parts):
-            source = part_ref.at[slots_ref[0, slot], :, pl.ds(c, step)]
+            source = part_ref.at[slots_ref[slot], :, pl.ds(c, step)]
             stores.append(pltpu.make_async_copy(source, part.at[:, pl.ds(c, step)], part_sem.at[len(stores)]))
             stores[-1].start()
         share += dot(partial, proj_ref[columns])
@@ -103,7 +104,7 @@
             put = slice((b % own) * size, (b % own + 1) * size)
             share_ref[b // own, i * piece : (i + 1) * piece, put] = share[cut][b * piece : (b + 1) * piece]
     for slot, out in enumerate(shares):
-        out[...] = share_ref[slots_ref[1, slot]]
+        out[...] = share_ref[slots_ref[slot]]
     for copy in stores:
         copy.wait()
 
@@ -111,7 +112,7 @@
 def local_part(me, scale, slots, x, gain, qkv, out, up, down, proj, span):
     rows, width = x.shape
     patches = rows // span
-    ways = slots.shape[1]
+    ways = slots.shape[0]
     own = span // ways
     weights = (qkv, up, out, down, proj)
     piece = math.gcd(patches, 32)
@@ -229,6 +230,7 @@
         out_specs=(VMEM, VMEM),
         out_shape=(shape, shape),
         compiler_params=pltpu.CompilerParams(vmem_limit_bytes=20 * 2**20),
+        cost_estimate=BRIEF,
         name="attend",
     )(me, ids, scale, kept, given, *pieces)
 
@@ -251,6 +253,7 @@
         out_specs=[VMEM] * ways,
         out_shape=[jax.ShapeDtypeStruct((own.shape[0], proj.shape[1] // ways), BF16)] * ways,
         compiler_params=pltpu.CompilerParams(vmem_limit_bytes=6 * 2**20),
+        cost_estimate=BRIEF,
         name="project",
     )(core, slots, own, other, proj)
 
@@ -271,12 +274,13 @@
         out_specs=(VMEM, VMEM),
         out_shape=(shape, shape),
         compiler_params=pltpu.CompilerParams(vmem_limit_bytes=4 * 2**20),
+        cost_estimate=BRIEF,
         name="finish_result",
     )(order, residual, *pieces)
 
 
-def bytes_kernel(count, counted_ref, result_ref, proj_ref, *refs):
-    sources, out_ref, held, sems = refs[:count], refs[count], refs[count + 1], refs[count + 2]
+def bytes_kernel(count, result_ref, proj_ref, *refs):
+    sources, (out_ref, held, sems) = refs[:count], refs[count:]
     copies = [pltpu.make_async_copy(p, held.at[i], sems.at[i]) for i, p in enumerate(sources)]
     for copy in copies:
         copy.start()
@@ -289,24 +293,22 @@
     order = (to == (at % own) * rows + at // own).astype(F32).astype(BF16)
     for copy in copies:
         copy.wait()
-    state = held[0].astype(F32)
-    for i in range(1, count):
-        state += jnp.where(counted_ref[i] != 0, held[i].astype(F32), 0.0)
-    state = state.astype(BF16).astype(F32)
+    state = sum(held[i].astype(F32) for i in range(count)).astype(BF16).astype(F32)
     out_ref[...] = dot(order, (state + back).astype(BF16)).astype(BF16)
 
 
-def finish_bytes(counted, result, proj, pieces):
+def finish_bytes(result, proj, pieces):
     shape = pieces[0].shape
     return pl.pallas_call(
         functools.partial(bytes_kernel, len(pieces)),
-        in_specs=[SMEM, VMEM, VMEM] + [pl.BlockSpec(memory_space=pl.ANY)] * len(pieces),
+        in_specs=[VMEM, VMEM] + [pl.BlockSpec(memory_space=pl.ANY)] * len(pieces),
         out_specs=VMEM,
         out_shape=jax.ShapeDtypeStruct(shape, BF16),
         scratch_shapes=[pltpu.VMEM((len(pieces), *shape), BF16), pltpu.SemaphoreType.DMA((len(pieces),))],
         compiler_params=pltpu.CompilerParams(vmem_limit_bytes=16 * 2**20),
+        cost_estimate=BRIEF,
         name="finish_bytes",
-    )(counted, result, proj, *pieces)
+    )(result, proj, *pieces)
 
 
 def shift(value, axis, step):
@@ -321,33 +323,6 @@
 def shift_slots(axis):
     count = lax.axis_size(axis)
     return ((lax.axis_index(axis) + jnp.arange(count)) % count).astype(jnp.int32)
-
-
-def relay_slots(axis):
-    me = lax.axis_index(axis)
-    outer = (me == 0) | (me == 3)
-    beside, across = me ^ 1, 3 - me
-    return jnp.stack([me, jnp.where(outer, across, beside), jnp.where(outer, beside, across), me ^ 2]).astype(jnp.int32)
-
-
-def relay_first(chunks, axis):
-    swapped = lax.ppermute(chunks[1], axis, [(0, 1), (1, 0), (2, 3), (3, 2)])
-    middle = lax.ppermute(chunks[2], axis, [(1, 2), (2, 1)])
-    return swapped, middle
-
-
-def relay_sum(chunks, swapped, axis):
-    me = lax.axis_index(axis)
-    relayed = jnp.where((me == 0) | (me == 3), 0.0, swapped.astype(F32))
-    return (chunks[3].astype(F32) + relayed).astype(BF16)
-
-
-def relay_rest(chunks, swapped, middle, sent, axis):
-    inward = lax.ppermute(chunks[2], axis, [(0, 1), (3, 2)])
-    crossed = lax.ppermute(sent, axis, [(0, 2), (2, 0), (1, 3), (3, 1)])
-    me = lax.axis_index(axis)
-    outer = ((me == 0) | (me == 3)).astype(jnp.int32)
-    return jnp.stack([1 + 0 * outer, outer, 1 - outer, 1 - outer, 1 + 0 * outer]), [chunks[0], swapped, middle, inward, crossed]
 
 
 def gather(value, axis):
@@ -401,8 +376,7 @@
     seq = lax.axis_index("seq").astype(jnp.int32)
     depth = global_qkv.shape[2] // global_scale.shape[0]
 
-    line = ways == 4
-    slots = jnp.stack([relay_slots("head") if line else shift_slots("head"), shift_slots("head")])
+    slots = shift_slots("head")
     parts, chunks = local_part(
         me.reshape(1),
         local_scale,
@@ -416,32 +390,25 @@
         patch_proj,
         span,
     )
-    chunks = scatter(chunks, "head")
-    if line:
-        swapped, middle = relay_first(parts, "head")
-        chunks, swapped, middle = lax.optimization_barrier((chunks, swapped, middle))
-        sent = relay_sum(parts, swapped, "head")
-    residual = sum(p.astype(F32) for p in chunks).astype(BF16)
+    residual = sum(p.astype(F32) for p in scatter(chunks, "head")).astype(BF16)
     weight, residual = lax.optimization_barrier((jnp.transpose(global_qkv, (1, 0, 2)), residual))
     shares = gather(residual, "head")
     ids = (me - jnp.arange(ways, dtype=jnp.int32)) % ways
     core = (seq % 2).reshape(1)
     kept, given = global_heads(depth, core, ids, global_gain.reshape(ways, 1, -1), shares, fetch(weight))
     received = swap_cores(given, "seq")
+    parts, received = lax.optimization_barrier((parts, received))
     half = kept.shape[1] // 3
     keyed = jnp.concatenate([kept[:, half:], received[:, half:]], axis=0)
     pieces = [shift(keyed, "seq", 2 * step) for step in range(1, lax.axis_size("seq") // 2)]
-    if line:
-        parts, sent, received = lax.optimization_barrier((parts, sent, received))
-        counted, parts = relay_rest(parts, swapped, middle, sent, "head")
-    else:
-        counted, parts = jnp.ones((ways,), jnp.int32), scatter(parts, "head")
+    parts = scatter(parts, "head")
     own_heads, other_heads = attend(depth, seq.reshape(1), twin_ids("seq"), global_scale, kept, received, pieces)
-    update = project(core, slots[1], own_heads, swap_cores(other_heads, "seq"), global_out)
-    updates, parts = lax.optimization_barrier((scatter(update, "head"), parts))
+    other_heads, parts[1] = lax.optimization_barrier((swap_cores(other_heads, "seq"), parts[1]))
+    updates = scatter(project(core, slots, own_heads, other_heads, global_out), "head")
+    updates, parts[2] = lax.optimization_barrier((updates, parts[2]))
     result, routed = finish_result(owner_order(owners, seq, patches), residual, updates)
     global_state = lax.all_to_all(routed, "seq", split_axis=0, concat_axis=0, tiled=True)
-    byte_out = finish_bytes(counted, result, back_proj, parts)
+    byte_out = finish_bytes(result, back_proj, parts)
     return byte_out.reshape(patches, own, width), global_state
 
 

time: 117 us -> 121 us (1.034)
  starting transfers between devices: 34.1 us -> 54.6 us
  waiting for transfers between devices: 51.6 us -> 37.8 us
    ppermute x12 -> x15, starting transfers between devices: 21.1 us -> 51.1 us  [shift(): lax.ppermute(value, axis, [(i, (i + step) % count) for i in range(count)])]
    ppermute x12 -> x15, waiting for transfers between devices: 47.5 us -> 32 us  [shift(): lax.ppermute(value, axis, [(i, (i + step) % count) for i in range(count)])]
    ppermute x4 -> x0, starting transfers between devices: 9.16 us -> none  [the longest x1 5.32 us: relay_rest(): inward = lax.ppermute(chunks[2], axis, [(0, 1), (3, 2)])]
    all_to_all x1, waiting for transfers between devices: 1.54 us -> 3.36 us  [on_device(): lax.all_to_all(routed, 'seq', split_axis=0, concat_axis=0, tiled=True)]
  transfers between devices with their start and end apart: 19 -> 18, of which waited for: 12 -> 11; matrix products, arithmetic and copies ran while one was open for 1% -> 1% of each run, Pallas kernels for 6% -> 6%
where the time goes in v7:
time: 121 us
  starting transfers between devices  54.6 us (45%)
  waiting for transfers between devices  37.8 us (31%)
  Pallas kernels  24.7 us (20%)
  local copies, waits for them, and re-layouts  1.72 us (1%)
    ppermute x15, starting transfers between devices, shift(): lax.ppermute(value, axis, [(i, (i + step) % count) for i in range(count)])  51.1 us
    ppermute x15, waiting for transfers between devices, shift(): lax.ppermute(value, axis, [(i, (i + step) % count) for i in range(count)])  32 us
    pallas_call x1, Pallas kernels, local_part(): pl.pallas_call(functools.partial(local_kernel, span, piece, step), in_spe...  15.4 us
    all_to_all x1, starting transfers between devices, on_device(): lax.all_to_all(routed, 'seq', split_axis=0, concat_axis=0, tiled=True)  3.37 us
    all_to_all x1, waiting for transfers between devices, on_device(): lax.all_to_all(routed, 'seq', split_axis=0, concat_axis=0, tiled=True)  3.36 us
    pallas_call x1, Pallas kernels, fetch(): pl.pallas_call(fetch_kernel, in_specs=[HBM], out_specs=VMEM, out_shape=pl...  2.89 us
    ppermute x2, waiting for transfers between devices, swap_cores(): lax.ppermute(value, axis, [(i, i ^ 1) for i in range(lax.axis_size(axis))])  2.43 us
  transfers between devices with their start and end apart: 18, of which 11 were waited for; matrix products, arithmetic and copies ran while one was open for 1% of the time, Pallas kernels for 6%

profile of v7, /device:TPU:0, one launch (start us, length us, event | category | flops | bytes accessed | tf_op | source)
XLA Modules:
  0.0 120.7 jit_solution(9977614389635340630)
XLA Ops:
  1.2 15.4 %local_part.1 = (bf16[256,1024]{1,0:T(8,128)(2,1)}, bf16[256,1024]{1,0:T(8,128)(2,1)}, bf16[256,1024]{1,0:T(8,128)(2,1)}, bf16[256,1024]{1,0:T(8,128)(2,1)}, bf1...) custom-call(s32[1]{0:T(128)} %bitcast.2.me_ref, ...), custom_call_target="tpu_custom_call" | custom-call | tf_op jit(solution)/shard_map/local_part/pallas_call | solution.py:122
  16.7 3.1 %collective-permute-start = (bf16[128,512]{1,0:T(8,128)(2,1)S(1)}, bf16[128,512]{1,0:T(8,128)(2,1)S(1)}, u32[]{:S(2)}, u32[]{:S(2)}) collective-permute-start(bf16[128,512]{1,0:T(8,128)(2,1)S(1)} %get-tuple-element.35), channel_id=1, source_target_pairs={{0,1},{1,2},{2,3},{3,0},{4,5},{5,6},{6,7},{7,4},{8,9},{9,10},{10,1... | collective-permute-start | bytes 393224 | tf_op jit(solution)/shard_map/ppermute | solution.py:316
  19.7 2.6 %collective-permute-start.1 = (bf16[128,512]{1,0:T(8,128)(2,1)S(1)}, bf16[128,512]{1,0:T(8,128)(2,1)S(1)}, u32[]{:S(2)}, u32[]{:S(2)}) collective-permute-start(bf16[128,512]{1,0:T(8,128)(2,1)S(1)} %get-tuple-element.36), channel_id=1, source_target_pairs={{0,2},{1,3},{2,0},{3,1},{4,6},{5,7},{6,4},{7,5},{8,10},{9,11},{10,... | collective-permute-start | bytes 393224 | tf_op jit(solution)/shard_map/ppermute | solution.py:316
  22.3 1.3 %collective-permute-start.2 = (bf16[128,512]{1,0:T(8,128)(2,1)S(1)}, bf16[128,512]{1,0:T(8,128)(2,1)S(1)}, u32[]{:S(2)}, u32[]{:S(2)}) collective-permute-start(bf16[128,512]{1,0:T(8,128)(2,1)S(1)} %get-tuple-element.37), channel_id=1, source_target_pairs={{0,3},{1,0},{2,1},{3,2},{4,7},{5,4},{6,5},{7,6},{8,11},{9,8},{10,9... | collective-permute-start | bytes 393224 | tf_op jit(solution)/shard_map/ppermute | solution.py:316
  23.7 2.5 %collective-permute-done = bf16[128,512]{1,0:T(8,128)(2,1)S(1)} collective-permute-done((bf16[128,512]{1,0:T(8,128)(2,1)S(1)}, bf16[128,512]{1,0:T(8,128)(2,1)S(1)}, u32[]{:S(2)}, u32[]{:S(2)}) %collective-permute-start) | collective-permute-done | bytes 131104 | tf_op jit(solution)/shard_map/ppermute | solution.py:316
  26.2 4.8 %collective-permute-done.1 = bf16[128,512]{1,0:T(8,128)(2,1)S(1)} collective-permute-done((bf16[128,512]{1,0:T(8,128)(2,1)S(1)}, bf16[128,512]{1,0:T(8,128)(2,1)S(1)}, u32[]{:S(2)}, u32[]{:S(2)}) %collective-permute-start.1) | collective-permute-done | bytes 131104 | tf_op jit(solution)/shard_map/ppermute | solution.py:316
  31.0 3.3 %collective-permute-start.3 = (bf16[128,512]{1,0:T(8,128)(2,1)S(1)}, bf16[128,512]{1,0:T(8,128)(2,1)S(1)}, u32[]{:S(2)}, u32[]{:S(2)}) collective-permute-start(bf16[128,512]{1,0:T(8,128)(2,1)S(1)} %add_convert_fusion.refs_0_.own_ref), channel_id=1, source_target_pairs={{0,1},{1,2},{2,3},{3,0},{4,5},{5,6},{6,7},{7,4},{8,9},{9,10},{10,1... | collective-permute-start | bytes 393224 | tf_op jit(solution)/shard_map/ppermute | solution.py:316
  34.4 1.6 %collective-permute-start.4 = (bf16[128,512]{1,0:T(8,128)(2,1)S(1)}, bf16[128,512]{1,0:T(8,128)(2,1)S(1)}, u32[]{:S(2)}, u32[]{:S(2)}) collective-permute-start(bf16[128,512]{1,0:T(8,128)(2,1)S(1)} %add_convert_fusion.refs_0_.own_ref), channel_id=1, source_target_pairs={{0,2},{1,3},{2,0},{3,1},{4,6},{5,7},{6,4},{7,5},{8,10},{9,11},{10,... | collective-permute-start | bytes 393224 | tf_op jit(solution)/shard_map/ppermute | solution.py:316
  36.0 0.8 collective-permute-start.5
  36.8 2.9 %fetch.1.refs_4_ = bf16[3,2048,512]{2,1,0:T(8,128)(2,1)S(1)} custom-call(bf16[3,2048,512]{2,1,0:T(8,128)(2,1)} %bitcast.13), custom_call_target="tpu_custom_call" | custom-call | tf_op jit(solution)/shard_map/fetch/pallas_call | solution.py:150
  39.7 4.4 %collective-permute-done.4.refs_2_ = bf16[128,512]{1,0:T(8,128)(2,1)S(1)} collective-permute-done((bf16[128,512]{1,0:T(8,128)(2,1)S(1)}, bf16[128,512]{1,0:T(8,128)(2,1)S(1)}, u32[]{:S(2)}, u32[]{:S(2)}) %collective-permute-start.4) | collective-permute-done | bytes 131104 | tf_op jit(solution)/shard_map/ppermute | solution.py:316
  44.1 1.7 %global_heads.1 = (bf16[128,768]{1,0:T(8,128)(2,1)S(1)}, bf16[128,768]{1,0:T(8,128)(2,1)S(1)}) custom-call(s32[1]{0:T(128)} %bitcast.6.core_ref, s32[4]{0:T(128)S(1)} %and_select_fusion.ids_ref, f32[4,1,512]{2,1,0:T(1,128)S(1)} %bitcast.12, bf16[128,512]{1,0:T(8,128)(2,1)S(1)} %add_convert_fusion.refs_0_.own_ref, ...), custom_call_target="tpu_custom_call" | custom-call | tf_op jit(solution)/shard_map/global_heads/pallas_call | solution.py:184
  46.2 1.2 collective-permute-done.6.given_ref
  47.4 1.5 %collective-permute-start.7 = (bf16[256,512]{1,0:T(8,128)(2,1)S(1)}, bf16[256,512]{1,0:T(8,128)(2,1)S(1)}, u32[]{:S(2)}, u32[]{:S(2)}) collective-permute-start(bf16[256,512]{1,0:T(8,128)(2,1)S(1)} %pad_maximum_fusion), channel_id=1, source_target_pairs={{0,8},{4,12},{8,16},{12,20},{16,24},{20,28},{24,0},{28,4},{1,9},{5... | collective-permute-start | bytes 786440 | tf_op jit(solution)/shard_map/ppermute | solution.py:316
  49.0 1.5 %collective-permute-start.8 = (bf16[256,512]{1,0:T(8,128)(2,1)S(1)}, bf16[256,512]{1,0:T(8,128)(2,1)S(1)}, u32[]{:S(2)}, u32[]{:S(2)}) collective-permute-start(bf16[256,512]{1,0:T(8,128)(2,1)S(1)} %pad_maximum_fusion), channel_id=1, source_target_pairs={{0,16},{4,20},{8,24},{12,28},{16,0},{20,4},{24,8},{28,12},{1,17},{... | collective-permute-start | bytes 786440 | tf_op jit(solution)/shard_map/ppermute | solution.py:316
  50.5 1.4 %collective-permute-start.9 = (bf16[256,512]{1,0:T(8,128)(2,1)S(1)}, bf16[256,512]{1,0:T(8,128)(2,1)S(1)}, u32[]{:S(2)}, u32[]{:S(2)}) collective-permute-start(bf16[256,512]{1,0:T(8,128)(2,1)S(1)} %pad_maximum_fusion), channel_id=1, source_target_pairs={{0,24},{4,28},{8,0},{12,4},{16,8},{20,12},{24,16},{28,20},{1,25},{... | collective-permute-start | bytes 786440 | tf_op jit(solution)/shard_map/ppermute | solution.py:316
  51.9 3.3 %collective-permute-start.11 = (bf16[256,1024]{1,0:T(8,128)(2,1)S(1)}, bf16[256,1024]{1,0:T(8,128)(2,1)S(1)}, u32[]{:S(2)}, u32[]{:S(2)}) collective-permute-start(bf16[256,1024]{1,0:T(8,128)(2,1)S(1)} %copy-done.8), channel_id=1, source_target_pairs={{0,1},{1,2},{2,3},{3,0},{4,5},{5,6},{6,7},{7,4},{8,9},{9,10},{10,1... | collective-permute-start | bytes 1572872 | tf_op jit(solution)/shard_map/ppermute | solution.py:316
  55.3 2.1 %collective-permute-start.15 = (bf16[256,1024]{1,0:T(8,128)(2,1)S(1)}, bf16[256,1024]{1,0:T(8,128)(2,1)S(1)}, u32[]{:S(2)}, u32[]{:S(2)}) collective-permute-start(bf16[256,1024]{1,0:T(8,128)(2,1)S(1)} %copy-done.7), channel_id=1, source_target_pairs={{0,2},{1,3},{2,0},{3,1},{4,6},{5,7},{6,4},{7,5},{8,10},{9,11},{10,... | collective-permute-start | bytes 1572872 | tf_op jit(solution)/shard_map/ppermute | solution.py:316
  57.6 4.7 %collective-permute-start.16 = (bf16[256,1024]{1,0:T(8,128)(2,1)}, bf16[256,1024]{1,0:T(8,128)(2,1)S(1)}, u32[]{:S(2)}, u32[]{:S(2)}) collective-permute-start(bf16[256,1024]{1,0:T(8,128)(2,1)} %get-tuple-element.64), channel_id=1, source_target_pairs={{0,3},{1,0},{2,1},{3,2},{4,7},{5,4},{6,5},{7,6},{8,11},{9,8},{10,9... | collective-permute-start | bytes 1572872 | tf_op jit(solution)/shard_map/ppermute | solution.py:316
  62.4 1.7 %attend.1 = (bf16[128,256]{1,0:T(8,128)(2,1)S(1)}, bf16[128,256]{1,0:T(8,128)(2,1)S(1)}) custom-call(s32[1]{0:T(128)} %bitcast.7.me_ref, s32[4]{0:T(128)S(1)} %and_select_fusion.1.ids_ref, f32[4]{0:T(128)S(1)} %copy-done.6, bf16[128,768]{1,0:T(8,128)(2,1)S(1)} %get-tuple-element.40.kept_ref, bf16[128,768]{1,0:T(8,128)(2,1)S(1)} %collective-permute-done.6.given_ref, ...), custom_call_target="tpu_custom_call" | custom-call | flops 1 | bytes 1 | tf_op jit(solution)/shard_map/attend/pallas_call | solution.py:227
  64.3 1.2 %collective-permute-done.10.other_ref = bf16[128,256]{1,0:T(8,128)(2,1)S(1)} collective-permute-done((bf16[128,256]{1,0:T(8,128)(2,1)S(1)}, bf16[128,256]{1,0:T(8,128)(2,1)S(1)}, u32[]{:S(2)}, u32[]{:S(2)}) %collective-permute-start.10) | collective-permute-done | bytes 65568 | tf_op jit(solution)/shard_map/ppermute | solution.py:333
  65.5 4.1 %collective-permute-done.11.refs_1_ = bf16[256,1024]{1,0:T(8,128)(2,1)S(1)} collective-permute-done((bf16[256,1024]{1,0:T(8,128)(2,1)S(1)}, bf16[256,1024]{1,0:T(8,128)(2,1)S(1)}, u32[]{:S(2)}, u32[]{:S(2)}) %collective-permute-start.11) | collective-permute-done | bytes 524320 | tf_op jit(solution)/shard_map/ppermute | solution.py:316
  69.6 1.0 project.1
  71.1 20.4 %collective-permute-start.13 = (bf16[128,512]{1,0:T(8,128)(2,1)S(1)}, bf16[128,512]{1,0:T(8,128)(2,1)S(1)}, u32[]{:S(2)}, u32[]{:S(2)}) collective-permute-start(bf16[128,512]{1,0:T(8,128)(2,1)S(1)} %get-tuple-element.53), channel_id=1, source_target_pairs={{0,2},{1,3},{2,0},{3,1},{4,6},{5,7},{6,4},{7,5},{8,10},{9,11},{10,... | collective-permute-start | bytes 393224 | tf_op jit(solution)/shard_map/ppermute | solution.py:316
  91.6 2.8 %collective-permute-start.14 = (bf16[128,512]{1,0:T(8,128)(2,1)S(1)}, bf16[128,512]{1,0:T(8,128)(2,1)S(1)}, u32[]{:S(2)}, u32[]{:S(2)}) collective-permute-start(bf16[128,512]{1,0:T(8,128)(2,1)S(1)} %get-tuple-element.54), channel_id=1, source_target_pairs={{0,3},{1,0},{2,1},{3,2},{4,7},{5,4},{6,5},{7,6},{8,11},{9,8},{10,9... | collective-permute-start | bytes 393224 | tf_op jit(solution)/shard_map/ppermute | solution.py:316
  94.9 15.4 %collective-permute-done.13.refs_2_ = bf16[128,512]{1,0:T(8,128)(2,1)S(1)} collective-permute-done((bf16[128,512]{1,0:T(8,128)(2,1)S(1)}, bf16[128,512]{1,0:T(8,128)(2,1)S(1)}, u32[]{:S(2)}, u32[]{:S(2)}) %collective-permute-start.13) | collective-permute-done | bytes 131104 | tf_op jit(solution)/shard_map/ppermute | solution.py:316
  110.3 0.9 finish_result.1
  111.3 3.4 %all-to-all-start = ((bf16[8,16,512]{2,1,0:T(8,128)(2,1)}), bf16[8,16,512]{2,1,0:T(8,128)(2,1)S(1)}, u32[]{:S(2)}, u32[]{:S(2)}) async-start(bf16[8,16,512]{2,1,0:T(8,128)(2,1)} %bitcast.9), calls=%async_computation | async-start | bytes 262144 | tf_op jit(solution)/shard_map/all_to_all | solution.py:410
  114.7 1.1 finish_bytes.1
  115.7 1.0 reshape.86
  116.7 3.4 %all-to-all-done = bf16[8,16,512]{2,1,0:T(8,128)(2,1)S(1)} async-done(((bf16[8,16,512]{2,1,0:T(8,128)(2,1)}), bf16[8,16,512]{2,1,0:T(8,128)(2,1)S(1)}, u32[]{:S(2)}, u32[]{:S(2)}) %all-to-all-start) | async-done | bytes 131104 | tf_op jit(solution)/shard_map/all_to_all | solution.py:410
  120.1 0.7 copy.17
  (44 shorter events, 2.5 us)
Async XLA Ops:
  0.6 45.3 %copy-start = (s32[8,16]{1,0:T(8,128)S(1)}, s32[8,16]{1,0:T(8,128)}, u32[]{:S(2)}) copy-start(s32[8,16]{1,0:T(8,128)} %param.27) | copy-start | bytes 1540
  16.7 9.5 %collective-permute-start = (bf16[128,512]{1,0:T(8,128)(2,1)S(1)}, bf16[128,512]{1,0:T(8,128)(2,1)S(1)}, u32[]{:S(2)}, u32[]{:S(2)}) collective-permute-start(bf16[128,512]{1,0:T(8,128)(2,1)S(1)} %get-tuple-element.35), channel_id=1, source_target_pairs={{0,1},{1,2},{2,3},{3,0},{4,5},{5,6},{6,7},{7,4},{8,9},{9,10},{10,1... | collective-permute-start | bytes 393224 | tf_op jit(solution)/shard_map/ppermute | solution.py:316
  19.7 11.2 %collective-permute-start.1 = (bf16[128,512]{1,0:T(8,128)(2,1)S(1)}, bf16[128,512]{1,0:T(8,128)(2,1)S(1)}, u32[]{:S(2)}, u32[]{:S(2)}) collective-permute-start(bf16[128,512]{1,0:T(8,128)(2,1)S(1)} %get-tuple-element.36), channel_id=1, source_target_pairs={{0,2},{1,3},{2,0},{3,1},{4,6},{5,7},{6,4},{7,5},{8,10},{9,11},{10,... | collective-permute-start | bytes 393224 | tf_op jit(solution)/shard_map/ppermute | solution.py:316
  22.3 8.6 %collective-permute-start.2 = (bf16[128,512]{1,0:T(8,128)(2,1)S(1)}, bf16[128,512]{1,0:T(8,128)(2,1)S(1)}, u32[]{:S(2)}, u32[]{:S(2)}) collective-permute-start(bf16[128,512]{1,0:T(8,128)(2,1)S(1)} %get-tuple-element.37), channel_id=1, source_target_pairs={{0,3},{1,0},{2,1},{3,2},{4,7},{5,4},{6,5},{7,6},{8,11},{9,8},{10,9... | collective-permute-start | bytes 393224 | tf_op jit(solution)/shard_map/ppermute | solution.py:316
  31.0 8.7 %collective-permute-start.3 = (bf16[128,512]{1,0:T(8,128)(2,1)S(1)}, bf16[128,512]{1,0:T(8,128)(2,1)S(1)}, u32[]{:S(2)}, u32[]{:S(2)}) collective-permute-start(bf16[128,512]{1,0:T(8,128)(2,1)S(1)} %add_convert_fusion.refs_0_.own_ref), channel_id=1, source_target_pairs={{0,1},{1,2},{2,3},{3,0},{4,5},{5,6},{6,7},{7,4},{8,9},{9,10},{10,1... | collective-permute-start | bytes 393224 | tf_op jit(solution)/shard_map/ppermute | solution.py:316
  34.4 9.7 %collective-permute-start.4 = (bf16[128,512]{1,0:T(8,128)(2,1)S(1)}, bf16[128,512]{1,0:T(8,128)(2,1)S(1)}, u32[]{:S(2)}, u32[]{:S(2)}) collective-permute-start(bf16[128,512]{1,0:T(8,128)(2,1)S(1)} %add_convert_fusion.refs_0_.own_ref), channel_id=1, source_target_pairs={{0,2},{1,3},{2,0},{3,1},{4,6},{5,7},{6,4},{7,5},{8,10},{9,11},{10,... | collective-permute-start | bytes 393224 | tf_op jit(solution)/shard_map/ppermute | solution.py:316
  36.0 8.1 %collective-permute-start.5 = (bf16[128,512]{1,0:T(8,128)(2,1)S(1)}, bf16[128,512]{1,0:T(8,128)(2,1)S(1)}, u32[]{:S(2)}, u32[]{:S(2)}) collective-permute-start(bf16[128,512]{1,0:T(8,128)(2,1)S(1)} %add_convert_fusion.refs_0_.own_ref), channel_id=1, source_target_pairs={{0,3},{1,0},{2,1},{3,2},{4,7},{5,4},{6,5},{7,6},{8,11},{9,8},{10,9... | collective-permute-start | bytes 393224 | tf_op jit(solution)/shard_map/ppermute | solution.py:316
  36.8 7.3 %copy-start.4 = (f32[2048]{0:T(1024)S(1)}, f32[2048]{0:T(1024)}, u32[]{:S(2)}) copy-start(f32[2048]{0:T(1024)} %param.22) | copy-start | bytes 24580
  44.1 7.8 %copy-start.8 = (bf16[256,1024]{1,0:T(8,128)(2,1)S(1)}, bf16[256,1024]{1,0:T(8,128)(2,1)}, u32[]{:S(2)}) copy-start(bf16[256,1024]{1,0:T(8,128)(2,1)} %get-tuple-element.49) | copy-start | bytes 1572868
  44.1 11.2 %copy-start.7 = (bf16[256,1024]{1,0:T(8,128)(2,1)S(1)}, bf16[256,1024]{1,0:T(8,128)(2,1)}, u32[]{:S(2)}) copy-start(bf16[256,1024]{1,0:T(8,128)(2,1)} %get-tuple-element.55) | copy-start | bytes 1572868
  44.1 18.3 %copy-start.6 = (f32[4]{0:T(128)S(1)}, f32[4]{0:T(128)}, u32[]{:S(2)}) copy-start(f32[4]{0:T(128)} %scale_ref.3) | copy-start | bytes 52
  45.8 23.8 %copy-start.1 = (bf16[512,2048]{1,0:T(8,128)(2,1)S(1)}, bf16[512,2048]{1,0:T(8,128)(2,1)}, u32[]{:S(2)}) copy-start(bf16[512,2048]{1,0:T(8,128)(2,1)} %proj_ref.2) | copy-start | bytes 6291460
  45.9 23.8 %copy-start.5 = (s32[4]{0:T(128)S(1)}, s32[4]{0:T(128)}, u32[]{:S(2)}) copy-start(s32[4]{0:T(128)} %and_select_fusion.2.slots_ref) | copy-start | bytes 52
  45.9 1.5 %collective-permute-start.6 = (bf16[128,768]{1,0:T(8,128)(2,1)S(1)}, bf16[128,768]{1,0:T(8,128)(2,1)S(1)}, u32[]{:S(2)}, u32[]{:S(2)}) collective-permute-start(bf16[128,768]{1,0:T(8,128)(2,1)S(1)} %get-tuple-element.45), channel_id=1, source_target_pairs={{0,4},{4,0},{8,12},{12,8},{16,20},{20,16},{24,28},{28,24},{1,5},{5... | collective-permute-start | bytes 589832 | tf_op jit(solution)/shard_map/ppermute | solution.py:333
  47.4 10.1 %collective-permute-start.7 = (bf16[256,512]{1,0:T(8,128)(2,1)S(1)}, bf16[256,512]{1,0:T(8,128)(2,1)S(1)}, u32[]{:S(2)}, u32[]{:S(2)}) collective-permute-start(bf16[256,512]{1,0:T(8,128)(2,1)S(1)} %pad_maximum_fusion), channel_id=1, source_target_pairs={{0,8},{4,12},{8,16},{12,20},{16,24},{20,28},{24,0},{28,4},{1,9},{5... | collective-permute-start | bytes 786440 | tf_op jit(solution)/shard_map/ppermute | solution.py:316
  49.0 13.4 %collective-permute-start.8 = (bf16[256,512]{1,0:T(8,128)(2,1)S(1)}, bf16[256,512]{1,0:T(8,128)(2,1)S(1)}, u32[]{:S(2)}, u32[]{:S(2)}) collective-permute-start(bf16[256,512]{1,0:T(8,128)(2,1)S(1)} %pad_maximum_fusion), channel_id=1, source_target_pairs={{0,16},{4,20},{8,24},{12,28},{16,0},{20,4},{24,8},{28,12},{1,17},{... | collective-permute-start | bytes 786440 | tf_op jit(solution)/shard_map/ppermute | solution.py:316
  50.5 12.0 %collective-permute-start.9 = (bf16[256,512]{1,0:T(8,128)(2,1)S(1)}, bf16[256,512]{1,0:T(8,128)(2,1)S(1)}, u32[]{:S(2)}, u32[]{:S(2)}) collective-permute-start(bf16[256,512]{1,0:T(8,128)(2,1)S(1)} %pad_maximum_fusion), channel_id=1, source_target_pairs={{0,24},{4,28},{8,0},{12,4},{16,8},{20,12},{24,16},{28,20},{1,25},{... | collective-permute-start | bytes 786440 | tf_op jit(solution)/shard_map/ppermute | solution.py:316
  51.9 17.7 %collective-permute-start.11 = (bf16[256,1024]{1,0:T(8,128)(2,1)S(1)}, bf16[256,1024]{1,0:T(8,128)(2,1)S(1)}, u32[]{:S(2)}, u32[]{:S(2)}) collective-permute-start(bf16[256,1024]{1,0:T(8,128)(2,1)S(1)} %copy-done.8), channel_id=1, source_target_pairs={{0,1},{1,2},{2,3},{3,0},{4,5},{5,6},{6,7},{7,4},{8,9},{9,10},{10,1... | collective-permute-start | bytes 1572872 | tf_op jit(solution)/shard_map/ppermute | solution.py:316
  55.3 39.1 %collective-permute-start.15 = (bf16[256,1024]{1,0:T(8,128)(2,1)S(1)}, bf16[256,1024]{1,0:T(8,128)(2,1)S(1)}, u32[]{:S(2)}, u32[]{:S(2)}) collective-permute-start(bf16[256,1024]{1,0:T(8,128)(2,1)S(1)} %copy-done.7), channel_id=1, source_target_pairs={{0,2},{1,3},{2,0},{3,1},{4,6},{5,7},{6,4},{7,5},{8,10},{9,11},{10,... | collective-permute-start | bytes 1572872 | tf_op jit(solution)/shard_map/ppermute | solution.py:316
  57.6 57.1 %collective-permute-start.16 = (bf16[256,1024]{1,0:T(8,128)(2,1)}, bf16[256,1024]{1,0:T(8,128)(2,1)S(1)}, u32[]{:S(2)}, u32[]{:S(2)}) collective-permute-start(bf16[256,1024]{1,0:T(8,128)(2,1)} %get-tuple-element.64), channel_id=1, source_target_pairs={{0,3},{1,0},{2,1},{3,2},{4,7},{5,4},{6,5},{7,6},{8,11},{9,8},{10,9... | collective-permute-start | bytes 1572872 | tf_op jit(solution)/shard_map/ppermute | solution.py:316
  62.4 52.2 %copy-start.2 = (bf16[256,1024]{1,0:T(8,128)(2,1)S(1)}, bf16[256,1024]{1,0:T(8,128)(2,1)}, u32[]{:S(2)}) copy-start(bf16[256,1024]{1,0:T(8,128)(2,1)} %proj_ref.3) | copy-start | bytes 1572868
  62.4 52.2 %copy-start.3 = (bf16[256,1024]{1,0:T(8,128)(2,1)S(1)}, bf16[256,1024]{1,0:T(8,128)(2,1)}, u32[]{:S(2)}) copy-start(bf16[256,1024]{1,0:T(8,128)(2,1)} %get-tuple-element.61.refs_0_) | copy-start | bytes 1572868
  64.2 1.3 %collective-permute-start.10 = (bf16[128,256]{1,0:T(8,128)(2,1)S(1)}, bf16[128,256]{1,0:T(8,128)(2,1)S(1)}, u32[]{:S(2)}, u32[]{:S(2)}) collective-permute-start(bf16[128,256]{1,0:T(8,128)(2,1)S(1)} %get-tuple-element.48), channel_id=1, source_target_pairs={{0,4},{4,0},{8,12},{12,8},{16,20},{20,16},{24,28},{28,24},{1,5},{5... | collective-permute-start | bytes 196616 | tf_op jit(solution)/shard_map/ppermute | solution.py:333
  70.6 24.3 %collective-permute-start.12 = (bf16[128,512]{1,0:T(8,128)(2,1)S(1)}, bf16[128,512]{1,0:T(8,128)(2,1)S(1)}, u32[]{:S(2)}, u32[]{:S(2)}) collective-permute-start(bf16[128,512]{1,0:T(8,128)(2,1)S(1)} %get-tuple-element.52), channel_id=1, source_target_pairs={{0,1},{1,2},{2,3},{3,0},{4,5},{5,6},{6,7},{7,4},{8,9},{9,10},{10,1... | collective-permute-start | bytes 393224 | tf_op jit(solution)/shard_map/ppermute | solution.py:316
  71.1 39.2 %collective-permute-start.13 = (bf16[128,512]{1,0:T(8,128)(2,1)S(1)}, bf16[128,512]{1,0:T(8,128)(2,1)S(1)}, u32[]{:S(2)}, u32[]{:S(2)}) collective-permute-start(bf16[128,512]{1,0:T(8,128)(2,1)S(1)} %get-tuple-element.53), channel_id=1, source_target_pairs={{0,2},{1,3},{2,0},{3,1},{4,6},{5,7},{6,4},{7,5},{8,10},{9,11},{10,... | collective-permute-start | bytes 393224 | tf_op jit(solution)/shard_map/ppermute | solution.py:316
  91.6 18.8 %collective-permute-start.14 = (bf16[128,512]{1,0:T(8,128)(2,1)S(1)}, bf16[128,512]{1,0:T(8,128)(2,1)S(1)}, u32[]{:S(2)}, u32[]{:S(2)}) collective-permute-start(bf16[128,512]{1,0:T(8,128)(2,1)S(1)} %get-tuple-element.54), channel_id=1, source_target_pairs={{0,3},{1,0},{2,1},{3,2},{4,7},{5,4},{6,5},{7,6},{8,11},{9,8},{10,9... | collective-permute-start | bytes 393224 | tf_op jit(solution)/shard_map/ppermute | solution.py:316
  111.3 8.8 %all-to-all-start = ((bf16[8,16,512]{2,1,0:T(8,128)(2,1)}), bf16[8,16,512]{2,1,0:T(8,128)(2,1)S(1)}, u32[]{:S(2)}, u32[]{:S(2)}) async-start(bf16[8,16,512]{2,1,0:T(8,128)(2,1)} %bitcast.9), calls=%async_computation | async-start | bytes 262144 | tf_op jit(solution)/shard_map/all_to_all | solution.py:410

commit v8 on v7

--- a/solution.py
+++ b/solution.py
@@ -35,30 +35,32 @@
     return 0.5 * values * (1.0 + jnp.tanh(inner))
 
 
-def local_kernel(span, piece, step, me_ref, scale_ref, slots_ref, gain_ref, x_hbm, *refs):
-    ways = slots_ref.shape[0]
-    sources, parts, shares = refs[:5], refs[5 : 5 + ways], refs[5 + ways : 5 + 2 * ways]
-    x_ref, part_ref, share_ref = refs[5 + 2 * ways : 8 + 2 * ways]
-    held, (in_sem, x_sem, part_sem) = refs[8 + 2 * ways : 13 + 2 * ways], refs[13 + 2 * ways :]
+def local_kernel(span, ways, piece, last, scale_ref, gain_ref, x_hbm, *refs):
+    sources, parts, others = refs[:5], refs[5 : 5 + ways], refs[5 + ways : -11]
+    held, (x_ref, part_ref, share_ref, in_sem, x_sem, part_sem) = refs[-11:-6], refs[-6:]
     patches = share_ref.shape[1]
-    width = x_ref.shape[1]
     own = span // ways
     rows = piece * span
     pieces = patches // piece
-    loads = [pltpu.make_async_copy(s, h, in_sem.at[i]) for i, (s, h) in enumerate(zip(sources, held))]
     cuts = [slice(i * rows, (i + 1) * rows) for i in range(pieces)]
-    x_loads = [pltpu.make_async_copy(x_hbm.at[pl.ds(c.start, rows)], x_ref.at[pl.ds(c.start, rows)], x_sem.at[i]) for i, c in enumerate(cuts)]
-    for copy in x_loads + loads:
+    skip = x_ref.shape[0] if last else 0
+    loads = [
+        pltpu.make_async_copy(x_hbm.at[pl.ds(skip + c.start, rows)], x_ref.at[pl.ds(c.start, rows)], x_sem.at[i])
+        for i, c in enumerate(cuts)
+    ]
+    loads += [pltpu.make_async_copy(s, h, in_sem.at[i]) for i, (s, h) in enumerate(zip(sources, held))]
+    for copy in loads:
         copy.start()
-    qkv_ref, up_ref, out_ref, down_ref, proj_ref = held
+    me = lax.axis_index("head")
     at = lax.broadcasted_iota(jnp.int32, (rows, rows), 0)
     to = lax.broadcasted_iota(jnp.int32, (rows, rows), 1)
     order = (to == (at % piece) * span + at // piece).astype(F32).astype(BF16)
-    kept = lax.broadcasted_iota(jnp.int32, (rows, 1), 0) // piece // own == me_ref[0]
+    kept = lax.broadcasted_iota(jnp.int32, (rows, 1), 0) // piece // own == me
+    for copy in loads:
+        copy.wait()
+    qkv_ref, up_ref, out_ref, down_ref, proj_ref = held
     xs, normed = [], []
-    for copy in x_loads + loads:
-        copy.wait()
-    for i, cut in enumerate(cuts):
+    for cut in cuts:
         x = dot(order, x_ref[cut])
         xs.append(jnp.where(kept, x, 0.0).astype(BF16))
         factor = lax.rsqrt(jnp.mean(x * x, axis=-1, keepdims=True) + EPSILON)
@@ -79,62 +81,83 @@
             total = jnp.sum(weights, axis=-1, keepdims=True)
             columns.append((dot(weights.astype(BF16), value[cut, head].astype(BF16)) / total).astype(BF16))
         attended.append(jnp.concatenate(columns, axis=1))
-    attended = jnp.concatenate(attended, axis=0)
     act = gelu(dot(normed, up_ref[...])).astype(BF16)
-    mixed = jnp.concatenate([attended, act], axis=1)
-    share = 0.0
+    mixed = jnp.concatenate([jnp.concatenate(attended, axis=0), act], axis=1)
+    partial = dot(mixed, jnp.concatenate([out_ref[...], down_ref[...]], axis=0)) + xs.astype(F32)
+    partial = partial.astype(BF16)
+    for i, cut in enumerate(cuts):
+        for b in range(span):
+            put = (b % own) * patches + i * piece
+            part_ref[b // own, put : put + piece] = partial[cut][b * piece : (b + 1) * piece]
     stores = []
-    for c in range(0, width, step):
-        columns = slice(c, c + step)
-        partial = dot(mixed, jnp.concatenate([out_ref[:, columns], down_ref[:, columns]], axis=0))
-        partial = (partial + xs[:, columns].astype(F32)).astype(BF16)
+    for slot, part in enumerate(parts):
+        stores.append(pltpu.make_async_copy(part_ref.at[lax.rem(me + slot, ways)], part, part_sem.at[slot]))
+        stores[-1].start()
+    if last:
+        share = dot(partial, proj_ref[...]).astype(BF16)
+        size = share.shape[1]
         for i, cut in enumerate(cuts):
             for b in range(span):
-                put = (b % own) * patches + i * piece
-                part_ref[b // own, put : put + piece, columns] = partial[cut][b * piece : (b + 1) * piece]
-        for slot, part in enumerate(parts):
-            source = part_ref.at[slots_ref[slot], :, pl.ds(c, step)]
-            stores.append(pltpu.make_async_copy(source, part.at[:, pl.ds(c, step)], part_sem.at[len(stores)]))
-            stores[-1].start()
-        share += dot(partial, proj_ref[columns])
-    share = share.astype(BF16)
-    size = share.shape[1]
-    for i, cut in enumerate(cuts):
-        for b in range(span):
-            put = slice((b % own) * size, (b % own + 1) * size)
-            share_ref[b // own, i * piece : (i + 1) * piece, put] = share[cut][b * piece : (b + 1) * piece]
-    for slot, out in enumerate(shares):
-        out[...] = share_ref[slots_ref[slot]]
+                put = slice((b % own) * size, (b % own + 1) * size)
+                share_ref[b // own, i * piece : (i + 1) * piece, put] = share[cut][b * piece : (b + 1) * piece]
+        for slot, out in enumerate(others):
+            out[...] = share_ref[lax.rem(me + slot, ways)]
     for copy in stores:
         copy.wait()
 
 
-def local_part(me, scale, slots, x, gain, qkv, out, up, down, proj, span):
-    rows, width = x.shape
+def local_part(scale, x, gain, weights, span, ways, last):
+    rows, width = x.shape[0] // 2, x.shape[1]
     patches = rows // span
-    ways = slots.shape[0]
     own = span // ways
-    weights = (qkv, up, out, down, proj)
     piece = math.gcd(patches, 32)
-    step = math.gcd(width, 1024)
     part = (own * patches, width)
-    share = (patches, own * proj.shape[1])
+    share = (patches, own * weights[-1].shape[1])
+    others = [pltpu.VMEM(share, BF16)] * (ways if last else 0)
     outs = pl.pallas_call(
-        functools.partial(local_kernel, span, piece, step),
-        in_specs=[SMEM, SMEM, SMEM, VMEM] + [HBM] * (1 + len(weights)),
-        out_specs=[HBM] * ways + [VMEM] * ways,
-        out_shape=[jax.ShapeDtypeStruct(part, BF16)] * ways + [pltpu.VMEM(share, BF16)] * ways,
-        scratch_shapes=[pltpu.VMEM(x.shape, BF16), pltpu.VMEM((ways, *part), BF16), pltpu.VMEM((ways, *share), BF16)]
-        + [pltpu.VMEM(w.shape, w.dtype) for w in weights]
+        functools.partial(local_kernel, span, ways, piece, last),
+        in_specs=[SMEM, VMEM, HBM] + [HBM] * len(weights),
+        out_specs=[HBM] * ways + [VMEM] * len(others),
+        out_shape=[jax.ShapeDtypeStruct(part, BF16)] * ways + others,
+        scratch_shapes=[pltpu.VMEM(w.shape, w.dtype) for w in weights]
         + [
+            pltpu.VMEM((rows, width), BF16),
+            pltpu.VMEM((ways, *part), BF16),
+            pltpu.VMEM((ways, *share), BF16),
             pltpu.SemaphoreType.DMA((len(weights),)),
             pltpu.SemaphoreType.DMA((patches // piece,)),
-            pltpu.SemaphoreType.DMA((ways * (width // step),)),
+            pltpu.SemaphoreType.DMA((ways,)),
         ],
         compiler_params=pltpu.CompilerParams(vmem_limit_bytes=60 * 2**20),
+        cost_estimate=pl.CostEstimate(flops=8 * rows * width * width, bytes_accessed=10 * 2**20, transcendentals=rows * width),
         name="local_part",
-    )(me, scale, slots, gain, x, *weights)
-    return outs[:ways], outs[ways:]
+    )(scale, gain, x, *weights)
+    return list(outs[:ways]), list(outs[ways:])
+
+
+def state_kernel(count, proj_ref, *refs):
+    pieces, (state_ref, share_ref) = refs[:count], refs[count:]
+    state = sum(p[...].astype(F32) for p in pieces).astype(BF16)
+    state_ref[...] = state
+    patches = share_ref.shape[0]
+    width = proj_ref.shape[1]
+    for b in range(state.shape[0] // patches):
+        share_ref[:, b * width : (b + 1) * width] = dot(state[b * patches : (b + 1) * patches], proj_ref[...]).astype(BF16)
+
+
+def finish_state(proj, pieces, own):
+    rows, width = pieces[0].shape
+    return pl.pallas_call(
+        functools.partial(state_kernel, len(pieces)),
+        in_specs=[VMEM] * (1 + len(pieces)),
+        out_specs=(VMEM, VMEM),
+        out_shape=(
+            jax.ShapeDtypeStruct((rows, width), BF16),
+            jax.ShapeDtypeStruct((rows // own, own * proj.shape[1]), BF16),
+        ),
+        compiler_params=pltpu.CompilerParams(vmem_limit_bytes=8 * 2**20),
+        name="finish_state",
+    )(proj, *pieces)
 
 
 def fetch_kernel(source, held, sems):
@@ -285,26 +308,30 @@
     for copy in copies:
         copy.start()
     rows = result_ref.shape[0]
+    half = rows // 2
     width = proj_ref.shape[0]
     own = out_ref.shape[0] // rows
-    back = jnp.concatenate([dot(result_ref[:, b * width : (b + 1) * width], proj_ref[...]) for b in range(own)], axis=0)
+    back = [dot(result_ref[:, b * width : (b + 1) * width], proj_ref[...]) for b in range(own)]
+    back = jnp.concatenate([b[:half] for b in back] + [b[half:] for b in back], axis=0)
     at = lax.broadcasted_iota(jnp.int32, (rows * own, rows * own), 0)
     to = lax.broadcasted_iota(jnp.int32, (rows * own, rows * own), 1)
-    order = (to == (at % own) * rows + at // own).astype(F32).astype(BF16)
+    patch = at // own
+    order = (to == patch // half * half * own + at % own * half + patch % half).astype(F32).astype(BF16)
     for copy in copies:
         copy.wait()
-    state = sum(held[i].astype(F32) for i in range(count)).astype(BF16).astype(F32)
+    late = sum(held[i].astype(F32) for i in range(1, count)).astype(BF16)
+    state = jnp.concatenate([held[0], late], axis=0).astype(F32)
     out_ref[...] = dot(order, (state + back).astype(BF16)).astype(BF16)
 
 
 def finish_bytes(result, proj, pieces):
-    shape = pieces[0].shape
+    rows, width = pieces[0].shape
     return pl.pallas_call(
         functools.partial(bytes_kernel, len(pieces)),
         in_specs=[VMEM, VMEM] + [pl.BlockSpec(memory_space=pl.ANY)] * len(pieces),
         out_specs=VMEM,
-        out_shape=jax.ShapeDtypeStruct(shape, BF16),
-        scratch_shapes=[pltpu.VMEM((len(pieces), *shape), BF16), pltpu.SemaphoreType.DMA((len(pieces),))],
+        out_shape=jax.ShapeDtypeStruct((2 * rows, width), BF16),
+        scratch_shapes=[pltpu.VMEM((len(pieces), rows, width), BF16), pltpu.SemaphoreType.DMA((len(pieces),))],
         compiler_params=pltpu.CompilerParams(vmem_limit_bytes=16 * 2**20),
         cost_estimate=BRIEF,
         name="finish_bytes",
@@ -377,20 +404,17 @@
     depth = global_qkv.shape[2] // global_scale.shape[0]
 
     slots = shift_slots("head")
-    parts, chunks = local_part(
-        me.reshape(1),
-        local_scale,
-        slots,
-        byte_in.reshape(-1, width),
-        local_gain.reshape(1, -1),
-        jnp.transpose(local_qkv, (1, 0, 2)),
-        local_out,
-        mlp_up,
-        mlp_down,
-        patch_proj,
-        span,
-    )
-    residual = sum(p.astype(F32) for p in scatter(chunks, "head")).astype(BF16)
+    rows = byte_in.reshape(-1, width)
+    weights = [jnp.transpose(local_qkv, (1, 0, 2)), mlp_up, local_out, mlp_down, patch_proj]
+    gain = local_gain.reshape(1, -1)
+    early, _ = local_part(local_scale, rows, gain, weights, span, ways, False)
+    early = scatter(early, "head")
+    parts, chunks = local_part(local_scale, rows, gain, weights, span, ways, True)
+    chunks, early[1], early[2] = lax.optimization_barrier((chunks, early[1], early[2]))
+    chunks = scatter(chunks, "head")
+    early, early_share = finish_state(patch_proj, early, own)
+    late_share = sum(p.astype(F32) for p in chunks).astype(BF16)
+    residual = jnp.concatenate([early_share, late_share], axis=0)
     weight, residual = lax.optimization_barrier((jnp.transpose(global_qkv, (1, 0, 2)), residual))
     shares = gather(residual, "head")
     ids = (me - jnp.arange(ways, dtype=jnp.int32)) % ways
@@ -408,7 +432,7 @@
     updates, parts[2] = lax.optimization_barrier((updates, parts[2]))
     result, routed = finish_result(owner_order(owners, seq, patches), residual, updates)
     global_state = lax.all_to_all(routed, "seq", split_axis=0, concat_axis=0, tiled=True)
-    byte_out = finish_bytes(result, back_proj, parts)
+    byte_out = finish_bytes(result, back_proj, [early] + parts)
     return byte_out.reshape(patches, own, width), global_state
 
 

time: 121 us -> 111 us (0.917)
  starting transfers between devices: 54.6 us -> 39.8 us
  Pallas kernels: 24.7 us -> 29.7 us
    ppermute x15 -> x18, starting transfers between devices: 51.1 us -> 36.3 us  [shift(): lax.ppermute(value, axis, [(i, (i + step) % count) for i in range(count)])]
    pallas_call x1 -> x3, Pallas kernels: 15.4 us -> 20.6 us  [the longest x2 20.3 us: local_part(): pl.pallas_call(functools.partial(local_kernel, span, ways, piece, last),...]
    ppermute x15 -> x18, waiting for transfers between devices: 32 us -> 33.1 us  [shift(): lax.ppermute(value, axis, [(i, (i + step) % count) for i in range(count)])]
  transfers between devices with their start and end apart: 18 -> 21, of which waited for: 11 -> 13; matrix products, arithmetic and copies ran while one was open for 1% -> 1% of each run, Pallas kernels for 6% -> 16%
where the time goes in v8:
time: 111 us; the launch traced here: 110 us
  starting transfers between devices  39.8 us (36%)
  waiting for transfers between devices  37.9 us (34%)
  Pallas kernels  29.7 us (27%)
  local copies, waits for them, and re-layouts  1.72 us (2%)
    ppermute x18, starting transfers between devices, shift(): lax.ppermute(value, axis, [(i, (i + step) % count) for i in range(count)])  36.3 us
    ppermute x18, waiting for transfers between devices, shift(): lax.ppermute(value, axis, [(i, (i + step) % count) for i in range(count)])  33.1 us
    pallas_call x2, Pallas kernels, local_part(): pl.pallas_call(functools.partial(local_kernel, span, ways, piece, last),...  20.3 us
    all_to_all x1, waiting for transfers between devices, on_device(): lax.all_to_all(routed, 'seq', split_axis=0, concat_axis=0, tiled=True)  3.51 us
    all_to_all x1, starting transfers between devices, on_device(): lax.all_to_all(routed, 'seq', split_axis=0, concat_axis=0, tiled=True)  3.37 us
    pallas_call x1, Pallas kernels, fetch(): pl.pallas_call(fetch_kernel, in_specs=[HBM], out_specs=VMEM, out_shape=pl...  2.9 us
  transfers between devices with their start and end apart: 21, of which 13 were waited for; matrix products, arithmetic and copies ran while one was open for 1% of the time, Pallas kernels for 16%

profile of v8, /device:TPU:0, one launch (start us, length us, event | category | flops | bytes accessed | tf_op | source)
XLA Modules:
  0.0 110.4 jit_solution(3630055403724512686)
XLA Ops:
  0.6 10.1 %local_part.2 = (bf16[128,1024]{1,0:T(8,128)(2,1)}, bf16[128,1024]{1,0:T(8,128)(2,1)}, bf16[128,1024]{1,0:T(8,128)(2,1)}, bf16[128,1024]{1,0:T(8,128)(2,1)}) custom-call(f32[2]{0:T(128)} %scale_ref.4, f32[1,1024]{1,0:T(1,128)} %bitcast.18, bf16[1024,1024]{1,0:T(8,128)(2,1)} %bitcast.14, bf16[3,1024,256]{2,1,0:T(8,128)(2,1)} %bitcast.16, ...), custom_call_target="tpu_custom_call" | custom-call | flops 4294967296 | bytes 10485760 | tf_op jit(solution)/shard_map/local_part/pallas_call | solution.py:117
  10.8 3.1 %collective-permute-start = (bf16[128,1024]{1,0:T(8,128)(2,1)}, bf16[128,1024]{1,0:T(8,128)(2,1)S(1)}, u32[]{:S(2)}, u32[]{:S(2)}) collective-permute-start(bf16[128,1024]{1,0:T(8,128)(2,1)} %get-tuple-element.51), channel_id=1, source_target_pairs={{0,1},{1,2},{2,3},{3,0},{4,5},{5,6},{6,7},{7,4},{8,9},{9,10},{10,1... | collective-permute-start | bytes 786440 | tf_op jit(solution)/shard_map/ppermute | solution.py:343
  13.9 2.6 %collective-permute-start.1 = (bf16[128,1024]{1,0:T(8,128)(2,1)}, bf16[128,1024]{1,0:T(8,128)(2,1)S(1)}, u32[]{:S(2)}, u32[]{:S(2)}) collective-permute-start(bf16[128,1024]{1,0:T(8,128)(2,1)} %get-tuple-element.52), channel_id=1, source_target_pairs={{0,2},{1,3},{2,0},{3,1},{4,6},{5,7},{6,4},{7,5},{8,10},{9,11},{10,... | collective-permute-start | bytes 786440 | tf_op jit(solution)/shard_map/ppermute | solution.py:343
  16.5 1.3 %collective-permute-start.2 = (bf16[128,1024]{1,0:T(8,128)(2,1)}, bf16[128,1024]{1,0:T(8,128)(2,1)S(1)}, u32[]{:S(2)}, u32[]{:S(2)}) collective-permute-start(bf16[128,1024]{1,0:T(8,128)(2,1)} %get-tuple-element.55), channel_id=1, source_target_pairs={{0,3},{1,0},{2,1},{3,2},{4,7},{5,4},{6,5},{7,6},{8,11},{9,8},{10,9... | collective-permute-start | bytes 786440 | tf_op jit(solution)/shard_map/ppermute | solution.py:343
  17.8 10.1 %local_part.3 = (bf16[128,1024]{1,0:T(8,128)(2,1)}, bf16[128,1024]{1,0:T(8,128)(2,1)}, bf16[128,1024]{1,0:T(8,128)(2,1)}, bf16[128,1024]{1,0:T(8,128)(2,1)}, bf1...) custom-call(f32[2]{0:T(128)} %scale_ref.4, ...), custom_call_target="tpu_custom_call" | custom-call | flops 4294967296 | bytes 10485760 | tf_op jit(solution)/shard_map/local_part/pallas_call | solution.py:117
  28.0 5.8 %collective-permute-done.1.refs_2_ = bf16[128,1024]{1,0:T(8,128)(2,1)S(1)} collective-permute-done((bf16[128,1024]{1,0:T(8,128)(2,1)}, bf16[128,1024]{1,0:T(8,128)(2,1)S(1)}, u32[]{:S(2)}, u32[]{:S(2)}) %collective-permute-start.1) | collective-permute-done | bytes 262176 | tf_op jit(solution)/shard_map/ppermute | solution.py:343
  33.8 4.9 %collective-permute-start.3 = (bf16[64,512]{1,0:T(8,128)(2,1)S(1)}, bf16[64,512]{1,0:T(8,128)(2,1)S(1)}, u32[]{:S(2)}, u32[]{:S(2)}) collective-permute-start(bf16[64,512]{1,0:T(8,128)(2,1)S(1)} %get-tuple-element.58), channel_id=1, source_target_pairs={{0,1},{1,2},{2,3},{3,0},{4,5},{5,6},{6,7},{7,4},{8,9},{9,10},{10,1... | collective-permute-start | bytes 196616 | tf_op jit(solution)/shard_map/ppermute | solution.py:343
  38.6 3.3 %collective-permute-start.4 = (bf16[64,512]{1,0:T(8,128)(2,1)S(1)}, bf16[64,512]{1,0:T(8,128)(2,1)S(1)}, u32[]{:S(2)}, u32[]{:S(2)}) collective-permute-start(bf16[64,512]{1,0:T(8,128)(2,1)S(1)} %get-tuple-element.59), channel_id=1, source_target_pairs={{0,2},{1,3},{2,0},{3,1},{4,6},{5,7},{6,4},{7,5},{8,10},{9,11},{10,... | collective-permute-start | bytes 196616 | tf_op jit(solution)/shard_map/ppermute | solution.py:343
  42.3 1.5 %collective-permute-done.3 = bf16[64,512]{1,0:T(8,128)(2,1)S(1)} collective-permute-done((bf16[64,512]{1,0:T(8,128)(2,1)S(1)}, bf16[64,512]{1,0:T(8,128)(2,1)S(1)}, u32[]{:S(2)}, u32[]{:S(2)}) %collective-permute-start.3) | collective-permute-done | bytes 65568 | tf_op jit(solution)/shard_map/ppermute | solution.py:343
  43.8 1.9 %collective-permute-done.4 = bf16[64,512]{1,0:T(8,128)(2,1)S(1)} collective-permute-done((bf16[64,512]{1,0:T(8,128)(2,1)S(1)}, bf16[64,512]{1,0:T(8,128)(2,1)S(1)}, u32[]{:S(2)}, u32[]{:S(2)}) %collective-permute-start.4) | collective-permute-done | bytes 65568 | tf_op jit(solution)/shard_map/ppermute | solution.py:343
  47.0 2.4 %collective-permute-start.7 = (bf16[128,512]{1,0:T(8,128)(2,1)S(1)}, bf16[128,512]{1,0:T(8,128)(2,1)S(1)}, u32[]{:S(2)}, u32[]{:S(2)}) collective-permute-start(bf16[128,512]{1,0:T(8,128)(2,1)S(1)} %pad_maximum_fusion.1.refs_0_.own_ref), channel_id=1, source_target_pairs={{0,2},{1,3},{2,0},{3,1},{4,6},{5,7},{6,4},{7,5},{8,10},{9,11},{10,... | collective-permute-start | bytes 393224 | tf_op jit(solution)/shard_map/ppermute | solution.py:343
  50.5 2.9 %fetch.1.refs_4_ = bf16[3,2048,512]{2,1,0:T(8,128)(2,1)S(1)} custom-call(bf16[3,2048,512]{2,1,0:T(8,128)(2,1)} %bitcast.12), custom_call_target="tpu_custom_call" | custom-call | tf_op jit(solution)/shard_map/fetch/pallas_call | solution.py:173
  54.3 2.8 %collective-permute-done.7.refs_2_ = bf16[128,512]{1,0:T(8,128)(2,1)S(1)} collective-permute-done((bf16[128,512]{1,0:T(8,128)(2,1)S(1)}, bf16[128,512]{1,0:T(8,128)(2,1)S(1)}, u32[]{:S(2)}, u32[]{:S(2)}) %collective-permute-start.7) | collective-permute-done | bytes 131104 | tf_op jit(solution)/shard_map/ppermute | solution.py:343
  57.1 1.7 %global_heads.1 = (bf16[128,768]{1,0:T(8,128)(2,1)S(1)}, bf16[128,768]{1,0:T(8,128)(2,1)S(1)}) custom-call(s32[1]{0:T(128)} %bitcast.5.core_ref, s32[4]{0:T(128)S(1)} %and_select_fusion.ids_ref, f32[4,1,512]{2,1,0:T(1,128)S(1)} %bitcast.11, bf16[128,512]{1,0:T(8,128)(2,1)S(1)} %pad_maximum_fusion.1.refs_0_.own_ref, ...), custom_call_target="tpu_custom_call" | custom-call | tf_op jit(solution)/shard_map/global_heads/pallas_call | solution.py:207
  59.0 1.3 %collective-permute-done.9.given_ref = bf16[128,768]{1,0:T(8,128)(2,1)S(1)} collective-permute-done((bf16[128,768]{1,0:T(8,128)(2,1)S(1)}, bf16[128,768]{1,0:T(8,128)(2,1)S(1)}, u32[]{:S(2)}, u32[]{:S(2)}) %collective-permute-start.9) | collective-permute-done | bytes 196640 | tf_op jit(solution)/shard_map/ppermute | solution.py:360
  60.4 1.5 %collective-permute-start.10 = (bf16[256,512]{1,0:T(8,128)(2,1)S(1)}, bf16[256,512]{1,0:T(8,128)(2,1)S(1)}, u32[]{:S(2)}, u32[]{:S(2)}) collective-permute-start(bf16[256,512]{1,0:T(8,128)(2,1)S(1)} %pad_maximum_fusion), channel_id=1, source_target_pairs={{0,8},{4,12},{8,16},{12,20},{16,24},{20,28},{24,0},{28,4},{1,9},{5... | collective-permute-start | bytes 786440 | tf_op jit(solution)/shard_map/ppermute | solution.py:343
  61.9 1.5 %collective-permute-start.11 = (bf16[256,512]{1,0:T(8,128)(2,1)S(1)}, bf16[256,512]{1,0:T(8,128)(2,1)S(1)}, u32[]{:S(2)}, u32[]{:S(2)}) collective-permute-start(bf16[256,512]{1,0:T(8,128)(2,1)S(1)} %pad_maximum_fusion), channel_id=1, source_target_pairs={{0,16},{4,20},{8,24},{12,28},{16,0},{20,4},{24,8},{28,12},{1,17},{... | collective-permute-start | bytes 786440 | tf_op jit(solution)/shard_map/ppermute | solution.py:343
  63.4 1.4 %collective-permute-start.12 = (bf16[256,512]{1,0:T(8,128)(2,1)S(1)}, bf16[256,512]{1,0:T(8,128)(2,1)S(1)}, u32[]{:S(2)}, u32[]{:S(2)}) collective-permute-start(bf16[256,512]{1,0:T(8,128)(2,1)S(1)} %pad_maximum_fusion), channel_id=1, source_target_pairs={{0,24},{4,28},{8,0},{12,4},{16,8},{20,12},{24,16},{28,20},{1,25},{... | collective-permute-start | bytes 786440 | tf_op jit(solution)/shard_map/ppermute | solution.py:343
  64.9 3.3 %collective-permute-start.14 = (bf16[128,1024]{1,0:T(8,128)(2,1)S(1)}, bf16[128,1024]{1,0:T(8,128)(2,1)S(1)}, u32[]{:S(2)}, u32[]{:S(2)}) collective-permute-start(bf16[128,1024]{1,0:T(8,128)(2,1)S(1)} %copy-done.10), channel_id=1, source_target_pairs={{0,1},{1,2},{2,3},{3,0},{4,5},{5,6},{6,7},{7,4},{8,9},{9,10},{10,1... | collective-permute-start | bytes 786440 | tf_op jit(solution)/shard_map/ppermute | solution.py:343
  68.2 1.3 %collective-permute-start.18 = (bf16[128,1024]{1,0:T(8,128)(2,1)S(1)}, bf16[128,1024]{1,0:T(8,128)(2,1)S(1)}, u32[]{:S(2)}, u32[]{:S(2)}) collective-permute-start(bf16[128,1024]{1,0:T(8,128)(2,1)S(1)} %copy-done.9), channel_id=1, source_target_pairs={{0,2},{1,3},{2,0},{3,1},{4,6},{5,7},{6,4},{7,5},{8,10},{9,11},{10,... | collective-permute-start | bytes 786440 | tf_op jit(solution)/shard_map/ppermute | solution.py:343
  69.5 1.0 collective-permute-done.10.refs_0_
  70.5 4.8 %collective-permute-done.11.refs_1_ = bf16[256,512]{1,0:T(8,128)(2,1)S(1)} collective-permute-done((bf16[256,512]{1,0:T(8,128)(2,1)S(1)}, bf16[256,512]{1,0:T(8,128)(2,1)S(1)}, u32[]{:S(2)}, u32[]{:S(2)}) %collective-permute-start.11) | collective-permute-done | bytes 262176 | tf_op jit(solution)/shard_map/ppermute | solution.py:343
  75.4 1.7 %attend.1 = (bf16[128,256]{1,0:T(8,128)(2,1)S(1)}, bf16[128,256]{1,0:T(8,128)(2,1)S(1)}) custom-call(s32[1]{0:T(128)} %bitcast.6.me_ref, s32[4]{0:T(128)S(1)} %and_select_fusion.1.ids_ref, f32[4]{0:T(128)S(1)} %copy-done.7, bf16[128,768]{1,0:T(8,128)(2,1)S(1)} %get-tuple-element.63.kept_ref, bf16[128,768]{1,0:T(8,128)(2,1)S(1)} %collective-permute-done.9.given_ref, ...), custom_call_target="tpu_custom_call" | custom-call | flops 1 | bytes 1 | tf_op jit(solution)/shard_map/attend/pallas_call | solution.py:250
  77.2 4.0 %collective-permute-start.19 = (bf16[128,1024]{1,0:T(8,128)(2,1)S(1)}, bf16[128,1024]{1,0:T(8,128)(2,1)S(1)}, u32[]{:S(2)}, u32[]{:S(2)}) collective-permute-start(bf16[128,1024]{1,0:T(8,128)(2,1)S(1)} %copy-done.8), channel_id=1, source_target_pairs={{0,3},{1,0},{2,1},{3,2},{4,7},{5,4},{6,5},{7,6},{8,11},{9,8},{10,9... | collective-permute-start | bytes 786440 | tf_op jit(solution)/shard_map/ppermute | solution.py:343
  81.2 1.0 project.1
  82.8 1.3 %collective-permute-start.16 = (bf16[128,512]{1,0:T(8,128)(2,1)S(1)}, bf16[128,512]{1,0:T(8,128)(2,1)S(1)}, u32[]{:S(2)}, u32[]{:S(2)}) collective-permute-start(bf16[128,512]{1,0:T(8,128)(2,1)S(1)} %get-tuple-element.76), channel_id=1, source_target_pairs={{0,2},{1,3},{2,0},{3,1},{4,6},{5,7},{6,4},{7,5},{8,10},{9,11},{10,... | collective-permute-start | bytes 393224 | tf_op jit(solution)/shard_map/ppermute | solution.py:343
  84.0 2.4 %collective-permute-start.17 = (bf16[128,512]{1,0:T(8,128)(2,1)S(1)}, bf16[128,512]{1,0:T(8,128)(2,1)S(1)}, u32[]{:S(2)}, u32[]{:S(2)}) collective-permute-start(bf16[128,512]{1,0:T(8,128)(2,1)S(1)} %get-tuple-element.77), channel_id=1, source_target_pairs={{0,3},{1,0},{2,1},{3,2},{4,7},{5,4},{6,5},{7,6},{8,11},{9,8},{10,9... | collective-permute-start | bytes 393224 | tf_op jit(solution)/shard_map/ppermute | solution.py:343
  86.4 4.9 %collective-permute-done.15.refs_1_ = bf16[128,512]{1,0:T(8,128)(2,1)S(1)} collective-permute-done((bf16[128,512]{1,0:T(8,128)(2,1)S(1)}, bf16[128,512]{1,0:T(8,128)(2,1)S(1)}, u32[]{:S(2)}, u32[]{:S(2)}) %collective-permute-start.15) | collective-permute-done | bytes 131104 | tf_op jit(solution)/shard_map/ppermute | solution.py:343
  91.3 8.7 %collective-permute-done.16.refs_2_ = bf16[128,512]{1,0:T(8,128)(2,1)S(1)} collective-permute-done((bf16[128,512]{1,0:T(8,128)(2,1)S(1)}, bf16[128,512]{1,0:T(8,128)(2,1)S(1)}, u32[]{:S(2)}, u32[]{:S(2)}) %collective-permute-start.16) | collective-permute-done | bytes 131104 | tf_op jit(solution)/shard_map/ppermute | solution.py:343
  100.9 3.4 %all-to-all-start = ((bf16[8,16,512]{2,1,0:T(8,128)(2,1)}), bf16[8,16,512]{2,1,0:T(8,128)(2,1)S(1)}, u32[]{:S(2)}, u32[]{:S(2)}) async-start(bf16[8,16,512]{2,1,0:T(8,128)(2,1)} %bitcast.8), calls=%async_computation | async-start | bytes 262144 | tf_op jit(solution)/shard_map/all_to_all | solution.py:434
  105.3 1.0 reshape.82
  106.3 3.5 %all-to-all-done = bf16[8,16,512]{2,1,0:T(8,128)(2,1)S(1)} async-done(((bf16[8,16,512]{2,1,0:T(8,128)(2,1)}), bf16[8,16,512]{2,1,0:T(8,128)(2,1)S(1)}, u32[]{:S(2)}, u32[]{:S(2)}) %all-to-all-start) | async-done | bytes 131104 | tf_op jit(solution)/shard_map/all_to_all | solution.py:434
  (57 shorter events, 7.2 us)
Async XLA Ops:
  0.6 49.6 %copy-start = (s32[8,16]{1,0:T(8,128)S(1)}, s32[8,16]{1,0:T(8,128)}, u32[]{:S(2)}) copy-start(s32[8,16]{1,0:T(8,128)} %param.27) | copy-start | bytes 1540
  10.8 17.2 %collective-permute-start = (bf16[128,1024]{1,0:T(8,128)(2,1)}, bf16[128,1024]{1,0:T(8,128)(2,1)S(1)}, u32[]{:S(2)}, u32[]{:S(2)}) collective-permute-start(bf16[128,1024]{1,0:T(8,128)(2,1)} %get-tuple-element.51), channel_id=1, source_target_pairs={{0,1},{1,2},{2,3},{3,0},{4,5},{5,6},{6,7},{7,4},{8,9},{9,10},{10,1... | collective-permute-start | bytes 786440 | tf_op jit(solution)/shard_map/ppermute | solution.py:343
  13.9 19.9 %collective-permute-start.1 = (bf16[128,1024]{1,0:T(8,128)(2,1)}, bf16[128,1024]{1,0:T(8,128)(2,1)S(1)}, u32[]{:S(2)}, u32[]{:S(2)}) collective-permute-start(bf16[128,1024]{1,0:T(8,128)(2,1)} %get-tuple-element.52), channel_id=1, source_target_pairs={{0,2},{1,3},{2,0},{3,1},{4,6},{5,7},{6,4},{7,5},{8,10},{9,11},{10,... | collective-permute-start | bytes 786440 | tf_op jit(solution)/shard_map/ppermute | solution.py:343
  16.5 25.5 %copy-start.2 = (bf16[1024,256]{1,0:T(8,128)(2,1)S(1)}, bf16[1024,256]{1,0:T(8,128)(2,1)}, u32[]{:S(2)}) copy-start(bf16[1024,256]{1,0:T(8,128)(2,1)} %proj_ref.3) | copy-start | bytes 1572868
  16.5 25.5 %copy-start.5 = (bf16[128,1024]{1,0:T(8,128)(2,1)S(1)}, bf16[128,1024]{1,0:T(8,128)(2,1)}, u32[]{:S(2)}) copy-start(bf16[128,1024]{1,0:T(8,128)(2,1)} %get-tuple-element.46.refs_0_) | copy-start | bytes 786436
  16.5 25.5 %collective-permute-start.2 = (bf16[128,1024]{1,0:T(8,128)(2,1)}, bf16[128,1024]{1,0:T(8,128)(2,1)S(1)}, u32[]{:S(2)}, u32[]{:S(2)}) collective-permute-start(bf16[128,1024]{1,0:T(8,128)(2,1)} %get-tuple-element.55), channel_id=1, source_target_pairs={{0,3},{1,0},{2,1},{3,2},{4,7},{5,4},{6,5},{7,6},{8,11},{9,8},{10,9... | collective-permute-start | bytes 786440 | tf_op jit(solution)/shard_map/ppermute | solution.py:343
  33.8 10.0 %collective-permute-start.3 = (bf16[64,512]{1,0:T(8,128)(2,1)S(1)}, bf16[64,512]{1,0:T(8,128)(2,1)S(1)}, u32[]{:S(2)}, u32[]{:S(2)}) collective-permute-start(bf16[64,512]{1,0:T(8,128)(2,1)S(1)} %get-tuple-element.58), channel_id=1, source_target_pairs={{0,1},{1,2},{2,3},{3,0},{4,5},{5,6},{6,7},{7,4},{8,9},{9,10},{10,1... | collective-permute-start | bytes 196616 | tf_op jit(solution)/shard_map/ppermute | solution.py:343
  38.6 7.0 %collective-permute-start.4 = (bf16[64,512]{1,0:T(8,128)(2,1)S(1)}, bf16[64,512]{1,0:T(8,128)(2,1)S(1)}, u32[]{:S(2)}, u32[]{:S(2)}) collective-permute-start(bf16[64,512]{1,0:T(8,128)(2,1)S(1)} %get-tuple-element.59), channel_id=1, source_target_pairs={{0,2},{1,3},{2,0},{3,1},{4,6},{5,7},{6,4},{7,5},{8,10},{9,11},{10,... | collective-permute-start | bytes 196616 | tf_op jit(solution)/shard_map/ppermute | solution.py:343
  41.9 4.4 %collective-permute-start.5 = (bf16[64,512]{1,0:T(8,128)(2,1)S(1)}, bf16[64,512]{1,0:T(8,128)(2,1)S(1)}, u32[]{:S(2)}, u32[]{:S(2)}) collective-permute-start(bf16[64,512]{1,0:T(8,128)(2,1)S(1)} %get-tuple-element.60), channel_id=1, source_target_pairs={{0,3},{1,0},{2,1},{3,2},{4,7},{5,4},{6,5},{7,6},{8,11},{9,8},{10,9... | collective-permute-start | bytes 196616 | tf_op jit(solution)/shard_map/ppermute | solution.py:343
  46.4 7.9 %collective-permute-start.6 = (bf16[128,512]{1,0:T(8,128)(2,1)S(1)}, bf16[128,512]{1,0:T(8,128)(2,1)S(1)}, u32[]{:S(2)}, u32[]{:S(2)}) collective-permute-start(bf16[128,512]{1,0:T(8,128)(2,1)S(1)} %pad_maximum_fusion.1.refs_0_.own_ref), channel_id=1, source_target_pairs={{0,1},{1,2},{2,3},{3,0},{4,5},{5,6},{6,7},{7,4},{8,9},{9,10},{10,1... | collective-permute-start | bytes 393224 | tf_op jit(solution)/shard_map/ppermute | solution.py:343
  47.0 10.1 %collective-permute-start.7 = (bf16[128,512]{1,0:T(8,128)(2,1)S(1)}, bf16[128,512]{1,0:T(8,128)(2,1)S(1)}, u32[]{:S(2)}, u32[]{:S(2)}) collective-permute-start(bf16[128,512]{1,0:T(8,128)(2,1)S(1)} %pad_maximum_fusion.1.refs_0_.own_ref), channel_id=1, source_target_pairs={{0,2},{1,3},{2,0},{3,1},{4,6},{5,7},{6,4},{7,5},{8,10},{9,11},{10,... | collective-permute-start | bytes 393224 | tf_op jit(solution)/shard_map/ppermute | solution.py:343
  49.4 7.7 %collective-permute-start.8 = (bf16[128,512]{1,0:T(8,128)(2,1)S(1)}, bf16[128,512]{1,0:T(8,128)(2,1)S(1)}, u32[]{:S(2)}, u32[]{:S(2)}) collective-permute-start(bf16[128,512]{1,0:T(8,128)(2,1)S(1)} %pad_maximum_fusion.1.refs_0_.own_ref), channel_id=1, source_target_pairs={{0,3},{1,0},{2,1},{3,2},{4,7},{5,4},{6,5},{7,6},{8,11},{9,8},{10,9... | collective-permute-start | bytes 393224 | tf_op jit(solution)/shard_map/ppermute | solution.py:343
  50.5 6.6 %copy-start.6 = (f32[2048]{0:T(1024)S(1)}, f32[2048]{0:T(1024)}, u32[]{:S(2)}) copy-start(f32[2048]{0:T(1024)} %param.22) | copy-start | bytes 24580
  57.1 7.8 %copy-start.10 = (bf16[128,1024]{1,0:T(8,128)(2,1)S(1)}, bf16[128,1024]{1,0:T(8,128)(2,1)}, u32[]{:S(2)}) copy-start(bf16[128,1024]{1,0:T(8,128)(2,1)} %get-tuple-element.72) | copy-start | bytes 786436
  57.1 11.1 %copy-start.9 = (bf16[128,1024]{1,0:T(8,128)(2,1)S(1)}, bf16[128,1024]{1,0:T(8,128)(2,1)}, u32[]{:S(2)}) copy-start(bf16[128,1024]{1,0:T(8,128)(2,1)} %get-tuple-element.78) | copy-start | bytes 786436
  57.1 18.3 %copy-start.7 = (f32[4]{0:T(128)S(1)}, f32[4]{0:T(128)}, u32[]{:S(2)}) copy-start(f32[4]{0:T(128)} %scale_ref.5) | copy-start | bytes 52
  57.1 20.1 %copy-start.8 = (bf16[128,1024]{1,0:T(8,128)(2,1)S(1)}, bf16[128,1024]{1,0:T(8,128)(2,1)}, u32[]{:S(2)}) copy-start(bf16[128,1024]{1,0:T(8,128)(2,1)} %get-tuple-element.88) | copy-start | bytes 786436
  58.8 22.4 %copy-start.1 = (bf16[512,2048]{1,0:T(8,128)(2,1)S(1)}, bf16[512,2048]{1,0:T(8,128)(2,1)}, u32[]{:S(2)}) copy-start(bf16[512,2048]{1,0:T(8,128)(2,1)} %proj_ref.4) | copy-start | bytes 6291460
  58.8 1.5 %collective-permute-start.9 = (bf16[128,768]{1,0:T(8,128)(2,1)S(1)}, bf16[128,768]{1,0:T(8,128)(2,1)S(1)}, u32[]{:S(2)}, u32[]{:S(2)}) collective-permute-start(bf16[128,768]{1,0:T(8,128)(2,1)S(1)} %get-tuple-element.68), channel_id=1, source_target_pairs={{0,4},{4,0},{8,12},{12,8},{16,20},{20,16},{24,28},{28,24},{1,5},{5... | collective-permute-start | bytes 589832 | tf_op jit(solution)/shard_map/ppermute | solution.py:360
  60.4 10.1 %collective-permute-start.10 = (bf16[256,512]{1,0:T(8,128)(2,1)S(1)}, bf16[256,512]{1,0:T(8,128)(2,1)S(1)}, u32[]{:S(2)}, u32[]{:S(2)}) collective-permute-start(bf16[256,512]{1,0:T(8,128)(2,1)S(1)} %pad_maximum_fusion), channel_id=1, source_target_pairs={{0,8},{4,12},{8,16},{12,20},{16,24},{20,28},{24,0},{28,4},{1,9},{5... | collective-permute-start | bytes 786440 | tf_op jit(solution)/shard_map/ppermute | solution.py:343
  61.9 13.4 %collective-permute-start.11 = (bf16[256,512]{1,0:T(8,128)(2,1)S(1)}, bf16[256,512]{1,0:T(8,128)(2,1)S(1)}, u32[]{:S(2)}, u32[]{:S(2)}) collective-permute-start(bf16[256,512]{1,0:T(8,128)(2,1)S(1)} %pad_maximum_fusion), channel_id=1, source_target_pairs={{0,16},{4,20},{8,24},{12,28},{16,0},{20,4},{24,8},{28,12},{1,17},{... | collective-permute-start | bytes 786440 | tf_op jit(solution)/shard_map/ppermute | solution.py:343
  63.4 12.0 %collective-permute-start.12 = (bf16[256,512]{1,0:T(8,128)(2,1)S(1)}, bf16[256,512]{1,0:T(8,128)(2,1)S(1)}, u32[]{:S(2)}, u32[]{:S(2)}) collective-permute-start(bf16[256,512]{1,0:T(8,128)(2,1)S(1)} %pad_maximum_fusion), channel_id=1, source_target_pairs={{0,24},{4,28},{8,0},{12,4},{16,8},{20,12},{24,16},{28,20},{1,25},{... | collective-permute-start | bytes 786440 | tf_op jit(solution)/shard_map/ppermute | solution.py:343
  64.9 16.3 %collective-permute-start.14 = (bf16[128,1024]{1,0:T(8,128)(2,1)S(1)}, bf16[128,1024]{1,0:T(8,128)(2,1)S(1)}, u32[]{:S(2)}, u32[]{:S(2)}) collective-permute-start(bf16[128,1024]{1,0:T(8,128)(2,1)S(1)} %copy-done.10), channel_id=1, source_target_pairs={{0,1},{1,2},{2,3},{3,0},{4,5},{5,6},{6,7},{7,4},{8,9},{9,10},{10,1... | collective-permute-start | bytes 786440 | tf_op jit(solution)/shard_map/ppermute | solution.py:343
  68.2 18.3 %collective-permute-start.18 = (bf16[128,1024]{1,0:T(8,128)(2,1)S(1)}, bf16[128,1024]{1,0:T(8,128)(2,1)S(1)}, u32[]{:S(2)}, u32[]{:S(2)}) collective-permute-start(bf16[128,1024]{1,0:T(8,128)(2,1)S(1)} %copy-done.9), channel_id=1, source_target_pairs={{0,2},{1,3},{2,0},{3,1},{4,6},{5,7},{6,4},{7,5},{8,10},{9,11},{10,... | collective-permute-start | bytes 786440 | tf_op jit(solution)/shard_map/ppermute | solution.py:343
  75.4 28.9 %copy-start.3 = (bf16[256,1024]{1,0:T(8,128)(2,1)S(1)}, bf16[256,1024]{1,0:T(8,128)(2,1)}, u32[]{:S(2)}) copy-start(bf16[256,1024]{1,0:T(8,128)(2,1)} %proj_ref.5) | copy-start | bytes 1572868
  75.4 28.9 %copy-start.4 = (bf16[128,1024]{1,0:T(8,128)(2,1)S(1)}, bf16[128,1024]{1,0:T(8,128)(2,1)}, u32[]{:S(2)}) copy-start(bf16[128,1024]{1,0:T(8,128)(2,1)} %get-tuple-element.85.refs_1_) | copy-start | bytes 786436
  77.1 4.1 %collective-permute-start.13 = (bf16[128,256]{1,0:T(8,128)(2,1)S(1)}, bf16[128,256]{1,0:T(8,128)(2,1)S(1)}, u32[]{:S(2)}, u32[]{:S(2)}) collective-permute-start(bf16[128,256]{1,0:T(8,128)(2,1)S(1)} %get-tuple-element.71), channel_id=1, source_target_pairs={{0,4},{4,0},{8,12},{12,8},{16,20},{20,16},{24,28},{28,24},{1,5},{5... | collective-permute-start | bytes 196616 | tf_op jit(solution)/shard_map/ppermute | solution.py:360
  77.2 27.1 %collective-permute-start.19 = (bf16[128,1024]{1,0:T(8,128)(2,1)S(1)}, bf16[128,1024]{1,0:T(8,128)(2,1)S(1)}, u32[]{:S(2)}, u32[]{:S(2)}) collective-permute-start(bf16[128,1024]{1,0:T(8,128)(2,1)S(1)} %copy-done.8), channel_id=1, source_target_pairs={{0,3},{1,0},{2,1},{3,2},{4,7},{5,4},{6,5},{7,6},{8,11},{9,8},{10,9... | collective-permute-start | bytes 786440 | tf_op jit(solution)/shard_map/ppermute | solution.py:343
  82.3 9.1 %collective-permute-start.15 = (bf16[128,512]{1,0:T(8,128)(2,1)S(1)}, bf16[128,512]{1,0:T(8,128)(2,1)S(1)}, u32[]{:S(2)}, u32[]{:S(2)}) collective-permute-start(bf16[128,512]{1,0:T(8,128)(2,1)S(1)} %get-tuple-element.75), channel_id=1, source_target_pairs={{0,1},{1,2},{2,3},{3,0},{4,5},{5,6},{6,7},{7,4},{8,9},{9,10},{10,1... | collective-permute-start | bytes 393224 | tf_op jit(solution)/shard_map/ppermute | solution.py:343
  82.8 17.3 %collective-permute-start.16 = (bf16[128,512]{1,0:T(8,128)(2,1)S(1)}, bf16[128,512]{1,0:T(8,128)(2,1)S(1)}, u32[]{:S(2)}, u32[]{:S(2)}) collective-permute-start(bf16[128,512]{1,0:T(8,128)(2,1)S(1)} %get-tuple-element.76), channel_id=1, source_target_pairs={{0,2},{1,3},{2,0},{3,1},{4,6},{5,7},{6,4},{7,5},{8,10},{9,11},{10,... | collective-permute-start | bytes 393224 | tf_op jit(solution)/shard_map/ppermute | solution.py:343
  84.0 16.0 %collective-permute-start.17 = (bf16[128,512]{1,0:T(8,128)(2,1)S(1)}, bf16[128,512]{1,0:T(8,128)(2,1)S(1)}, u32[]{:S(2)}, u32[]{:S(2)}) collective-permute-start(bf16[128,512]{1,0:T(8,128)(2,1)S(1)} %get-tuple-element.77), channel_id=1, source_target_pairs={{0,3},{1,0},{2,1},{3,2},{4,7},{5,4},{6,5},{7,6},{8,11},{9,8},{10,9... | collective-permute-start | bytes 393224 | tf_op jit(solution)/shard_map/ppermute | solution.py:343
  100.9 8.8 %all-to-all-start = ((bf16[8,16,512]{2,1,0:T(8,128)(2,1)}), bf16[8,16,512]{2,1,0:T(8,128)(2,1)S(1)}, u32[]{:S(2)}, u32[]{:S(2)}) async-start(bf16[8,16,512]{2,1,0:T(8,128)(2,1)} %bitcast.8), calls=%async_computation | async-start | bytes 262144 | tf_op jit(solution)/shard_map/all_to_all | solution.py:434

commit v9 on v8

--- a/solution.py
+++ b/solution.py
@@ -183,9 +183,9 @@
 
 def heads_kernel(depth, core_ref, ids_ref, gain_ref, *refs):
     ways = gain_ref.shape[0]
-    shares, weight, outs = refs[:ways], refs[ways], refs[ways + 1 :]
-    width = shares[0].shape[1]
-    values = [s[...].astype(F32) for s in shares]
+    early, late, weight, outs = refs[:ways], refs[ways : 2 * ways], refs[2 * ways], refs[2 * ways + 1 :]
+    width = early[0].shape[1]
+    values = [jnp.concatenate([a[...], b[...]], axis=0).astype(F32) for a, b in zip(early, late)]
     square = sum(jnp.sum(v * v, axis=-1, keepdims=True) for v in values)
     factor = lax.rsqrt(square / (ways * width) + EPSILON)
     normed = [(v * factor * gain_ref[ids_ref[c]]).astype(BF16) for c, v in enumerate(values)]
@@ -202,16 +202,16 @@
             out[:, kind * size : (kind + 1) * size] = mixed.astype(BF16)
 
 
-def global_heads(depth, core, ids, gain, shares, qkv):
-    shape = jax.ShapeDtypeStruct((shares[0].shape[0], 3 * qkv.shape[2] // 2), BF16)
+def global_heads(depth, core, ids, gain, early, late, qkv):
+    shape = jax.ShapeDtypeStruct((2 * early[0].shape[0], 3 * qkv.shape[2] // 2), BF16)
     return pl.pallas_call(
         functools.partial(heads_kernel, depth),
-        in_specs=[SMEM, SMEM] + [VMEM] * (2 + len(shares)),
+        in_specs=[SMEM, SMEM] + [VMEM] * (2 + len(early) + len(late)),
         out_specs=(VMEM, VMEM),
         out_shape=(shape, shape),
         compiler_params=pltpu.CompilerParams(vmem_limit_bytes=8 * 2**20),
         name="global_heads",
-    )(core, ids, gain, *shares, qkv)
+    )(core, ids, gain, *early, *late, qkv)
 
 
 def attend_kernel(depth, me_ref, ids_ref, scale_ref, kept_ref, given_ref, *refs):
@@ -410,16 +410,17 @@
     early, _ = local_part(local_scale, rows, gain, weights, span, ways, False)
     early = scatter(early, "head")
     parts, chunks = local_part(local_scale, rows, gain, weights, span, ways, True)
-    chunks, early[1], early[2] = lax.optimization_barrier((chunks, early[1], early[2]))
+    chunks, early[1] = lax.optimization_barrier((chunks, early[1]))
     chunks = scatter(chunks, "head")
     early, early_share = finish_state(patch_proj, early, own)
+    early_shares = gather(early_share, "head")
     late_share = sum(p.astype(F32) for p in chunks).astype(BF16)
+    weight, late_share = lax.optimization_barrier((jnp.transpose(global_qkv, (1, 0, 2)), late_share))
+    late_shares = gather(late_share, "head")
     residual = jnp.concatenate([early_share, late_share], axis=0)
-    weight, residual = lax.optimization_barrier((jnp.transpose(global_qkv, (1, 0, 2)), residual))
-    shares = gather(residual, "head")
     ids = (me - jnp.arange(ways, dtype=jnp.int32)) % ways
     core = (seq % 2).reshape(1)
-    kept, given = global_heads(depth, core, ids, global_gain.reshape(ways, 1, -1), shares, fetch(weight))
+    kept, given = global_heads(depth, core, ids, global_gain.reshape(ways, 1, -1), early_shares, late_shares, fetch(weight))
     received = swap_cores(given, "seq")
     parts, received = lax.optimization_barrier((parts, received))
     half = kept.shape[1] // 3

time: 111 us -> 116 us (1.045)
  waiting for transfers between devices: 37.9 us -> 41.9 us
  starting transfers between devices: 39.8 us -> 41.2 us
    ppermute x18 -> x21, waiting for transfers between devices: 33.1 us -> 37.1 us  [shift(): lax.ppermute(value, axis, [(i, (i + step) % count) for i in range(count)])]
    ppermute x18 -> x21, starting transfers between devices: 36.3 us -> 37.7 us  [shift(): lax.ppermute(value, axis, [(i, (i + step) % count) for i in range(count)])]
  transfers between devices with their start and end apart: 21 -> 24, of which waited for: 13 -> 9; matrix products, arithmetic and copies ran while one was open for 1% -> 1% of each run, Pallas kernels for 16% -> 15%
where the time goes in v9:
time: 116 us
  waiting for transfers between devices  41.9 us (36%)
  starting transfers between devices  41.2 us (36%)
  Pallas kernels  29.6 us (26%)
  local copies, waits for them, and re-layouts  1.73 us (1%)
    ppermute x21, starting transfers between devices, shift(): lax.ppermute(value, axis, [(i, (i + step) % count) for i in range(count)])  37.7 us
    ppermute x21, waiting for transfers between devices, shift(): lax.ppermute(value, axis, [(i, (i + step) % count) for i in range(count)])  37.1 us
    pallas_call x2, Pallas kernels, local_part(): pl.pallas_call(functools.partial(local_kernel, span, ways, piece, last),...  20.2 us
    all_to_all x1, waiting for transfers between devices, on_device(): lax.all_to_all(routed, 'seq', split_axis=0, concat_axis=0, tiled=True)  3.51 us
    all_to_all x1, starting transfers between devices, on_device(): lax.all_to_all(routed, 'seq', split_axis=0, concat_axis=0, tiled=True)  3.37 us
    pallas_call x1, Pallas kernels, fetch(): pl.pallas_call(fetch_kernel, in_specs=[HBM], out_specs=VMEM, out_shape=pl...  2.89 us
  transfers between devices with their start and end apart: 24, of which 9 were waited for; matrix products, arithmetic and copies ran while one was open for 1% of the time, Pallas kernels for 15%

profile of v9, /device:TPU:0, one launch (start us, length us, event | category | flops | bytes accessed | tf_op | source)
XLA Modules:
  0.0 115.8 jit_solution(14426071330014725184)
XLA Ops:
  0.6 10.1 %local_part.2 = (bf16[128,1024]{1,0:T(8,128)(2,1)}, bf16[128,1024]{1,0:T(8,128)(2,1)}, bf16[128,1024]{1,0:T(8,128)(2,1)}, bf16[128,1024]{1,0:T(8,128)(2,1)}) custom-call(f32[2]{0:T(128)} %scale_ref.4, f32[1,1024]{1,0:T(1,128)} %bitcast.18, bf16[1024,1024]{1,0:T(8,128)(2,1)} %bitcast.14, bf16[3,1024,256]{2,1,0:T(8,128)(2,1)} %bitcast.16, ...), custom_call_target="tpu_custom_call" | custom-call | flops 4294967296 | bytes 10485760 | tf_op jit(solution)/shard_map/local_part/pallas_call | solution.py:117
  10.8 3.1 %collective-permute-start = (bf16[128,1024]{1,0:T(8,128)(2,1)}, bf16[128,1024]{1,0:T(8,128)(2,1)S(1)}, u32[]{:S(2)}, u32[]{:S(2)}) collective-permute-start(bf16[128,1024]{1,0:T(8,128)(2,1)} %get-tuple-element.50), channel_id=1, source_target_pairs={{0,1},{1,2},{2,3},{3,0},{4,5},{5,6},{6,7},{7,4},{8,9},{9,10},{10,1... | collective-permute-start | bytes 786440 | tf_op jit(solution)/shard_map/ppermute | solution.py:343
  13.8 2.6 %collective-permute-start.1 = (bf16[128,1024]{1,0:T(8,128)(2,1)}, bf16[128,1024]{1,0:T(8,128)(2,1)S(1)}, u32[]{:S(2)}, u32[]{:S(2)}) collective-permute-start(bf16[128,1024]{1,0:T(8,128)(2,1)} %get-tuple-element.52), channel_id=1, source_target_pairs={{0,2},{1,3},{2,0},{3,1},{4,6},{5,7},{6,4},{7,5},{8,10},{9,11},{10,... | collective-permute-start | bytes 786440 | tf_op jit(solution)/shard_map/ppermute | solution.py:343
  16.4 1.3 %collective-permute-start.2 = (bf16[128,1024]{1,0:T(8,128)(2,1)}, bf16[128,1024]{1,0:T(8,128)(2,1)S(1)}, u32[]{:S(2)}, u32[]{:S(2)}) collective-permute-start(bf16[128,1024]{1,0:T(8,128)(2,1)} %get-tuple-element.53), channel_id=1, source_target_pairs={{0,3},{1,0},{2,1},{3,2},{4,7},{5,4},{6,5},{7,6},{8,11},{9,8},{10,9... | collective-permute-start | bytes 786440 | tf_op jit(solution)/shard_map/ppermute | solution.py:343
  17.8 10.1 %local_part.3 = (bf16[128,1024]{1,0:T(8,128)(2,1)}, bf16[128,1024]{1,0:T(8,128)(2,1)}, bf16[128,1024]{1,0:T(8,128)(2,1)}, bf16[128,1024]{1,0:T(8,128)(2,1)}, bf1...) custom-call(f32[2]{0:T(128)} %scale_ref.4, ...), custom_call_target="tpu_custom_call" | custom-call | flops 4294967296 | bytes 10485760 | tf_op jit(solution)/shard_map/local_part/pallas_call | solution.py:117
  28.0 7.0 %collective-permute-start.3 = (bf16[64,512]{1,0:T(8,128)(2,1)S(1)}, bf16[64,512]{1,0:T(8,128)(2,1)S(1)}, u32[]{:S(2)}, u32[]{:S(2)}) collective-permute-start(bf16[64,512]{1,0:T(8,128)(2,1)S(1)} %get-tuple-element.56), channel_id=1, source_target_pairs={{0,1},{1,2},{2,3},{3,0},{4,5},{5,6},{6,7},{7,4},{8,9},{9,10},{10,1... | collective-permute-start | bytes 196616 | tf_op jit(solution)/shard_map/ppermute | solution.py:343
  35.0 2.0 %collective-permute-start.4 = (bf16[64,512]{1,0:T(8,128)(2,1)S(1)}, bf16[64,512]{1,0:T(8,128)(2,1)S(1)}, u32[]{:S(2)}, u32[]{:S(2)}) collective-permute-start(bf16[64,512]{1,0:T(8,128)(2,1)S(1)} %get-tuple-element.57), channel_id=1, source_target_pairs={{0,2},{1,3},{2,0},{3,1},{4,6},{5,7},{6,4},{7,5},{8,10},{9,11},{10,... | collective-permute-start | bytes 196616 | tf_op jit(solution)/shard_map/ppermute | solution.py:343
  36.9 2.9 %collective-permute-start.5 = (bf16[64,512]{1,0:T(8,128)(2,1)S(1)}, bf16[64,512]{1,0:T(8,128)(2,1)S(1)}, u32[]{:S(2)}, u32[]{:S(2)}) collective-permute-start(bf16[64,512]{1,0:T(8,128)(2,1)S(1)} %get-tuple-element.58), channel_id=1, source_target_pairs={{0,3},{1,0},{2,1},{3,2},{4,7},{5,4},{6,5},{7,6},{8,11},{9,8},{10,9... | collective-permute-start | bytes 196616 | tf_op jit(solution)/shard_map/ppermute | solution.py:343
  40.4 4.1 %collective-permute-start.8 = (bf16[64,512]{1,0:T(8,128)(2,1)S(1)}, bf16[64,512]{1,0:T(8,128)(2,1)S(1)}, u32[]{:S(2)}, u32[]{:S(2)}) collective-permute-start(bf16[64,512]{1,0:T(8,128)(2,1)S(1)} %get-tuple-element.54.refs_0_), channel_id=1, source_target_pairs={{0,3},{1,0},{2,1},{3,2},{4,7},{5,4},{6,5},{7,6},{8,11},{9,8},{10,9... | collective-permute-start | bytes 196616 | tf_op jit(solution)/shard_map/ppermute | solution.py:343
  45.2 3.3 %collective-permute-start.11 = (bf16[64,512]{1,0:T(8,128)(2,1)S(1)}, bf16[64,512]{1,0:T(8,128)(2,1)S(1)}, u32[]{:S(2)}, u32[]{:S(2)}) collective-permute-start(bf16[64,512]{1,0:T(8,128)(2,1)S(1)} %add_convert_fusion.refs_4_), channel_id=1, source_target_pairs={{0,3},{1,0},{2,1},{3,2},{4,7},{5,4},{6,5},{7,6},{8,11},{9,8},{10,9... | collective-permute-start | bytes 196616 | tf_op jit(solution)/shard_map/ppermute | solution.py:343
  48.5 1.0 collective-permute-start.10
  49.6 2.9 %fetch.1.refs_8_ = bf16[3,2048,512]{2,1,0:T(8,128)(2,1)S(1)} custom-call(bf16[3,2048,512]{2,1,0:T(8,128)(2,1)} %bitcast.12), custom_call_target="tpu_custom_call" | custom-call | tf_op jit(solution)/shard_map/fetch/pallas_call | solution.py:173
  53.3 2.9 %collective-permute-done.10.refs_6_ = bf16[64,512]{1,0:T(8,128)(2,1)S(1)} collective-permute-done((bf16[64,512]{1,0:T(8,128)(2,1)S(1)}, bf16[64,512]{1,0:T(8,128)(2,1)S(1)}, u32[]{:S(2)}, u32[]{:S(2)}) %collective-permute-start.10) | collective-permute-done | bytes 65568 | tf_op jit(solution)/shard_map/ppermute | solution.py:343
  56.2 1.7 %global_heads.1 = (bf16[128,768]{1,0:T(8,128)(2,1)S(1)}, bf16[128,768]{1,0:T(8,128)(2,1)S(1)}) custom-call(s32[1]{0:T(128)} %bitcast.5.core_ref, s32[4]{0:T(128)S(1)} %and_select_fusion.ids_ref, f32[4,1,512]{2,1,0:T(1,128)S(1)} %bitcast.11, bf16[64,512]{1,0:T(8,128)(2,1)S(1)} %get-tuple-element.54.refs_0_, ...), custom_call_target="tpu_custom_call" | custom-call | tf_op jit(solution)/shard_map/global_heads/pallas_call | solution.py:207
  58.1 1.3 %collective-permute-done.12.given_ref = bf16[128,768]{1,0:T(8,128)(2,1)S(1)} collective-permute-done((bf16[128,768]{1,0:T(8,128)(2,1)S(1)}, bf16[128,768]{1,0:T(8,128)(2,1)S(1)}, u32[]{:S(2)}, u32[]{:S(2)}) %collective-permute-start.12) | collective-permute-done | bytes 196640 | tf_op jit(solution)/shard_map/ppermute | solution.py:360
  59.5 2.5 %collective-permute-start.15 = (bf16[256,512]{1,0:T(8,128)(2,1)S(1)}, bf16[256,512]{1,0:T(8,128)(2,1)S(1)}, u32[]{:S(2)}, u32[]{:S(2)}) collective-permute-start(bf16[256,512]{1,0:T(8,128)(2,1)S(1)} %pad_maximum_fusion), channel_id=1, source_target_pairs={{0,24},{4,28},{8,0},{12,4},{16,8},{20,12},{24,16},{28,20},{1,25},{... | collective-permute-start | bytes 786440 | tf_op jit(solution)/shard_map/ppermute | solution.py:343
  63.1 5.6 %collective-permute-done.15.refs_2_ = bf16[256,512]{1,0:T(8,128)(2,1)S(1)} collective-permute-done((bf16[256,512]{1,0:T(8,128)(2,1)S(1)}, bf16[256,512]{1,0:T(8,128)(2,1)S(1)}, u32[]{:S(2)}, u32[]{:S(2)}) %collective-permute-start.15) | collective-permute-done | bytes 262176 | tf_op jit(solution)/shard_map/ppermute | solution.py:343
  68.7 7.0 %collective-permute-done.14.refs_1_ = bf16[256,512]{1,0:T(8,128)(2,1)S(1)} collective-permute-done((bf16[256,512]{1,0:T(8,128)(2,1)S(1)}, bf16[256,512]{1,0:T(8,128)(2,1)S(1)}, u32[]{:S(2)}, u32[]{:S(2)}) %collective-permute-start.14) | collective-permute-done | bytes 262176 | tf_op jit(solution)/shard_map/ppermute | solution.py:343
  75.7 1.7 %attend.1 = (bf16[128,256]{1,0:T(8,128)(2,1)S(1)}, bf16[128,256]{1,0:T(8,128)(2,1)S(1)}) custom-call(s32[1]{0:T(128)} %bitcast.6.me_ref, s32[4]{0:T(128)S(1)} %and_select_fusion.1.ids_ref, f32[4]{0:T(128)S(1)} %copy-done.7, bf16[128,768]{1,0:T(8,128)(2,1)S(1)} %get-tuple-element.61.kept_ref, bf16[128,768]{1,0:T(8,128)(2,1)S(1)} %collective-permute-done.12.given_ref, ...), custom_call_target="tpu_custom_call" | custom-call | flops 1 | bytes 1 | tf_op jit(solution)/shard_map/attend/pallas_call | solution.py:250
  78.2 0.8 collective-permute-start.22
  79.0 1.0 project.1
  80.0 1.3 %collective-permute-start.18 = (bf16[128,512]{1,0:T(8,128)(2,1)S(1)}, bf16[128,512]{1,0:T(8,128)(2,1)S(1)}, u32[]{:S(2)}, u32[]{:S(2)}) collective-permute-start(bf16[128,512]{1,0:T(8,128)(2,1)S(1)} %get-tuple-element.73), channel_id=1, source_target_pairs={{0,1},{1,2},{2,3},{3,0},{4,5},{5,6},{6,7},{7,4},{8,9},{9,10},{10,1... | collective-permute-start | bytes 393224 | tf_op jit(solution)/shard_map/ppermute | solution.py:343
  81.3 2.3 %collective-permute-start.19 = (bf16[128,512]{1,0:T(8,128)(2,1)S(1)}, bf16[128,512]{1,0:T(8,128)(2,1)S(1)}, u32[]{:S(2)}, u32[]{:S(2)}) collective-permute-start(bf16[128,512]{1,0:T(8,128)(2,1)S(1)} %get-tuple-element.74), channel_id=1, source_target_pairs={{0,2},{1,3},{2,0},{3,1},{4,6},{5,7},{6,4},{7,5},{8,10},{9,11},{10,... | collective-permute-start | bytes 393224 | tf_op jit(solution)/shard_map/ppermute | solution.py:343
  83.6 0.9 collective-permute-start.20
  84.5 7.3 %collective-permute-done.21.refs_3_ = bf16[128,1024]{1,0:T(8,128)(2,1)S(1)} collective-permute-done((bf16[128,1024]{1,0:T(8,128)(2,1)S(1)}, bf16[128,1024]{1,0:T(8,128)(2,1)S(1)}, u32[]{:S(2)}, u32[]{:S(2)}) %collective-permute-start.21) | collective-permute-done | bytes 262176 | tf_op jit(solution)/shard_map/ppermute | solution.py:343
  91.8 2.8 %collective-permute-done.18.refs_1_ = bf16[128,512]{1,0:T(8,128)(2,1)S(1)} collective-permute-done((bf16[128,512]{1,0:T(8,128)(2,1)S(1)}, bf16[128,512]{1,0:T(8,128)(2,1)S(1)}, u32[]{:S(2)}, u32[]{:S(2)}) %collective-permute-start.18) | collective-permute-done | bytes 131104 | tf_op jit(solution)/shard_map/ppermute | solution.py:343
  94.7 10.8 %collective-permute-done.19.refs_2_ = bf16[128,512]{1,0:T(8,128)(2,1)S(1)} collective-permute-done((bf16[128,512]{1,0:T(8,128)(2,1)S(1)}, bf16[128,512]{1,0:T(8,128)(2,1)S(1)}, u32[]{:S(2)}, u32[]{:S(2)}) %collective-permute-start.19) | collective-permute-done | bytes 131104 | tf_op jit(solution)/shard_map/ppermute | solution.py:343
  105.4 0.9 finish_result.1
  106.3 3.4 %all-to-all-start = ((bf16[8,16,512]{2,1,0:T(8,128)(2,1)}), bf16[8,16,512]{2,1,0:T(8,128)(2,1)S(1)}, u32[]{:S(2)}, u32[]{:S(2)}) async-start(bf16[8,16,512]{2,1,0:T(8,128)(2,1)} %bitcast.8), calls=%async_computation | async-start | bytes 262144 | tf_op jit(solution)/shard_map/all_to_all | solution.py:435
  109.7 0.9 finish_bytes.1
  110.7 1.0 reshape.82
  111.7 3.5 %all-to-all-done = bf16[8,16,512]{2,1,0:T(8,128)(2,1)S(1)} async-done(((bf16[8,16,512]{2,1,0:T(8,128)(2,1)}), bf16[8,16,512]{2,1,0:T(8,128)(2,1)S(1)}, u32[]{:S(2)}, u32[]{:S(2)}) %all-to-all-start) | async-done | bytes 131104 | tf_op jit(solution)/shard_map/all_to_all | solution.py:435
  (63 shorter events, 4.8 us)
Async XLA Ops:
  0.6 27.3 %copy-start = (s32[8,16]{1,0:T(8,128)S(1)}, s32[8,16]{1,0:T(8,128)}, u32[]{:S(2)}) copy-start(s32[8,16]{1,0:T(8,128)} %param.27) | copy-start | bytes 1540
  10.8 17.2 %collective-permute-start = (bf16[128,1024]{1,0:T(8,128)(2,1)}, bf16[128,1024]{1,0:T(8,128)(2,1)S(1)}, u32[]{:S(2)}, u32[]{:S(2)}) collective-permute-start(bf16[128,1024]{1,0:T(8,128)(2,1)} %get-tuple-element.50), channel_id=1, source_target_pairs={{0,1},{1,2},{2,3},{3,0},{4,5},{5,6},{6,7},{7,4},{8,9},{9,10},{10,1... | collective-permute-start | bytes 786440 | tf_op jit(solution)/shard_map/ppermute | solution.py:343
  13.8 26.2 %collective-permute-start.1 = (bf16[128,1024]{1,0:T(8,128)(2,1)}, bf16[128,1024]{1,0:T(8,128)(2,1)S(1)}, u32[]{:S(2)}, u32[]{:S(2)}) collective-permute-start(bf16[128,1024]{1,0:T(8,128)(2,1)} %get-tuple-element.52), channel_id=1, source_target_pairs={{0,2},{1,3},{2,0},{3,1},{4,6},{5,7},{6,4},{7,5},{8,10},{9,11},{10,... | collective-permute-start | bytes 786440 | tf_op jit(solution)/shard_map/ppermute | solution.py:343
  16.4 23.6 %copy-start.2 = (bf16[1024,256]{1,0:T(8,128)(2,1)S(1)}, bf16[1024,256]{1,0:T(8,128)(2,1)}, u32[]{:S(2)}) copy-start(bf16[1024,256]{1,0:T(8,128)(2,1)} %proj_ref.3) | copy-start | bytes 1572868
  16.4 23.6 %copy-start.5 = (bf16[128,1024]{1,0:T(8,128)(2,1)S(1)}, bf16[128,1024]{1,0:T(8,128)(2,1)}, u32[]{:S(2)}) copy-start(bf16[128,1024]{1,0:T(8,128)(2,1)} %get-tuple-element.45.refs_0_) | copy-start | bytes 786436
  16.4 23.6 %collective-permute-start.2 = (bf16[128,1024]{1,0:T(8,128)(2,1)}, bf16[128,1024]{1,0:T(8,128)(2,1)S(1)}, u32[]{:S(2)}, u32[]{:S(2)}) collective-permute-start(bf16[128,1024]{1,0:T(8,128)(2,1)} %get-tuple-element.53), channel_id=1, source_target_pairs={{0,3},{1,0},{2,1},{3,2},{4,7},{5,4},{6,5},{7,6},{8,11},{9,8},{10,9... | collective-permute-start | bytes 786440 | tf_op jit(solution)/shard_map/ppermute | solution.py:343
  28.0 16.7 %collective-permute-start.3 = (bf16[64,512]{1,0:T(8,128)(2,1)S(1)}, bf16[64,512]{1,0:T(8,128)(2,1)S(1)}, u32[]{:S(2)}, u32[]{:S(2)}) collective-permute-start(bf16[64,512]{1,0:T(8,128)(2,1)S(1)} %get-tuple-element.56), channel_id=1, source_target_pairs={{0,1},{1,2},{2,3},{3,0},{4,5},{5,6},{6,7},{7,4},{8,9},{9,10},{10,1... | collective-permute-start | bytes 196616 | tf_op jit(solution)/shard_map/ppermute | solution.py:343
  35.0 10.2 %collective-permute-start.4 = (bf16[64,512]{1,0:T(8,128)(2,1)S(1)}, bf16[64,512]{1,0:T(8,128)(2,1)S(1)}, u32[]{:S(2)}, u32[]{:S(2)}) collective-permute-start(bf16[64,512]{1,0:T(8,128)(2,1)S(1)} %get-tuple-element.57), channel_id=1, source_target_pairs={{0,2},{1,3},{2,0},{3,1},{4,6},{5,7},{6,4},{7,5},{8,10},{9,11},{10,... | collective-permute-start | bytes 196616 | tf_op jit(solution)/shard_map/ppermute | solution.py:343
  36.9 8.2 %collective-permute-start.5 = (bf16[64,512]{1,0:T(8,128)(2,1)S(1)}, bf16[64,512]{1,0:T(8,128)(2,1)S(1)}, u32[]{:S(2)}, u32[]{:S(2)}) collective-permute-start(bf16[64,512]{1,0:T(8,128)(2,1)S(1)} %get-tuple-element.58), channel_id=1, source_target_pairs={{0,3},{1,0},{2,1},{3,2},{4,7},{5,4},{6,5},{7,6},{8,11},{9,8},{10,9... | collective-permute-start | bytes 196616 | tf_op jit(solution)/shard_map/ppermute | solution.py:343
  40.4 9.2 %collective-permute-start.8 = (bf16[64,512]{1,0:T(8,128)(2,1)S(1)}, bf16[64,512]{1,0:T(8,128)(2,1)S(1)}, u32[]{:S(2)}, u32[]{:S(2)}) collective-permute-start(bf16[64,512]{1,0:T(8,128)(2,1)S(1)} %get-tuple-element.54.refs_0_), channel_id=1, source_target_pairs={{0,3},{1,0},{2,1},{3,2},{4,7},{5,4},{6,5},{7,6},{8,11},{9,8},{10,9... | collective-permute-start | bytes 196616 | tf_op jit(solution)/shard_map/ppermute | solution.py:343
  44.5 8.7 %collective-permute-start.7 = (bf16[64,512]{1,0:T(8,128)(2,1)S(1)}, bf16[64,512]{1,0:T(8,128)(2,1)S(1)}, u32[]{:S(2)}, u32[]{:S(2)}) collective-permute-start(bf16[64,512]{1,0:T(8,128)(2,1)S(1)} %get-tuple-element.54.refs_0_), channel_id=1, source_target_pairs={{0,2},{1,3},{2,0},{3,1},{4,6},{5,7},{6,4},{7,5},{8,10},{9,11},{10,... | collective-permute-start | bytes 196616 | tf_op jit(solution)/shard_map/ppermute | solution.py:343
  44.6 8.7 %collective-permute-start.6 = (bf16[64,512]{1,0:T(8,128)(2,1)S(1)}, bf16[64,512]{1,0:T(8,128)(2,1)S(1)}, u32[]{:S(2)}, u32[]{:S(2)}) collective-permute-start(bf16[64,512]{1,0:T(8,128)(2,1)S(1)} %get-tuple-element.54.refs_0_), channel_id=1, source_target_pairs={{0,1},{1,2},{2,3},{3,0},{4,5},{5,6},{6,7},{7,4},{8,9},{9,10},{10,1... | collective-permute-start | bytes 196616 | tf_op jit(solution)/shard_map/ppermute | solution.py:343
  45.2 8.0 %collective-permute-start.11 = (bf16[64,512]{1,0:T(8,128)(2,1)S(1)}, bf16[64,512]{1,0:T(8,128)(2,1)S(1)}, u32[]{:S(2)}, u32[]{:S(2)}) collective-permute-start(bf16[64,512]{1,0:T(8,128)(2,1)S(1)} %add_convert_fusion.refs_4_), channel_id=1, source_target_pairs={{0,3},{1,0},{2,1},{3,2},{4,7},{5,4},{6,5},{7,6},{8,11},{9,8},{10,9... | collective-permute-start | bytes 196616 | tf_op jit(solution)/shard_map/ppermute | solution.py:343
  48.5 7.6 %collective-permute-start.10 = (bf16[64,512]{1,0:T(8,128)(2,1)S(1)}, bf16[64,512]{1,0:T(8,128)(2,1)S(1)}, u32[]{:S(2)}, u32[]{:S(2)}) collective-permute-start(bf16[64,512]{1,0:T(8,128)(2,1)S(1)} %add_convert_fusion.refs_4_), channel_id=1, source_target_pairs={{0,2},{1,3},{2,0},{3,1},{4,6},{5,7},{6,4},{7,5},{8,10},{9,11},{10,... | collective-permute-start | bytes 196616 | tf_op jit(solution)/shard_map/ppermute | solution.py:343
  49.6 6.6 %collective-permute-start.9 = (bf16[64,512]{1,0:T(8,128)(2,1)S(1)}, bf16[64,512]{1,0:T(8,128)(2,1)S(1)}, u32[]{:S(2)}, u32[]{:S(2)}) collective-permute-start(bf16[64,512]{1,0:T(8,128)(2,1)S(1)} %add_convert_fusion.refs_4_), channel_id=1, source_target_pairs={{0,1},{1,2},{2,3},{3,0},{4,5},{5,6},{6,7},{7,4},{8,9},{9,10},{10,1... | collective-permute-start | bytes 196616 | tf_op jit(solution)/shard_map/ppermute | solution.py:343
  56.2 21.3 %copy-start.9 = (bf16[128,1024]{1,0:T(8,128)(2,1)S(1)}, bf16[128,1024]{1,0:T(8,128)(2,1)}, u32[]{:S(2)}) copy-start(bf16[128,1024]{1,0:T(8,128)(2,1)} %get-tuple-element.76) | copy-start | bytes 786436
  56.2 22.0 %copy-start.8 = (bf16[128,1024]{1,0:T(8,128)(2,1)S(1)}, bf16[128,1024]{1,0:T(8,128)(2,1)}, u32[]{:S(2)}) copy-start(bf16[128,1024]{1,0:T(8,128)(2,1)} %get-tuple-element.86) | copy-start | bytes 786436
  57.9 21.1 %copy-start.1 = (bf16[512,2048]{1,0:T(8,128)(2,1)S(1)}, bf16[512,2048]{1,0:T(8,128)(2,1)}, u32[]{:S(2)}) copy-start(bf16[512,2048]{1,0:T(8,128)(2,1)} %proj_ref.4) | copy-start | bytes 6291460
  57.9 1.5 %collective-permute-start.12 = (bf16[128,768]{1,0:T(8,128)(2,1)S(1)}, bf16[128,768]{1,0:T(8,128)(2,1)S(1)}, u32[]{:S(2)}, u32[]{:S(2)}) collective-permute-start(bf16[128,768]{1,0:T(8,128)(2,1)S(1)} %get-tuple-element.66), channel_id=1, source_target_pairs={{0,4},{4,0},{8,12},{12,8},{16,20},{20,16},{24,28},{28,24},{1,5},{5... | collective-permute-start | bytes 589832 | tf_op jit(solution)/shard_map/ppermute | solution.py:360
  59.5 9.2 %collective-permute-start.15 = (bf16[256,512]{1,0:T(8,128)(2,1)S(1)}, bf16[256,512]{1,0:T(8,128)(2,1)S(1)}, u32[]{:S(2)}, u32[]{:S(2)}) collective-permute-start(bf16[256,512]{1,0:T(8,128)(2,1)S(1)} %pad_maximum_fusion), channel_id=1, source_target_pairs={{0,24},{4,28},{8,0},{12,4},{16,8},{20,12},{24,16},{28,20},{1,25},{... | collective-permute-start | bytes 786440 | tf_op jit(solution)/shard_map/ppermute | solution.py:343
  62.0 13.7 %collective-permute-start.14 = (bf16[256,512]{1,0:T(8,128)(2,1)S(1)}, bf16[256,512]{1,0:T(8,128)(2,1)S(1)}, u32[]{:S(2)}, u32[]{:S(2)}) collective-permute-start(bf16[256,512]{1,0:T(8,128)(2,1)S(1)} %pad_maximum_fusion), channel_id=1, source_target_pairs={{0,16},{4,20},{8,24},{12,28},{16,0},{20,4},{24,8},{28,12},{1,17},{... | collective-permute-start | bytes 786440 | tf_op jit(solution)/shard_map/ppermute | solution.py:343
  62.5 13.2 %collective-permute-start.13 = (bf16[256,512]{1,0:T(8,128)(2,1)S(1)}, bf16[256,512]{1,0:T(8,128)(2,1)S(1)}, u32[]{:S(2)}, u32[]{:S(2)}) collective-permute-start(bf16[256,512]{1,0:T(8,128)(2,1)S(1)} %pad_maximum_fusion), channel_id=1, source_target_pairs={{0,8},{4,12},{8,16},{12,20},{16,24},{20,28},{24,0},{28,4},{1,9},{5... | collective-permute-start | bytes 786440 | tf_op jit(solution)/shard_map/ppermute | solution.py:343
  63.1 15.9 %collective-permute-start.17 = (bf16[128,1024]{1,0:T(8,128)(2,1)S(1)}, bf16[128,1024]{1,0:T(8,128)(2,1)S(1)}, u32[]{:S(2)}, u32[]{:S(2)}) collective-permute-start(bf16[128,1024]{1,0:T(8,128)(2,1)S(1)} %copy-done.10), channel_id=1, source_target_pairs={{0,1},{1,2},{2,3},{3,0},{4,5},{5,6},{6,7},{7,4},{8,9},{9,10},{10,1... | collective-permute-start | bytes 786440 | tf_op jit(solution)/shard_map/ppermute | solution.py:343
  75.7 34.1 %copy-start.3 = (bf16[256,1024]{1,0:T(8,128)(2,1)S(1)}, bf16[256,1024]{1,0:T(8,128)(2,1)}, u32[]{:S(2)}) copy-start(bf16[256,1024]{1,0:T(8,128)(2,1)} %proj_ref.5) | copy-start | bytes 1572868
  75.7 34.1 %copy-start.4 = (bf16[128,1024]{1,0:T(8,128)(2,1)S(1)}, bf16[128,1024]{1,0:T(8,128)(2,1)}, u32[]{:S(2)}) copy-start(bf16[128,1024]{1,0:T(8,128)(2,1)} %get-tuple-element.83.refs_1_) | copy-start | bytes 786436
  77.4 1.6 %collective-permute-start.16 = (bf16[128,256]{1,0:T(8,128)(2,1)S(1)}, bf16[128,256]{1,0:T(8,128)(2,1)S(1)}, u32[]{:S(2)}, u32[]{:S(2)}) collective-permute-start(bf16[128,256]{1,0:T(8,128)(2,1)S(1)} %get-tuple-element.69), channel_id=1, source_target_pairs={{0,4},{4,0},{8,12},{12,8},{16,20},{20,16},{24,28},{28,24},{1,5},{5... | collective-permute-start | bytes 196616 | tf_op jit(solution)/shard_map/ppermute | solution.py:360
  77.5 14.3 %collective-permute-start.21 = (bf16[128,1024]{1,0:T(8,128)(2,1)S(1)}, bf16[128,1024]{1,0:T(8,128)(2,1)S(1)}, u32[]{:S(2)}, u32[]{:S(2)}) collective-permute-start(bf16[128,1024]{1,0:T(8,128)(2,1)S(1)} %copy-done.9), channel_id=1, source_target_pairs={{0,2},{1,3},{2,0},{3,1},{4,6},{5,7},{6,4},{7,5},{8,10},{9,11},{10,... | collective-permute-start | bytes 786440 | tf_op jit(solution)/shard_map/ppermute | solution.py:343
  78.2 31.5 %collective-permute-start.22 = (bf16[128,1024]{1,0:T(8,128)(2,1)S(1)}, bf16[128,1024]{1,0:T(8,128)(2,1)S(1)}, u32[]{:S(2)}, u32[]{:S(2)}) collective-permute-start(bf16[128,1024]{1,0:T(8,128)(2,1)S(1)} %copy-done.8), channel_id=1, source_target_pairs={{0,3},{1,0},{2,1},{3,2},{4,7},{5,4},{6,5},{7,6},{8,11},{9,8},{10,9... | collective-permute-start | bytes 786440 | tf_op jit(solution)/shard_map/ppermute | solution.py:343
  80.0 14.6 %collective-permute-start.18 = (bf16[128,512]{1,0:T(8,128)(2,1)S(1)}, bf16[128,512]{1,0:T(8,128)(2,1)S(1)}, u32[]{:S(2)}, u32[]{:S(2)}) collective-permute-start(bf16[128,512]{1,0:T(8,128)(2,1)S(1)} %get-tuple-element.73), channel_id=1, source_target_pairs={{0,1},{1,2},{2,3},{3,0},{4,5},{5,6},{6,7},{7,4},{8,9},{9,10},{10,1... | collective-permute-start | bytes 393224 | tf_op jit(solution)/shard_map/ppermute | solution.py:343
  81.3 24.1 %collective-permute-start.19 = (bf16[128,512]{1,0:T(8,128)(2,1)S(1)}, bf16[128,512]{1,0:T(8,128)(2,1)S(1)}, u32[]{:S(2)}, u32[]{:S(2)}) collective-permute-start(bf16[128,512]{1,0:T(8,128)(2,1)S(1)} %get-tuple-element.74), channel_id=1, source_target_pairs={{0,2},{1,3},{2,0},{3,1},{4,6},{5,7},{6,4},{7,5},{8,10},{9,11},{10,... | collective-permute-start | bytes 393224 | tf_op jit(solution)/shard_map/ppermute | solution.py:343
  83.6 21.8 %collective-permute-start.20 = (bf16[128,512]{1,0:T(8,128)(2,1)S(1)}, bf16[128,512]{1,0:T(8,128)(2,1)S(1)}, u32[]{:S(2)}, u32[]{:S(2)}) collective-permute-start(bf16[128,512]{1,0:T(8,128)(2,1)S(1)} %get-tuple-element.75), channel_id=1, source_target_pairs={{0,3},{1,0},{2,1},{3,2},{4,7},{5,4},{6,5},{7,6},{8,11},{9,8},{10,9... | collective-permute-start | bytes 393224 | tf_op jit(solution)/shard_map/ppermute | solution.py:343
  106.3 8.8 %all-to-all-start = ((bf16[8,16,512]{2,1,0:T(8,128)(2,1)}), bf16[8,16,512]{2,1,0:T(8,128)(2,1)S(1)}, u32[]{:S(2)}, u32[]{:S(2)}) async-start(bf16[8,16,512]{2,1,0:T(8,128)(2,1)} %bitcast.8), calls=%async_computation | async-start | bytes 262144 | tf_op jit(solution)/shard_map/all_to_all | solution.py:435
  (3 other events, 32.9 us)

commit v10 on v9

--- a/solution.py
+++ b/solution.py
@@ -415,22 +415,23 @@
     early, early_share = finish_state(patch_proj, early, own)
     early_shares = gather(early_share, "head")
     late_share = sum(p.astype(F32) for p in chunks).astype(BF16)
-    weight, late_share = lax.optimization_barrier((jnp.transpose(global_qkv, (1, 0, 2)), late_share))
+    weight = jnp.transpose(global_qkv, (1, 0, 2))
+    weight, late_share, parts = lax.optimization_barrier((weight, late_share, parts))
     late_shares = gather(late_share, "head")
     residual = jnp.concatenate([early_share, late_share], axis=0)
     ids = (me - jnp.arange(ways, dtype=jnp.int32)) % ways
     core = (seq % 2).reshape(1)
     kept, given = global_heads(depth, core, ids, global_gain.reshape(ways, 1, -1), early_shares, late_shares, fetch(weight))
     received = swap_cores(given, "seq")
-    parts, received = lax.optimization_barrier((parts, received))
+    parts = scatter(parts, "head")
+    received, parts[1] = lax.optimization_barrier((received, parts[1]))
     half = kept.shape[1] // 3
     keyed = jnp.concatenate([kept[:, half:], received[:, half:]], axis=0)
     pieces = [shift(keyed, "seq", 2 * step) for step in range(1, lax.axis_size("seq") // 2)]
-    parts = scatter(parts, "head")
+    kept, parts[2] = lax.optimization_barrier((kept, parts[2]))
     own_heads, other_heads = attend(depth, seq.reshape(1), twin_ids("seq"), global_scale, kept, received, pieces)
-    other_heads, parts[1] = lax.optimization_barrier((swap_cores(other_heads, "seq"), parts[1]))
+    other_heads, parts[3:] = lax.optimization_barrier((swap_cores(other_heads, "seq"), parts[3:]))
     updates = scatter(project(core, slots, own_heads, other_heads, global_out), "head")
-    updates, parts[2] = lax.optimization_barrier((updates, parts[2]))
     result, routed = finish_result(owner_order(owners, seq, patches), residual, updates)
     global_state = lax.all_to_all(routed, "seq", split_axis=0, concat_axis=0, tiled=True)
     byte_out = finish_bytes(result, back_proj, [early] + parts)

time: 116 us -> 109 us (0.940)
  waiting for transfers between devices: 41.9 us -> 36.1 us
    ppermute x21, waiting for transfers between devices: 37.1 us -> 30.2 us  [shift(): lax.ppermute(value, axis, [(i, (i + step) % count) for i in range(count)])]
  transfers between devices with their start and end apart: 24 -> 24, of which waited for: 9 -> 9; matrix products, arithmetic and copies ran while one was open for 1% -> 1% of each run, Pallas kernels for 15% -> 16%
where the time goes in v10:
time: 109 us
  starting transfers between devices  40.1 us (37%)
  waiting for transfers between devices  36.1 us (33%)
  Pallas kernels  29.7 us (27%)
  local copies, waits for them, and re-layouts  1.73 us (2%)
    ppermute x21, starting transfers between devices, shift(): lax.ppermute(value, axis, [(i, (i + step) % count) for i in range(count)])  36.6 us
    ppermute x21, waiting for transfers between devices, shift(): lax.ppermute(value, axis, [(i, (i + step) % count) for i in range(count)])  30.2 us
    pallas_call x2, Pallas kernels, local_part(): pl.pallas_call(functools.partial(local_kernel, span, ways, piece, last),...  20.2 us
    all_to_all x1, waiting for transfers between devices, on_device(): lax.all_to_all(routed, 'seq', split_axis=0, concat_axis=0, tiled=True)  3.52 us
    all_to_all x1, starting transfers between devices, on_device(): lax.all_to_all(routed, 'seq', split_axis=0, concat_axis=0, tiled=True)  3.37 us
    pallas_call x1, Pallas kernels, fetch(): pl.pallas_call(fetch_kernel, in_specs=[HBM], out_specs=VMEM, out_shape=pl...  2.89 us
    ppermute x2, waiting for transfers between devices, swap_cores(): lax.ppermute(value, axis, [(i, i ^ 1) for i in range(lax.axis_size(axis))])  2.37 us
  transfers between devices with their start and end apart: 24, of which 9 were waited for; matrix products, arithmetic and copies ran while one was open for 1% of the time, Pallas kernels for 16%

profile of v10, /device:TPU:0, one launch (start us, length us, event | category | flops | bytes accessed | tf_op | source)
XLA Modules:
  0.0 108.9 jit_solution(15037248348531490098)
XLA Ops:
  0.6 10.1 %local_part.2 = (bf16[128,1024]{1,0:T(8,128)(2,1)}, bf16[128,1024]{1,0:T(8,128)(2,1)}, bf16[128,1024]{1,0:T(8,128)(2,1)}, bf16[128,1024]{1,0:T(8,128)(2,1)}) custom-call(f32[2]{0:T(128)} %scale_ref.4, f32[1,1024]{1,0:T(1,128)} %bitcast.18, bf16[1024,1024]{1,0:T(8,128)(2,1)} %bitcast.14, bf16[3,1024,256]{2,1,0:T(8,128)(2,1)} %bitcast.16, ...), custom_call_target="tpu_custom_call" | custom-call | flops 4294967296 | bytes 10485760 | tf_op jit(solution)/shard_map/local_part/pallas_call | solution.py:117
  10.8 3.1 %collective-permute-start = (bf16[128,1024]{1,0:T(8,128)(2,1)}, bf16[128,1024]{1,0:T(8,128)(2,1)S(1)}, u32[]{:S(2)}, u32[]{:S(2)}) collective-permute-start(bf16[128,1024]{1,0:T(8,128)(2,1)} %get-tuple-element.48), channel_id=1, source_target_pairs={{0,1},{1,2},{2,3},{3,0},{4,5},{5,6},{6,7},{7,4},{8,9},{9,10},{10,1... | collective-permute-start | bytes 786440 | tf_op jit(solution)/shard_map/ppermute | solution.py:343
  13.8 2.6 %collective-permute-start.1 = (bf16[128,1024]{1,0:T(8,128)(2,1)}, bf16[128,1024]{1,0:T(8,128)(2,1)S(1)}, u32[]{:S(2)}, u32[]{:S(2)}) collective-permute-start(bf16[128,1024]{1,0:T(8,128)(2,1)} %get-tuple-element.50), channel_id=1, source_target_pairs={{0,2},{1,3},{2,0},{3,1},{4,6},{5,7},{6,4},{7,5},{8,10},{9,11},{10,... | collective-permute-start | bytes 786440 | tf_op jit(solution)/shard_map/ppermute | solution.py:343
  16.4 1.3 %collective-permute-start.2 = (bf16[128,1024]{1,0:T(8,128)(2,1)}, bf16[128,1024]{1,0:T(8,128)(2,1)S(1)}, u32[]{:S(2)}, u32[]{:S(2)}) collective-permute-start(bf16[128,1024]{1,0:T(8,128)(2,1)} %get-tuple-element.51), channel_id=1, source_target_pairs={{0,3},{1,0},{2,1},{3,2},{4,7},{5,4},{6,5},{7,6},{8,11},{9,8},{10,9... | collective-permute-start | bytes 786440 | tf_op jit(solution)/shard_map/ppermute | solution.py:343
  17.8 10.1 %local_part.3 = (bf16[128,1024]{1,0:T(8,128)(2,1)}, bf16[128,1024]{1,0:T(8,128)(2,1)}, bf16[128,1024]{1,0:T(8,128)(2,1)}, bf16[128,1024]{1,0:T(8,128)(2,1)}, bf1...) custom-call(f32[2]{0:T(128)} %scale_ref.4, ...), custom_call_target="tpu_custom_call" | custom-call | flops 4294967296 | bytes 10485760 | tf_op jit(solution)/shard_map/local_part/pallas_call | solution.py:117
  28.0 7.0 %collective-permute-start.3 = (bf16[64,512]{1,0:T(8,128)(2,1)S(1)}, bf16[64,512]{1,0:T(8,128)(2,1)S(1)}, u32[]{:S(2)}, u32[]{:S(2)}) collective-permute-start(bf16[64,512]{1,0:T(8,128)(2,1)S(1)} %get-tuple-element.54), channel_id=1, source_target_pairs={{0,1},{1,2},{2,3},{3,0},{4,5},{5,6},{6,7},{7,4},{8,9},{9,10},{10,1... | collective-permute-start | bytes 196616 | tf_op jit(solution)/shard_map/ppermute | solution.py:343
  35.0 2.0 %collective-permute-start.4 = (bf16[64,512]{1,0:T(8,128)(2,1)S(1)}, bf16[64,512]{1,0:T(8,128)(2,1)S(1)}, u32[]{:S(2)}, u32[]{:S(2)}) collective-permute-start(bf16[64,512]{1,0:T(8,128)(2,1)S(1)} %get-tuple-element.55), channel_id=1, source_target_pairs={{0,2},{1,3},{2,0},{3,1},{4,6},{5,7},{6,4},{7,5},{8,10},{9,11},{10,... | collective-permute-start | bytes 196616 | tf_op jit(solution)/shard_map/ppermute | solution.py:343
  36.9 2.9 %collective-permute-start.5 = (bf16[64,512]{1,0:T(8,128)(2,1)S(1)}, bf16[64,512]{1,0:T(8,128)(2,1)S(1)}, u32[]{:S(2)}, u32[]{:S(2)}) collective-permute-start(bf16[64,512]{1,0:T(8,128)(2,1)S(1)} %get-tuple-element.56), channel_id=1, source_target_pairs={{0,3},{1,0},{2,1},{3,2},{4,7},{5,4},{6,5},{7,6},{8,11},{9,8},{10,9... | collective-permute-start | bytes 196616 | tf_op jit(solution)/shard_map/ppermute | solution.py:343
  40.4 4.1 %collective-permute-start.8 = (bf16[64,512]{1,0:T(8,128)(2,1)S(1)}, bf16[64,512]{1,0:T(8,128)(2,1)S(1)}, u32[]{:S(2)}, u32[]{:S(2)}) collective-permute-start(bf16[64,512]{1,0:T(8,128)(2,1)S(1)} %get-tuple-element.52.refs_0_), channel_id=1, source_target_pairs={{0,3},{1,0},{2,1},{3,2},{4,7},{5,4},{6,5},{7,6},{8,11},{9,8},{10,9... | collective-permute-start | bytes 196616 | tf_op jit(solution)/shard_map/ppermute | solution.py:343
  45.2 3.3 %collective-permute-start.11 = (bf16[64,512]{1,0:T(8,128)(2,1)S(1)}, bf16[64,512]{1,0:T(8,128)(2,1)S(1)}, u32[]{:S(2)}, u32[]{:S(2)}) collective-permute-start(bf16[64,512]{1,0:T(8,128)(2,1)S(1)} %add_convert_fusion.refs_4_), channel_id=1, source_target_pairs={{0,3},{1,0},{2,1},{3,2},{4,7},{5,4},{6,5},{7,6},{8,11},{9,8},{10,9... | collective-permute-start | bytes 196616 | tf_op jit(solution)/shard_map/ppermute | solution.py:343
  48.5 1.0 collective-permute-start.10
  49.6 3.6 %collective-permute-done.7.refs_2_ = bf16[64,512]{1,0:T(8,128)(2,1)S(1)} collective-permute-done((bf16[64,512]{1,0:T(8,128)(2,1)S(1)}, bf16[64,512]{1,0:T(8,128)(2,1)S(1)}, u32[]{:S(2)}, u32[]{:S(2)}) %collective-permute-start.7) | collective-permute-done | bytes 65568 | tf_op jit(solution)/shard_map/ppermute | solution.py:343
  53.3 2.9 %fetch.1.refs_8_ = bf16[3,2048,512]{2,1,0:T(8,128)(2,1)S(1)} custom-call(bf16[3,2048,512]{2,1,0:T(8,128)(2,1)} %bitcast.12), custom_call_target="tpu_custom_call" | custom-call | tf_op jit(solution)/shard_map/fetch/pallas_call | solution.py:173
  56.2 5.6 %collective-permute-done.10.refs_6_ = bf16[64,512]{1,0:T(8,128)(2,1)S(1)} collective-permute-done((bf16[64,512]{1,0:T(8,128)(2,1)S(1)}, bf16[64,512]{1,0:T(8,128)(2,1)S(1)}, u32[]{:S(2)}, u32[]{:S(2)}) %collective-permute-start.10) | collective-permute-done | bytes 65568 | tf_op jit(solution)/shard_map/ppermute | solution.py:343
  61.8 1.7 %global_heads.1 = (bf16[128,768]{1,0:T(8,128)(2,1)S(1)}, bf16[128,768]{1,0:T(8,128)(2,1)S(1)}) custom-call(s32[1]{0:T(128)} %bitcast.5.core_ref, s32[4]{0:T(128)S(1)} %and_select_fusion.ids_ref, f32[4,1,512]{2,1,0:T(1,128)S(1)} %bitcast.11, bf16[64,512]{1,0:T(8,128)(2,1)S(1)} %get-tuple-element.52.refs_0_, ...), custom_call_target="tpu_custom_call" | custom-call | tf_op jit(solution)/shard_map/global_heads/pallas_call | solution.py:207
  63.9 1.1 %collective-permute-done.13.given_ref = bf16[128,768]{1,0:T(8,128)(2,1)S(1)} collective-permute-done((bf16[128,768]{1,0:T(8,128)(2,1)S(1)}, bf16[128,768]{1,0:T(8,128)(2,1)S(1)}, u32[]{:S(2)}, u32[]{:S(2)}) %collective-permute-start.13) | collective-permute-done | bytes 196640 | tf_op jit(solution)/shard_map/ppermute | solution.py:360
  65.1 2.5 %collective-permute-start.17 = (bf16[256,512]{1,0:T(8,128)(2,1)S(1)}, bf16[256,512]{1,0:T(8,128)(2,1)S(1)}, u32[]{:S(2)}, u32[]{:S(2)}) collective-permute-start(bf16[256,512]{1,0:T(8,128)(2,1)S(1)} %pad_maximum_fusion), channel_id=1, source_target_pairs={{0,24},{4,28},{8,0},{12,4},{16,8},{20,12},{24,16},{28,20},{1,25},{... | collective-permute-start | bytes 786440 | tf_op jit(solution)/shard_map/ppermute | solution.py:343
  68.7 6.8 %collective-permute-done.12.refs_3_ = bf16[128,1024]{1,0:T(8,128)(2,1)S(1)} collective-permute-done((bf16[128,1024]{1,0:T(8,128)(2,1)S(1)}, bf16[128,1024]{1,0:T(8,128)(2,1)S(1)}, u32[]{:S(2)}, u32[]{:S(2)}) %collective-permute-start.12) | collective-permute-done | bytes 262176 | tf_op jit(solution)/shard_map/ppermute | solution.py:343
  75.5 5.8 %collective-permute-done.16.refs_1_ = bf16[256,512]{1,0:T(8,128)(2,1)S(1)} collective-permute-done((bf16[256,512]{1,0:T(8,128)(2,1)S(1)}, bf16[256,512]{1,0:T(8,128)(2,1)S(1)}, u32[]{:S(2)}, u32[]{:S(2)}) %collective-permute-start.16) | collective-permute-done | bytes 262176 | tf_op jit(solution)/shard_map/ppermute | solution.py:343
  81.3 1.7 %attend.1 = (bf16[128,256]{1,0:T(8,128)(2,1)S(1)}, bf16[128,256]{1,0:T(8,128)(2,1)S(1)}) custom-call(s32[1]{0:T(128)} %bitcast.6.me_ref, s32[4]{0:T(128)S(1)} %and_select_fusion.1.ids_ref, f32[4]{0:T(128)S(1)} %copy-done.7, bf16[128,768]{1,0:T(8,128)(2,1)S(1)} %get-tuple-element.65.kept_ref, bf16[128,768]{1,0:T(8,128)(2,1)S(1)} %collective-permute-done.13.given_ref, ...), custom_call_target="tpu_custom_call" | custom-call | flops 1 | bytes 1 | tf_op jit(solution)/shard_map/attend/pallas_call | solution.py:250
  83.1 1.2 %collective-permute-done.18.other_ref = bf16[128,256]{1,0:T(8,128)(2,1)S(1)} collective-permute-done((bf16[128,256]{1,0:T(8,128)(2,1)S(1)}, bf16[128,256]{1,0:T(8,128)(2,1)S(1)}, u32[]{:S(2)}, u32[]{:S(2)}) %collective-permute-start.18) | collective-permute-done | bytes 65568 | tf_op jit(solution)/shard_map/ppermute | solution.py:360
  84.3 1.0 project.1
  85.4 1.0 collective-permute-start.20
  86.3 2.6 %collective-permute-start.21 = (bf16[128,512]{1,0:T(8,128)(2,1)S(1)}, bf16[128,512]{1,0:T(8,128)(2,1)S(1)}, u32[]{:S(2)}, u32[]{:S(2)}) collective-permute-start(bf16[128,512]{1,0:T(8,128)(2,1)S(1)} %get-tuple-element.75), channel_id=1, source_target_pairs={{0,2},{1,3},{2,0},{3,1},{4,6},{5,7},{6,4},{7,5},{8,10},{9,11},{10,... | collective-permute-start | bytes 393224 | tf_op jit(solution)/shard_map/ppermute | solution.py:343
  88.9 1.2 %collective-permute-start.22 = (bf16[128,512]{1,0:T(8,128)(2,1)S(1)}, bf16[128,512]{1,0:T(8,128)(2,1)S(1)}, u32[]{:S(2)}, u32[]{:S(2)}) collective-permute-start(bf16[128,512]{1,0:T(8,128)(2,1)S(1)} %get-tuple-element.76), channel_id=1, source_target_pairs={{0,3},{1,0},{2,1},{3,2},{4,7},{5,4},{6,5},{7,6},{8,11},{9,8},{10,9... | collective-permute-start | bytes 393224 | tf_op jit(solution)/shard_map/ppermute | solution.py:343
  90.1 3.5 %collective-permute-done.20.refs_1_ = bf16[128,512]{1,0:T(8,128)(2,1)S(1)} collective-permute-done((bf16[128,512]{1,0:T(8,128)(2,1)S(1)}, bf16[128,512]{1,0:T(8,128)(2,1)S(1)}, u32[]{:S(2)}, u32[]{:S(2)}) %collective-permute-start.20) | collective-permute-done | bytes 131104 | tf_op jit(solution)/shard_map/ppermute | solution.py:343
  93.7 4.8 %collective-permute-done.21.refs_2_ = bf16[128,512]{1,0:T(8,128)(2,1)S(1)} collective-permute-done((bf16[128,512]{1,0:T(8,128)(2,1)S(1)}, bf16[128,512]{1,0:T(8,128)(2,1)S(1)}, u32[]{:S(2)}, u32[]{:S(2)}) %collective-permute-start.21) | collective-permute-done | bytes 131104 | tf_op jit(solution)/shard_map/ppermute | solution.py:343
  98.5 0.9 finish_result.1
  99.4 3.4 %all-to-all-start = ((bf16[8,16,512]{2,1,0:T(8,128)(2,1)}), bf16[8,16,512]{2,1,0:T(8,128)(2,1)S(1)}, u32[]{:S(2)}, u32[]{:S(2)}) async-start(bf16[8,16,512]{2,1,0:T(8,128)(2,1)} %bitcast.8), calls=%async_computation | async-start | bytes 262144 | tf_op jit(solution)/shard_map/all_to_all | solution.py:436
  102.8 0.9 finish_bytes.1
  103.7 1.0 reshape.82
  104.7 3.5 %all-to-all-done = bf16[8,16,512]{2,1,0:T(8,128)(2,1)S(1)} async-done(((bf16[8,16,512]{2,1,0:T(8,128)(2,1)}), bf16[8,16,512]{2,1,0:T(8,128)(2,1)S(1)}, u32[]{:S(2)}, u32[]{:S(2)}) %all-to-all-start) | async-done | bytes 131104 | tf_op jit(solution)/shard_map/all_to_all | solution.py:436
  (61 shorter events, 3.5 us)
Async XLA Ops:
  0.6 27.3 %copy-start = (s32[8,16]{1,0:T(8,128)S(1)}, s32[8,16]{1,0:T(8,128)}, u32[]{:S(2)}) copy-start(s32[8,16]{1,0:T(8,128)} %param.27) | copy-start | bytes 1540
  10.8 17.2 %collective-permute-start = (bf16[128,1024]{1,0:T(8,128)(2,1)}, bf16[128,1024]{1,0:T(8,128)(2,1)S(1)}, u32[]{:S(2)}, u32[]{:S(2)}) collective-permute-start(bf16[128,1024]{1,0:T(8,128)(2,1)} %get-tuple-element.48), channel_id=1, source_target_pairs={{0,1},{1,2},{2,3},{3,0},{4,5},{5,6},{6,7},{7,4},{8,9},{9,10},{10,1... | collective-permute-start | bytes 786440 | tf_op jit(solution)/shard_map/ppermute | solution.py:343
  13.8 26.2 %collective-permute-start.1 = (bf16[128,1024]{1,0:T(8,128)(2,1)}, bf16[128,1024]{1,0:T(8,128)(2,1)S(1)}, u32[]{:S(2)}, u32[]{:S(2)}) collective-permute-start(bf16[128,1024]{1,0:T(8,128)(2,1)} %get-tuple-element.50), channel_id=1, source_target_pairs={{0,2},{1,3},{2,0},{3,1},{4,6},{5,7},{6,4},{7,5},{8,10},{9,11},{10,... | collective-permute-start | bytes 786440 | tf_op jit(solution)/shard_map/ppermute | solution.py:343
  16.4 23.6 %copy-start.2 = (bf16[1024,256]{1,0:T(8,128)(2,1)S(1)}, bf16[1024,256]{1,0:T(8,128)(2,1)}, u32[]{:S(2)}) copy-start(bf16[1024,256]{1,0:T(8,128)(2,1)} %proj_ref.3) | copy-start | bytes 1572868
  16.4 23.6 %copy-start.5 = (bf16[128,1024]{1,0:T(8,128)(2,1)S(1)}, bf16[128,1024]{1,0:T(8,128)(2,1)}, u32[]{:S(2)}) copy-start(bf16[128,1024]{1,0:T(8,128)(2,1)} %get-tuple-element.43.refs_0_) | copy-start | bytes 786436
  16.4 23.6 %collective-permute-start.2 = (bf16[128,1024]{1,0:T(8,128)(2,1)}, bf16[128,1024]{1,0:T(8,128)(2,1)S(1)}, u32[]{:S(2)}, u32[]{:S(2)}) collective-permute-start(bf16[128,1024]{1,0:T(8,128)(2,1)} %get-tuple-element.51), channel_id=1, source_target_pairs={{0,3},{1,0},{2,1},{3,2},{4,7},{5,4},{6,5},{7,6},{8,11},{9,8},{10,9... | collective-permute-start | bytes 786440 | tf_op jit(solution)/shard_map/ppermute | solution.py:343
  28.0 16.7 %collective-permute-start.3 = (bf16[64,512]{1,0:T(8,128)(2,1)S(1)}, bf16[64,512]{1,0:T(8,128)(2,1)S(1)}, u32[]{:S(2)}, u32[]{:S(2)}) collective-permute-start(bf16[64,512]{1,0:T(8,128)(2,1)S(1)} %get-tuple-element.54), channel_id=1, source_target_pairs={{0,1},{1,2},{2,3},{3,0},{4,5},{5,6},{6,7},{7,4},{8,9},{9,10},{10,1... | collective-permute-start | bytes 196616 | tf_op jit(solution)/shard_map/ppermute | solution.py:343
  35.0 10.2 %collective-permute-start.4 = (bf16[64,512]{1,0:T(8,128)(2,1)S(1)}, bf16[64,512]{1,0:T(8,128)(2,1)S(1)}, u32[]{:S(2)}, u32[]{:S(2)}) collective-permute-start(bf16[64,512]{1,0:T(8,128)(2,1)S(1)} %get-tuple-element.55), channel_id=1, source_target_pairs={{0,2},{1,3},{2,0},{3,1},{4,6},{5,7},{6,4},{7,5},{8,10},{9,11},{10,... | collective-permute-start | bytes 196616 | tf_op jit(solution)/shard_map/ppermute | solution.py:343
  36.9 8.2 %collective-permute-start.5 = (bf16[64,512]{1,0:T(8,128)(2,1)S(1)}, bf16[64,512]{1,0:T(8,128)(2,1)S(1)}, u32[]{:S(2)}, u32[]{:S(2)}) collective-permute-start(bf16[64,512]{1,0:T(8,128)(2,1)S(1)} %get-tuple-element.56), channel_id=1, source_target_pairs={{0,3},{1,0},{2,1},{3,2},{4,7},{5,4},{6,5},{7,6},{8,11},{9,8},{10,9... | collective-permute-start | bytes 196616 | tf_op jit(solution)/shard_map/ppermute | solution.py:343
  40.4 9.2 %collective-permute-start.8 = (bf16[64,512]{1,0:T(8,128)(2,1)S(1)}, bf16[64,512]{1,0:T(8,128)(2,1)S(1)}, u32[]{:S(2)}, u32[]{:S(2)}) collective-permute-start(bf16[64,512]{1,0:T(8,128)(2,1)S(1)} %get-tuple-element.52.refs_0_), channel_id=1, source_target_pairs={{0,3},{1,0},{2,1},{3,2},{4,7},{5,4},{6,5},{7,6},{8,11},{9,8},{10,9... | collective-permute-start | bytes 196616 | tf_op jit(solution)/shard_map/ppermute | solution.py:343
  44.5 8.7 %collective-permute-start.7 = (bf16[64,512]{1,0:T(8,128)(2,1)S(1)}, bf16[64,512]{1,0:T(8,128)(2,1)S(1)}, u32[]{:S(2)}, u32[]{:S(2)}) collective-permute-start(bf16[64,512]{1,0:T(8,128)(2,1)S(1)} %get-tuple-element.52.refs_0_), channel_id=1, source_target_pairs={{0,2},{1,3},{2,0},{3,1},{4,6},{5,7},{6,4},{7,5},{8,10},{9,11},{10,... | collective-permute-start | bytes 196616 | tf_op jit(solution)/shard_map/ppermute | solution.py:343
  44.6 11.6 %collective-permute-start.6 = (bf16[64,512]{1,0:T(8,128)(2,1)S(1)}, bf16[64,512]{1,0:T(8,128)(2,1)S(1)}, u32[]{:S(2)}, u32[]{:S(2)}) collective-permute-start(bf16[64,512]{1,0:T(8,128)(2,1)S(1)} %get-tuple-element.52.refs_0_), channel_id=1, source_target_pairs={{0,1},{1,2},{2,3},{3,0},{4,5},{5,6},{6,7},{7,4},{8,9},{9,10},{10,1... | collective-permute-start | bytes 196616 | tf_op jit(solution)/shard_map/ppermute | solution.py:343
  45.2 11.0 %collective-permute-start.11 = (bf16[64,512]{1,0:T(8,128)(2,1)S(1)}, bf16[64,512]{1,0:T(8,128)(2,1)S(1)}, u32[]{:S(2)}, u32[]{:S(2)}) collective-permute-start(bf16[64,512]{1,0:T(8,128)(2,1)S(1)} %add_convert_fusion.refs_4_), channel_id=1, source_target_pairs={{0,3},{1,0},{2,1},{3,2},{4,7},{5,4},{6,5},{7,6},{8,11},{9,8},{10,9... | collective-permute-start | bytes 196616 | tf_op jit(solution)/shard_map/ppermute | solution.py:343
  48.5 13.2 %collective-permute-start.10 = (bf16[64,512]{1,0:T(8,128)(2,1)S(1)}, bf16[64,512]{1,0:T(8,128)(2,1)S(1)}, u32[]{:S(2)}, u32[]{:S(2)}) collective-permute-start(bf16[64,512]{1,0:T(8,128)(2,1)S(1)} %add_convert_fusion.refs_4_), channel_id=1, source_target_pairs={{0,2},{1,3},{2,0},{3,1},{4,6},{5,7},{6,4},{7,5},{8,10},{9,11},{10,... | collective-permute-start | bytes 196616 | tf_op jit(solution)/shard_map/ppermute | solution.py:343
  49.6 12.2 %collective-permute-start.9 = (bf16[64,512]{1,0:T(8,128)(2,1)S(1)}, bf16[64,512]{1,0:T(8,128)(2,1)S(1)}, u32[]{:S(2)}, u32[]{:S(2)}) collective-permute-start(bf16[64,512]{1,0:T(8,128)(2,1)S(1)} %add_convert_fusion.refs_4_), channel_id=1, source_target_pairs={{0,1},{1,2},{2,3},{3,0},{4,5},{5,6},{6,7},{7,4},{8,9},{9,10},{10,1... | collective-permute-start | bytes 196616 | tf_op jit(solution)/shard_map/ppermute | solution.py:343
  53.3 10.6 %collective-permute-start.14 = (bf16[128,1024]{1,0:T(8,128)(2,1)}, bf16[128,1024]{1,0:T(8,128)(2,1)S(1)}, u32[]{:S(2)}, u32[]{:S(2)}) collective-permute-start(bf16[128,1024]{1,0:T(8,128)(2,1)} %get-tuple-element.67), channel_id=1, source_target_pairs={{0,1},{1,2},{2,3},{3,0},{4,5},{5,6},{6,7},{7,4},{8,9},{9,10},{10,1... | collective-permute-start | bytes 786440 | tf_op jit(solution)/shard_map/ppermute | solution.py:343
  53.3 8.5 %copy-start.6 = (f32[2048]{0:T(1024)S(1)}, f32[2048]{0:T(1024)}, u32[]{:S(2)}) copy-start(f32[2048]{0:T(1024)} %param.22) | copy-start | bytes 24580
  61.8 19.5 %copy-start.7 = (f32[4]{0:T(128)S(1)}, f32[4]{0:T(128)}, u32[]{:S(2)}) copy-start(f32[4]{0:T(128)} %scale_ref.5) | copy-start | bytes 52
  63.5 20.8 %copy-start.1 = (bf16[512,2048]{1,0:T(8,128)(2,1)S(1)}, bf16[512,2048]{1,0:T(8,128)(2,1)}, u32[]{:S(2)}) copy-start(bf16[512,2048]{1,0:T(8,128)(2,1)} %proj_ref.4) | copy-start | bytes 6291460
  63.5 1.5 %collective-permute-start.13 = (bf16[128,768]{1,0:T(8,128)(2,1)S(1)}, bf16[128,768]{1,0:T(8,128)(2,1)S(1)}, u32[]{:S(2)}, u32[]{:S(2)}) collective-permute-start(bf16[128,768]{1,0:T(8,128)(2,1)S(1)} %get-tuple-element.66), channel_id=1, source_target_pairs={{0,4},{4,0},{8,12},{12,8},{16,20},{20,16},{24,28},{28,24},{1,5},{5... | collective-permute-start | bytes 589832 | tf_op jit(solution)/shard_map/ppermute | solution.py:360
  63.7 11.8 %collective-permute-start.12 = (bf16[128,1024]{1,0:T(8,128)(2,1)S(1)}, bf16[128,1024]{1,0:T(8,128)(2,1)S(1)}, u32[]{:S(2)}, u32[]{:S(2)}) collective-permute-start(bf16[128,1024]{1,0:T(8,128)(2,1)S(1)} %copy-done.9), channel_id=1, source_target_pairs={{0,2},{1,3},{2,0},{3,1},{4,6},{5,7},{6,4},{7,5},{8,10},{9,11},{10,... | collective-permute-start | bytes 786440 | tf_op jit(solution)/shard_map/ppermute | solution.py:343
  63.8 19.3 %collective-permute-start.19 = (bf16[128,1024]{1,0:T(8,128)(2,1)S(1)}, bf16[128,1024]{1,0:T(8,128)(2,1)S(1)}, u32[]{:S(2)}, u32[]{:S(2)}) collective-permute-start(bf16[128,1024]{1,0:T(8,128)(2,1)S(1)} %copy-done.8), channel_id=1, source_target_pairs={{0,3},{1,0},{2,1},{3,2},{4,7},{5,4},{6,5},{7,6},{8,11},{9,8},{10,9... | collective-permute-start | bytes 786440 | tf_op jit(solution)/shard_map/ppermute | solution.py:343
  65.1 10.4 %collective-permute-start.17 = (bf16[256,512]{1,0:T(8,128)(2,1)S(1)}, bf16[256,512]{1,0:T(8,128)(2,1)S(1)}, u32[]{:S(2)}, u32[]{:S(2)}) collective-permute-start(bf16[256,512]{1,0:T(8,128)(2,1)S(1)} %pad_maximum_fusion), channel_id=1, source_target_pairs={{0,24},{4,28},{8,0},{12,4},{16,8},{20,12},{24,16},{28,20},{1,25},{... | collective-permute-start | bytes 786440 | tf_op jit(solution)/shard_map/ppermute | solution.py:343
  67.6 13.7 %collective-permute-start.16 = (bf16[256,512]{1,0:T(8,128)(2,1)S(1)}, bf16[256,512]{1,0:T(8,128)(2,1)S(1)}, u32[]{:S(2)}, u32[]{:S(2)}) collective-permute-start(bf16[256,512]{1,0:T(8,128)(2,1)S(1)} %pad_maximum_fusion), channel_id=1, source_target_pairs={{0,16},{4,20},{8,24},{12,28},{16,0},{20,4},{24,8},{28,12},{1,17},{... | collective-permute-start | bytes 786440 | tf_op jit(solution)/shard_map/ppermute | solution.py:343
  68.1 13.2 %collective-permute-start.15 = (bf16[256,512]{1,0:T(8,128)(2,1)S(1)}, bf16[256,512]{1,0:T(8,128)(2,1)S(1)}, u32[]{:S(2)}, u32[]{:S(2)}) collective-permute-start(bf16[256,512]{1,0:T(8,128)(2,1)S(1)} %pad_maximum_fusion), channel_id=1, source_target_pairs={{0,8},{4,12},{8,16},{12,20},{16,24},{20,28},{24,0},{28,4},{1,9},{5... | collective-permute-start | bytes 786440 | tf_op jit(solution)/shard_map/ppermute | solution.py:343
  81.3 21.5 %copy-start.3 = (bf16[256,1024]{1,0:T(8,128)(2,1)S(1)}, bf16[256,1024]{1,0:T(8,128)(2,1)}, u32[]{:S(2)}) copy-start(bf16[256,1024]{1,0:T(8,128)(2,1)} %proj_ref.5) | copy-start | bytes 1572868
  81.3 21.5 %copy-start.4 = (bf16[128,1024]{1,0:T(8,128)(2,1)S(1)}, bf16[128,1024]{1,0:T(8,128)(2,1)}, u32[]{:S(2)}) copy-start(bf16[128,1024]{1,0:T(8,128)(2,1)} %get-tuple-element.79.refs_1_) | copy-start | bytes 786436
  83.0 1.3 %collective-permute-start.18 = (bf16[128,256]{1,0:T(8,128)(2,1)S(1)}, bf16[128,256]{1,0:T(8,128)(2,1)S(1)}, u32[]{:S(2)}, u32[]{:S(2)}) collective-permute-start(bf16[128,256]{1,0:T(8,128)(2,1)S(1)} %get-tuple-element.70), channel_id=1, source_target_pairs={{0,4},{4,0},{8,12},{12,8},{16,20},{20,16},{24,28},{28,24},{1,5},{5... | collective-permute-start | bytes 196616 | tf_op jit(solution)/shard_map/ppermute | solution.py:360
  85.4 8.3 %collective-permute-start.20 = (bf16[128,512]{1,0:T(8,128)(2,1)S(1)}, bf16[128,512]{1,0:T(8,128)(2,1)S(1)}, u32[]{:S(2)}, u32[]{:S(2)}) collective-permute-start(bf16[128,512]{1,0:T(8,128)(2,1)S(1)} %get-tuple-element.74), channel_id=1, source_target_pairs={{0,1},{1,2},{2,3},{3,0},{4,5},{5,6},{6,7},{7,4},{8,9},{9,10},{10,1... | collective-permute-start | bytes 393224 | tf_op jit(solution)/shard_map/ppermute | solution.py:343
  86.3 12.2 %collective-permute-start.21 = (bf16[128,512]{1,0:T(8,128)(2,1)S(1)}, bf16[128,512]{1,0:T(8,128)(2,1)S(1)}, u32[]{:S(2)}, u32[]{:S(2)}) collective-permute-start(bf16[128,512]{1,0:T(8,128)(2,1)S(1)} %get-tuple-element.75), channel_id=1, source_target_pairs={{0,2},{1,3},{2,0},{3,1},{4,6},{5,7},{6,4},{7,5},{8,10},{9,11},{10,... | collective-permute-start | bytes 393224 | tf_op jit(solution)/shard_map/ppermute | solution.py:343
  88.9 9.6 %collective-permute-start.22 = (bf16[128,512]{1,0:T(8,128)(2,1)S(1)}, bf16[128,512]{1,0:T(8,128)(2,1)S(1)}, u32[]{:S(2)}, u32[]{:S(2)}) collective-permute-start(bf16[128,512]{1,0:T(8,128)(2,1)S(1)} %get-tuple-element.76), channel_id=1, source_target_pairs={{0,3},{1,0},{2,1},{3,2},{4,7},{5,4},{6,5},{7,6},{8,11},{9,8},{10,9... | collective-permute-start | bytes 393224 | tf_op jit(solution)/shard_map/ppermute | solution.py:343
  99.4 8.8 %all-to-all-start = ((bf16[8,16,512]{2,1,0:T(8,128)(2,1)}), bf16[8,16,512]{2,1,0:T(8,128)(2,1)S(1)}, u32[]{:S(2)}, u32[]{:S(2)}) async-start(bf16[8,16,512]{2,1,0:T(8,128)(2,1)} %bitcast.8), calls=%async_computation | async-start | bytes 262144 | tf_op jit(solution)/shard_map/all_to_all | solution.py:436
  (2 other events, 3.9 us)

commit v11 on v10

--- a/solution.py
+++ b/solution.py
@@ -423,14 +423,14 @@
     core = (seq % 2).reshape(1)
     kept, given = global_heads(depth, core, ids, global_gain.reshape(ways, 1, -1), early_shares, late_shares, fetch(weight))
     received = swap_cores(given, "seq")
-    parts = scatter(parts, "head")
-    received, parts[1] = lax.optimization_barrier((received, parts[1]))
+    parts[1] = shift(parts[1], "head", 1)
+    received, *parts = lax.optimization_barrier((received, *parts))
     half = kept.shape[1] // 3
     keyed = jnp.concatenate([kept[:, half:], received[:, half:]], axis=0)
     pieces = [shift(keyed, "seq", 2 * step) for step in range(1, lax.axis_size("seq") // 2)]
-    kept, parts[2] = lax.optimization_barrier((kept, parts[2]))
+    parts[2:] = [shift(part, "head", step) for step, part in enumerate(parts[2:], 2)]
     own_heads, other_heads = attend(depth, seq.reshape(1), twin_ids("seq"), global_scale, kept, received, pieces)
-    other_heads, parts[3:] = lax.optimization_barrier((swap_cores(other_heads, "seq"), parts[3:]))
+    other_heads, parts[2:] = lax.optimization_barrier((swap_cores(other_heads, "seq"), parts[2:]))
     updates = scatter(project(core, slots, own_heads, other_heads, global_out), "head")
     result, routed = finish_result(owner_order(owners, seq, patches), residual, updates)
     global_state = lax.all_to_all(routed, "seq", split_axis=0, concat_axis=0, tiled=True)

time: 109 us -> 109 us (level)
  no operation moved by 1% of the time
where the time goes in v11:
time: 109 us
  starting transfers between devices  39.3 us (36%)
  waiting for transfers between devices  36.9 us (34%)
  Pallas kernels  29.7 us (27%)
  local copies, waits for them, and re-layouts  1.73 us (2%)
    ppermute x21, starting transfers between devices, shift(): lax.ppermute(value, axis, [(i, (i + step) % count) for i in range(count)])  35.8 us
    ppermute x21, waiting for transfers between devices, shift(): lax.ppermute(value, axis, [(i, (i + step) % count) for i in range(count)])  30.9 us
    pallas_call x2, Pallas kernels, local_part(): pl.pallas_call(functools.partial(local_kernel, span, ways, piece, last),...  20.2 us
    all_to_all x1, waiting for transfers between devices, on_device(): lax.all_to_all(routed, 'seq', split_axis=0, concat_axis=0, tiled=True)  3.52 us
    all_to_all x1, starting transfers between devices, on_device(): lax.all_to_all(routed, 'seq', split_axis=0, concat_axis=0, tiled=True)  3.37 us
    pallas_call x1, Pallas kernels, fetch(): pl.pallas_call(fetch_kernel, in_specs=[HBM], out_specs=VMEM, out_shape=pl...  2.89 us
    ppermute x2, waiting for transfers between devices, swap_cores(): lax.ppermute(value, axis, [(i, i ^ 1) for i in range(lax.axis_size(axis))])  2.51 us
  transfers between devices with their start and end apart: 24, of which 9 were waited for; matrix products, arithmetic and copies ran while one was open for 1% of the time, Pallas kernels for 16%

profile of v11, /device:TPU:0, one launch (start us, length us, event | category | flops | bytes accessed | tf_op | source)
XLA Modules:
  0.0 109.0 jit_solution(2712179487768396080)
XLA Ops:
  0.6 10.1 %local_part.2 = (bf16[128,1024]{1,0:T(8,128)(2,1)}, bf16[128,1024]{1,0:T(8,128)(2,1)}, bf16[128,1024]{1,0:T(8,128)(2,1)}, bf16[128,1024]{1,0:T(8,128)(2,1)}) custom-call(f32[2]{0:T(128)} %scale_ref.4, f32[1,1024]{1,0:T(1,128)} %bitcast.18, bf16[1024,1024]{1,0:T(8,128)(2,1)} %bitcast.14, bf16[3,1024,256]{2,1,0:T(8,128)(2,1)} %bitcast.16, ...), custom_call_target="tpu_custom_call" | custom-call | flops 4294967296 | bytes 10485760 | tf_op jit(solution)/shard_map/local_part/pallas_call | solution.py:117
  10.8 3.1 %collective-permute-start = (bf16[128,1024]{1,0:T(8,128)(2,1)}, bf16[128,1024]{1,0:T(8,128)(2,1)S(1)}, u32[]{:S(2)}, u32[]{:S(2)}) collective-permute-start(bf16[128,1024]{1,0:T(8,128)(2,1)} %get-tuple-element.50), channel_id=1, source_target_pairs={{0,1},{1,2},{2,3},{3,0},{4,5},{5,6},{6,7},{7,4},{8,9},{9,10},{10,1... | collective-permute-start | bytes 786440 | tf_op jit(solution)/shard_map/ppermute | solution.py:343
  13.8 2.6 %collective-permute-start.1 = (bf16[128,1024]{1,0:T(8,128)(2,1)}, bf16[128,1024]{1,0:T(8,128)(2,1)S(1)}, u32[]{:S(2)}, u32[]{:S(2)}) collective-permute-start(bf16[128,1024]{1,0:T(8,128)(2,1)} %get-tuple-element.52), channel_id=1, source_target_pairs={{0,2},{1,3},{2,0},{3,1},{4,6},{5,7},{6,4},{7,5},{8,10},{9,11},{10,... | collective-permute-start | bytes 786440 | tf_op jit(solution)/shard_map/ppermute | solution.py:343
  16.4 1.3 %collective-permute-start.2 = (bf16[128,1024]{1,0:T(8,128)(2,1)}, bf16[128,1024]{1,0:T(8,128)(2,1)S(1)}, u32[]{:S(2)}, u32[]{:S(2)}) collective-permute-start(bf16[128,1024]{1,0:T(8,128)(2,1)} %get-tuple-element.53), channel_id=1, source_target_pairs={{0,3},{1,0},{2,1},{3,2},{4,7},{5,4},{6,5},{7,6},{8,11},{9,8},{10,9... | collective-permute-start | bytes 786440 | tf_op jit(solution)/shard_map/ppermute | solution.py:343
  17.8 10.1 %local_part.3 = (bf16[128,1024]{1,0:T(8,128)(2,1)}, bf16[128,1024]{1,0:T(8,128)(2,1)}, bf16[128,1024]{1,0:T(8,128)(2,1)}, bf16[128,1024]{1,0:T(8,128)(2,1)}, bf1...) custom-call(f32[2]{0:T(128)} %scale_ref.4, ...), custom_call_target="tpu_custom_call" | custom-call | flops 4294967296 | bytes 10485760 | tf_op jit(solution)/shard_map/local_part/pallas_call | solution.py:117
  28.0 7.0 %collective-permute-start.3 = (bf16[64,512]{1,0:T(8,128)(2,1)S(1)}, bf16[64,512]{1,0:T(8,128)(2,1)S(1)}, u32[]{:S(2)}, u32[]{:S(2)}) collective-permute-start(bf16[64,512]{1,0:T(8,128)(2,1)S(1)} %get-tuple-element.56), channel_id=1, source_target_pairs={{0,1},{1,2},{2,3},{3,0},{4,5},{5,6},{6,7},{7,4},{8,9},{9,10},{10,1... | collective-permute-start | bytes 196616 | tf_op jit(solution)/shard_map/ppermute | solution.py:343
  35.0 2.0 %collective-permute-start.4 = (bf16[64,512]{1,0:T(8,128)(2,1)S(1)}, bf16[64,512]{1,0:T(8,128)(2,1)S(1)}, u32[]{:S(2)}, u32[]{:S(2)}) collective-permute-start(bf16[64,512]{1,0:T(8,128)(2,1)S(1)} %get-tuple-element.57), channel_id=1, source_target_pairs={{0,2},{1,3},{2,0},{3,1},{4,6},{5,7},{6,4},{7,5},{8,10},{9,11},{10,... | collective-permute-start | bytes 196616 | tf_op jit(solution)/shard_map/ppermute | solution.py:343
  36.9 2.9 %collective-permute-start.5 = (bf16[64,512]{1,0:T(8,128)(2,1)S(1)}, bf16[64,512]{1,0:T(8,128)(2,1)S(1)}, u32[]{:S(2)}, u32[]{:S(2)}) collective-permute-start(bf16[64,512]{1,0:T(8,128)(2,1)S(1)} %get-tuple-element.58), channel_id=1, source_target_pairs={{0,3},{1,0},{2,1},{3,2},{4,7},{5,4},{6,5},{7,6},{8,11},{9,8},{10,9... | collective-permute-start | bytes 196616 | tf_op jit(solution)/shard_map/ppermute | solution.py:343
  40.4 4.1 %collective-permute-start.8 = (bf16[64,512]{1,0:T(8,128)(2,1)S(1)}, bf16[64,512]{1,0:T(8,128)(2,1)S(1)}, u32[]{:S(2)}, u32[]{:S(2)}) collective-permute-start(bf16[64,512]{1,0:T(8,128)(2,1)S(1)} %get-tuple-element.54.refs_0_), channel_id=1, source_target_pairs={{0,3},{1,0},{2,1},{3,2},{4,7},{5,4},{6,5},{7,6},{8,11},{9,8},{10,9... | collective-permute-start | bytes 196616 | tf_op jit(solution)/shard_map/ppermute | solution.py:343
  45.2 3.3 %collective-permute-start.11 = (bf16[64,512]{1,0:T(8,128)(2,1)S(1)}, bf16[64,512]{1,0:T(8,128)(2,1)S(1)}, u32[]{:S(2)}, u32[]{:S(2)}) collective-permute-start(bf16[64,512]{1,0:T(8,128)(2,1)S(1)} %add_convert_fusion.refs_4_), channel_id=1, source_target_pairs={{0,3},{1,0},{2,1},{3,2},{4,7},{5,4},{6,5},{7,6},{8,11},{9,8},{10,9... | collective-permute-start | bytes 196616 | tf_op jit(solution)/shard_map/ppermute | solution.py:343
  48.5 1.0 collective-permute-start.10
  49.6 3.6 %collective-permute-done.7.refs_2_ = bf16[64,512]{1,0:T(8,128)(2,1)S(1)} collective-permute-done((bf16[64,512]{1,0:T(8,128)(2,1)S(1)}, bf16[64,512]{1,0:T(8,128)(2,1)S(1)}, u32[]{:S(2)}, u32[]{:S(2)}) %collective-permute-start.7) | collective-permute-done | bytes 65568 | tf_op jit(solution)/shard_map/ppermute | solution.py:343
  53.3 2.9 %fetch.1.refs_8_ = bf16[3,2048,512]{2,1,0:T(8,128)(2,1)S(1)} custom-call(bf16[3,2048,512]{2,1,0:T(8,128)(2,1)} %bitcast.12), custom_call_target="tpu_custom_call" | custom-call | tf_op jit(solution)/shard_map/fetch/pallas_call | solution.py:173
  56.2 5.6 %collective-permute-done.10.refs_6_ = bf16[64,512]{1,0:T(8,128)(2,1)S(1)} collective-permute-done((bf16[64,512]{1,0:T(8,128)(2,1)S(1)}, bf16[64,512]{1,0:T(8,128)(2,1)S(1)}, u32[]{:S(2)}, u32[]{:S(2)}) %collective-permute-start.10) | collective-permute-done | bytes 65568 | tf_op jit(solution)/shard_map/ppermute | solution.py:343
  61.8 1.7 %global_heads.1 = (bf16[128,768]{1,0:T(8,128)(2,1)S(1)}, bf16[128,768]{1,0:T(8,128)(2,1)S(1)}) custom-call(s32[1]{0:T(128)} %bitcast.5.core_ref, s32[4]{0:T(128)S(1)} %and_select_fusion.ids_ref, f32[4,1,512]{2,1,0:T(1,128)S(1)} %bitcast.11, bf16[64,512]{1,0:T(8,128)(2,1)S(1)} %get-tuple-element.54.refs_0_, ...), custom_call_target="tpu_custom_call" | custom-call | tf_op jit(solution)/shard_map/global_heads/pallas_call | solution.py:207
  63.7 1.3 %collective-permute-done.12.given_ref = bf16[128,768]{1,0:T(8,128)(2,1)S(1)} collective-permute-done((bf16[128,768]{1,0:T(8,128)(2,1)S(1)}, bf16[128,768]{1,0:T(8,128)(2,1)S(1)}, u32[]{:S(2)}, u32[]{:S(2)}) %collective-permute-start.12) | collective-permute-done | bytes 196640 | tf_op jit(solution)/shard_map/ppermute | solution.py:360
  65.1 2.5 %collective-permute-start.16 = (bf16[256,512]{1,0:T(8,128)(2,1)S(1)}, bf16[256,512]{1,0:T(8,128)(2,1)S(1)}, u32[]{:S(2)}, u32[]{:S(2)}) collective-permute-start(bf16[256,512]{1,0:T(8,128)(2,1)S(1)} %pad_maximum_fusion), channel_id=1, source_target_pairs={{0,24},{4,28},{8,0},{12,4},{16,8},{20,12},{24,16},{28,20},{1,25},{... | collective-permute-start | bytes 786440 | tf_op jit(solution)/shard_map/ppermute | solution.py:343
  69.0 5.3 %collective-permute-done.16.refs_2_ = bf16[256,512]{1,0:T(8,128)(2,1)S(1)} collective-permute-done((bf16[256,512]{1,0:T(8,128)(2,1)S(1)}, bf16[256,512]{1,0:T(8,128)(2,1)S(1)}, u32[]{:S(2)}, u32[]{:S(2)}) %collective-permute-start.16) | collective-permute-done | bytes 262176 | tf_op jit(solution)/shard_map/ppermute | solution.py:343
  74.3 7.0 %collective-permute-done.15.refs_1_ = bf16[256,512]{1,0:T(8,128)(2,1)S(1)} collective-permute-done((bf16[256,512]{1,0:T(8,128)(2,1)S(1)}, bf16[256,512]{1,0:T(8,128)(2,1)S(1)}, u32[]{:S(2)}, u32[]{:S(2)}) %collective-permute-start.15) | collective-permute-done | bytes 262176 | tf_op jit(solution)/shard_map/ppermute | solution.py:343
  81.3 1.7 %attend.1 = (bf16[128,256]{1,0:T(8,128)(2,1)S(1)}, bf16[128,256]{1,0:T(8,128)(2,1)S(1)}) custom-call(s32[1]{0:T(128)} %bitcast.6.me_ref, s32[4]{0:T(128)S(1)} %and_select_fusion.1.ids_ref, f32[4]{0:T(128)S(1)} %copy-done.7, bf16[128,768]{1,0:T(8,128)(2,1)S(1)} %get-tuple-element.65.kept_ref, bf16[128,768]{1,0:T(8,128)(2,1)S(1)} %collective-permute-done.12.given_ref, ...), custom_call_target="tpu_custom_call" | custom-call | flops 1 | bytes 1 | tf_op jit(solution)/shard_map/attend/pallas_call | solution.py:250
  83.1 1.2 %collective-permute-done.17.other_ref = bf16[128,256]{1,0:T(8,128)(2,1)S(1)} collective-permute-done((bf16[128,256]{1,0:T(8,128)(2,1)S(1)}, bf16[128,256]{1,0:T(8,128)(2,1)S(1)}, u32[]{:S(2)}, u32[]{:S(2)}) %collective-permute-start.17) | collective-permute-done | bytes 65568 | tf_op jit(solution)/shard_map/ppermute | solution.py:360
  84.3 1.0 project.1
  85.4 1.0 collective-permute-start.20
  86.4 1.8 %collective-permute-start.21 = (bf16[128,512]{1,0:T(8,128)(2,1)S(1)}, bf16[128,512]{1,0:T(8,128)(2,1)S(1)}, u32[]{:S(2)}, u32[]{:S(2)}) collective-permute-start(bf16[128,512]{1,0:T(8,128)(2,1)S(1)} %get-tuple-element.79), channel_id=1, source_target_pairs={{0,2},{1,3},{2,0},{3,1},{4,6},{5,7},{6,4},{7,5},{8,10},{9,11},{10,... | collective-permute-start | bytes 393224 | tf_op jit(solution)/shard_map/ppermute | solution.py:343
  88.2 1.0 collective-permute-start.22
  89.3 4.4 %collective-permute-done.20.refs_1_ = bf16[128,512]{1,0:T(8,128)(2,1)S(1)} collective-permute-done((bf16[128,512]{1,0:T(8,128)(2,1)S(1)}, bf16[128,512]{1,0:T(8,128)(2,1)S(1)}, u32[]{:S(2)}, u32[]{:S(2)}) %collective-permute-start.20) | collective-permute-done | bytes 131104 | tf_op jit(solution)/shard_map/ppermute | solution.py:343
  93.7 4.9 %collective-permute-done.21.refs_2_ = bf16[128,512]{1,0:T(8,128)(2,1)S(1)} collective-permute-done((bf16[128,512]{1,0:T(8,128)(2,1)S(1)}, bf16[128,512]{1,0:T(8,128)(2,1)S(1)}, u32[]{:S(2)}, u32[]{:S(2)}) %collective-permute-start.21) | collective-permute-done | bytes 131104 | tf_op jit(solution)/shard_map/ppermute | solution.py:343
  98.6 0.9 finish_result.1
  99.5 3.4 %all-to-all-start = ((bf16[8,16,512]{2,1,0:T(8,128)(2,1)}), bf16[8,16,512]{2,1,0:T(8,128)(2,1)S(1)}, u32[]{:S(2)}, u32[]{:S(2)}) async-start(bf16[8,16,512]{2,1,0:T(8,128)(2,1)} %bitcast.8), calls=%async_computation | async-start | bytes 262144 | tf_op jit(solution)/shard_map/all_to_all | solution.py:436
  102.9 0.9 finish_bytes.1
  103.8 1.0 reshape.82
  104.8 3.5 %all-to-all-done = bf16[8,16,512]{2,1,0:T(8,128)(2,1)S(1)} async-done(((bf16[8,16,512]{2,1,0:T(8,128)(2,1)}), bf16[8,16,512]{2,1,0:T(8,128)(2,1)S(1)}, u32[]{:S(2)}, u32[]{:S(2)}) %all-to-all-start) | async-done | bytes 131104 | tf_op jit(solution)/shard_map/all_to_all | solution.py:436
  (61 shorter events, 3.6 us)
Async XLA Ops:
  0.6 27.3 %copy-start = (s32[8,16]{1,0:T(8,128)S(1)}, s32[8,16]{1,0:T(8,128)}, u32[]{:S(2)}) copy-start(s32[8,16]{1,0:T(8,128)} %param.27) | copy-start | bytes 1540
  10.8 17.2 %collective-permute-start = (bf16[128,1024]{1,0:T(8,128)(2,1)}, bf16[128,1024]{1,0:T(8,128)(2,1)S(1)}, u32[]{:S(2)}, u32[]{:S(2)}) collective-permute-start(bf16[128,1024]{1,0:T(8,128)(2,1)} %get-tuple-element.50), channel_id=1, source_target_pairs={{0,1},{1,2},{2,3},{3,0},{4,5},{5,6},{6,7},{7,4},{8,9},{9,10},{10,1... | collective-permute-start | bytes 786440 | tf_op jit(solution)/shard_map/ppermute | solution.py:343
  13.8 26.2 %collective-permute-start.1 = (bf16[128,1024]{1,0:T(8,128)(2,1)}, bf16[128,1024]{1,0:T(8,128)(2,1)S(1)}, u32[]{:S(2)}, u32[]{:S(2)}) collective-permute-start(bf16[128,1024]{1,0:T(8,128)(2,1)} %get-tuple-element.52), channel_id=1, source_target_pairs={{0,2},{1,3},{2,0},{3,1},{4,6},{5,7},{6,4},{7,5},{8,10},{9,11},{10,... | collective-permute-start | bytes 786440 | tf_op jit(solution)/shard_map/ppermute | solution.py:343
  16.4 23.6 %copy-start.2 = (bf16[1024,256]{1,0:T(8,128)(2,1)S(1)}, bf16[1024,256]{1,0:T(8,128)(2,1)}, u32[]{:S(2)}) copy-start(bf16[1024,256]{1,0:T(8,128)(2,1)} %proj_ref.3) | copy-start | bytes 1572868
  16.4 23.6 %copy-start.5 = (bf16[128,1024]{1,0:T(8,128)(2,1)S(1)}, bf16[128,1024]{1,0:T(8,128)(2,1)}, u32[]{:S(2)}) copy-start(bf16[128,1024]{1,0:T(8,128)(2,1)} %get-tuple-element.45.refs_0_) | copy-start | bytes 786436
  16.4 23.6 %collective-permute-start.2 = (bf16[128,1024]{1,0:T(8,128)(2,1)}, bf16[128,1024]{1,0:T(8,128)(2,1)S(1)}, u32[]{:S(2)}, u32[]{:S(2)}) collective-permute-start(bf16[128,1024]{1,0:T(8,128)(2,1)} %get-tuple-element.53), channel_id=1, source_target_pairs={{0,3},{1,0},{2,1},{3,2},{4,7},{5,4},{6,5},{7,6},{8,11},{9,8},{10,9... | collective-permute-start | bytes 786440 | tf_op jit(solution)/shard_map/ppermute | solution.py:343
  28.0 16.7 %collective-permute-start.3 = (bf16[64,512]{1,0:T(8,128)(2,1)S(1)}, bf16[64,512]{1,0:T(8,128)(2,1)S(1)}, u32[]{:S(2)}, u32[]{:S(2)}) collective-permute-start(bf16[64,512]{1,0:T(8,128)(2,1)S(1)} %get-tuple-element.56), channel_id=1, source_target_pairs={{0,1},{1,2},{2,3},{3,0},{4,5},{5,6},{6,7},{7,4},{8,9},{9,10},{10,1... | collective-permute-start | bytes 196616 | tf_op jit(solution)/shard_map/ppermute | solution.py:343
  35.0 10.2 %collective-permute-start.4 = (bf16[64,512]{1,0:T(8,128)(2,1)S(1)}, bf16[64,512]{1,0:T(8,128)(2,1)S(1)}, u32[]{:S(2)}, u32[]{:S(2)}) collective-permute-start(bf16[64,512]{1,0:T(8,128)(2,1)S(1)} %get-tuple-element.57), channel_id=1, source_target_pairs={{0,2},{1,3},{2,0},{3,1},{4,6},{5,7},{6,4},{7,5},{8,10},{9,11},{10,... | collective-permute-start | bytes 196616 | tf_op jit(solution)/shard_map/ppermute | solution.py:343
  36.9 8.2 %collective-permute-start.5 = (bf16[64,512]{1,0:T(8,128)(2,1)S(1)}, bf16[64,512]{1,0:T(8,128)(2,1)S(1)}, u32[]{:S(2)}, u32[]{:S(2)}) collective-permute-start(bf16[64,512]{1,0:T(8,128)(2,1)S(1)} %get-tuple-element.58), channel_id=1, source_target_pairs={{0,3},{1,0},{2,1},{3,2},{4,7},{5,4},{6,5},{7,6},{8,11},{9,8},{10,9... | collective-permute-start | bytes 196616 | tf_op jit(solution)/shard_map/ppermute | solution.py:343
  40.4 9.2 %collective-permute-start.8 = (bf16[64,512]{1,0:T(8,128)(2,1)S(1)}, bf16[64,512]{1,0:T(8,128)(2,1)S(1)}, u32[]{:S(2)}, u32[]{:S(2)}) collective-permute-start(bf16[64,512]{1,0:T(8,128)(2,1)S(1)} %get-tuple-element.54.refs_0_), channel_id=1, source_target_pairs={{0,3},{1,0},{2,1},{3,2},{4,7},{5,4},{6,5},{7,6},{8,11},{9,8},{10,9... | collective-permute-start | bytes 196616 | tf_op jit(solution)/shard_map/ppermute | solution.py:343
  44.5 8.7 %collective-permute-start.7 = (bf16[64,512]{1,0:T(8,128)(2,1)S(1)}, bf16[64,512]{1,0:T(8,128)(2,1)S(1)}, u32[]{:S(2)}, u32[]{:S(2)}) collective-permute-start(bf16[64,512]{1,0:T(8,128)(2,1)S(1)} %get-tuple-element.54.refs_0_), channel_id=1, source_target_pairs={{0,2},{1,3},{2,0},{3,1},{4,6},{5,7},{6,4},{7,5},{8,10},{9,11},{10,... | collective-permute-start | bytes 196616 | tf_op jit(solution)/shard_map/ppermute | solution.py:343
  44.6 11.6 %collective-permute-start.6 = (bf16[64,512]{1,0:T(8,128)(2,1)S(1)}, bf16[64,512]{1,0:T(8,128)(2,1)S(1)}, u32[]{:S(2)}, u32[]{:S(2)}) collective-permute-start(bf16[64,512]{1,0:T(8,128)(2,1)S(1)} %get-tuple-element.54.refs_0_), channel_id=1, source_target_pairs={{0,1},{1,2},{2,3},{3,0},{4,5},{5,6},{6,7},{7,4},{8,9},{9,10},{10,1... | collective-permute-start | bytes 196616 | tf_op jit(solution)/shard_map/ppermute | solution.py:343
  45.2 11.0 %collective-permute-start.11 = (bf16[64,512]{1,0:T(8,128)(2,1)S(1)}, bf16[64,512]{1,0:T(8,128)(2,1)S(1)}, u32[]{:S(2)}, u32[]{:S(2)}) collective-permute-start(bf16[64,512]{1,0:T(8,128)(2,1)S(1)} %add_convert_fusion.refs_4_), channel_id=1, source_target_pairs={{0,3},{1,0},{2,1},{3,2},{4,7},{5,4},{6,5},{7,6},{8,11},{9,8},{10,9... | collective-permute-start | bytes 196616 | tf_op jit(solution)/shard_map/ppermute | solution.py:343
  48.5 13.2 %collective-permute-start.10 = (bf16[64,512]{1,0:T(8,128)(2,1)S(1)}, bf16[64,512]{1,0:T(8,128)(2,1)S(1)}, u32[]{:S(2)}, u32[]{:S(2)}) collective-permute-start(bf16[64,512]{1,0:T(8,128)(2,1)S(1)} %add_convert_fusion.refs_4_), channel_id=1, source_target_pairs={{0,2},{1,3},{2,0},{3,1},{4,6},{5,7},{6,4},{7,5},{8,10},{9,11},{10,... | collective-permute-start | bytes 196616 | tf_op jit(solution)/shard_map/ppermute | solution.py:343
  49.6 12.2 %collective-permute-start.9 = (bf16[64,512]{1,0:T(8,128)(2,1)S(1)}, bf16[64,512]{1,0:T(8,128)(2,1)S(1)}, u32[]{:S(2)}, u32[]{:S(2)}) collective-permute-start(bf16[64,512]{1,0:T(8,128)(2,1)S(1)} %add_convert_fusion.refs_4_), channel_id=1, source_target_pairs={{0,1},{1,2},{2,3},{3,0},{4,5},{5,6},{6,7},{7,4},{8,9},{9,10},{10,1... | collective-permute-start | bytes 196616 | tf_op jit(solution)/shard_map/ppermute | solution.py:343
  53.3 10.5 %collective-permute-start.13 = (bf16[128,1024]{1,0:T(8,128)(2,1)}, bf16[128,1024]{1,0:T(8,128)(2,1)S(1)}, u32[]{:S(2)}, u32[]{:S(2)}) collective-permute-start(bf16[128,1024]{1,0:T(8,128)(2,1)} %get-tuple-element.68), channel_id=1, source_target_pairs={{0,1},{1,2},{2,3},{3,0},{4,5},{5,6},{6,7},{7,4},{8,9},{9,10},{10,1... | collective-permute-start | bytes 786440 | tf_op jit(solution)/shard_map/ppermute | solution.py:343
  53.3 8.5 %copy-start.6 = (f32[2048]{0:T(1024)S(1)}, f32[2048]{0:T(1024)}, u32[]{:S(2)}) copy-start(f32[2048]{0:T(1024)} %param.22) | copy-start | bytes 24580
  61.8 19.5 %copy-start.7 = (f32[4]{0:T(128)S(1)}, f32[4]{0:T(128)}, u32[]{:S(2)}) copy-start(f32[4]{0:T(128)} %scale_ref.5) | copy-start | bytes 52
  63.5 20.8 %copy-start.1 = (bf16[512,2048]{1,0:T(8,128)(2,1)S(1)}, bf16[512,2048]{1,0:T(8,128)(2,1)}, u32[]{:S(2)}) copy-start(bf16[512,2048]{1,0:T(8,128)(2,1)} %proj_ref.4) | copy-start | bytes 6291460
  63.5 1.5 %collective-permute-start.12 = (bf16[128,768]{1,0:T(8,128)(2,1)S(1)}, bf16[128,768]{1,0:T(8,128)(2,1)S(1)}, u32[]{:S(2)}, u32[]{:S(2)}) collective-permute-start(bf16[128,768]{1,0:T(8,128)(2,1)S(1)} %get-tuple-element.66), channel_id=1, source_target_pairs={{0,4},{4,0},{8,12},{12,8},{16,20},{20,16},{24,28},{28,24},{1,5},{5... | collective-permute-start | bytes 589832 | tf_op jit(solution)/shard_map/ppermute | solution.py:360
  65.1 9.2 %collective-permute-start.16 = (bf16[256,512]{1,0:T(8,128)(2,1)S(1)}, bf16[256,512]{1,0:T(8,128)(2,1)S(1)}, u32[]{:S(2)}, u32[]{:S(2)}) collective-permute-start(bf16[256,512]{1,0:T(8,128)(2,1)S(1)} %pad_maximum_fusion), channel_id=1, source_target_pairs={{0,24},{4,28},{8,0},{12,4},{16,8},{20,12},{24,16},{28,20},{1,25},{... | collective-permute-start | bytes 786440 | tf_op jit(solution)/shard_map/ppermute | solution.py:343
  67.6 13.7 %collective-permute-start.15 = (bf16[256,512]{1,0:T(8,128)(2,1)S(1)}, bf16[256,512]{1,0:T(8,128)(2,1)S(1)}, u32[]{:S(2)}, u32[]{:S(2)}) collective-permute-start(bf16[256,512]{1,0:T(8,128)(2,1)S(1)} %pad_maximum_fusion), channel_id=1, source_target_pairs={{0,16},{4,20},{8,24},{12,28},{16,0},{20,4},{24,8},{28,12},{1,17},{... | collective-permute-start | bytes 786440 | tf_op jit(solution)/shard_map/ppermute | solution.py:343
  68.1 13.2 %collective-permute-start.14 = (bf16[256,512]{1,0:T(8,128)(2,1)S(1)}, bf16[256,512]{1,0:T(8,128)(2,1)S(1)}, u32[]{:S(2)}, u32[]{:S(2)}) collective-permute-start(bf16[256,512]{1,0:T(8,128)(2,1)S(1)} %pad_maximum_fusion), channel_id=1, source_target_pairs={{0,8},{4,12},{8,16},{12,20},{16,24},{20,28},{24,0},{28,4},{1,9},{5... | collective-permute-start | bytes 786440 | tf_op jit(solution)/shard_map/ppermute | solution.py:343
  68.7 14.4 %collective-permute-start.18 = (bf16[128,1024]{1,0:T(8,128)(2,1)S(1)}, bf16[128,1024]{1,0:T(8,128)(2,1)S(1)}, u32[]{:S(2)}, u32[]{:S(2)}) collective-permute-start(bf16[128,1024]{1,0:T(8,128)(2,1)S(1)} %copy-done.9), channel_id=1, source_target_pairs={{0,2},{1,3},{2,0},{3,1},{4,6},{5,7},{6,4},{7,5},{8,10},{9,11},{10,... | collective-permute-start | bytes 786440 | tf_op jit(solution)/shard_map/ppermute | solution.py:343
  68.7 14.4 %collective-permute-start.19 = (bf16[128,1024]{1,0:T(8,128)(2,1)S(1)}, bf16[128,1024]{1,0:T(8,128)(2,1)S(1)}, u32[]{:S(2)}, u32[]{:S(2)}) collective-permute-start(bf16[128,1024]{1,0:T(8,128)(2,1)S(1)} %copy-done.8), channel_id=1, source_target_pairs={{0,3},{1,0},{2,1},{3,2},{4,7},{5,4},{6,5},{7,6},{8,11},{9,8},{10,9... | collective-permute-start | bytes 786440 | tf_op jit(solution)/shard_map/ppermute | solution.py:343
  81.3 21.6 %copy-start.3 = (bf16[256,1024]{1,0:T(8,128)(2,1)S(1)}, bf16[256,1024]{1,0:T(8,128)(2,1)}, u32[]{:S(2)}) copy-start(bf16[256,1024]{1,0:T(8,128)(2,1)} %proj_ref.5) | copy-start | bytes 1572868
  81.3 21.6 %copy-start.4 = (bf16[128,1024]{1,0:T(8,128)(2,1)S(1)}, bf16[128,1024]{1,0:T(8,128)(2,1)}, u32[]{:S(2)}) copy-start(bf16[128,1024]{1,0:T(8,128)(2,1)} %get-tuple-element.83.refs_1_) | copy-start | bytes 786436
  83.0 1.3 %collective-permute-start.17 = (bf16[128,256]{1,0:T(8,128)(2,1)S(1)}, bf16[128,256]{1,0:T(8,128)(2,1)S(1)}, u32[]{:S(2)}, u32[]{:S(2)}) collective-permute-start(bf16[128,256]{1,0:T(8,128)(2,1)S(1)} %get-tuple-element.73), channel_id=1, source_target_pairs={{0,4},{4,0},{8,12},{12,8},{16,20},{20,16},{24,28},{28,24},{1,5},{5... | collective-permute-start | bytes 196616 | tf_op jit(solution)/shard_map/ppermute | solution.py:360
  85.4 8.3 %collective-permute-start.20 = (bf16[128,512]{1,0:T(8,128)(2,1)S(1)}, bf16[128,512]{1,0:T(8,128)(2,1)S(1)}, u32[]{:S(2)}, u32[]{:S(2)}) collective-permute-start(bf16[128,512]{1,0:T(8,128)(2,1)S(1)} %get-tuple-element.78), channel_id=1, source_target_pairs={{0,1},{1,2},{2,3},{3,0},{4,5},{5,6},{6,7},{7,4},{8,9},{9,10},{10,1... | collective-permute-start | bytes 393224 | tf_op jit(solution)/shard_map/ppermute | solution.py:343
  86.4 12.2 %collective-permute-start.21 = (bf16[128,512]{1,0:T(8,128)(2,1)S(1)}, bf16[128,512]{1,0:T(8,128)(2,1)S(1)}, u32[]{:S(2)}, u32[]{:S(2)}) collective-permute-start(bf16[128,512]{1,0:T(8,128)(2,1)S(1)} %get-tuple-element.79), channel_id=1, source_target_pairs={{0,2},{1,3},{2,0},{3,1},{4,6},{5,7},{6,4},{7,5},{8,10},{9,11},{10,... | collective-permute-start | bytes 393224 | tf_op jit(solution)/shard_map/ppermute | solution.py:343
  88.2 10.3 %collective-permute-start.22 = (bf16[128,512]{1,0:T(8,128)(2,1)S(1)}, bf16[128,512]{1,0:T(8,128)(2,1)S(1)}, u32[]{:S(2)}, u32[]{:S(2)}) collective-permute-start(bf16[128,512]{1,0:T(8,128)(2,1)S(1)} %get-tuple-element.80), channel_id=1, source_target_pairs={{0,3},{1,0},{2,1},{3,2},{4,7},{5,4},{6,5},{7,6},{8,11},{9,8},{10,9... | collective-permute-start | bytes 393224 | tf_op jit(solution)/shard_map/ppermute | solution.py:343
  99.5 8.8 %all-to-all-start = ((bf16[8,16,512]{2,1,0:T(8,128)(2,1)}), bf16[8,16,512]{2,1,0:T(8,128)(2,1)S(1)}, u32[]{:S(2)}, u32[]{:S(2)}) async-start(bf16[8,16,512]{2,1,0:T(8,128)(2,1)} %bitcast.8), calls=%async_computation | async-start | bytes 262144 | tf_op jit(solution)/shard_map/all_to_all | solution.py:436
  (2 other events, 13.8 us)

commit v12 on v11

--- a/solution.py
+++ b/solution.py
@@ -416,14 +416,13 @@
     early_shares = gather(early_share, "head")
     late_share = sum(p.astype(F32) for p in chunks).astype(BF16)
     weight = jnp.transpose(global_qkv, (1, 0, 2))
-    weight, late_share, parts = lax.optimization_barrier((weight, late_share, parts))
+    weight, late_share = lax.optimization_barrier((weight, late_share))
     late_shares = gather(late_share, "head")
     residual = jnp.concatenate([early_share, late_share], axis=0)
     ids = (me - jnp.arange(ways, dtype=jnp.int32)) % ways
     core = (seq % 2).reshape(1)
     kept, given = global_heads(depth, core, ids, global_gain.reshape(ways, 1, -1), early_shares, late_shares, fetch(weight))
     received = swap_cores(given, "seq")
-    parts[1] = shift(parts[1], "head", 1)
     received, *parts = lax.optimization_barrier((received, *parts))
     half = kept.shape[1] // 3
     keyed = jnp.concatenate([kept[:, half:], received[:, half:]], axis=0)
@@ -432,6 +431,8 @@
     own_heads, other_heads = attend(depth, seq.reshape(1), twin_ids("seq"), global_scale, kept, received, pieces)
     other_heads, parts[2:] = lax.optimization_barrier((swap_cores(other_heads, "seq"), parts[2:]))
     updates = scatter(project(core, slots, own_heads, other_heads, global_out), "head")
+    updates, parts[1] = lax.optimization_barrier((updates, parts[1]))
+    parts[1] = shift(parts[1], "head", 1)
     result, routed = finish_result(owner_order(owners, seq, patches), residual, updates)
     global_state = lax.all_to_all(routed, "seq", split_axis=0, concat_axis=0, tiled=True)
     byte_out = finish_bytes(result, back_proj, [early] + parts)

time: 109 us -> 109 us (level)
  waiting for transfers between devices: 36.9 us -> 25.1 us
  blocking collectives: 0 us -> 8.99 us
  starting transfers between devices: 39.3 us -> 42.4 us
    all_to_all x0 -> x1, blocking collectives: none -> 8.99 us  [on_device(): lax.all_to_all(routed, 'seq', split_axis=0, concat_axis=0, tiled=True)]
    ppermute x21, waiting for transfers between devices: 30.9 us -> 22.7 us  [shift(): lax.ppermute(value, axis, [(i, (i + step) % count) for i in range(count)])]
    ppermute x21, starting transfers between devices: 35.8 us -> 42.3 us  [shift(): lax.ppermute(value, axis, [(i, (i + step) % count) for i in range(count)])]
    all_to_all x1 -> x0, waiting for transfers between devices: 3.52 us -> none  [on_device(): lax.all_to_all(routed, 'seq', split_axis=0, concat_axis=0, tiled=True)]
    all_to_all x1 -> x0, starting transfers between devices: 3.37 us -> none  [on_device(): lax.all_to_all(routed, 'seq', split_axis=0, concat_axis=0, tiled=True)]
  transfers between devices with their start and end apart: 24 -> 23, of which waited for: 9 -> 9; matrix products, arithmetic and copies ran while one was open for 1% -> 0% of each run, Pallas kernels for 16% -> 14%
where the time goes in v12:
time: 109 us
  starting transfers between devices  42.4 us (39%)
  Pallas kernels  29 us (27%)
  waiting for transfers between devices  25.1 us (23%)
  blocking collectives  8.99 us (8%)
  local copies, waits for them, and re-layouts  1.73 us (2%)
    ppermute x21, starting transfers between devices, shift(): lax.ppermute(value, axis, [(i, (i + step) % count) for i in range(count)])  42.3 us
    ppermute x21, waiting for transfers between devices, shift(): lax.ppermute(value, axis, [(i, (i + step) % count) for i in range(count)])  22.7 us
    pallas_call x2, Pallas kernels, local_part(): pl.pallas_call(functools.partial(local_kernel, span, ways, piece, last),...  20.2 us
    all_to_all x1, blocking collectives, on_device(): lax.all_to_all(routed, 'seq', split_axis=0, concat_axis=0, tiled=True)  8.99 us
    pallas_call x1, Pallas kernels, fetch(): pl.pallas_call(fetch_kernel, in_specs=[HBM], out_specs=VMEM, out_shape=pl...  2.89 us
    ppermute x2, waiting for transfers between devices, swap_cores(): lax.ppermute(value, axis, [(i, i ^ 1) for i in range(lax.axis_size(axis))])  2.41 us
  transfers between devices with their start and end apart: 23, of which 9 were waited for; matrix products, arithmetic and copies ran while one was open for 0% of the time, Pallas kernels for 14%

profile of v12, /device:TPU:0, one launch (start us, length us, event | category | flops | bytes accessed | tf_op | source)
XLA Modules:
  0.0 108.5 jit_solution(17371026670926448090)
XLA Ops:
  0.6 10.1 %local_part.2 = (bf16[128,1024]{1,0:T(8,128)(2,1)}, bf16[128,1024]{1,0:T(8,128)(2,1)}, bf16[128,1024]{1,0:T(8,128)(2,1)}, bf16[128,1024]{1,0:T(8,128)(2,1)}) custom-call(f32[2]{0:T(128)} %scale_ref.4, f32[1,1024]{1,0:T(1,128)} %bitcast.19, bf16[1024,1024]{1,0:T(8,128)(2,1)} %bitcast.15, bf16[3,1024,256]{2,1,0:T(8,128)(2,1)} %bitcast.17, ...), custom_call_target="tpu_custom_call" | custom-call | flops 4294967296 | bytes 10485760 | tf_op jit(solution)/shard_map/local_part/pallas_call | solution.py:117
  10.8 3.1 %collective-permute-start = (bf16[128,1024]{1,0:T(8,128)(2,1)}, bf16[128,1024]{1,0:T(8,128)(2,1)S(1)}, u32[]{:S(2)}, u32[]{:S(2)}) collective-permute-start(bf16[128,1024]{1,0:T(8,128)(2,1)} %get-tuple-element.51), channel_id=1, source_target_pairs={{0,1},{1,2},{2,3},{3,0},{4,5},{5,6},{6,7},{7,4},{8,9},{9,10},{10,1... | collective-permute-start | bytes 786440 | tf_op jit(solution)/shard_map/ppermute | solution.py:343
  13.9 2.6 %collective-permute-start.1 = (bf16[128,1024]{1,0:T(8,128)(2,1)}, bf16[128,1024]{1,0:T(8,128)(2,1)S(1)}, u32[]{:S(2)}, u32[]{:S(2)}) collective-permute-start(bf16[128,1024]{1,0:T(8,128)(2,1)} %get-tuple-element.53), channel_id=1, source_target_pairs={{0,2},{1,3},{2,0},{3,1},{4,6},{5,7},{6,4},{7,5},{8,10},{9,11},{10,... | collective-permute-start | bytes 786440 | tf_op jit(solution)/shard_map/ppermute | solution.py:343
  16.4 1.3 %collective-permute-start.2 = (bf16[128,1024]{1,0:T(8,128)(2,1)}, bf16[128,1024]{1,0:T(8,128)(2,1)S(1)}, u32[]{:S(2)}, u32[]{:S(2)}) collective-permute-start(bf16[128,1024]{1,0:T(8,128)(2,1)} %get-tuple-element.54), channel_id=1, source_target_pairs={{0,3},{1,0},{2,1},{3,2},{4,7},{5,4},{6,5},{7,6},{8,11},{9,8},{10,9... | collective-permute-start | bytes 786440 | tf_op jit(solution)/shard_map/ppermute | solution.py:343
  17.8 10.1 %local_part.3 = (bf16[128,1024]{1,0:T(8,128)(2,1)}, bf16[128,1024]{1,0:T(8,128)(2,1)}, bf16[128,1024]{1,0:T(8,128)(2,1)}, bf16[128,1024]{1,0:T(8,128)(2,1)}, bf1...) custom-call(f32[2]{0:T(128)} %scale_ref.4, ...), custom_call_target="tpu_custom_call" | custom-call | flops 4294967296 | bytes 10485760 | tf_op jit(solution)/shard_map/local_part/pallas_call | solution.py:117
  27.9 7.1 %collective-permute-start.3 = (bf16[64,512]{1,0:T(8,128)(2,1)S(1)}, bf16[64,512]{1,0:T(8,128)(2,1)S(1)}, u32[]{:S(2)}, u32[]{:S(2)}) collective-permute-start(bf16[64,512]{1,0:T(8,128)(2,1)S(1)} %get-tuple-element.57), channel_id=1, source_target_pairs={{0,1},{1,2},{2,3},{3,0},{4,5},{5,6},{6,7},{7,4},{8,9},{9,10},{10,1... | collective-permute-start | bytes 196616 | tf_op jit(solution)/shard_map/ppermute | solution.py:343
  35.0 2.0 %collective-permute-start.4 = (bf16[64,512]{1,0:T(8,128)(2,1)S(1)}, bf16[64,512]{1,0:T(8,128)(2,1)S(1)}, u32[]{:S(2)}, u32[]{:S(2)}) collective-permute-start(bf16[64,512]{1,0:T(8,128)(2,1)S(1)} %get-tuple-element.58), channel_id=1, source_target_pairs={{0,2},{1,3},{2,0},{3,1},{4,6},{5,7},{6,4},{7,5},{8,10},{9,11},{10,... | collective-permute-start | bytes 196616 | tf_op jit(solution)/shard_map/ppermute | solution.py:343
  37.0 2.9 %collective-permute-start.5 = (bf16[64,512]{1,0:T(8,128)(2,1)S(1)}, bf16[64,512]{1,0:T(8,128)(2,1)S(1)}, u32[]{:S(2)}, u32[]{:S(2)}) collective-permute-start(bf16[64,512]{1,0:T(8,128)(2,1)S(1)} %get-tuple-element.59), channel_id=1, source_target_pairs={{0,3},{1,0},{2,1},{3,2},{4,7},{5,4},{6,5},{7,6},{8,11},{9,8},{10,9... | collective-permute-start | bytes 196616 | tf_op jit(solution)/shard_map/ppermute | solution.py:343
  40.2 4.3 %collective-permute-start.8 = (bf16[64,512]{1,0:T(8,128)(2,1)S(1)}, bf16[64,512]{1,0:T(8,128)(2,1)S(1)}, u32[]{:S(2)}, u32[]{:S(2)}) collective-permute-start(bf16[64,512]{1,0:T(8,128)(2,1)S(1)} %get-tuple-element.55.refs_0_), channel_id=1, source_target_pairs={{0,3},{1,0},{2,1},{3,2},{4,7},{5,4},{6,5},{7,6},{8,11},{9,8},{10,9... | collective-permute-start | bytes 196616 | tf_op jit(solution)/shard_map/ppermute | solution.py:343
  45.2 3.3 %collective-permute-start.11 = (bf16[64,512]{1,0:T(8,128)(2,1)S(1)}, bf16[64,512]{1,0:T(8,128)(2,1)S(1)}, u32[]{:S(2)}, u32[]{:S(2)}) collective-permute-start(bf16[64,512]{1,0:T(8,128)(2,1)S(1)} %add_convert_fusion.refs_4_), channel_id=1, source_target_pairs={{0,3},{1,0},{2,1},{3,2},{4,7},{5,4},{6,5},{7,6},{8,11},{9,8},{10,9... | collective-permute-start | bytes 196616 | tf_op jit(solution)/shard_map/ppermute | solution.py:343
  48.5 1.1 collective-permute-start.10
  49.6 2.9 %fetch.1.refs_8_ = bf16[3,2048,512]{2,1,0:T(8,128)(2,1)S(1)} custom-call(bf16[3,2048,512]{2,1,0:T(8,128)(2,1)} %bitcast.13), custom_call_target="tpu_custom_call" | custom-call | tf_op jit(solution)/shard_map/fetch/pallas_call | solution.py:173
  52.5 0.7 collective-permute-done.7.refs_2_
  53.3 2.9 %collective-permute-done.10.refs_6_ = bf16[64,512]{1,0:T(8,128)(2,1)S(1)} collective-permute-done((bf16[64,512]{1,0:T(8,128)(2,1)S(1)}, bf16[64,512]{1,0:T(8,128)(2,1)S(1)}, u32[]{:S(2)}, u32[]{:S(2)}) %collective-permute-start.10) | collective-permute-done | bytes 65568 | tf_op jit(solution)/shard_map/ppermute | solution.py:343
  56.2 1.7 %global_heads.1 = (bf16[128,768]{1,0:T(8,128)(2,1)S(1)}, bf16[128,768]{1,0:T(8,128)(2,1)S(1)}) custom-call(s32[1]{0:T(128)} %bitcast.5.core_ref, s32[4]{0:T(128)S(1)} %and_select_fusion.ids_ref, f32[4,1,512]{2,1,0:T(1,128)S(1)} %bitcast.12, bf16[64,512]{1,0:T(8,128)(2,1)S(1)} %get-tuple-element.55.refs_0_, ...), custom_call_target="tpu_custom_call" | custom-call | tf_op jit(solution)/shard_map/global_heads/pallas_call | solution.py:207
  58.2 1.2 %collective-permute-done.12.given_ref = bf16[128,768]{1,0:T(8,128)(2,1)S(1)} collective-permute-done((bf16[128,768]{1,0:T(8,128)(2,1)S(1)}, bf16[128,768]{1,0:T(8,128)(2,1)S(1)}, u32[]{:S(2)}, u32[]{:S(2)}) %collective-permute-start.12) | collective-permute-done | bytes 196640 | tf_op jit(solution)/shard_map/ppermute | solution.py:360
  59.5 2.5 %collective-permute-start.15 = (bf16[256,512]{1,0:T(8,128)(2,1)S(1)}, bf16[256,512]{1,0:T(8,128)(2,1)S(1)}, u32[]{:S(2)}, u32[]{:S(2)}) collective-permute-start(bf16[256,512]{1,0:T(8,128)(2,1)S(1)} %pad_maximum_fusion), channel_id=1, source_target_pairs={{0,24},{4,28},{8,0},{12,4},{16,8},{20,12},{24,16},{28,20},{1,25},{... | collective-permute-start | bytes 786440 | tf_op jit(solution)/shard_map/ppermute | solution.py:343
  63.1 0.7 collective-permute-start.17
  63.8 0.8 collective-permute-start.18
  64.7 4.0 %collective-permute-done.15.refs_2_ = bf16[256,512]{1,0:T(8,128)(2,1)S(1)} collective-permute-done((bf16[256,512]{1,0:T(8,128)(2,1)S(1)}, bf16[256,512]{1,0:T(8,128)(2,1)S(1)}, u32[]{:S(2)}, u32[]{:S(2)}) %collective-permute-start.15) | collective-permute-done | bytes 262176 | tf_op jit(solution)/shard_map/ppermute | solution.py:343
  68.7 7.0 %collective-permute-done.14.refs_1_ = bf16[256,512]{1,0:T(8,128)(2,1)S(1)} collective-permute-done((bf16[256,512]{1,0:T(8,128)(2,1)S(1)}, bf16[256,512]{1,0:T(8,128)(2,1)S(1)}, u32[]{:S(2)}, u32[]{:S(2)}) %collective-permute-start.14) | collective-permute-done | bytes 262176 | tf_op jit(solution)/shard_map/ppermute | solution.py:343
  75.7 1.7 %attend.1 = (bf16[128,256]{1,0:T(8,128)(2,1)S(1)}, bf16[128,256]{1,0:T(8,128)(2,1)S(1)}) custom-call(s32[1]{0:T(128)} %bitcast.6.me_ref, s32[4]{0:T(128)S(1)} %and_select_fusion.1.ids_ref, f32[4]{0:T(128)S(1)} %copy-done.7, bf16[128,768]{1,0:T(8,128)(2,1)S(1)} %get-tuple-element.62.kept_ref, bf16[128,768]{1,0:T(8,128)(2,1)S(1)} %collective-permute-done.12.given_ref, ...), custom_call_target="tpu_custom_call" | custom-call | flops 1 | bytes 1 | tf_op jit(solution)/shard_map/attend/pallas_call | solution.py:250
  77.5 1.2 %collective-permute-done.16.other_ref = bf16[128,256]{1,0:T(8,128)(2,1)S(1)} collective-permute-done((bf16[128,256]{1,0:T(8,128)(2,1)S(1)}, bf16[128,256]{1,0:T(8,128)(2,1)S(1)}, u32[]{:S(2)}, u32[]{:S(2)}) %collective-permute-start.16) | collective-permute-done | bytes 65568 | tf_op jit(solution)/shard_map/ppermute | solution.py:360
  78.7 1.0 project.1
  79.7 3.2 %collective-permute-start.19 = (bf16[128,512]{1,0:T(8,128)(2,1)S(1)}, bf16[128,512]{1,0:T(8,128)(2,1)S(1)}, u32[]{:S(2)}, u32[]{:S(2)}) collective-permute-start(bf16[128,512]{1,0:T(8,128)(2,1)S(1)} %get-tuple-element.75), channel_id=1, source_target_pairs={{0,1},{1,2},{2,3},{3,0},{4,5},{5,6},{6,7},{7,4},{8,9},{9,10},{10,1... | collective-permute-start | bytes 393224 | tf_op jit(solution)/shard_map/ppermute | solution.py:343
  83.0 2.3 %collective-permute-start.20 = (bf16[128,512]{1,0:T(8,128)(2,1)S(1)}, bf16[128,512]{1,0:T(8,128)(2,1)S(1)}, u32[]{:S(2)}, u32[]{:S(2)}) collective-permute-start(bf16[128,512]{1,0:T(8,128)(2,1)S(1)} %get-tuple-element.76), channel_id=1, source_target_pairs={{0,2},{1,3},{2,0},{3,1},{4,6},{5,7},{6,4},{7,5},{8,10},{9,11},{10,... | collective-permute-start | bytes 393224 | tf_op jit(solution)/shard_map/ppermute | solution.py:343
  85.4 3.8 %collective-permute-done.19.refs_1_ = bf16[128,512]{1,0:T(8,128)(2,1)S(1)} collective-permute-done((bf16[128,512]{1,0:T(8,128)(2,1)S(1)}, bf16[128,512]{1,0:T(8,128)(2,1)S(1)}, u32[]{:S(2)}, u32[]{:S(2)}) %collective-permute-start.19) | collective-permute-done | bytes 131104 | tf_op jit(solution)/shard_map/ppermute | solution.py:343
  89.2 4.2 %collective-permute-done.20.refs_2_ = bf16[128,512]{1,0:T(8,128)(2,1)S(1)} collective-permute-done((bf16[128,512]{1,0:T(8,128)(2,1)S(1)}, bf16[128,512]{1,0:T(8,128)(2,1)S(1)}, u32[]{:S(2)}, u32[]{:S(2)}) %collective-permute-start.20) | collective-permute-done | bytes 131104 | tf_op jit(solution)/shard_map/ppermute | solution.py:343
  93.5 3.2 %collective-permute-start.22 = (bf16[128,1024]{1,0:T(8,128)(2,1)S(1)}, bf16[128,1024]{1,0:T(8,128)(2,1)S(1)}, u32[]{:S(2)}, u32[]{:S(2)}) collective-permute-start(bf16[128,1024]{1,0:T(8,128)(2,1)S(1)} %copy-done.8), channel_id=1, source_target_pairs={{0,1},{1,2},{2,3},{3,0},{4,5},{5,6},{6,7},{7,4},{8,9},{9,10},{10,1... | collective-permute-start | bytes 786440 | tf_op jit(solution)/shard_map/ppermute | solution.py:343
  97.0 9.0 %all_to_all.12 = bf16[8,16,512]{2,1,0:T(8,128)(2,1)S(1)} all-to-all(bf16[8,16,512]{2,1,0:T(8,128)(2,1)S(1)} %bitcast.11), channel_id=1, replica_groups=mesh['seq'=8,'head'=4] {'seq'}, dimensions={0} | all-to-all | bytes 262144 | tf_op jit(solution)/shard_map/all_to_all | solution.py:437
  106.0 0.9 finish_bytes.1
  106.9 1.0 reshape.82
  (62 shorter events, 3.8 us)
Async XLA Ops:
  0.6 57.4 %copy-start = (s32[8,16]{1,0:T(8,128)S(1)}, s32[8,16]{1,0:T(8,128)}, u32[]{:S(2)}) copy-start(s32[8,16]{1,0:T(8,128)} %param.27) | copy-start | bytes 1540
  10.8 17.2 %collective-permute-start = (bf16[128,1024]{1,0:T(8,128)(2,1)}, bf16[128,1024]{1,0:T(8,128)(2,1)S(1)}, u32[]{:S(2)}, u32[]{:S(2)}) collective-permute-start(bf16[128,1024]{1,0:T(8,128)(2,1)} %get-tuple-element.51), channel_id=1, source_target_pairs={{0,1},{1,2},{2,3},{3,0},{4,5},{5,6},{6,7},{7,4},{8,9},{9,10},{10,1... | collective-permute-start | bytes 786440 | tf_op jit(solution)/shard_map/ppermute | solution.py:343
  13.9 26.0 %collective-permute-start.1 = (bf16[128,1024]{1,0:T(8,128)(2,1)}, bf16[128,1024]{1,0:T(8,128)(2,1)S(1)}, u32[]{:S(2)}, u32[]{:S(2)}) collective-permute-start(bf16[128,1024]{1,0:T(8,128)(2,1)} %get-tuple-element.53), channel_id=1, source_target_pairs={{0,2},{1,3},{2,0},{3,1},{4,6},{5,7},{6,4},{7,5},{8,10},{9,11},{10,... | collective-permute-start | bytes 786440 | tf_op jit(solution)/shard_map/ppermute | solution.py:343
  16.4 23.4 %copy-start.2 = (bf16[1024,256]{1,0:T(8,128)(2,1)S(1)}, bf16[1024,256]{1,0:T(8,128)(2,1)}, u32[]{:S(2)}) copy-start(bf16[1024,256]{1,0:T(8,128)(2,1)} %proj_ref.3) | copy-start | bytes 1572868
  16.4 23.4 %copy-start.5 = (bf16[128,1024]{1,0:T(8,128)(2,1)S(1)}, bf16[128,1024]{1,0:T(8,128)(2,1)}, u32[]{:S(2)}) copy-start(bf16[128,1024]{1,0:T(8,128)(2,1)} %get-tuple-element.46.refs_0_) | copy-start | bytes 786436
  16.4 23.4 %collective-permute-start.2 = (bf16[128,1024]{1,0:T(8,128)(2,1)}, bf16[128,1024]{1,0:T(8,128)(2,1)S(1)}, u32[]{:S(2)}, u32[]{:S(2)}) collective-permute-start(bf16[128,1024]{1,0:T(8,128)(2,1)} %get-tuple-element.54), channel_id=1, source_target_pairs={{0,3},{1,0},{2,1},{3,2},{4,7},{5,4},{6,5},{7,6},{8,11},{9,8},{10,9... | collective-permute-start | bytes 786440 | tf_op jit(solution)/shard_map/ppermute | solution.py:343
  27.9 16.7 %collective-permute-start.3 = (bf16[64,512]{1,0:T(8,128)(2,1)S(1)}, bf16[64,512]{1,0:T(8,128)(2,1)S(1)}, u32[]{:S(2)}, u32[]{:S(2)}) collective-permute-start(bf16[64,512]{1,0:T(8,128)(2,1)S(1)} %get-tuple-element.57), channel_id=1, source_target_pairs={{0,1},{1,2},{2,3},{3,0},{4,5},{5,6},{6,7},{7,4},{8,9},{9,10},{10,1... | collective-permute-start | bytes 196616 | tf_op jit(solution)/shard_map/ppermute | solution.py:343
  35.0 10.2 %collective-permute-start.4 = (bf16[64,512]{1,0:T(8,128)(2,1)S(1)}, bf16[64,512]{1,0:T(8,128)(2,1)S(1)}, u32[]{:S(2)}, u32[]{:S(2)}) collective-permute-start(bf16[64,512]{1,0:T(8,128)(2,1)S(1)} %get-tuple-element.58), channel_id=1, source_target_pairs={{0,2},{1,3},{2,0},{3,1},{4,6},{5,7},{6,4},{7,5},{8,10},{9,11},{10,... | collective-permute-start | bytes 196616 | tf_op jit(solution)/shard_map/ppermute | solution.py:343
  37.0 8.2 %collective-permute-start.5 = (bf16[64,512]{1,0:T(8,128)(2,1)S(1)}, bf16[64,512]{1,0:T(8,128)(2,1)S(1)}, u32[]{:S(2)}, u32[]{:S(2)}) collective-permute-start(bf16[64,512]{1,0:T(8,128)(2,1)S(1)} %get-tuple-element.59), channel_id=1, source_target_pairs={{0,3},{1,0},{2,1},{3,2},{4,7},{5,4},{6,5},{7,6},{8,11},{9,8},{10,9... | collective-permute-start | bytes 196616 | tf_op jit(solution)/shard_map/ppermute | solution.py:343
  40.2 9.4 %collective-permute-start.8 = (bf16[64,512]{1,0:T(8,128)(2,1)S(1)}, bf16[64,512]{1,0:T(8,128)(2,1)S(1)}, u32[]{:S(2)}, u32[]{:S(2)}) collective-permute-start(bf16[64,512]{1,0:T(8,128)(2,1)S(1)} %get-tuple-element.55.refs_0_), channel_id=1, source_target_pairs={{0,3},{1,0},{2,1},{3,2},{4,7},{5,4},{6,5},{7,6},{8,11},{9,8},{10,9... | collective-permute-start | bytes 196616 | tf_op jit(solution)/shard_map/ppermute | solution.py:343
  44.5 8.7 %collective-permute-start.7 = (bf16[64,512]{1,0:T(8,128)(2,1)S(1)}, bf16[64,512]{1,0:T(8,128)(2,1)S(1)}, u32[]{:S(2)}, u32[]{:S(2)}) collective-permute-start(bf16[64,512]{1,0:T(8,128)(2,1)S(1)} %get-tuple-element.55.refs_0_), channel_id=1, source_target_pairs={{0,2},{1,3},{2,0},{3,1},{4,6},{5,7},{6,4},{7,5},{8,10},{9,11},{10,... | collective-permute-start | bytes 196616 | tf_op jit(solution)/shard_map/ppermute | solution.py:343
  44.6 8.6 %collective-permute-start.6 = (bf16[64,512]{1,0:T(8,128)(2,1)S(1)}, bf16[64,512]{1,0:T(8,128)(2,1)S(1)}, u32[]{:S(2)}, u32[]{:S(2)}) collective-permute-start(bf16[64,512]{1,0:T(8,128)(2,1)S(1)} %get-tuple-element.55.refs_0_), channel_id=1, source_target_pairs={{0,1},{1,2},{2,3},{3,0},{4,5},{5,6},{6,7},{7,4},{8,9},{9,10},{10,1... | collective-permute-start | bytes 196616 | tf_op jit(solution)/shard_map/ppermute | solution.py:343
  45.2 8.0 %collective-permute-start.11 = (bf16[64,512]{1,0:T(8,128)(2,1)S(1)}, bf16[64,512]{1,0:T(8,128)(2,1)S(1)}, u32[]{:S(2)}, u32[]{:S(2)}) collective-permute-start(bf16[64,512]{1,0:T(8,128)(2,1)S(1)} %add_convert_fusion.refs_4_), channel_id=1, source_target_pairs={{0,3},{1,0},{2,1},{3,2},{4,7},{5,4},{6,5},{7,6},{8,11},{9,8},{10,9... | collective-permute-start | bytes 196616 | tf_op jit(solution)/shard_map/ppermute | solution.py:343
  48.5 7.6 %collective-permute-start.10 = (bf16[64,512]{1,0:T(8,128)(2,1)S(1)}, bf16[64,512]{1,0:T(8,128)(2,1)S(1)}, u32[]{:S(2)}, u32[]{:S(2)}) collective-permute-start(bf16[64,512]{1,0:T(8,128)(2,1)S(1)} %add_convert_fusion.refs_4_), channel_id=1, source_target_pairs={{0,2},{1,3},{2,0},{3,1},{4,6},{5,7},{6,4},{7,5},{8,10},{9,11},{10,... | collective-permute-start | bytes 196616 | tf_op jit(solution)/shard_map/ppermute | solution.py:343
  49.6 6.6 %collective-permute-start.9 = (bf16[64,512]{1,0:T(8,128)(2,1)S(1)}, bf16[64,512]{1,0:T(8,128)(2,1)S(1)}, u32[]{:S(2)}, u32[]{:S(2)}) collective-permute-start(bf16[64,512]{1,0:T(8,128)(2,1)S(1)} %add_convert_fusion.refs_4_), channel_id=1, source_target_pairs={{0,1},{1,2},{2,3},{3,0},{4,5},{5,6},{6,7},{7,4},{8,9},{9,10},{10,1... | collective-permute-start | bytes 196616 | tf_op jit(solution)/shard_map/ppermute | solution.py:343
  56.2 7.6 %copy-start.9 = (bf16[128,1024]{1,0:T(8,128)(2,1)S(1)}, bf16[128,1024]{1,0:T(8,128)(2,1)}, u32[]{:S(2)}) copy-start(bf16[128,1024]{1,0:T(8,128)(2,1)} %get-tuple-element.72) | copy-start | bytes 786436
  56.2 19.5 %copy-start.7 = (f32[4]{0:T(128)S(1)}, f32[4]{0:T(128)}, u32[]{:S(2)}) copy-start(f32[4]{0:T(128)} %scale_ref.5) | copy-start | bytes 52
  57.9 20.8 %copy-start.1 = (bf16[512,2048]{1,0:T(8,128)(2,1)S(1)}, bf16[512,2048]{1,0:T(8,128)(2,1)}, u32[]{:S(2)}) copy-start(bf16[512,2048]{1,0:T(8,128)(2,1)} %proj_ref.4) | copy-start | bytes 6291460
  57.9 1.5 %collective-permute-start.12 = (bf16[128,768]{1,0:T(8,128)(2,1)S(1)}, bf16[128,768]{1,0:T(8,128)(2,1)S(1)}, u32[]{:S(2)}, u32[]{:S(2)}) collective-permute-start(bf16[128,768]{1,0:T(8,128)(2,1)S(1)} %get-tuple-element.63), channel_id=1, source_target_pairs={{0,4},{4,0},{8,12},{12,8},{16,20},{20,16},{24,28},{28,24},{1,5},{5... | collective-permute-start | bytes 589832 | tf_op jit(solution)/shard_map/ppermute | solution.py:360
  59.4 34.1 %copy-start.8 = (bf16[128,1024]{1,0:T(8,128)(2,1)S(1)}, bf16[128,1024]{1,0:T(8,128)(2,1)}, u32[]{:S(2)}) copy-start(bf16[128,1024]{1,0:T(8,128)(2,1)} %get-tuple-element.86) | copy-start | bytes 786436
  59.5 9.2 %collective-permute-start.15 = (bf16[256,512]{1,0:T(8,128)(2,1)S(1)}, bf16[256,512]{1,0:T(8,128)(2,1)S(1)}, u32[]{:S(2)}, u32[]{:S(2)}) collective-permute-start(bf16[256,512]{1,0:T(8,128)(2,1)S(1)} %pad_maximum_fusion), channel_id=1, source_target_pairs={{0,24},{4,28},{8,0},{12,4},{16,8},{20,12},{24,16},{28,20},{1,25},{... | collective-permute-start | bytes 786440 | tf_op jit(solution)/shard_map/ppermute | solution.py:343
  62.0 13.7 %collective-permute-start.14 = (bf16[256,512]{1,0:T(8,128)(2,1)S(1)}, bf16[256,512]{1,0:T(8,128)(2,1)S(1)}, u32[]{:S(2)}, u32[]{:S(2)}) collective-permute-start(bf16[256,512]{1,0:T(8,128)(2,1)S(1)} %pad_maximum_fusion), channel_id=1, source_target_pairs={{0,16},{4,20},{8,24},{12,28},{16,0},{20,4},{24,8},{28,12},{1,17},{... | collective-permute-start | bytes 786440 | tf_op jit(solution)/shard_map/ppermute | solution.py:343
  62.5 13.2 %collective-permute-start.13 = (bf16[256,512]{1,0:T(8,128)(2,1)S(1)}, bf16[256,512]{1,0:T(8,128)(2,1)S(1)}, u32[]{:S(2)}, u32[]{:S(2)}) collective-permute-start(bf16[256,512]{1,0:T(8,128)(2,1)S(1)} %pad_maximum_fusion), channel_id=1, source_target_pairs={{0,8},{4,12},{8,16},{12,20},{16,24},{20,28},{24,0},{28,4},{1,9},{5... | collective-permute-start | bytes 786440 | tf_op jit(solution)/shard_map/ppermute | solution.py:343
  63.1 14.4 %collective-permute-start.17 = (bf16[128,1024]{1,0:T(8,128)(2,1)S(1)}, bf16[128,1024]{1,0:T(8,128)(2,1)S(1)}, u32[]{:S(2)}, u32[]{:S(2)}) collective-permute-start(bf16[128,1024]{1,0:T(8,128)(2,1)S(1)} %copy-done.10), channel_id=1, source_target_pairs={{0,2},{1,3},{2,0},{3,1},{4,6},{5,7},{6,4},{7,5},{8,10},{9,11},{10,... | collective-permute-start | bytes 786440 | tf_op jit(solution)/shard_map/ppermute | solution.py:343
  63.8 13.7 %collective-permute-start.18 = (bf16[128,1024]{1,0:T(8,128)(2,1)S(1)}, bf16[128,1024]{1,0:T(8,128)(2,1)S(1)}, u32[]{:S(2)}, u32[]{:S(2)}) collective-permute-start(bf16[128,1024]{1,0:T(8,128)(2,1)S(1)} %copy-done.9), channel_id=1, source_target_pairs={{0,3},{1,0},{2,1},{3,2},{4,7},{5,4},{6,5},{7,6},{8,11},{9,8},{10,9... | collective-permute-start | bytes 786440 | tf_op jit(solution)/shard_map/ppermute | solution.py:343
  75.7 30.3 %copy-start.3 = (bf16[256,1024]{1,0:T(8,128)(2,1)S(1)}, bf16[256,1024]{1,0:T(8,128)(2,1)}, u32[]{:S(2)}) copy-start(bf16[256,1024]{1,0:T(8,128)(2,1)} %proj_ref.5) | copy-start | bytes 1572868
  75.7 30.3 %copy-start.4 = (bf16[128,1024]{1,0:T(8,128)(2,1)S(1)}, bf16[128,1024]{1,0:T(8,128)(2,1)}, u32[]{:S(2)}) copy-start(bf16[128,1024]{1,0:T(8,128)(2,1)} %get-tuple-element.85.refs_1_) | copy-start | bytes 786436
  77.4 1.3 %collective-permute-start.16 = (bf16[128,256]{1,0:T(8,128)(2,1)S(1)}, bf16[128,256]{1,0:T(8,128)(2,1)S(1)}, u32[]{:S(2)}, u32[]{:S(2)}) collective-permute-start(bf16[128,256]{1,0:T(8,128)(2,1)S(1)} %get-tuple-element.70), channel_id=1, source_target_pairs={{0,4},{4,0},{8,12},{12,8},{16,20},{20,16},{24,28},{28,24},{1,5},{5... | collective-permute-start | bytes 196616 | tf_op jit(solution)/shard_map/ppermute | solution.py:360
  79.7 9.5 %collective-permute-start.19 = (bf16[128,512]{1,0:T(8,128)(2,1)S(1)}, bf16[128,512]{1,0:T(8,128)(2,1)S(1)}, u32[]{:S(2)}, u32[]{:S(2)}) collective-permute-start(bf16[128,512]{1,0:T(8,128)(2,1)S(1)} %get-tuple-element.75), channel_id=1, source_target_pairs={{0,1},{1,2},{2,3},{3,0},{4,5},{5,6},{6,7},{7,4},{8,9},{9,10},{10,1... | collective-permute-start | bytes 393224 | tf_op jit(solution)/shard_map/ppermute | solution.py:343
  83.0 10.4 %collective-permute-start.20 = (bf16[128,512]{1,0:T(8,128)(2,1)S(1)}, bf16[128,512]{1,0:T(8,128)(2,1)S(1)}, u32[]{:S(2)}, u32[]{:S(2)}) collective-permute-start(bf16[128,512]{1,0:T(8,128)(2,1)S(1)} %get-tuple-element.76), channel_id=1, source_target_pairs={{0,2},{1,3},{2,0},{3,1},{4,6},{5,7},{6,4},{7,5},{8,10},{9,11},{10,... | collective-permute-start | bytes 393224 | tf_op jit(solution)/shard_map/ppermute | solution.py:343
  85.3 8.2 %collective-permute-start.21 = (bf16[128,512]{1,0:T(8,128)(2,1)S(1)}, bf16[128,512]{1,0:T(8,128)(2,1)S(1)}, u32[]{:S(2)}, u32[]{:S(2)}) collective-permute-start(bf16[128,512]{1,0:T(8,128)(2,1)S(1)} %get-tuple-element.77), channel_id=1, source_target_pairs={{0,3},{1,0},{2,1},{3,2},{4,7},{5,4},{6,5},{7,6},{8,11},{9,8},{10,9... | collective-permute-start | bytes 393224 | tf_op jit(solution)/shard_map/ppermute | solution.py:343
  93.5 12.5 %collective-permute-start.22 = (bf16[128,1024]{1,0:T(8,128)(2,1)S(1)}, bf16[128,1024]{1,0:T(8,128)(2,1)S(1)}, u32[]{:S(2)}, u32[]{:S(2)}) collective-permute-start(bf16[128,1024]{1,0:T(8,128)(2,1)S(1)} %copy-done.8), channel_id=1, source_target_pairs={{0,1},{1,2},{2,3},{3,0},{4,5},{5,6},{6,7},{7,4},{8,9},{9,10},{10,1... | collective-permute-start | bytes 786440 | tf_op jit(solution)/shard_map/ppermute | solution.py:343
  (2 other events, 13.5 us)

commit v13 on v12

--- a/solution.py
+++ b/solution.py
@@ -282,24 +282,52 @@
 
 
 def result_kernel(count, order_ref, own_ref, *refs):
-    pieces, (result_ref, routed_ref) = refs[:count], refs[count:]
+    pieces, (result_ref, kept_ref, given_ref) = refs[:count], refs[count:]
     total = own_ref[...].astype(F32) + sum(p[...].astype(F32) for p in pieces)
     result = total.astype(BF16)
     result_ref[...] = result
-    routed_ref[...] = dot(order_ref[...], result).astype(BF16)
+    routed = dot(order_ref[...], result).astype(BF16)
+    half = kept_ref.shape[0]
+    kept_ref[...] = routed[:half]
+    given_ref[...] = routed[half:]
 
 
 def finish_result(order, residual, pieces):
+    rows, width = residual.shape
     shape = jax.ShapeDtypeStruct(residual.shape, BF16)
+    half = jax.ShapeDtypeStruct((rows // 2, width), BF16)
     return pl.pallas_call(
         functools.partial(result_kernel, len(pieces)),
         in_specs=[VMEM] * (2 + len(pieces)),
-        out_specs=(VMEM, VMEM),
-        out_shape=(shape, shape),
+        out_specs=(VMEM, VMEM, VMEM),
+        out_shape=(shape, half, half),
         compiler_params=pltpu.CompilerParams(vmem_limit_bytes=4 * 2**20),
         cost_estimate=BRIEF,
         name="finish_result",
     )(order, residual, *pieces)
+
+
+def sort_kernel(block, devices, rows_ref, out_ref):
+    me = lax.axis_index("seq")
+    rows = rows_ref.shape[0]
+    to = lax.broadcasted_iota(jnp.int32, (rows, rows), 0)
+    at = lax.broadcasted_iota(jnp.int32, (rows, rows), 1)
+    twin = lax.rem(me - at // (2 * block) * 2 + devices, devices)
+    source = twin ^ (at // block % 2)
+    order = (to == source * block + at % block).astype(F32).astype(BF16)
+    out_ref[...] = dot(order, rows_ref[...]).astype(BF16)
+
+
+def sort_rows(rows, devices):
+    return pl.pallas_call(
+        functools.partial(sort_kernel, rows.shape[0] // devices, devices),
+        in_specs=[VMEM],
+        out_specs=VMEM,
+        out_shape=jax.ShapeDtypeStruct(rows.shape, BF16),
+        compiler_params=pltpu.CompilerParams(vmem_limit_bytes=4 * 2**20),
+        cost_estimate=BRIEF,
+        name="sort_rows",
+    )(rows)
 
 
 def bytes_kernel(count, result_ref, proj_ref, *refs):
@@ -366,18 +394,28 @@
 
 
 def owner_order(owners, source, patches):
+    devices, count = owners.shape
     listed = lax.dynamic_index_in_dim(owners, source, 0, keepdims=False)
-    count = listed.shape[0]
     block = patches // count
     index = jnp.arange(count, dtype=jnp.int32)
-    before = (listed[None, :] < listed[:, None]) | (
-        (listed[None, :] == listed[:, None]) & (index[None, :] < index[:, None])
-    )
-    slot = jnp.sum(before, axis=1).astype(jnp.int32)
+    rank = jnp.sum((listed[None, :] == listed[:, None]) & (index[None, :] < index[:, None]), axis=1).astype(jnp.int32)
+    chips = devices // 2
+    order = (listed % 2 ^ source % 2) * chips + (listed // 2 - source // 2 + chips) % chips
+    slot = order * (count // devices) + rank
     row = jnp.arange(patches, dtype=jnp.int32)
     spread = jnp.sum(jnp.where(row[:, None] // block == index[None, :], slot[None, :], 0), axis=1).astype(jnp.int32)
     place = spread * block + row % block
     return (row[:, None] == place[None, :]).astype(BF16)
+
+
+def route(kept, given, axis):
+    devices = lax.axis_size(axis)
+    chips = devices // 2
+    width = kept.shape[1]
+    received = swap_cores(given, axis)
+    bundles = jnp.concatenate([a.reshape(chips, -1, width) for a in (kept, received)], axis=1)
+    arrived = [bundles[0]] + [shift(bundles[step], axis, 2 * step) for step in range(1, chips)]
+    return sort_rows(jnp.concatenate(arrived, axis=0), devices)
 
 
 def on_device(
@@ -433,8 +471,8 @@
     updates = scatter(project(core, slots, own_heads, other_heads, global_out), "head")
     updates, parts[1] = lax.optimization_barrier((updates, parts[1]))
     parts[1] = shift(parts[1], "head", 1)
-    result, routed = finish_result(owner_order(owners, seq, patches), residual, updates)
-    global_state = lax.all_to_all(routed, "seq", split_axis=0, concat_axis=0, tiled=True)
+    result, kept, given = finish_result(owner_order(owners, seq, patches), residual, updates)
+    global_state = route(kept, given, "seq")
     byte_out = finish_bytes(result, back_proj, [early] + parts)
     return byte_out.reshape(patches, own, width), global_state
 

time: 109 us -> 107 us (0.982)
  blocking collectives: 8.99 us -> 0 us
  waiting for transfers between devices: 25.1 us -> 28 us
  starting transfers between devices: 42.4 us -> 45 us
    all_to_all x1 -> x0, blocking collectives: 8.99 us -> none  [on_device(): lax.all_to_all(routed, 'seq', split_axis=0, concat_axis=0, tiled=True)]
    ppermute x21 -> x24, waiting for transfers between devices: 22.7 us -> 25.5 us  [shift(): lax.ppermute(value, axis, [(i, (i + step) % count) for i in range(count)])]
    ppermute x21 -> x24, starting transfers between devices: 42.3 us -> 44.8 us  [shift(): lax.ppermute(value, axis, [(i, (i + step) % count) for i in range(count)])]
    ppermute x2 -> x3, waiting for transfers between devices: 2.41 us -> 2.52 us  [swap_cores(): lax.ppermute(value, axis, [(i, i ^ 1) for i in range(lax.axis_size(axis))])]
  transfers between devices with their start and end apart: 23 -> 27, of which waited for: 9 -> 12; matrix products, arithmetic and copies ran while one was open for 0% -> 2% of each run, Pallas kernels for 14% -> 15%
where the time goes in v13:
time: 107 us
  starting transfers between devices  45 us (42%)
  Pallas kernels  29.8 us (28%)
  waiting for transfers between devices  28 us (26%)
  local copies, waits for them, and re-layouts  1.75 us (2%)
  other arithmetic  1.12 us (1%)
    ppermute x24, starting transfers between devices, shift(): lax.ppermute(value, axis, [(i, (i + step) % count) for i in range(count)])  44.8 us
    ppermute x24, waiting for transfers between devices, shift(): lax.ppermute(value, axis, [(i, (i + step) % count) for i in range(count)])  25.5 us
    pallas_call x2, Pallas kernels, local_part(): pl.pallas_call(functools.partial(local_kernel, span, ways, piece, last),...  20.2 us
    pallas_call x1, Pallas kernels, fetch(): pl.pallas_call(fetch_kernel, in_specs=[HBM], out_specs=VMEM, out_shape=pl...  2.89 us
    ppermute x3, waiting for transfers between devices, swap_cores(): lax.ppermute(value, axis, [(i, i ^ 1) for i in range(lax.axis_size(axis))])  2.52 us
  transfers between devices with their start and end apart: 27, of which 12 were waited for; matrix products, arithmetic and copies ran while one was open for 2% of the time, Pallas kernels for 15%

profile of v13, /device:TPU:0, one launch (start us, length us, event | category | flops | bytes accessed | tf_op | source)
XLA Modules:
  0.0 106.7 jit_solution(18320376980406406615)
XLA Ops:
  0.6 10.1 %local_part.2 = (bf16[128,1024]{1,0:T(8,128)(2,1)}, bf16[128,1024]{1,0:T(8,128)(2,1)}, bf16[128,1024]{1,0:T(8,128)(2,1)}, bf16[128,1024]{1,0:T(8,128)(2,1)}) custom-call(f32[2]{0:T(128)} %scale_ref.4, f32[1,1024]{1,0:T(1,128)} %bitcast.33, bf16[1024,1024]{1,0:T(8,128)(2,1)} %bitcast.29, bf16[3,1024,256]{2,1,0:T(8,128)(2,1)} %bitcast.31, ...), custom_call_target="tpu_custom_call" | custom-call | flops 4294967296 | bytes 10485760 | tf_op jit(solution)/shard_map/local_part/pallas_call | solution.py:117
  10.7 3.1 %collective-permute-start = (bf16[128,1024]{1,0:T(8,128)(2,1)}, bf16[128,1024]{1,0:T(8,128)(2,1)S(1)}, u32[]{:S(2)}, u32[]{:S(2)}) collective-permute-start(bf16[128,1024]{1,0:T(8,128)(2,1)} %get-tuple-element.52), channel_id=1, source_target_pairs={{0,1},{1,2},{2,3},{3,0},{4,5},{5,6},{6,7},{7,4},{8,9},{9,10},{10,1... | collective-permute-start | bytes 786440 | tf_op jit(solution)/shard_map/ppermute | solution.py:371
  13.8 2.6 %collective-permute-start.1 = (bf16[128,1024]{1,0:T(8,128)(2,1)}, bf16[128,1024]{1,0:T(8,128)(2,1)S(1)}, u32[]{:S(2)}, u32[]{:S(2)}) collective-permute-start(bf16[128,1024]{1,0:T(8,128)(2,1)} %get-tuple-element.54), channel_id=1, source_target_pairs={{0,2},{1,3},{2,0},{3,1},{4,6},{5,7},{6,4},{7,5},{8,10},{9,11},{10,... | collective-permute-start | bytes 786440 | tf_op jit(solution)/shard_map/ppermute | solution.py:371
  16.4 1.3 %collective-permute-start.2 = (bf16[128,1024]{1,0:T(8,128)(2,1)}, bf16[128,1024]{1,0:T(8,128)(2,1)S(1)}, u32[]{:S(2)}, u32[]{:S(2)}) collective-permute-start(bf16[128,1024]{1,0:T(8,128)(2,1)} %get-tuple-element.55), channel_id=1, source_target_pairs={{0,3},{1,0},{2,1},{3,2},{4,7},{5,4},{6,5},{7,6},{8,11},{9,8},{10,9... | collective-permute-start | bytes 786440 | tf_op jit(solution)/shard_map/ppermute | solution.py:371
  17.8 10.1 %local_part.3 = (bf16[128,1024]{1,0:T(8,128)(2,1)}, bf16[128,1024]{1,0:T(8,128)(2,1)}, bf16[128,1024]{1,0:T(8,128)(2,1)}, bf16[128,1024]{1,0:T(8,128)(2,1)}, bf1...) custom-call(f32[2]{0:T(128)} %scale_ref.4, ...), custom_call_target="tpu_custom_call" | custom-call | flops 4294967296 | bytes 10485760 | tf_op jit(solution)/shard_map/local_part/pallas_call | solution.py:117
  28.8 6.2 %collective-permute-start.3 = (bf16[64,512]{1,0:T(8,128)(2,1)S(1)}, bf16[64,512]{1,0:T(8,128)(2,1)S(1)}, u32[]{:S(2)}, u32[]{:S(2)}) collective-permute-start(bf16[64,512]{1,0:T(8,128)(2,1)S(1)} %get-tuple-element.58), channel_id=1, source_target_pairs={{0,1},{1,2},{2,3},{3,0},{4,5},{5,6},{6,7},{7,4},{8,9},{9,10},{10,1... | collective-permute-start | bytes 196616 | tf_op jit(solution)/shard_map/ppermute | solution.py:371
  35.0 2.0 %collective-permute-start.4 = (bf16[64,512]{1,0:T(8,128)(2,1)S(1)}, bf16[64,512]{1,0:T(8,128)(2,1)S(1)}, u32[]{:S(2)}, u32[]{:S(2)}) collective-permute-start(bf16[64,512]{1,0:T(8,128)(2,1)S(1)} %get-tuple-element.59), channel_id=1, source_target_pairs={{0,2},{1,3},{2,0},{3,1},{4,6},{5,7},{6,4},{7,5},{8,10},{9,11},{10,... | collective-permute-start | bytes 196616 | tf_op jit(solution)/shard_map/ppermute | solution.py:371
  36.9 2.9 %collective-permute-start.5 = (bf16[64,512]{1,0:T(8,128)(2,1)S(1)}, bf16[64,512]{1,0:T(8,128)(2,1)S(1)}, u32[]{:S(2)}, u32[]{:S(2)}) collective-permute-start(bf16[64,512]{1,0:T(8,128)(2,1)S(1)} %get-tuple-element.60), channel_id=1, source_target_pairs={{0,3},{1,0},{2,1},{3,2},{4,7},{5,4},{6,5},{7,6},{8,11},{9,8},{10,9... | collective-permute-start | bytes 196616 | tf_op jit(solution)/shard_map/ppermute | solution.py:371
  40.9 3.6 %collective-permute-start.8 = (bf16[64,512]{1,0:T(8,128)(2,1)S(1)}, bf16[64,512]{1,0:T(8,128)(2,1)S(1)}, u32[]{:S(2)}, u32[]{:S(2)}) collective-permute-start(bf16[64,512]{1,0:T(8,128)(2,1)S(1)} %get-tuple-element.56.refs_0_), channel_id=1, source_target_pairs={{0,3},{1,0},{2,1},{3,2},{4,7},{5,4},{6,5},{7,6},{8,11},{9,8},{10,9... | collective-permute-start | bytes 196616 | tf_op jit(solution)/shard_map/ppermute | solution.py:371
  45.2 3.3 %collective-permute-start.11 = (bf16[64,512]{1,0:T(8,128)(2,1)S(1)}, bf16[64,512]{1,0:T(8,128)(2,1)S(1)}, u32[]{:S(2)}, u32[]{:S(2)}) collective-permute-start(bf16[64,512]{1,0:T(8,128)(2,1)S(1)} %add_convert_fusion.refs_4_), channel_id=1, source_target_pairs={{0,3},{1,0},{2,1},{3,2},{4,7},{5,4},{6,5},{7,6},{8,11},{9,8},{10,9... | collective-permute-start | bytes 196616 | tf_op jit(solution)/shard_map/ppermute | solution.py:371
  48.5 1.1 collective-permute-start.10
  49.6 2.9 %fetch.1.refs_8_ = bf16[3,2048,512]{2,1,0:T(8,128)(2,1)S(1)} custom-call(bf16[3,2048,512]{2,1,0:T(8,128)(2,1)} %bitcast.27), custom_call_target="tpu_custom_call" | custom-call | tf_op jit(solution)/shard_map/fetch/pallas_call | solution.py:173
  53.2 2.9 %collective-permute-done.10.refs_6_ = bf16[64,512]{1,0:T(8,128)(2,1)S(1)} collective-permute-done((bf16[64,512]{1,0:T(8,128)(2,1)S(1)}, bf16[64,512]{1,0:T(8,128)(2,1)S(1)}, u32[]{:S(2)}, u32[]{:S(2)}) %collective-permute-start.10) | collective-permute-done | bytes 65568 | tf_op jit(solution)/shard_map/ppermute | solution.py:371
  56.2 1.7 %global_heads.1 = (bf16[128,768]{1,0:T(8,128)(2,1)S(1)}, bf16[128,768]{1,0:T(8,128)(2,1)S(1)}) custom-call(s32[1]{0:T(128)} %bitcast.7.core_ref, s32[4]{0:T(128)S(1)} %and_select_fusion.ids_ref, f32[4,1,512]{2,1,0:T(1,128)S(1)} %bitcast.26, bf16[64,512]{1,0:T(8,128)(2,1)S(1)} %get-tuple-element.56.refs_0_, ...), custom_call_target="tpu_custom_call" | custom-call | tf_op jit(solution)/shard_map/global_heads/pallas_call | solution.py:207
  58.1 1.3 %collective-permute-done.12.given_ref = bf16[128,768]{1,0:T(8,128)(2,1)S(1)} collective-permute-done((bf16[128,768]{1,0:T(8,128)(2,1)S(1)}, bf16[128,768]{1,0:T(8,128)(2,1)S(1)}, u32[]{:S(2)}, u32[]{:S(2)}) %collective-permute-start.12) | collective-permute-done | bytes 196640 | tf_op jit(solution)/shard_map/ppermute | solution.py:388
  59.4 2.5 %collective-permute-start.15 = (bf16[256,512]{1,0:T(8,128)(2,1)S(1)}, bf16[256,512]{1,0:T(8,128)(2,1)S(1)}, u32[]{:S(2)}, u32[]{:S(2)}) collective-permute-start(bf16[256,512]{1,0:T(8,128)(2,1)S(1)} %pad_maximum_fusion), channel_id=1, source_target_pairs={{0,24},{4,28},{8,0},{12,4},{16,8},{20,12},{24,16},{28,20},{1,25},{... | collective-permute-start | bytes 786440 | tf_op jit(solution)/shard_map/ppermute | solution.py:371
  64.5 4.1 %collective-permute-done.15.refs_2_ = bf16[256,512]{1,0:T(8,128)(2,1)S(1)} collective-permute-done((bf16[256,512]{1,0:T(8,128)(2,1)S(1)}, bf16[256,512]{1,0:T(8,128)(2,1)S(1)}, u32[]{:S(2)}, u32[]{:S(2)}) %collective-permute-start.15) | collective-permute-done | bytes 262176 | tf_op jit(solution)/shard_map/ppermute | solution.py:371
  68.6 7.0 %collective-permute-done.14.refs_1_ = bf16[256,512]{1,0:T(8,128)(2,1)S(1)} collective-permute-done((bf16[256,512]{1,0:T(8,128)(2,1)S(1)}, bf16[256,512]{1,0:T(8,128)(2,1)S(1)}, u32[]{:S(2)}, u32[]{:S(2)}) %collective-permute-start.14) | collective-permute-done | bytes 262176 | tf_op jit(solution)/shard_map/ppermute | solution.py:371
  75.6 1.7 %attend.1 = (bf16[128,256]{1,0:T(8,128)(2,1)S(1)}, bf16[128,256]{1,0:T(8,128)(2,1)S(1)}) custom-call(s32[1]{0:T(128)} %bitcast.8.me_ref, s32[4]{0:T(128)S(1)} %and_select_fusion.1.ids_ref, f32[4]{0:T(128)S(1)} %copy-done.6, bf16[128,768]{1,0:T(8,128)(2,1)S(1)} %get-tuple-element.63.kept_ref, bf16[128,768]{1,0:T(8,128)(2,1)S(1)} %collective-permute-done.12.given_ref, ...), custom_call_target="tpu_custom_call" | custom-call | flops 1 | bytes 1 | tf_op jit(solution)/shard_map/attend/pallas_call | solution.py:250
  77.5 1.2 %collective-permute-done.16.other_ref = bf16[128,256]{1,0:T(8,128)(2,1)S(1)} collective-permute-done((bf16[128,256]{1,0:T(8,128)(2,1)S(1)}, bf16[128,256]{1,0:T(8,128)(2,1)S(1)}, u32[]{:S(2)}, u32[]{:S(2)}) %collective-permute-start.16) | collective-permute-done | bytes 65568 | tf_op jit(solution)/shard_map/ppermute | solution.py:388
  78.7 1.0 project.1
  79.7 3.2 %collective-permute-start.19 = (bf16[128,512]{1,0:T(8,128)(2,1)S(1)}, bf16[128,512]{1,0:T(8,128)(2,1)S(1)}, u32[]{:S(2)}, u32[]{:S(2)}) collective-permute-start(bf16[128,512]{1,0:T(8,128)(2,1)S(1)} %get-tuple-element.76), channel_id=1, source_target_pairs={{0,1},{1,2},{2,3},{3,0},{4,5},{5,6},{6,7},{7,4},{8,9},{9,10},{10,1... | collective-permute-start | bytes 393224 | tf_op jit(solution)/shard_map/ppermute | solution.py:371
  82.9 2.3 %collective-permute-start.20 = (bf16[128,512]{1,0:T(8,128)(2,1)S(1)}, bf16[128,512]{1,0:T(8,128)(2,1)S(1)}, u32[]{:S(2)}, u32[]{:S(2)}) collective-permute-start(bf16[128,512]{1,0:T(8,128)(2,1)S(1)} %get-tuple-element.77), channel_id=1, source_target_pairs={{0,2},{1,3},{2,0},{3,1},{4,6},{5,7},{6,4},{7,5},{8,10},{9,11},{10,... | collective-permute-start | bytes 393224 | tf_op jit(solution)/shard_map/ppermute | solution.py:371
  85.3 3.7 %collective-permute-done.19.refs_1_ = bf16[128,512]{1,0:T(8,128)(2,1)S(1)} collective-permute-done((bf16[128,512]{1,0:T(8,128)(2,1)S(1)}, bf16[128,512]{1,0:T(8,128)(2,1)S(1)}, u32[]{:S(2)}, u32[]{:S(2)}) %collective-permute-start.19) | collective-permute-done | bytes 131104 | tf_op jit(solution)/shard_map/ppermute | solution.py:371
  89.1 4.2 %collective-permute-done.20.refs_2_ = bf16[128,512]{1,0:T(8,128)(2,1)S(1)} collective-permute-done((bf16[128,512]{1,0:T(8,128)(2,1)S(1)}, bf16[128,512]{1,0:T(8,128)(2,1)S(1)}, u32[]{:S(2)}, u32[]{:S(2)}) %collective-permute-start.20) | collective-permute-done | bytes 131104 | tf_op jit(solution)/shard_map/ppermute | solution.py:371
  93.7 3.2 %collective-permute-start.22 = (bf16[128,1024]{1,0:T(8,128)(2,1)S(1)}, bf16[128,1024]{1,0:T(8,128)(2,1)S(1)}, u32[]{:S(2)}, u32[]{:S(2)}) collective-permute-start(bf16[128,1024]{1,0:T(8,128)(2,1)S(1)} %copy-done.7), channel_id=1, source_target_pairs={{0,1},{1,2},{2,3},{3,0},{4,5},{5,6},{6,7},{7,4},{8,9},{9,10},{10,1... | collective-permute-start | bytes 786440 | tf_op jit(solution)/shard_map/ppermute | solution.py:371
  97.0 2.4 %collective-permute-start.24 = (bf16[32,512]{1,0:T(8,128)(2,1)S(1)}, bf16[32,512]{1,0:T(8,128)(2,1)S(1)}, u32[]{:S(2)}, u32[]{:S(2)}) collective-permute-start(bf16[32,512]{1,0:T(8,128)(2,1)S(1)} %get-tuple-element.93), channel_id=1, source_target_pairs={{0,8},{4,12},{8,16},{12,20},{16,24},{20,28},{24,0},{28,4},{1,9},{5... | collective-permute-start | bytes 98312 | tf_op jit(solution)/shard_map/ppermute | solution.py:371
  99.9 1.2 %collective-permute-start.25 = (bf16[32,512]{1,0:T(8,128)(2,1)S(1)}, bf16[32,512]{1,0:T(8,128)(2,1)S(1)}, u32[]{:S(2)}, u32[]{:S(2)}) collective-permute-start(bf16[32,512]{1,0:T(8,128)(2,1)S(1)} %get-tuple-element.95), channel_id=1, source_target_pairs={{0,16},{4,20},{8,24},{12,28},{16,0},{20,4},{24,8},{28,12},{1,17},{... | collective-permute-start | bytes 98312 | tf_op jit(solution)/shard_map/ppermute | solution.py:371
  101.9 1.5 %collective-permute-done.26 = bf16[32,512]{1,0:T(8,128)(2,1)S(1)} collective-permute-done((bf16[32,512]{1,0:T(8,128)(2,1)S(1)}, bf16[32,512]{1,0:T(8,128)(2,1)S(1)}, u32[]{:S(2)}, u32[]{:S(2)}) %collective-permute-start.26) | collective-permute-done | bytes 32800 | tf_op jit(solution)/shard_map/ppermute | solution.py:371
  103.9 0.8 sort_rows.1
  104.7 0.9 finish_bytes.1
  105.7 1.0 reshape.86
  (70 shorter events, 8.6 us)
Async XLA Ops:
  10.7 18.0 %collective-permute-start = (bf16[128,1024]{1,0:T(8,128)(2,1)}, bf16[128,1024]{1,0:T(8,128)(2,1)S(1)}, u32[]{:S(2)}, u32[]{:S(2)}) collective-permute-start(bf16[128,1024]{1,0:T(8,128)(2,1)} %get-tuple-element.52), channel_id=1, source_target_pairs={{0,1},{1,2},{2,3},{3,0},{4,5},{5,6},{6,7},{7,4},{8,9},{9,10},{10,1... | collective-permute-start | bytes 786440 | tf_op jit(solution)/shard_map/ppermute | solution.py:371
  13.8 26.7 %collective-permute-start.1 = (bf16[128,1024]{1,0:T(8,128)(2,1)}, bf16[128,1024]{1,0:T(8,128)(2,1)S(1)}, u32[]{:S(2)}, u32[]{:S(2)}) collective-permute-start(bf16[128,1024]{1,0:T(8,128)(2,1)} %get-tuple-element.54), channel_id=1, source_target_pairs={{0,2},{1,3},{2,0},{3,1},{4,6},{5,7},{6,4},{7,5},{8,10},{9,11},{10,... | collective-permute-start | bytes 786440 | tf_op jit(solution)/shard_map/ppermute | solution.py:371
  16.4 24.2 %copy-start.1 = (bf16[1024,256]{1,0:T(8,128)(2,1)S(1)}, bf16[1024,256]{1,0:T(8,128)(2,1)}, u32[]{:S(2)}) copy-start(bf16[1024,256]{1,0:T(8,128)(2,1)} %proj_ref.3) | copy-start | bytes 1572868
  16.4 24.2 %copy-start.4 = (bf16[128,1024]{1,0:T(8,128)(2,1)S(1)}, bf16[128,1024]{1,0:T(8,128)(2,1)}, u32[]{:S(2)}) copy-start(bf16[128,1024]{1,0:T(8,128)(2,1)} %get-tuple-element.47.refs_0_) | copy-start | bytes 786436
  16.4 24.1 %collective-permute-start.2 = (bf16[128,1024]{1,0:T(8,128)(2,1)}, bf16[128,1024]{1,0:T(8,128)(2,1)S(1)}, u32[]{:S(2)}, u32[]{:S(2)}) collective-permute-start(bf16[128,1024]{1,0:T(8,128)(2,1)} %get-tuple-element.55), channel_id=1, source_target_pairs={{0,3},{1,0},{2,1},{3,2},{4,7},{5,4},{6,5},{7,6},{8,11},{9,8},{10,9... | collective-permute-start | bytes 786440 | tf_op jit(solution)/shard_map/ppermute | solution.py:371
  28.8 15.8 %collective-permute-start.3 = (bf16[64,512]{1,0:T(8,128)(2,1)S(1)}, bf16[64,512]{1,0:T(8,128)(2,1)S(1)}, u32[]{:S(2)}, u32[]{:S(2)}) collective-permute-start(bf16[64,512]{1,0:T(8,128)(2,1)S(1)} %get-tuple-element.58), channel_id=1, source_target_pairs={{0,1},{1,2},{2,3},{3,0},{4,5},{5,6},{6,7},{7,4},{8,9},{9,10},{10,1... | collective-permute-start | bytes 196616 | tf_op jit(solution)/shard_map/ppermute | solution.py:371
  35.0 10.2 %collective-permute-start.4 = (bf16[64,512]{1,0:T(8,128)(2,1)S(1)}, bf16[64,512]{1,0:T(8,128)(2,1)S(1)}, u32[]{:S(2)}, u32[]{:S(2)}) collective-permute-start(bf16[64,512]{1,0:T(8,128)(2,1)S(1)} %get-tuple-element.59), channel_id=1, source_target_pairs={{0,2},{1,3},{2,0},{3,1},{4,6},{5,7},{6,4},{7,5},{8,10},{9,11},{10,... | collective-permute-start | bytes 196616 | tf_op jit(solution)/shard_map/ppermute | solution.py:371
  36.9 8.2 %collective-permute-start.5 = (bf16[64,512]{1,0:T(8,128)(2,1)S(1)}, bf16[64,512]{1,0:T(8,128)(2,1)S(1)}, u32[]{:S(2)}, u32[]{:S(2)}) collective-permute-start(bf16[64,512]{1,0:T(8,128)(2,1)S(1)} %get-tuple-element.60), channel_id=1, source_target_pairs={{0,3},{1,0},{2,1},{3,2},{4,7},{5,4},{6,5},{7,6},{8,11},{9,8},{10,9... | collective-permute-start | bytes 196616 | tf_op jit(solution)/shard_map/ppermute | solution.py:371
  40.9 8.7 %collective-permute-start.8 = (bf16[64,512]{1,0:T(8,128)(2,1)S(1)}, bf16[64,512]{1,0:T(8,128)(2,1)S(1)}, u32[]{:S(2)}, u32[]{:S(2)}) collective-permute-start(bf16[64,512]{1,0:T(8,128)(2,1)S(1)} %get-tuple-element.56.refs_0_), channel_id=1, source_target_pairs={{0,3},{1,0},{2,1},{3,2},{4,7},{5,4},{6,5},{7,6},{8,11},{9,8},{10,9... | collective-permute-start | bytes 196616 | tf_op jit(solution)/shard_map/ppermute | solution.py:371
  44.5 8.7 %collective-permute-start.7 = (bf16[64,512]{1,0:T(8,128)(2,1)S(1)}, bf16[64,512]{1,0:T(8,128)(2,1)S(1)}, u32[]{:S(2)}, u32[]{:S(2)}) collective-permute-start(bf16[64,512]{1,0:T(8,128)(2,1)S(1)} %get-tuple-element.56.refs_0_), channel_id=1, source_target_pairs={{0,2},{1,3},{2,0},{3,1},{4,6},{5,7},{6,4},{7,5},{8,10},{9,11},{10,... | collective-permute-start | bytes 196616 | tf_op jit(solution)/shard_map/ppermute | solution.py:371
  44.6 8.7 %collective-permute-start.6 = (bf16[64,512]{1,0:T(8,128)(2,1)S(1)}, bf16[64,512]{1,0:T(8,128)(2,1)S(1)}, u32[]{:S(2)}, u32[]{:S(2)}) collective-permute-start(bf16[64,512]{1,0:T(8,128)(2,1)S(1)} %get-tuple-element.56.refs_0_), channel_id=1, source_target_pairs={{0,1},{1,2},{2,3},{3,0},{4,5},{5,6},{6,7},{7,4},{8,9},{9,10},{10,1... | collective-permute-start | bytes 196616 | tf_op jit(solution)/shard_map/ppermute | solution.py:371
  45.2 8.0 %collective-permute-start.11 = (bf16[64,512]{1,0:T(8,128)(2,1)S(1)}, bf16[64,512]{1,0:T(8,128)(2,1)S(1)}, u32[]{:S(2)}, u32[]{:S(2)}) collective-permute-start(bf16[64,512]{1,0:T(8,128)(2,1)S(1)} %add_convert_fusion.refs_4_), channel_id=1, source_target_pairs={{0,3},{1,0},{2,1},{3,2},{4,7},{5,4},{6,5},{7,6},{8,11},{9,8},{10,9... | collective-permute-start | bytes 196616 | tf_op jit(solution)/shard_map/ppermute | solution.py:371
  48.5 7.6 %collective-permute-start.10 = (bf16[64,512]{1,0:T(8,128)(2,1)S(1)}, bf16[64,512]{1,0:T(8,128)(2,1)S(1)}, u32[]{:S(2)}, u32[]{:S(2)}) collective-permute-start(bf16[64,512]{1,0:T(8,128)(2,1)S(1)} %add_convert_fusion.refs_4_), channel_id=1, source_target_pairs={{0,2},{1,3},{2,0},{3,1},{4,6},{5,7},{6,4},{7,5},{8,10},{9,11},{10,... | collective-permute-start | bytes 196616 | tf_op jit(solution)/shard_map/ppermute | solution.py:371
  49.6 6.6 %collective-permute-start.9 = (bf16[64,512]{1,0:T(8,128)(2,1)S(1)}, bf16[64,512]{1,0:T(8,128)(2,1)S(1)}, u32[]{:S(2)}, u32[]{:S(2)}) collective-permute-start(bf16[64,512]{1,0:T(8,128)(2,1)S(1)} %add_convert_fusion.refs_4_), channel_id=1, source_target_pairs={{0,1},{1,2},{2,3},{3,0},{4,5},{5,6},{6,7},{7,4},{8,9},{9,10},{10,1... | collective-permute-start | bytes 196616 | tf_op jit(solution)/shard_map/ppermute | solution.py:371
  57.9 20.8 %copy-start = (bf16[512,2048]{1,0:T(8,128)(2,1)S(1)}, bf16[512,2048]{1,0:T(8,128)(2,1)}, u32[]{:S(2)}) copy-start(bf16[512,2048]{1,0:T(8,128)(2,1)} %proj_ref.4) | copy-start | bytes 6291460
  57.9 1.5 %collective-permute-start.12 = (bf16[128,768]{1,0:T(8,128)(2,1)S(1)}, bf16[128,768]{1,0:T(8,128)(2,1)S(1)}, u32[]{:S(2)}, u32[]{:S(2)}) collective-permute-start(bf16[128,768]{1,0:T(8,128)(2,1)S(1)} %get-tuple-element.64), channel_id=1, source_target_pairs={{0,4},{4,0},{8,12},{12,8},{16,20},{20,16},{24,28},{28,24},{1,5},{5... | collective-permute-start | bytes 589832 | tf_op jit(solution)/shard_map/ppermute | solution.py:388
  59.4 9.2 %collective-permute-start.15 = (bf16[256,512]{1,0:T(8,128)(2,1)S(1)}, bf16[256,512]{1,0:T(8,128)(2,1)S(1)}, u32[]{:S(2)}, u32[]{:S(2)}) collective-permute-start(bf16[256,512]{1,0:T(8,128)(2,1)S(1)} %pad_maximum_fusion), channel_id=1, source_target_pairs={{0,24},{4,28},{8,0},{12,4},{16,8},{20,12},{24,16},{28,20},{1,25},{... | collective-permute-start | bytes 786440 | tf_op jit(solution)/shard_map/ppermute | solution.py:371
  61.9 13.7 %collective-permute-start.14 = (bf16[256,512]{1,0:T(8,128)(2,1)S(1)}, bf16[256,512]{1,0:T(8,128)(2,1)S(1)}, u32[]{:S(2)}, u32[]{:S(2)}) collective-permute-start(bf16[256,512]{1,0:T(8,128)(2,1)S(1)} %pad_maximum_fusion), channel_id=1, source_target_pairs={{0,16},{4,20},{8,24},{12,28},{16,0},{20,4},{24,8},{28,12},{1,17},{... | collective-permute-start | bytes 786440 | tf_op jit(solution)/shard_map/ppermute | solution.py:371
  62.4 13.2 %collective-permute-start.13 = (bf16[256,512]{1,0:T(8,128)(2,1)S(1)}, bf16[256,512]{1,0:T(8,128)(2,1)S(1)}, u32[]{:S(2)}, u32[]{:S(2)}) collective-permute-start(bf16[256,512]{1,0:T(8,128)(2,1)S(1)} %pad_maximum_fusion), channel_id=1, source_target_pairs={{0,8},{4,12},{8,16},{12,20},{16,24},{20,28},{24,0},{28,4},{1,9},{5... | collective-permute-start | bytes 786440 | tf_op jit(solution)/shard_map/ppermute | solution.py:371
  63.0 14.4 %collective-permute-start.17 = (bf16[128,1024]{1,0:T(8,128)(2,1)S(1)}, bf16[128,1024]{1,0:T(8,128)(2,1)S(1)}, u32[]{:S(2)}, u32[]{:S(2)}) collective-permute-start(bf16[128,1024]{1,0:T(8,128)(2,1)S(1)} %copy-done.9), channel_id=1, source_target_pairs={{0,2},{1,3},{2,0},{3,1},{4,6},{5,7},{6,4},{7,5},{8,10},{9,11},{10,... | collective-permute-start | bytes 786440 | tf_op jit(solution)/shard_map/ppermute | solution.py:371
  63.7 13.7 %collective-permute-start.18 = (bf16[128,1024]{1,0:T(8,128)(2,1)S(1)}, bf16[128,1024]{1,0:T(8,128)(2,1)S(1)}, u32[]{:S(2)}, u32[]{:S(2)}) collective-permute-start(bf16[128,1024]{1,0:T(8,128)(2,1)S(1)} %copy-done.8), channel_id=1, source_target_pairs={{0,3},{1,0},{2,1},{3,2},{4,7},{5,4},{6,5},{7,6},{8,11},{9,8},{10,9... | collective-permute-start | bytes 786440 | tf_op jit(solution)/shard_map/ppermute | solution.py:371
  77.3 27.4 %copy-start.2 = (bf16[256,1024]{1,0:T(8,128)(2,1)S(1)}, bf16[256,1024]{1,0:T(8,128)(2,1)}, u32[]{:S(2)}) copy-start(bf16[256,1024]{1,0:T(8,128)(2,1)} %proj_ref.5) | copy-start | bytes 1572868
  77.3 27.4 %copy-start.3 = (bf16[128,1024]{1,0:T(8,128)(2,1)S(1)}, bf16[128,1024]{1,0:T(8,128)(2,1)}, u32[]{:S(2)}) copy-start(bf16[128,1024]{1,0:T(8,128)(2,1)} %get-tuple-element.86.refs_1_) | copy-start | bytes 786436
  77.3 1.3 %collective-permute-start.16 = (bf16[128,256]{1,0:T(8,128)(2,1)S(1)}, bf16[128,256]{1,0:T(8,128)(2,1)S(1)}, u32[]{:S(2)}, u32[]{:S(2)}) collective-permute-start(bf16[128,256]{1,0:T(8,128)(2,1)S(1)} %get-tuple-element.71), channel_id=1, source_target_pairs={{0,4},{4,0},{8,12},{12,8},{16,20},{20,16},{24,28},{28,24},{1,5},{5... | collective-permute-start | bytes 196616 | tf_op jit(solution)/shard_map/ppermute | solution.py:388
  79.7 9.4 %collective-permute-start.19 = (bf16[128,512]{1,0:T(8,128)(2,1)S(1)}, bf16[128,512]{1,0:T(8,128)(2,1)S(1)}, u32[]{:S(2)}, u32[]{:S(2)}) collective-permute-start(bf16[128,512]{1,0:T(8,128)(2,1)S(1)} %get-tuple-element.76), channel_id=1, source_target_pairs={{0,1},{1,2},{2,3},{3,0},{4,5},{5,6},{6,7},{7,4},{8,9},{9,10},{10,1... | collective-permute-start | bytes 393224 | tf_op jit(solution)/shard_map/ppermute | solution.py:371
  82.9 10.4 %collective-permute-start.20 = (bf16[128,512]{1,0:T(8,128)(2,1)S(1)}, bf16[128,512]{1,0:T(8,128)(2,1)S(1)}, u32[]{:S(2)}, u32[]{:S(2)}) collective-permute-start(bf16[128,512]{1,0:T(8,128)(2,1)S(1)} %get-tuple-element.77), channel_id=1, source_target_pairs={{0,2},{1,3},{2,0},{3,1},{4,6},{5,7},{6,4},{7,5},{8,10},{9,11},{10,... | collective-permute-start | bytes 393224 | tf_op jit(solution)/shard_map/ppermute | solution.py:371
  85.2 8.2 %collective-permute-start.21 = (bf16[128,512]{1,0:T(8,128)(2,1)S(1)}, bf16[128,512]{1,0:T(8,128)(2,1)S(1)}, u32[]{:S(2)}, u32[]{:S(2)}) collective-permute-start(bf16[128,512]{1,0:T(8,128)(2,1)S(1)} %get-tuple-element.78), channel_id=1, source_target_pairs={{0,3},{1,0},{2,1},{3,2},{4,7},{5,4},{6,5},{7,6},{8,11},{9,8},{10,9... | collective-permute-start | bytes 393224 | tf_op jit(solution)/shard_map/ppermute | solution.py:371
  93.6 3.3 %collective-permute-start.23 = (bf16[64,512]{1,0:T(8,128)(2,1)S(1)}, bf16[64,512]{1,0:T(8,128)(2,1)S(1)}, u32[]{:S(2)}, u32[]{:S(2)}) collective-permute-start(bf16[64,512]{1,0:T(8,128)(2,1)S(1)} %get-tuple-element.91), channel_id=1, source_target_pairs={{0,4},{4,0},{8,12},{12,8},{16,20},{20,16},{24,28},{28,24},{1,5},{5... | collective-permute-start | bytes 196616 | tf_op jit(solution)/shard_map/ppermute | solution.py:388
  93.7 11.0 %collective-permute-start.22 = (bf16[128,1024]{1,0:T(8,128)(2,1)S(1)}, bf16[128,1024]{1,0:T(8,128)(2,1)S(1)}, u32[]{:S(2)}, u32[]{:S(2)}) collective-permute-start(bf16[128,1024]{1,0:T(8,128)(2,1)S(1)} %copy-done.7), channel_id=1, source_target_pairs={{0,1},{1,2},{2,3},{3,0},{4,5},{5,6},{6,7},{7,4},{8,9},{9,10},{10,1... | collective-permute-start | bytes 786440 | tf_op jit(solution)/shard_map/ppermute | solution.py:371
  97.0 4.9 %collective-permute-start.24 = (bf16[32,512]{1,0:T(8,128)(2,1)S(1)}, bf16[32,512]{1,0:T(8,128)(2,1)S(1)}, u32[]{:S(2)}, u32[]{:S(2)}) collective-permute-start(bf16[32,512]{1,0:T(8,128)(2,1)S(1)} %get-tuple-element.93), channel_id=1, source_target_pairs={{0,8},{4,12},{8,16},{12,20},{16,24},{20,28},{24,0},{28,4},{1,9},{5... | collective-permute-start | bytes 98312 | tf_op jit(solution)/shard_map/ppermute | solution.py:371
  99.4 3.9 %collective-permute-start.26 = (bf16[32,512]{1,0:T(8,128)(2,1)S(1)}, bf16[32,512]{1,0:T(8,128)(2,1)S(1)}, u32[]{:S(2)}, u32[]{:S(2)}) collective-permute-start(bf16[32,512]{1,0:T(8,128)(2,1)S(1)} %get-tuple-element.94), channel_id=1, source_target_pairs={{0,24},{4,28},{8,0},{12,4},{16,8},{20,12},{24,16},{28,20},{1,25},{... | collective-permute-start | bytes 98312 | tf_op jit(solution)/shard_map/ppermute | solution.py:371
  99.9 3.9 %collective-permute-start.25 = (bf16[32,512]{1,0:T(8,128)(2,1)S(1)}, bf16[32,512]{1,0:T(8,128)(2,1)S(1)}, u32[]{:S(2)}, u32[]{:S(2)}) collective-permute-start(bf16[32,512]{1,0:T(8,128)(2,1)S(1)} %get-tuple-element.95), channel_id=1, source_target_pairs={{0,16},{4,20},{8,24},{12,28},{16,0},{20,4},{24,8},{28,12},{1,17},{... | collective-permute-start | bytes 98312 | tf_op jit(solution)/shard_map/ppermute | solution.py:371
  (5 other events, 58.5 us)

commit v14 on v13

--- a/solution.py
+++ b/solution.py
@@ -456,10 +456,14 @@
     weight = jnp.transpose(global_qkv, (1, 0, 2))
     weight, late_share = lax.optimization_barrier((weight, late_share))
     late_shares = gather(late_share, "head")
+    early_shares, late_shares, weight, parts[1] = lax.optimization_barrier(
+        (early_shares, late_shares, fetch(weight), parts[1])
+    )
+    parts[1] = shift(parts[1], "head", 1)
     residual = jnp.concatenate([early_share, late_share], axis=0)
     ids = (me - jnp.arange(ways, dtype=jnp.int32)) % ways
     core = (seq % 2).reshape(1)
-    kept, given = global_heads(depth, core, ids, global_gain.reshape(ways, 1, -1), early_shares, late_shares, fetch(weight))
+    kept, given = global_heads(depth, core, ids, global_gain.reshape(ways, 1, -1), early_shares, late_shares, weight)
     received = swap_cores(given, "seq")
     received, *parts = lax.optimization_barrier((received, *parts))
     half = kept.shape[1] // 3
@@ -469,8 +473,6 @@
     own_heads, other_heads = attend(depth, seq.reshape(1), twin_ids("seq"), global_scale, kept, received, pieces)
     other_heads, parts[2:] = lax.optimization_barrier((swap_cores(other_heads, "seq"), parts[2:]))
     updates = scatter(project(core, slots, own_heads, other_heads, global_out), "head")
-    updates, parts[1] = lax.optimization_barrier((updates, parts[1]))
-    parts[1] = shift(parts[1], "head", 1)
     result, kept, given = finish_result(owner_order(owners, seq, patches), residual, updates)
     global_state = route(kept, given, "seq")
     byte_out = finish_bytes(result, back_proj, [early] + parts)

time: 107 us -> 107 us (level)
  starting transfers between devices: 45 us -> 41.5 us
  waiting for transfers between devices: 28 us -> 31.4 us
    ppermute x24, starting transfers between devices: 44.8 us -> 41.3 us  [shift(): lax.ppermute(value, axis, [(i, (i + step) % count) for i in range(count)])]
    ppermute x24, waiting for transfers between devices: 25.5 us -> 27.6 us  [shift(): lax.ppermute(value, axis, [(i, (i + step) % count) for i in range(count)])]
    ppermute x3, waiting for transfers between devices: 2.52 us -> 3.76 us  [swap_cores(): lax.ppermute(value, axis, [(i, i ^ 1) for i in range(lax.axis_size(axis))])]
  transfers between devices with their start and end apart: 27 -> 27, of which waited for: 12 -> 12; matrix products, arithmetic and copies ran while one was open for 2% -> 2% of each run, Pallas kernels for 15% -> 17%
where the time goes in v14:
time: 107 us
  starting transfers between devices  41.5 us (39%)
  waiting for transfers between devices  31.4 us (29%)
  Pallas kernels  29.9 us (28%)
  local copies, waits for them, and re-layouts  1.76 us (2%)
  other arithmetic  1.13 us (1%)
    ppermute x24, starting transfers between devices, shift(): lax.ppermute(value, axis, [(i, (i + step) % count) for i in range(count)])  41.3 us
    ppermute x24, waiting for transfers between devices, shift(): lax.ppermute(value, axis, [(i, (i + step) % count) for i in range(count)])  27.6 us
    pallas_call x2, Pallas kernels, local_part(): pl.pallas_call(functools.partial(local_kernel, span, ways, piece, last),...  20.2 us
    ppermute x3, waiting for transfers between devices, swap_cores(): lax.ppermute(value, axis, [(i, i ^ 1) for i in range(lax.axis_size(axis))])  3.76 us
    pallas_call x1, Pallas kernels, fetch(): pl.pallas_call(fetch_kernel, in_specs=[HBM], out_specs=VMEM, out_shape=pl...  2.92 us
  transfers between devices with their start and end apart: 27, of which 12 were waited for; matrix products, arithmetic and copies ran while one was open for 2% of the time, Pallas kernels for 17%

profile of v14, /device:TPU:0, one launch (start us, length us, event | category | flops | bytes accessed | tf_op | source)
XLA Modules:
  0.0 106.6 jit_solution(1807732006377968394)
XLA Ops:
  0.6 10.1 %local_part.2 = (bf16[128,1024]{1,0:T(8,128)(2,1)}, bf16[128,1024]{1,0:T(8,128)(2,1)}, bf16[128,1024]{1,0:T(8,128)(2,1)}, bf16[128,1024]{1,0:T(8,128)(2,1)}) custom-call(f32[2]{0:T(128)} %scale_ref.4, f32[1,1024]{1,0:T(1,128)} %bitcast.33, bf16[1024,1024]{1,0:T(8,128)(2,1)} %bitcast.29, bf16[3,1024,256]{2,1,0:T(8,128)(2,1)} %bitcast.31, ...), custom_call_target="tpu_custom_call" | custom-call | flops 4294967296 | bytes 10485760 | tf_op jit(solution)/shard_map/local_part/pallas_call | solution.py:117
  10.7 3.1 %collective-permute-start = (bf16[128,1024]{1,0:T(8,128)(2,1)}, bf16[128,1024]{1,0:T(8,128)(2,1)S(1)}, u32[]{:S(2)}, u32[]{:S(2)}) collective-permute-start(bf16[128,1024]{1,0:T(8,128)(2,1)} %get-tuple-element.57), channel_id=1, source_target_pairs={{0,1},{1,2},{2,3},{3,0},{4,5},{5,6},{6,7},{7,4},{8,9},{9,10},{10,1... | collective-permute-start | bytes 786440 | tf_op jit(solution)/shard_map/ppermute | solution.py:371
  13.8 2.6 %collective-permute-start.1 = (bf16[128,1024]{1,0:T(8,128)(2,1)}, bf16[128,1024]{1,0:T(8,128)(2,1)S(1)}, u32[]{:S(2)}, u32[]{:S(2)}) collective-permute-start(bf16[128,1024]{1,0:T(8,128)(2,1)} %get-tuple-element.59), channel_id=1, source_target_pairs={{0,2},{1,3},{2,0},{3,1},{4,6},{5,7},{6,4},{7,5},{8,10},{9,11},{10,... | collective-permute-start | bytes 786440 | tf_op jit(solution)/shard_map/ppermute | solution.py:371
  16.4 1.3 %collective-permute-start.2 = (bf16[128,1024]{1,0:T(8,128)(2,1)}, bf16[128,1024]{1,0:T(8,128)(2,1)S(1)}, u32[]{:S(2)}, u32[]{:S(2)}) collective-permute-start(bf16[128,1024]{1,0:T(8,128)(2,1)} %get-tuple-element.60), channel_id=1, source_target_pairs={{0,3},{1,0},{2,1},{3,2},{4,7},{5,4},{6,5},{7,6},{8,11},{9,8},{10,9... | collective-permute-start | bytes 786440 | tf_op jit(solution)/shard_map/ppermute | solution.py:371
  17.8 10.1 %local_part.3 = (bf16[128,1024]{1,0:T(8,128)(2,1)}, bf16[128,1024]{1,0:T(8,128)(2,1)}, bf16[128,1024]{1,0:T(8,128)(2,1)}, bf16[128,1024]{1,0:T(8,128)(2,1)}, bf1...) custom-call(f32[2]{0:T(128)} %scale_ref.4, ...), custom_call_target="tpu_custom_call" | custom-call | flops 4294967296 | bytes 10485760 | tf_op jit(solution)/shard_map/local_part/pallas_call | solution.py:117
  28.6 6.4 %collective-permute-start.3 = (bf16[64,512]{1,0:T(8,128)(2,1)S(1)}, bf16[64,512]{1,0:T(8,128)(2,1)S(1)}, u32[]{:S(2)}, u32[]{:S(2)}) collective-permute-start(bf16[64,512]{1,0:T(8,128)(2,1)S(1)} %get-tuple-element.63), channel_id=1, source_target_pairs={{0,1},{1,2},{2,3},{3,0},{4,5},{5,6},{6,7},{7,4},{8,9},{9,10},{10,1... | collective-permute-start | bytes 196616 | tf_op jit(solution)/shard_map/ppermute | solution.py:371
  35.0 2.0 %collective-permute-start.4 = (bf16[64,512]{1,0:T(8,128)(2,1)S(1)}, bf16[64,512]{1,0:T(8,128)(2,1)S(1)}, u32[]{:S(2)}, u32[]{:S(2)}) collective-permute-start(bf16[64,512]{1,0:T(8,128)(2,1)S(1)} %get-tuple-element.64), channel_id=1, source_target_pairs={{0,2},{1,3},{2,0},{3,1},{4,6},{5,7},{6,4},{7,5},{8,10},{9,11},{10,... | collective-permute-start | bytes 196616 | tf_op jit(solution)/shard_map/ppermute | solution.py:371
  36.9 2.9 %collective-permute-start.5 = (bf16[64,512]{1,0:T(8,128)(2,1)S(1)}, bf16[64,512]{1,0:T(8,128)(2,1)S(1)}, u32[]{:S(2)}, u32[]{:S(2)}) collective-permute-start(bf16[64,512]{1,0:T(8,128)(2,1)S(1)} %get-tuple-element.65), channel_id=1, source_target_pairs={{0,3},{1,0},{2,1},{3,2},{4,7},{5,4},{6,5},{7,6},{8,11},{9,8},{10,9... | collective-permute-start | bytes 196616 | tf_op jit(solution)/shard_map/ppermute | solution.py:371
  40.4 4.1 %collective-permute-start.8 = (bf16[64,512]{1,0:T(8,128)(2,1)S(1)}, bf16[64,512]{1,0:T(8,128)(2,1)S(1)}, u32[]{:S(2)}, u32[]{:S(2)}) collective-permute-start(bf16[64,512]{1,0:T(8,128)(2,1)S(1)} %get-tuple-element.69.refs_0_), channel_id=1, source_target_pairs={{0,3},{1,0},{2,1},{3,2},{4,7},{5,4},{6,5},{7,6},{8,11},{9,8},{10,9... | collective-permute-start | bytes 196616 | tf_op jit(solution)/shard_map/ppermute | solution.py:371
  45.2 3.3 %collective-permute-start.11 = (bf16[64,512]{1,0:T(8,128)(2,1)S(1)}, bf16[64,512]{1,0:T(8,128)(2,1)S(1)}, u32[]{:S(2)}, u32[]{:S(2)}) collective-permute-start(bf16[64,512]{1,0:T(8,128)(2,1)S(1)} %add_convert_fusion.refs_4_), channel_id=1, source_target_pairs={{0,3},{1,0},{2,1},{3,2},{4,7},{5,4},{6,5},{7,6},{8,11},{9,8},{10,9... | collective-permute-start | bytes 196616 | tf_op jit(solution)/shard_map/ppermute | solution.py:371
  48.5 1.0 collective-permute-start.10
  50.3 2.9 %fetch.1.refs_8_ = bf16[3,2048,512]{2,1,0:T(8,128)(2,1)S(1)} custom-call(bf16[3,2048,512]{2,1,0:T(8,128)(2,1)} %bitcast.27), custom_call_target="tpu_custom_call" | custom-call | tf_op jit(solution)/shard_map/fetch/pallas_call | solution.py:173
  53.3 2.9 %collective-permute-done.10.refs_6_ = bf16[64,512]{1,0:T(8,128)(2,1)S(1)} collective-permute-done((bf16[64,512]{1,0:T(8,128)(2,1)S(1)}, bf16[64,512]{1,0:T(8,128)(2,1)S(1)}, u32[]{:S(2)}, u32[]{:S(2)}) %collective-permute-start.10) | collective-permute-done | bytes 65568 | tf_op jit(solution)/shard_map/ppermute | solution.py:371
  56.2 1.7 %global_heads.1 = (bf16[128,768]{1,0:T(8,128)(2,1)S(1)}, bf16[128,768]{1,0:T(8,128)(2,1)S(1)}) custom-call(s32[1]{0:T(128)} %bitcast.7.core_ref, s32[4]{0:T(128)S(1)} %and_select_fusion.ids_ref, f32[4,1,512]{2,1,0:T(1,128)S(1)} %bitcast.26, bf16[64,512]{1,0:T(8,128)(2,1)S(1)} %get-tuple-element.69.refs_0_, ...), custom_call_target="tpu_custom_call" | custom-call | tf_op jit(solution)/shard_map/global_heads/pallas_call | solution.py:207
  58.1 1.3 %collective-permute-done.12.given_ref = bf16[128,768]{1,0:T(8,128)(2,1)S(1)} collective-permute-done((bf16[128,768]{1,0:T(8,128)(2,1)S(1)}, bf16[128,768]{1,0:T(8,128)(2,1)S(1)}, u32[]{:S(2)}, u32[]{:S(2)}) %collective-permute-start.12) | collective-permute-done | bytes 196640 | tf_op jit(solution)/shard_map/ppermute | solution.py:388
  59.4 5.5 %collective-permute-done.13.refs_2_ = bf16[128,1024]{1,0:T(8,128)(2,1)S(1)} collective-permute-done((bf16[128,1024]{1,0:T(8,128)(2,1)S(1)}, bf16[128,1024]{1,0:T(8,128)(2,1)S(1)}, u32[]{:S(2)}, u32[]{:S(2)}) %collective-permute-start.13) | collective-permute-done | bytes 262176 | tf_op jit(solution)/shard_map/ppermute | solution.py:371
  65.0 2.5 %collective-permute-start.16 = (bf16[256,512]{1,0:T(8,128)(2,1)S(1)}, bf16[256,512]{1,0:T(8,128)(2,1)S(1)}, u32[]{:S(2)}, u32[]{:S(2)}) collective-permute-start(bf16[256,512]{1,0:T(8,128)(2,1)S(1)} %pad_maximum_fusion), channel_id=1, source_target_pairs={{0,24},{4,28},{8,0},{12,4},{16,8},{20,12},{24,16},{28,20},{1,25},{... | collective-permute-start | bytes 786440 | tf_op jit(solution)/shard_map/ppermute | solution.py:371
  69.5 4.5 %collective-permute-done.16.refs_2_ = bf16[256,512]{1,0:T(8,128)(2,1)S(1)} collective-permute-done((bf16[256,512]{1,0:T(8,128)(2,1)S(1)}, bf16[256,512]{1,0:T(8,128)(2,1)S(1)}, u32[]{:S(2)}, u32[]{:S(2)}) %collective-permute-start.16) | collective-permute-done | bytes 262176 | tf_op jit(solution)/shard_map/ppermute | solution.py:371
  74.0 5.0 %collective-permute-done.15.refs_1_ = bf16[256,512]{1,0:T(8,128)(2,1)S(1)} collective-permute-done((bf16[256,512]{1,0:T(8,128)(2,1)S(1)}, bf16[256,512]{1,0:T(8,128)(2,1)S(1)}, u32[]{:S(2)}, u32[]{:S(2)}) %collective-permute-start.15) | collective-permute-done | bytes 262176 | tf_op jit(solution)/shard_map/ppermute | solution.py:371
  79.0 1.7 %attend.1 = (bf16[128,256]{1,0:T(8,128)(2,1)S(1)}, bf16[128,256]{1,0:T(8,128)(2,1)S(1)}) custom-call(s32[1]{0:T(128)} %bitcast.8.me_ref, s32[4]{0:T(128)S(1)} %and_select_fusion.1.ids_ref, f32[4]{0:T(128)S(1)} %copy-done.6, bf16[128,768]{1,0:T(8,128)(2,1)S(1)} %get-tuple-element.78.kept_ref, bf16[128,768]{1,0:T(8,128)(2,1)S(1)} %collective-permute-done.12.given_ref, ...), custom_call_target="tpu_custom_call" | custom-call | flops 1 | bytes 1 | tf_op jit(solution)/shard_map/attend/pallas_call | solution.py:250
  80.9 1.2 %collective-permute-done.17.other_ref = bf16[128,256]{1,0:T(8,128)(2,1)S(1)} collective-permute-done((bf16[128,256]{1,0:T(8,128)(2,1)S(1)}, bf16[128,256]{1,0:T(8,128)(2,1)S(1)}, u32[]{:S(2)}, u32[]{:S(2)}) %collective-permute-start.17) | collective-permute-done | bytes 65568 | tf_op jit(solution)/shard_map/ppermute | solution.py:388
  82.1 1.0 project.1
  83.1 2.8 %collective-permute-start.20 = (bf16[128,512]{1,0:T(8,128)(2,1)S(1)}, bf16[128,512]{1,0:T(8,128)(2,1)S(1)}, u32[]{:S(2)}, u32[]{:S(2)}) collective-permute-start(bf16[128,512]{1,0:T(8,128)(2,1)S(1)} %get-tuple-element.91), channel_id=1, source_target_pairs={{0,1},{1,2},{2,3},{3,0},{4,5},{5,6},{6,7},{7,4},{8,9},{9,10},{10,1... | collective-permute-start | bytes 393224 | tf_op jit(solution)/shard_map/ppermute | solution.py:371
  85.9 2.3 %collective-permute-start.21 = (bf16[128,512]{1,0:T(8,128)(2,1)S(1)}, bf16[128,512]{1,0:T(8,128)(2,1)S(1)}, u32[]{:S(2)}, u32[]{:S(2)}) collective-permute-start(bf16[128,512]{1,0:T(8,128)(2,1)S(1)} %get-tuple-element.92), channel_id=1, source_target_pairs={{0,2},{1,3},{2,0},{3,1},{4,6},{5,7},{6,4},{7,5},{8,10},{9,11},{10,... | collective-permute-start | bytes 393224 | tf_op jit(solution)/shard_map/ppermute | solution.py:371
  88.4 3.8 %collective-permute-done.20.refs_1_ = bf16[128,512]{1,0:T(8,128)(2,1)S(1)} collective-permute-done((bf16[128,512]{1,0:T(8,128)(2,1)S(1)}, bf16[128,512]{1,0:T(8,128)(2,1)S(1)}, u32[]{:S(2)}, u32[]{:S(2)}) %collective-permute-start.20) | collective-permute-done | bytes 131104 | tf_op jit(solution)/shard_map/ppermute | solution.py:371
  92.2 4.0 %collective-permute-done.21.refs_2_ = bf16[128,512]{1,0:T(8,128)(2,1)S(1)} collective-permute-done((bf16[128,512]{1,0:T(8,128)(2,1)S(1)}, bf16[128,512]{1,0:T(8,128)(2,1)S(1)}, u32[]{:S(2)}, u32[]{:S(2)}) %collective-permute-start.21) | collective-permute-done | bytes 131104 | tf_op jit(solution)/shard_map/ppermute | solution.py:371
  96.6 1.2 %collective-permute-done.23 = bf16[64,512]{1,0:T(8,128)(2,1)S(1)} collective-permute-done((bf16[64,512]{1,0:T(8,128)(2,1)S(1)}, bf16[64,512]{1,0:T(8,128)(2,1)S(1)}, u32[]{:S(2)}, u32[]{:S(2)}) %collective-permute-start.23) | collective-permute-done | bytes 65568 | tf_op jit(solution)/shard_map/ppermute | solution.py:388
  97.9 2.4 %collective-permute-start.24 = (bf16[32,512]{1,0:T(8,128)(2,1)S(1)}, bf16[32,512]{1,0:T(8,128)(2,1)S(1)}, u32[]{:S(2)}, u32[]{:S(2)}) collective-permute-start(bf16[32,512]{1,0:T(8,128)(2,1)S(1)} %get-tuple-element.103), channel_id=1, source_target_pairs={{0,8},{4,12},{8,16},{12,20},{16,24},{20,28},{24,0},{28,4},{1,9},{5... | collective-permute-start | bytes 98312 | tf_op jit(solution)/shard_map/ppermute | solution.py:371
  100.8 1.2 %collective-permute-start.25 = (bf16[32,512]{1,0:T(8,128)(2,1)S(1)}, bf16[32,512]{1,0:T(8,128)(2,1)S(1)}, u32[]{:S(2)}, u32[]{:S(2)}) collective-permute-start(bf16[32,512]{1,0:T(8,128)(2,1)S(1)} %get-tuple-element.105), channel_id=1, source_target_pairs={{0,16},{4,20},{8,24},{12,28},{16,0},{20,4},{24,8},{28,12},{1,17},{... | collective-permute-start | bytes 98312 | tf_op jit(solution)/shard_map/ppermute | solution.py:371
  102.1 0.9 finish_bytes.1
  103.0 1.2 %collective-permute-done.26 = bf16[32,512]{1,0:T(8,128)(2,1)S(1)} collective-permute-done((bf16[32,512]{1,0:T(8,128)(2,1)S(1)}, bf16[32,512]{1,0:T(8,128)(2,1)S(1)}, u32[]{:S(2)}, u32[]{:S(2)}) %collective-permute-start.26) | collective-permute-done | bytes 32800 | tf_op jit(solution)/shard_map/ppermute | solution.py:371
  104.8 1.0 reshape.86
  (70 shorter events, 7.5 us)
Async XLA Ops:
  10.7 17.9 %collective-permute-start = (bf16[128,1024]{1,0:T(8,128)(2,1)}, bf16[128,1024]{1,0:T(8,128)(2,1)S(1)}, u32[]{:S(2)}, u32[]{:S(2)}) collective-permute-start(bf16[128,1024]{1,0:T(8,128)(2,1)} %get-tuple-element.57), channel_id=1, source_target_pairs={{0,1},{1,2},{2,3},{3,0},{4,5},{5,6},{6,7},{7,4},{8,9},{9,10},{10,1... | collective-permute-start | bytes 786440 | tf_op jit(solution)/shard_map/ppermute | solution.py:371
  13.8 26.2 %collective-permute-start.1 = (bf16[128,1024]{1,0:T(8,128)(2,1)}, bf16[128,1024]{1,0:T(8,128)(2,1)S(1)}, u32[]{:S(2)}, u32[]{:S(2)}) collective-permute-start(bf16[128,1024]{1,0:T(8,128)(2,1)} %get-tuple-element.59), channel_id=1, source_target_pairs={{0,2},{1,3},{2,0},{3,1},{4,6},{5,7},{6,4},{7,5},{8,10},{9,11},{10,... | collective-permute-start | bytes 786440 | tf_op jit(solution)/shard_map/ppermute | solution.py:371
  16.4 23.6 %copy-start.1 = (bf16[1024,256]{1,0:T(8,128)(2,1)S(1)}, bf16[1024,256]{1,0:T(8,128)(2,1)}, u32[]{:S(2)}) copy-start(bf16[1024,256]{1,0:T(8,128)(2,1)} %proj_ref.3) | copy-start | bytes 1572868
  16.4 23.6 %copy-start.4 = (bf16[128,1024]{1,0:T(8,128)(2,1)S(1)}, bf16[128,1024]{1,0:T(8,128)(2,1)}, u32[]{:S(2)}) copy-start(bf16[128,1024]{1,0:T(8,128)(2,1)} %get-tuple-element.52.refs_0_) | copy-start | bytes 786436
  16.4 23.6 %collective-permute-start.2 = (bf16[128,1024]{1,0:T(8,128)(2,1)}, bf16[128,1024]{1,0:T(8,128)(2,1)S(1)}, u32[]{:S(2)}, u32[]{:S(2)}) collective-permute-start(bf16[128,1024]{1,0:T(8,128)(2,1)} %get-tuple-element.60), channel_id=1, source_target_pairs={{0,3},{1,0},{2,1},{3,2},{4,7},{5,4},{6,5},{7,6},{8,11},{9,8},{10,9... | collective-permute-start | bytes 786440 | tf_op jit(solution)/shard_map/ppermute | solution.py:371
  28.6 16.0 %collective-permute-start.3 = (bf16[64,512]{1,0:T(8,128)(2,1)S(1)}, bf16[64,512]{1,0:T(8,128)(2,1)S(1)}, u32[]{:S(2)}, u32[]{:S(2)}) collective-permute-start(bf16[64,512]{1,0:T(8,128)(2,1)S(1)} %get-tuple-element.63), channel_id=1, source_target_pairs={{0,1},{1,2},{2,3},{3,0},{4,5},{5,6},{6,7},{7,4},{8,9},{9,10},{10,1... | collective-permute-start | bytes 196616 | tf_op jit(solution)/shard_map/ppermute | solution.py:371
  35.0 10.2 %collective-permute-start.4 = (bf16[64,512]{1,0:T(8,128)(2,1)S(1)}, bf16[64,512]{1,0:T(8,128)(2,1)S(1)}, u32[]{:S(2)}, u32[]{:S(2)}) collective-permute-start(bf16[64,512]{1,0:T(8,128)(2,1)S(1)} %get-tuple-element.64), channel_id=1, source_target_pairs={{0,2},{1,3},{2,0},{3,1},{4,6},{5,7},{6,4},{7,5},{8,10},{9,11},{10,... | collective-permute-start | bytes 196616 | tf_op jit(solution)/shard_map/ppermute | solution.py:371
  36.9 8.2 %collective-permute-start.5 = (bf16[64,512]{1,0:T(8,128)(2,1)S(1)}, bf16[64,512]{1,0:T(8,128)(2,1)S(1)}, u32[]{:S(2)}, u32[]{:S(2)}) collective-permute-start(bf16[64,512]{1,0:T(8,128)(2,1)S(1)} %get-tuple-element.65), channel_id=1, source_target_pairs={{0,3},{1,0},{2,1},{3,2},{4,7},{5,4},{6,5},{7,6},{8,11},{9,8},{10,9... | collective-permute-start | bytes 196616 | tf_op jit(solution)/shard_map/ppermute | solution.py:371
  40.4 9.2 %collective-permute-start.8 = (bf16[64,512]{1,0:T(8,128)(2,1)S(1)}, bf16[64,512]{1,0:T(8,128)(2,1)S(1)}, u32[]{:S(2)}, u32[]{:S(2)}) collective-permute-start(bf16[64,512]{1,0:T(8,128)(2,1)S(1)} %get-tuple-element.69.refs_0_), channel_id=1, source_target_pairs={{0,3},{1,0},{2,1},{3,2},{4,7},{5,4},{6,5},{7,6},{8,11},{9,8},{10,9... | collective-permute-start | bytes 196616 | tf_op jit(solution)/shard_map/ppermute | solution.py:371
  44.5 8.8 %collective-permute-start.7 = (bf16[64,512]{1,0:T(8,128)(2,1)S(1)}, bf16[64,512]{1,0:T(8,128)(2,1)S(1)}, u32[]{:S(2)}, u32[]{:S(2)}) collective-permute-start(bf16[64,512]{1,0:T(8,128)(2,1)S(1)} %get-tuple-element.69.refs_0_), channel_id=1, source_target_pairs={{0,2},{1,3},{2,0},{3,1},{4,6},{5,7},{6,4},{7,5},{8,10},{9,11},{10,... | collective-permute-start | bytes 196616 | tf_op jit(solution)/shard_map/ppermute | solution.py:371
  44.6 8.7 %collective-permute-start.6 = (bf16[64,512]{1,0:T(8,128)(2,1)S(1)}, bf16[64,512]{1,0:T(8,128)(2,1)S(1)}, u32[]{:S(2)}, u32[]{:S(2)}) collective-permute-start(bf16[64,512]{1,0:T(8,128)(2,1)S(1)} %get-tuple-element.69.refs_0_), channel_id=1, source_target_pairs={{0,1},{1,2},{2,3},{3,0},{4,5},{5,6},{6,7},{7,4},{8,9},{9,10},{10,1... | collective-permute-start | bytes 196616 | tf_op jit(solution)/shard_map/ppermute | solution.py:371
  45.2 8.1 %collective-permute-start.11 = (bf16[64,512]{1,0:T(8,128)(2,1)S(1)}, bf16[64,512]{1,0:T(8,128)(2,1)S(1)}, u32[]{:S(2)}, u32[]{:S(2)}) collective-permute-start(bf16[64,512]{1,0:T(8,128)(2,1)S(1)} %add_convert_fusion.refs_4_), channel_id=1, source_target_pairs={{0,3},{1,0},{2,1},{3,2},{4,7},{5,4},{6,5},{7,6},{8,11},{9,8},{10,9... | collective-permute-start | bytes 196616 | tf_op jit(solution)/shard_map/ppermute | solution.py:371
  48.5 7.6 %collective-permute-start.10 = (bf16[64,512]{1,0:T(8,128)(2,1)S(1)}, bf16[64,512]{1,0:T(8,128)(2,1)S(1)}, u32[]{:S(2)}, u32[]{:S(2)}) collective-permute-start(bf16[64,512]{1,0:T(8,128)(2,1)S(1)} %add_convert_fusion.refs_4_), channel_id=1, source_target_pairs={{0,2},{1,3},{2,0},{3,1},{4,6},{5,7},{6,4},{7,5},{8,10},{9,11},{10,... | collective-permute-start | bytes 196616 | tf_op jit(solution)/shard_map/ppermute | solution.py:371
  49.6 6.6 %collective-permute-start.9 = (bf16[64,512]{1,0:T(8,128)(2,1)S(1)}, bf16[64,512]{1,0:T(8,128)(2,1)S(1)}, u32[]{:S(2)}, u32[]{:S(2)}) collective-permute-start(bf16[64,512]{1,0:T(8,128)(2,1)S(1)} %add_convert_fusion.refs_4_), channel_id=1, source_target_pairs={{0,1},{1,2},{2,3},{3,0},{4,5},{5,6},{6,7},{7,4},{8,9},{9,10},{10,1... | collective-permute-start | bytes 196616 | tf_op jit(solution)/shard_map/ppermute | solution.py:371
  56.2 8.8 %collective-permute-start.13 = (bf16[128,1024]{1,0:T(8,128)(2,1)S(1)}, bf16[128,1024]{1,0:T(8,128)(2,1)S(1)}, u32[]{:S(2)}, u32[]{:S(2)}) collective-permute-start(bf16[128,1024]{1,0:T(8,128)(2,1)S(1)} %copy-done.9), channel_id=1, source_target_pairs={{0,1},{1,2},{2,3},{3,0},{4,5},{5,6},{6,7},{7,4},{8,9},{9,10},{10,1... | collective-permute-start | bytes 786440 | tf_op jit(solution)/shard_map/ppermute | solution.py:371
  57.9 24.1 %copy-start = (bf16[512,2048]{1,0:T(8,128)(2,1)S(1)}, bf16[512,2048]{1,0:T(8,128)(2,1)}, u32[]{:S(2)}) copy-start(bf16[512,2048]{1,0:T(8,128)(2,1)} %proj_ref.4) | copy-start | bytes 6291460
  57.9 1.5 %collective-permute-start.12 = (bf16[128,768]{1,0:T(8,128)(2,1)S(1)}, bf16[128,768]{1,0:T(8,128)(2,1)S(1)}, u32[]{:S(2)}, u32[]{:S(2)}) collective-permute-start(bf16[128,768]{1,0:T(8,128)(2,1)S(1)} %get-tuple-element.79), channel_id=1, source_target_pairs={{0,4},{4,0},{8,12},{12,8},{16,20},{20,16},{24,28},{28,24},{1,5},{5... | collective-permute-start | bytes 589832 | tf_op jit(solution)/shard_map/ppermute | solution.py:388
  65.0 9.0 %collective-permute-start.16 = (bf16[256,512]{1,0:T(8,128)(2,1)S(1)}, bf16[256,512]{1,0:T(8,128)(2,1)S(1)}, u32[]{:S(2)}, u32[]{:S(2)}) collective-permute-start(bf16[256,512]{1,0:T(8,128)(2,1)S(1)} %pad_maximum_fusion), channel_id=1, source_target_pairs={{0,24},{4,28},{8,0},{12,4},{16,8},{20,12},{24,16},{28,20},{1,25},{... | collective-permute-start | bytes 786440 | tf_op jit(solution)/shard_map/ppermute | solution.py:371
  67.5 11.5 %collective-permute-start.15 = (bf16[256,512]{1,0:T(8,128)(2,1)S(1)}, bf16[256,512]{1,0:T(8,128)(2,1)S(1)}, u32[]{:S(2)}, u32[]{:S(2)}) collective-permute-start(bf16[256,512]{1,0:T(8,128)(2,1)S(1)} %pad_maximum_fusion), channel_id=1, source_target_pairs={{0,16},{4,20},{8,24},{12,28},{16,0},{20,4},{24,8},{28,12},{1,17},{... | collective-permute-start | bytes 786440 | tf_op jit(solution)/shard_map/ppermute | solution.py:371
  68.0 11.0 %collective-permute-start.14 = (bf16[256,512]{1,0:T(8,128)(2,1)S(1)}, bf16[256,512]{1,0:T(8,128)(2,1)S(1)}, u32[]{:S(2)}, u32[]{:S(2)}) collective-permute-start(bf16[256,512]{1,0:T(8,128)(2,1)S(1)} %pad_maximum_fusion), channel_id=1, source_target_pairs={{0,8},{4,12},{8,16},{12,20},{16,24},{20,28},{24,0},{28,4},{1,9},{5... | collective-permute-start | bytes 786440 | tf_op jit(solution)/shard_map/ppermute | solution.py:371
  68.6 12.2 %collective-permute-start.18 = (bf16[128,1024]{1,0:T(8,128)(2,1)S(1)}, bf16[128,1024]{1,0:T(8,128)(2,1)S(1)}, u32[]{:S(2)}, u32[]{:S(2)}) collective-permute-start(bf16[128,1024]{1,0:T(8,128)(2,1)S(1)} %copy-done.8), channel_id=1, source_target_pairs={{0,2},{1,3},{2,0},{3,1},{4,6},{5,7},{6,4},{7,5},{8,10},{9,11},{10,... | collective-permute-start | bytes 786440 | tf_op jit(solution)/shard_map/ppermute | solution.py:371
  68.6 12.2 %collective-permute-start.19 = (bf16[128,1024]{1,0:T(8,128)(2,1)S(1)}, bf16[128,1024]{1,0:T(8,128)(2,1)S(1)}, u32[]{:S(2)}, u32[]{:S(2)}) collective-permute-start(bf16[128,1024]{1,0:T(8,128)(2,1)S(1)} %copy-done.7), channel_id=1, source_target_pairs={{0,3},{1,0},{2,1},{3,2},{4,7},{5,4},{6,5},{7,6},{8,11},{9,8},{10,9... | collective-permute-start | bytes 786440 | tf_op jit(solution)/shard_map/ppermute | solution.py:371
  79.0 23.1 %copy-start.2 = (bf16[256,1024]{1,0:T(8,128)(2,1)S(1)}, bf16[256,1024]{1,0:T(8,128)(2,1)}, u32[]{:S(2)}) copy-start(bf16[256,1024]{1,0:T(8,128)(2,1)} %proj_ref.5) | copy-start | bytes 1572868
  79.0 23.1 %copy-start.3 = (bf16[128,1024]{1,0:T(8,128)(2,1)S(1)}, bf16[128,1024]{1,0:T(8,128)(2,1)}, u32[]{:S(2)}) copy-start(bf16[128,1024]{1,0:T(8,128)(2,1)} %get-tuple-element.96.refs_1_) | copy-start | bytes 786436
  80.7 1.3 %collective-permute-start.17 = (bf16[128,256]{1,0:T(8,128)(2,1)S(1)}, bf16[128,256]{1,0:T(8,128)(2,1)S(1)}, u32[]{:S(2)}, u32[]{:S(2)}) collective-permute-start(bf16[128,256]{1,0:T(8,128)(2,1)S(1)} %get-tuple-element.86), channel_id=1, source_target_pairs={{0,4},{4,0},{8,12},{12,8},{16,20},{20,16},{24,28},{28,24},{1,5},{5... | collective-permute-start | bytes 196616 | tf_op jit(solution)/shard_map/ppermute | solution.py:388
  83.1 9.1 %collective-permute-start.20 = (bf16[128,512]{1,0:T(8,128)(2,1)S(1)}, bf16[128,512]{1,0:T(8,128)(2,1)S(1)}, u32[]{:S(2)}, u32[]{:S(2)}) collective-permute-start(bf16[128,512]{1,0:T(8,128)(2,1)S(1)} %get-tuple-element.91), channel_id=1, source_target_pairs={{0,1},{1,2},{2,3},{3,0},{4,5},{5,6},{6,7},{7,4},{8,9},{9,10},{10,1... | collective-permute-start | bytes 393224 | tf_op jit(solution)/shard_map/ppermute | solution.py:371
  85.9 10.3 %collective-permute-start.21 = (bf16[128,512]{1,0:T(8,128)(2,1)S(1)}, bf16[128,512]{1,0:T(8,128)(2,1)S(1)}, u32[]{:S(2)}, u32[]{:S(2)}) collective-permute-start(bf16[128,512]{1,0:T(8,128)(2,1)S(1)} %get-tuple-element.92), channel_id=1, source_target_pairs={{0,2},{1,3},{2,0},{3,1},{4,6},{5,7},{6,4},{7,5},{8,10},{9,11},{10,... | collective-permute-start | bytes 393224 | tf_op jit(solution)/shard_map/ppermute | solution.py:371
  88.2 8.1 %collective-permute-start.22 = (bf16[128,512]{1,0:T(8,128)(2,1)S(1)}, bf16[128,512]{1,0:T(8,128)(2,1)S(1)}, u32[]{:S(2)}, u32[]{:S(2)}) collective-permute-start(bf16[128,512]{1,0:T(8,128)(2,1)S(1)} %get-tuple-element.93), channel_id=1, source_target_pairs={{0,3},{1,0},{2,1},{3,2},{4,7},{5,4},{6,5},{7,6},{8,11},{9,8},{10,9... | collective-permute-start | bytes 393224 | tf_op jit(solution)/shard_map/ppermute | solution.py:371
  96.5 1.3 %collective-permute-start.23 = (bf16[64,512]{1,0:T(8,128)(2,1)S(1)}, bf16[64,512]{1,0:T(8,128)(2,1)S(1)}, u32[]{:S(2)}, u32[]{:S(2)}) collective-permute-start(bf16[64,512]{1,0:T(8,128)(2,1)S(1)} %get-tuple-element.101), channel_id=1, source_target_pairs={{0,4},{4,0},{8,12},{12,8},{16,20},{20,16},{24,28},{28,24},{1,5},{5... | collective-permute-start | bytes 196616 | tf_op jit(solution)/shard_map/ppermute | solution.py:388
  97.9 5.1 %collective-permute-start.24 = (bf16[32,512]{1,0:T(8,128)(2,1)S(1)}, bf16[32,512]{1,0:T(8,128)(2,1)S(1)}, u32[]{:S(2)}, u32[]{:S(2)}) collective-permute-start(bf16[32,512]{1,0:T(8,128)(2,1)S(1)} %get-tuple-element.103), channel_id=1, source_target_pairs={{0,8},{4,12},{8,16},{12,20},{16,24},{20,28},{24,0},{28,4},{1,9},{5... | collective-permute-start | bytes 98312 | tf_op jit(solution)/shard_map/ppermute | solution.py:371
  100.3 3.9 %collective-permute-start.26 = (bf16[32,512]{1,0:T(8,128)(2,1)S(1)}, bf16[32,512]{1,0:T(8,128)(2,1)S(1)}, u32[]{:S(2)}, u32[]{:S(2)}) collective-permute-start(bf16[32,512]{1,0:T(8,128)(2,1)S(1)} %get-tuple-element.104), channel_id=1, source_target_pairs={{0,24},{4,28},{8,0},{12,4},{16,8},{20,12},{24,16},{28,20},{1,25},{... | collective-permute-start | bytes 98312 | tf_op jit(solution)/shard_map/ppermute | solution.py:371
  100.8 3.9 %collective-permute-start.25 = (bf16[32,512]{1,0:T(8,128)(2,1)S(1)}, bf16[32,512]{1,0:T(8,128)(2,1)S(1)}, u32[]{:S(2)}, u32[]{:S(2)}) collective-permute-start(bf16[32,512]{1,0:T(8,128)(2,1)S(1)} %get-tuple-element.105), channel_id=1, source_target_pairs={{0,16},{4,20},{8,24},{12,28},{16,0},{20,4},{24,8},{28,12},{1,17},{... | collective-permute-start | bytes 98312 | tf_op jit(solution)/shard_map/ppermute | solution.py:371
  (5 other events, 59.4 us)

commit v15 on v14

--- a/solution.py
+++ b/solution.py
@@ -465,11 +465,12 @@
     core = (seq % 2).reshape(1)
     kept, given = global_heads(depth, core, ids, global_gain.reshape(ways, 1, -1), early_shares, late_shares, weight)
     received = swap_cores(given, "seq")
-    received, *parts = lax.optimization_barrier((received, *parts))
+    received, parts[2:] = lax.optimization_barrier((received, parts[2:]))
     half = kept.shape[1] // 3
     keyed = jnp.concatenate([kept[:, half:], received[:, half:]], axis=0)
     pieces = [shift(keyed, "seq", 2 * step) for step in range(1, lax.axis_size("seq") // 2)]
     parts[2:] = [shift(part, "head", step) for step, part in enumerate(parts[2:], 2)]
+    kept, parts[1] = lax.optimization_barrier((kept, parts[1]))
     own_heads, other_heads = attend(depth, seq.reshape(1), twin_ids("seq"), global_scale, kept, received, pieces)
     other_heads, parts[2:] = lax.optimization_barrier((swap_cores(other_heads, "seq"), parts[2:]))
     updates = scatter(project(core, slots, own_heads, other_heads, global_out), "head")

time: 107 us -> 107 us (level)
  waiting for transfers between devices: 31.4 us -> 30.2 us
    ppermute x3, waiting for transfers between devices: 3.76 us -> 2.48 us  [swap_cores(): lax.ppermute(value, axis, [(i, i ^ 1) for i in range(lax.axis_size(axis))])]
  transfers between devices with their start and end apart: 27 -> 27, of which waited for: 12 -> 12; matrix products, arithmetic and copies ran while one was open for 2% -> 2% of each run, Pallas kernels for 17% -> 15%
where the time goes in v15:
time: 107 us; the launch traced here: 106 us
  starting transfers between devices  42.3 us (40%)
  waiting for transfers between devices  30.2 us (28%)
  Pallas kernels  29.8 us (28%)
  local copies, waits for them, and re-layouts  1.75 us (2%)
  other arithmetic  1.12 us (1%)
    ppermute x24, starting transfers between devices, shift(): lax.ppermute(value, axis, [(i, (i + step) % count) for i in range(count)])  42 us
    ppermute x24, waiting for transfers between devices, shift(): lax.ppermute(value, axis, [(i, (i + step) % count) for i in range(count)])  27.7 us
    pallas_call x2, Pallas kernels, local_part(): pl.pallas_call(functools.partial(local_kernel, span, ways, piece, last),...  20.2 us
    pallas_call x1, Pallas kernels, fetch(): pl.pallas_call(fetch_kernel, in_specs=[HBM], out_specs=VMEM, out_shape=pl...  2.89 us
    ppermute x3, waiting for transfers between devices, swap_cores(): lax.ppermute(value, axis, [(i, i ^ 1) for i in range(lax.axis_size(axis))])  2.48 us
  transfers between devices with their start and end apart: 27, of which 12 were waited for; matrix products, arithmetic and copies ran while one was open for 2% of the time, Pallas kernels for 15%

profile of v15, /device:TPU:0, one launch (start us, length us, event | category | flops | bytes accessed | tf_op | source)
XLA Modules:
  0.0 106.1 jit_solution(2090302627465735133)
XLA Ops:
  0.6 10.1 %local_part.2 = (bf16[128,1024]{1,0:T(8,128)(2,1)}, bf16[128,1024]{1,0:T(8,128)(2,1)}, bf16[128,1024]{1,0:T(8,128)(2,1)}, bf16[128,1024]{1,0:T(8,128)(2,1)}) custom-call(f32[2]{0:T(128)} %scale_ref.4, f32[1,1024]{1,0:T(1,128)} %bitcast.33, bf16[1024,1024]{1,0:T(8,128)(2,1)} %bitcast.29, bf16[3,1024,256]{2,1,0:T(8,128)(2,1)} %bitcast.31, ...), custom_call_target="tpu_custom_call" | custom-call | flops 4294967296 | bytes 10485760 | tf_op jit(solution)/shard_map/local_part/pallas_call | solution.py:117
  10.7 3.1 %collective-permute-start = (bf16[128,1024]{1,0:T(8,128)(2,1)}, bf16[128,1024]{1,0:T(8,128)(2,1)S(1)}, u32[]{:S(2)}, u32[]{:S(2)}) collective-permute-start(bf16[128,1024]{1,0:T(8,128)(2,1)} %get-tuple-element.57), channel_id=1, source_target_pairs={{0,1},{1,2},{2,3},{3,0},{4,5},{5,6},{6,7},{7,4},{8,9},{9,10},{10,1... | collective-permute-start | bytes 786440 | tf_op jit(solution)/shard_map/ppermute | solution.py:371
  13.8 2.6 %collective-permute-start.1 = (bf16[128,1024]{1,0:T(8,128)(2,1)}, bf16[128,1024]{1,0:T(8,128)(2,1)S(1)}, u32[]{:S(2)}, u32[]{:S(2)}) collective-permute-start(bf16[128,1024]{1,0:T(8,128)(2,1)} %get-tuple-element.59), channel_id=1, source_target_pairs={{0,2},{1,3},{2,0},{3,1},{4,6},{5,7},{6,4},{7,5},{8,10},{9,11},{10,... | collective-permute-start | bytes 786440 | tf_op jit(solution)/shard_map/ppermute | solution.py:371
  16.4 1.3 %collective-permute-start.2 = (bf16[128,1024]{1,0:T(8,128)(2,1)}, bf16[128,1024]{1,0:T(8,128)(2,1)S(1)}, u32[]{:S(2)}, u32[]{:S(2)}) collective-permute-start(bf16[128,1024]{1,0:T(8,128)(2,1)} %get-tuple-element.60), channel_id=1, source_target_pairs={{0,3},{1,0},{2,1},{3,2},{4,7},{5,4},{6,5},{7,6},{8,11},{9,8},{10,9... | collective-permute-start | bytes 786440 | tf_op jit(solution)/shard_map/ppermute | solution.py:371
  17.8 10.1 %local_part.3 = (bf16[128,1024]{1,0:T(8,128)(2,1)}, bf16[128,1024]{1,0:T(8,128)(2,1)}, bf16[128,1024]{1,0:T(8,128)(2,1)}, bf16[128,1024]{1,0:T(8,128)(2,1)}, bf1...) custom-call(f32[2]{0:T(128)} %scale_ref.4, ...), custom_call_target="tpu_custom_call" | custom-call | flops 4294967296 | bytes 10485760 | tf_op jit(solution)/shard_map/local_part/pallas_call | solution.py:117
  28.8 6.2 %collective-permute-start.3 = (bf16[64,512]{1,0:T(8,128)(2,1)S(1)}, bf16[64,512]{1,0:T(8,128)(2,1)S(1)}, u32[]{:S(2)}, u32[]{:S(2)}) collective-permute-start(bf16[64,512]{1,0:T(8,128)(2,1)S(1)} %get-tuple-element.63), channel_id=1, source_target_pairs={{0,1},{1,2},{2,3},{3,0},{4,5},{5,6},{6,7},{7,4},{8,9},{9,10},{10,1... | collective-permute-start | bytes 196616 | tf_op jit(solution)/shard_map/ppermute | solution.py:371
  35.0 2.0 %collective-permute-start.4 = (bf16[64,512]{1,0:T(8,128)(2,1)S(1)}, bf16[64,512]{1,0:T(8,128)(2,1)S(1)}, u32[]{:S(2)}, u32[]{:S(2)}) collective-permute-start(bf16[64,512]{1,0:T(8,128)(2,1)S(1)} %get-tuple-element.64), channel_id=1, source_target_pairs={{0,2},{1,3},{2,0},{3,1},{4,6},{5,7},{6,4},{7,5},{8,10},{9,11},{10,... | collective-permute-start | bytes 196616 | tf_op jit(solution)/shard_map/ppermute | solution.py:371
  36.9 2.9 %collective-permute-start.5 = (bf16[64,512]{1,0:T(8,128)(2,1)S(1)}, bf16[64,512]{1,0:T(8,128)(2,1)S(1)}, u32[]{:S(2)}, u32[]{:S(2)}) collective-permute-start(bf16[64,512]{1,0:T(8,128)(2,1)S(1)} %get-tuple-element.65), channel_id=1, source_target_pairs={{0,3},{1,0},{2,1},{3,2},{4,7},{5,4},{6,5},{7,6},{8,11},{9,8},{10,9... | collective-permute-start | bytes 196616 | tf_op jit(solution)/shard_map/ppermute | solution.py:371
  40.9 3.6 %collective-permute-start.8 = (bf16[64,512]{1,0:T(8,128)(2,1)S(1)}, bf16[64,512]{1,0:T(8,128)(2,1)S(1)}, u32[]{:S(2)}, u32[]{:S(2)}) collective-permute-start(bf16[64,512]{1,0:T(8,128)(2,1)S(1)} %get-tuple-element.69.refs_0_), channel_id=1, source_target_pairs={{0,3},{1,0},{2,1},{3,2},{4,7},{5,4},{6,5},{7,6},{8,11},{9,8},{10,9... | collective-permute-start | bytes 196616 | tf_op jit(solution)/shard_map/ppermute | solution.py:371
  45.2 3.3 %collective-permute-start.11 = (bf16[64,512]{1,0:T(8,128)(2,1)S(1)}, bf16[64,512]{1,0:T(8,128)(2,1)S(1)}, u32[]{:S(2)}, u32[]{:S(2)}) collective-permute-start(bf16[64,512]{1,0:T(8,128)(2,1)S(1)} %add_convert_fusion.refs_4_), channel_id=1, source_target_pairs={{0,3},{1,0},{2,1},{3,2},{4,7},{5,4},{6,5},{7,6},{8,11},{9,8},{10,9... | collective-permute-start | bytes 196616 | tf_op jit(solution)/shard_map/ppermute | solution.py:371
  48.5 1.1 collective-permute-start.10
  49.6 2.9 %fetch.1.refs_8_ = bf16[3,2048,512]{2,1,0:T(8,128)(2,1)S(1)} custom-call(bf16[3,2048,512]{2,1,0:T(8,128)(2,1)} %bitcast.27), custom_call_target="tpu_custom_call" | custom-call | tf_op jit(solution)/shard_map/fetch/pallas_call | solution.py:173
  53.2 2.9 %collective-permute-done.10.refs_6_ = bf16[64,512]{1,0:T(8,128)(2,1)S(1)} collective-permute-done((bf16[64,512]{1,0:T(8,128)(2,1)S(1)}, bf16[64,512]{1,0:T(8,128)(2,1)S(1)}, u32[]{:S(2)}, u32[]{:S(2)}) %collective-permute-start.10) | collective-permute-done | bytes 65568 | tf_op jit(solution)/shard_map/ppermute | solution.py:371
  56.2 1.7 %global_heads.1 = (bf16[128,768]{1,0:T(8,128)(2,1)S(1)}, bf16[128,768]{1,0:T(8,128)(2,1)S(1)}) custom-call(s32[1]{0:T(128)} %bitcast.7.core_ref, s32[4]{0:T(128)S(1)} %and_select_fusion.ids_ref, f32[4,1,512]{2,1,0:T(1,128)S(1)} %bitcast.26, bf16[64,512]{1,0:T(8,128)(2,1)S(1)} %get-tuple-element.69.refs_0_, ...), custom_call_target="tpu_custom_call" | custom-call | tf_op jit(solution)/shard_map/global_heads/pallas_call | solution.py:207
  58.2 1.2 %collective-permute-done.13.given_ref = bf16[128,768]{1,0:T(8,128)(2,1)S(1)} collective-permute-done((bf16[128,768]{1,0:T(8,128)(2,1)S(1)}, bf16[128,768]{1,0:T(8,128)(2,1)S(1)}, u32[]{:S(2)}, u32[]{:S(2)}) %collective-permute-start.13) | collective-permute-done | bytes 196640 | tf_op jit(solution)/shard_map/ppermute | solution.py:388
  59.4 2.5 %collective-permute-start.16 = (bf16[256,512]{1,0:T(8,128)(2,1)S(1)}, bf16[256,512]{1,0:T(8,128)(2,1)S(1)}, u32[]{:S(2)}, u32[]{:S(2)}) collective-permute-start(bf16[256,512]{1,0:T(8,128)(2,1)S(1)} %pad_maximum_fusion), channel_id=1, source_target_pairs={{0,24},{4,28},{8,0},{12,4},{16,8},{20,12},{24,16},{28,20},{1,25},{... | collective-permute-start | bytes 786440 | tf_op jit(solution)/shard_map/ppermute | solution.py:371
  63.7 5.3 %collective-permute-done.12.refs_2_ = bf16[128,1024]{1,0:T(8,128)(2,1)S(1)} collective-permute-done((bf16[128,1024]{1,0:T(8,128)(2,1)S(1)}, bf16[128,1024]{1,0:T(8,128)(2,1)S(1)}, u32[]{:S(2)}, u32[]{:S(2)}) %collective-permute-start.12) | collective-permute-done | bytes 262176 | tf_op jit(solution)/shard_map/ppermute | solution.py:371
  69.1 6.5 %collective-permute-done.15.refs_1_ = bf16[256,512]{1,0:T(8,128)(2,1)S(1)} collective-permute-done((bf16[256,512]{1,0:T(8,128)(2,1)S(1)}, bf16[256,512]{1,0:T(8,128)(2,1)S(1)}, u32[]{:S(2)}, u32[]{:S(2)}) %collective-permute-start.15) | collective-permute-done | bytes 262176 | tf_op jit(solution)/shard_map/ppermute | solution.py:371
  75.6 1.7 %attend.1 = (bf16[128,256]{1,0:T(8,128)(2,1)S(1)}, bf16[128,256]{1,0:T(8,128)(2,1)S(1)}) custom-call(s32[1]{0:T(128)} %bitcast.8.me_ref, s32[4]{0:T(128)S(1)} %and_select_fusion.1.ids_ref, f32[4]{0:T(128)S(1)} %copy-done.6, bf16[128,768]{1,0:T(8,128)(2,1)S(1)} %get-tuple-element.80.kept_ref, bf16[128,768]{1,0:T(8,128)(2,1)S(1)} %collective-permute-done.13.given_ref, ...), custom_call_target="tpu_custom_call" | custom-call | flops 1 | bytes 1 | tf_op jit(solution)/shard_map/attend/pallas_call | solution.py:250
  77.4 2.4 %collective-permute-done.18.refs_3_ = bf16[128,1024]{1,0:T(8,128)(2,1)S(1)} collective-permute-done((bf16[128,1024]{1,0:T(8,128)(2,1)S(1)}, bf16[128,1024]{1,0:T(8,128)(2,1)S(1)}, u32[]{:S(2)}, u32[]{:S(2)}) %collective-permute-start.18) | collective-permute-done | bytes 262176 | tf_op jit(solution)/shard_map/ppermute | solution.py:371
  79.8 2.0 %collective-permute-done.19.refs_4_ = bf16[128,1024]{1,0:T(8,128)(2,1)S(1)} collective-permute-done((bf16[128,1024]{1,0:T(8,128)(2,1)S(1)}, bf16[128,1024]{1,0:T(8,128)(2,1)S(1)}, u32[]{:S(2)}, u32[]{:S(2)}) %collective-permute-start.19) | collective-permute-done | bytes 262176 | tf_op jit(solution)/shard_map/ppermute | solution.py:371
  81.9 1.0 project.1
  82.9 4.1 %collective-permute-start.20 = (bf16[128,512]{1,0:T(8,128)(2,1)S(1)}, bf16[128,512]{1,0:T(8,128)(2,1)S(1)}, u32[]{:S(2)}, u32[]{:S(2)}) collective-permute-start(bf16[128,512]{1,0:T(8,128)(2,1)S(1)} %get-tuple-element.91), channel_id=1, source_target_pairs={{0,1},{1,2},{2,3},{3,0},{4,5},{5,6},{6,7},{7,4},{8,9},{9,10},{10,1... | collective-permute-start | bytes 393224 | tf_op jit(solution)/shard_map/ppermute | solution.py:371
  87.0 2.4 %collective-permute-start.22 = (bf16[128,512]{1,0:T(8,128)(2,1)S(1)}, bf16[128,512]{1,0:T(8,128)(2,1)S(1)}, u32[]{:S(2)}, u32[]{:S(2)}) collective-permute-start(bf16[128,512]{1,0:T(8,128)(2,1)S(1)} %get-tuple-element.93), channel_id=1, source_target_pairs={{0,3},{1,0},{2,1},{3,2},{4,7},{5,4},{6,5},{7,6},{8,11},{9,8},{10,9... | collective-permute-start | bytes 393224 | tf_op jit(solution)/shard_map/ppermute | solution.py:371
  89.5 1.4 %collective-permute-done.20.refs_1_ = bf16[128,512]{1,0:T(8,128)(2,1)S(1)} collective-permute-done((bf16[128,512]{1,0:T(8,128)(2,1)S(1)}, bf16[128,512]{1,0:T(8,128)(2,1)S(1)}, u32[]{:S(2)}, u32[]{:S(2)}) %collective-permute-start.20) | collective-permute-done | bytes 131104 | tf_op jit(solution)/shard_map/ppermute | solution.py:371
  90.9 4.9 %collective-permute-done.21.refs_2_ = bf16[128,512]{1,0:T(8,128)(2,1)S(1)} collective-permute-done((bf16[128,512]{1,0:T(8,128)(2,1)S(1)}, bf16[128,512]{1,0:T(8,128)(2,1)S(1)}, u32[]{:S(2)}, u32[]{:S(2)}) %collective-permute-start.21) | collective-permute-done | bytes 131104 | tf_op jit(solution)/shard_map/ppermute | solution.py:371
  96.1 1.2 %collective-permute-done.23 = bf16[64,512]{1,0:T(8,128)(2,1)S(1)} collective-permute-done((bf16[64,512]{1,0:T(8,128)(2,1)S(1)}, bf16[64,512]{1,0:T(8,128)(2,1)S(1)}, u32[]{:S(2)}, u32[]{:S(2)}) %collective-permute-start.23) | collective-permute-done | bytes 65568 | tf_op jit(solution)/shard_map/ppermute | solution.py:388
  97.3 1.9 %collective-permute-start.24 = (bf16[32,512]{1,0:T(8,128)(2,1)S(1)}, bf16[32,512]{1,0:T(8,128)(2,1)S(1)}, u32[]{:S(2)}, u32[]{:S(2)}) collective-permute-start(bf16[32,512]{1,0:T(8,128)(2,1)S(1)} %get-tuple-element.103), channel_id=1, source_target_pairs={{0,8},{4,12},{8,16},{12,20},{16,24},{20,28},{24,0},{28,4},{1,9},{5... | collective-permute-start | bytes 98312 | tf_op jit(solution)/shard_map/ppermute | solution.py:371
  99.2 1.1 %collective-permute-start.26 = (bf16[32,512]{1,0:T(8,128)(2,1)S(1)}, bf16[32,512]{1,0:T(8,128)(2,1)S(1)}, u32[]{:S(2)}, u32[]{:S(2)}) collective-permute-start(bf16[32,512]{1,0:T(8,128)(2,1)S(1)} %get-tuple-element.104), channel_id=1, source_target_pairs={{0,24},{4,28},{8,0},{12,4},{16,8},{20,12},{24,16},{28,20},{1,25},{... | collective-permute-start | bytes 98312 | tf_op jit(solution)/shard_map/ppermute | solution.py:371
  100.3 1.5 %collective-permute-start.25 = (bf16[32,512]{1,0:T(8,128)(2,1)S(1)}, bf16[32,512]{1,0:T(8,128)(2,1)S(1)}, u32[]{:S(2)}, u32[]{:S(2)}) collective-permute-start(bf16[32,512]{1,0:T(8,128)(2,1)S(1)} %get-tuple-element.105), channel_id=1, source_target_pairs={{0,16},{4,20},{8,24},{12,28},{16,0},{20,4},{24,8},{28,12},{1,17},{... | collective-permute-start | bytes 98312 | tf_op jit(solution)/shard_map/ppermute | solution.py:371
  103.1 1.1 %collective-permute-done.25 = bf16[32,512]{1,0:T(8,128)(2,1)S(1)} collective-permute-done((bf16[32,512]{1,0:T(8,128)(2,1)S(1)}, bf16[32,512]{1,0:T(8,128)(2,1)S(1)}, u32[]{:S(2)}, u32[]{:S(2)}) %collective-permute-start.25) | collective-permute-done | bytes 32800 | tf_op jit(solution)/shard_map/ppermute | solution.py:371
  104.2 1.0 reshape.86
  (70 shorter events, 8.1 us)
Async XLA Ops:
  10.7 18.0 %collective-permute-start = (bf16[128,1024]{1,0:T(8,128)(2,1)}, bf16[128,1024]{1,0:T(8,128)(2,1)S(1)}, u32[]{:S(2)}, u32[]{:S(2)}) collective-permute-start(bf16[128,1024]{1,0:T(8,128)(2,1)} %get-tuple-element.57), channel_id=1, source_target_pairs={{0,1},{1,2},{2,3},{3,0},{4,5},{5,6},{6,7},{7,4},{8,9},{9,10},{10,1... | collective-permute-start | bytes 786440 | tf_op jit(solution)/shard_map/ppermute | solution.py:371
  13.8 26.7 %collective-permute-start.1 = (bf16[128,1024]{1,0:T(8,128)(2,1)}, bf16[128,1024]{1,0:T(8,128)(2,1)S(1)}, u32[]{:S(2)}, u32[]{:S(2)}) collective-permute-start(bf16[128,1024]{1,0:T(8,128)(2,1)} %get-tuple-element.59), channel_id=1, source_target_pairs={{0,2},{1,3},{2,0},{3,1},{4,6},{5,7},{6,4},{7,5},{8,10},{9,11},{10,... | collective-permute-start | bytes 786440 | tf_op jit(solution)/shard_map/ppermute | solution.py:371
  16.4 24.2 %copy-start.1 = (bf16[1024,256]{1,0:T(8,128)(2,1)S(1)}, bf16[1024,256]{1,0:T(8,128)(2,1)}, u32[]{:S(2)}) copy-start(bf16[1024,256]{1,0:T(8,128)(2,1)} %proj_ref.3) | copy-start | bytes 1572868
  16.4 24.2 %copy-start.4 = (bf16[128,1024]{1,0:T(8,128)(2,1)S(1)}, bf16[128,1024]{1,0:T(8,128)(2,1)}, u32[]{:S(2)}) copy-start(bf16[128,1024]{1,0:T(8,128)(2,1)} %get-tuple-element.52.refs_0_) | copy-start | bytes 786436
  16.4 24.1 %collective-permute-start.2 = (bf16[128,1024]{1,0:T(8,128)(2,1)}, bf16[128,1024]{1,0:T(8,128)(2,1)S(1)}, u32[]{:S(2)}, u32[]{:S(2)}) collective-permute-start(bf16[128,1024]{1,0:T(8,128)(2,1)} %get-tuple-element.60), channel_id=1, source_target_pairs={{0,3},{1,0},{2,1},{3,2},{4,7},{5,4},{6,5},{7,6},{8,11},{9,8},{10,9... | collective-permute-start | bytes 786440 | tf_op jit(solution)/shard_map/ppermute | solution.py:371
  28.8 15.8 %collective-permute-start.3 = (bf16[64,512]{1,0:T(8,128)(2,1)S(1)}, bf16[64,512]{1,0:T(8,128)(2,1)S(1)}, u32[]{:S(2)}, u32[]{:S(2)}) collective-permute-start(bf16[64,512]{1,0:T(8,128)(2,1)S(1)} %get-tuple-element.63), channel_id=1, source_target_pairs={{0,1},{1,2},{2,3},{3,0},{4,5},{5,6},{6,7},{7,4},{8,9},{9,10},{10,1... | collective-permute-start | bytes 196616 | tf_op jit(solution)/shard_map/ppermute | solution.py:371
  35.0 10.2 %collective-permute-start.4 = (bf16[64,512]{1,0:T(8,128)(2,1)S(1)}, bf16[64,512]{1,0:T(8,128)(2,1)S(1)}, u32[]{:S(2)}, u32[]{:S(2)}) collective-permute-start(bf16[64,512]{1,0:T(8,128)(2,1)S(1)} %get-tuple-element.64), channel_id=1, source_target_pairs={{0,2},{1,3},{2,0},{3,1},{4,6},{5,7},{6,4},{7,5},{8,10},{9,11},{10,... | collective-permute-start | bytes 196616 | tf_op jit(solution)/shard_map/ppermute | solution.py:371
  36.9 8.2 %collective-permute-start.5 = (bf16[64,512]{1,0:T(8,128)(2,1)S(1)}, bf16[64,512]{1,0:T(8,128)(2,1)S(1)}, u32[]{:S(2)}, u32[]{:S(2)}) collective-permute-start(bf16[64,512]{1,0:T(8,128)(2,1)S(1)} %get-tuple-element.65), channel_id=1, source_target_pairs={{0,3},{1,0},{2,1},{3,2},{4,7},{5,4},{6,5},{7,6},{8,11},{9,8},{10,9... | collective-permute-start | bytes 196616 | tf_op jit(solution)/shard_map/ppermute | solution.py:371
  40.9 8.7 %collective-permute-start.8 = (bf16[64,512]{1,0:T(8,128)(2,1)S(1)}, bf16[64,512]{1,0:T(8,128)(2,1)S(1)}, u32[]{:S(2)}, u32[]{:S(2)}) collective-permute-start(bf16[64,512]{1,0:T(8,128)(2,1)S(1)} %get-tuple-element.69.refs_0_), channel_id=1, source_target_pairs={{0,3},{1,0},{2,1},{3,2},{4,7},{5,4},{6,5},{7,6},{8,11},{9,8},{10,9... | collective-permute-start | bytes 196616 | tf_op jit(solution)/shard_map/ppermute | solution.py:371
  44.5 8.7 %collective-permute-start.7 = (bf16[64,512]{1,0:T(8,128)(2,1)S(1)}, bf16[64,512]{1,0:T(8,128)(2,1)S(1)}, u32[]{:S(2)}, u32[]{:S(2)}) collective-permute-start(bf16[64,512]{1,0:T(8,128)(2,1)S(1)} %get-tuple-element.69.refs_0_), channel_id=1, source_target_pairs={{0,2},{1,3},{2,0},{3,1},{4,6},{5,7},{6,4},{7,5},{8,10},{9,11},{10,... | collective-permute-start | bytes 196616 | tf_op jit(solution)/shard_map/ppermute | solution.py:371
  44.6 8.7 %collective-permute-start.6 = (bf16[64,512]{1,0:T(8,128)(2,1)S(1)}, bf16[64,512]{1,0:T(8,128)(2,1)S(1)}, u32[]{:S(2)}, u32[]{:S(2)}) collective-permute-start(bf16[64,512]{1,0:T(8,128)(2,1)S(1)} %get-tuple-element.69.refs_0_), channel_id=1, source_target_pairs={{0,1},{1,2},{2,3},{3,0},{4,5},{5,6},{6,7},{7,4},{8,9},{9,10},{10,1... | collective-permute-start | bytes 196616 | tf_op jit(solution)/shard_map/ppermute | solution.py:371
  45.2 8.0 %collective-permute-start.11 = (bf16[64,512]{1,0:T(8,128)(2,1)S(1)}, bf16[64,512]{1,0:T(8,128)(2,1)S(1)}, u32[]{:S(2)}, u32[]{:S(2)}) collective-permute-start(bf16[64,512]{1,0:T(8,128)(2,1)S(1)} %add_convert_fusion.refs_4_), channel_id=1, source_target_pairs={{0,3},{1,0},{2,1},{3,2},{4,7},{5,4},{6,5},{7,6},{8,11},{9,8},{10,9... | collective-permute-start | bytes 196616 | tf_op jit(solution)/shard_map/ppermute | solution.py:371
  48.5 7.6 %collective-permute-start.10 = (bf16[64,512]{1,0:T(8,128)(2,1)S(1)}, bf16[64,512]{1,0:T(8,128)(2,1)S(1)}, u32[]{:S(2)}, u32[]{:S(2)}) collective-permute-start(bf16[64,512]{1,0:T(8,128)(2,1)S(1)} %add_convert_fusion.refs_4_), channel_id=1, source_target_pairs={{0,2},{1,3},{2,0},{3,1},{4,6},{5,7},{6,4},{7,5},{8,10},{9,11},{10,... | collective-permute-start | bytes 196616 | tf_op jit(solution)/shard_map/ppermute | solution.py:371
  49.6 6.6 %collective-permute-start.9 = (bf16[64,512]{1,0:T(8,128)(2,1)S(1)}, bf16[64,512]{1,0:T(8,128)(2,1)S(1)}, u32[]{:S(2)}, u32[]{:S(2)}) collective-permute-start(bf16[64,512]{1,0:T(8,128)(2,1)S(1)} %add_convert_fusion.refs_4_), channel_id=1, source_target_pairs={{0,1},{1,2},{2,3},{3,0},{4,5},{5,6},{6,7},{7,4},{8,9},{9,10},{10,1... | collective-permute-start | bytes 196616 | tf_op jit(solution)/shard_map/ppermute | solution.py:371
  57.9 24.0 %copy-start = (bf16[512,2048]{1,0:T(8,128)(2,1)S(1)}, bf16[512,2048]{1,0:T(8,128)(2,1)}, u32[]{:S(2)}) copy-start(bf16[512,2048]{1,0:T(8,128)(2,1)} %proj_ref.4) | copy-start | bytes 6291460
  57.9 1.5 %collective-permute-start.13 = (bf16[128,768]{1,0:T(8,128)(2,1)S(1)}, bf16[128,768]{1,0:T(8,128)(2,1)S(1)}, u32[]{:S(2)}, u32[]{:S(2)}) collective-permute-start(bf16[128,768]{1,0:T(8,128)(2,1)S(1)} %get-tuple-element.81), channel_id=1, source_target_pairs={{0,4},{4,0},{8,12},{12,8},{16,20},{20,16},{24,28},{28,24},{1,5},{5... | collective-permute-start | bytes 589832 | tf_op jit(solution)/shard_map/ppermute | solution.py:388
  58.0 11.1 %collective-permute-start.12 = (bf16[128,1024]{1,0:T(8,128)(2,1)S(1)}, bf16[128,1024]{1,0:T(8,128)(2,1)S(1)}, u32[]{:S(2)}, u32[]{:S(2)}) collective-permute-start(bf16[128,1024]{1,0:T(8,128)(2,1)S(1)} %copy-done.9), channel_id=1, source_target_pairs={{0,1},{1,2},{2,3},{3,0},{4,5},{5,6},{6,7},{7,4},{8,9},{9,10},{10,1... | collective-permute-start | bytes 786440 | tf_op jit(solution)/shard_map/ppermute | solution.py:371
  59.4 9.6 %collective-permute-start.16 = (bf16[256,512]{1,0:T(8,128)(2,1)S(1)}, bf16[256,512]{1,0:T(8,128)(2,1)S(1)}, u32[]{:S(2)}, u32[]{:S(2)}) collective-permute-start(bf16[256,512]{1,0:T(8,128)(2,1)S(1)} %pad_maximum_fusion), channel_id=1, source_target_pairs={{0,24},{4,28},{8,0},{12,4},{16,8},{20,12},{24,16},{28,20},{1,25},{... | collective-permute-start | bytes 786440 | tf_op jit(solution)/shard_map/ppermute | solution.py:371
  61.9 13.7 %collective-permute-start.15 = (bf16[256,512]{1,0:T(8,128)(2,1)S(1)}, bf16[256,512]{1,0:T(8,128)(2,1)S(1)}, u32[]{:S(2)}, u32[]{:S(2)}) collective-permute-start(bf16[256,512]{1,0:T(8,128)(2,1)S(1)} %pad_maximum_fusion), channel_id=1, source_target_pairs={{0,16},{4,20},{8,24},{12,28},{16,0},{20,4},{24,8},{28,12},{1,17},{... | collective-permute-start | bytes 786440 | tf_op jit(solution)/shard_map/ppermute | solution.py:371
  62.4 13.2 %collective-permute-start.14 = (bf16[256,512]{1,0:T(8,128)(2,1)S(1)}, bf16[256,512]{1,0:T(8,128)(2,1)S(1)}, u32[]{:S(2)}, u32[]{:S(2)}) collective-permute-start(bf16[256,512]{1,0:T(8,128)(2,1)S(1)} %pad_maximum_fusion), channel_id=1, source_target_pairs={{0,8},{4,12},{8,16},{12,20},{16,24},{20,28},{24,0},{28,4},{1,9},{5... | collective-permute-start | bytes 786440 | tf_op jit(solution)/shard_map/ppermute | solution.py:371
  63.0 16.8 %collective-permute-start.18 = (bf16[128,1024]{1,0:T(8,128)(2,1)S(1)}, bf16[128,1024]{1,0:T(8,128)(2,1)S(1)}, u32[]{:S(2)}, u32[]{:S(2)}) collective-permute-start(bf16[128,1024]{1,0:T(8,128)(2,1)S(1)} %copy-done.8), channel_id=1, source_target_pairs={{0,2},{1,3},{2,0},{3,1},{4,6},{5,7},{6,4},{7,5},{8,10},{9,11},{10,... | collective-permute-start | bytes 786440 | tf_op jit(solution)/shard_map/ppermute | solution.py:371
  69.0 12.9 %collective-permute-start.19 = (bf16[128,1024]{1,0:T(8,128)(2,1)S(1)}, bf16[128,1024]{1,0:T(8,128)(2,1)S(1)}, u32[]{:S(2)}, u32[]{:S(2)}) collective-permute-start(bf16[128,1024]{1,0:T(8,128)(2,1)S(1)} %copy-done.7), channel_id=1, source_target_pairs={{0,3},{1,0},{2,1},{3,2},{4,7},{5,4},{6,5},{7,6},{8,11},{9,8},{10,9... | collective-permute-start | bytes 786440 | tf_op jit(solution)/shard_map/ppermute | solution.py:371
  75.6 26.2 %copy-start.2 = (bf16[256,1024]{1,0:T(8,128)(2,1)S(1)}, bf16[256,1024]{1,0:T(8,128)(2,1)}, u32[]{:S(2)}) copy-start(bf16[256,1024]{1,0:T(8,128)(2,1)} %proj_ref.5) | copy-start | bytes 1572868
  75.6 26.2 %copy-start.3 = (bf16[128,1024]{1,0:T(8,128)(2,1)S(1)}, bf16[128,1024]{1,0:T(8,128)(2,1)}, u32[]{:S(2)}) copy-start(bf16[128,1024]{1,0:T(8,128)(2,1)} %get-tuple-element.96.refs_1_) | copy-start | bytes 786436
  77.3 4.6 %collective-permute-start.17 = (bf16[128,256]{1,0:T(8,128)(2,1)S(1)}, bf16[128,256]{1,0:T(8,128)(2,1)S(1)}, u32[]{:S(2)}, u32[]{:S(2)}) collective-permute-start(bf16[128,256]{1,0:T(8,128)(2,1)S(1)} %get-tuple-element.86), channel_id=1, source_target_pairs={{0,4},{4,0},{8,12},{12,8},{16,20},{20,16},{24,28},{28,24},{1,5},{5... | collective-permute-start | bytes 196616 | tf_op jit(solution)/shard_map/ppermute | solution.py:388
  82.9 8.0 %collective-permute-start.20 = (bf16[128,512]{1,0:T(8,128)(2,1)S(1)}, bf16[128,512]{1,0:T(8,128)(2,1)S(1)}, u32[]{:S(2)}, u32[]{:S(2)}) collective-permute-start(bf16[128,512]{1,0:T(8,128)(2,1)S(1)} %get-tuple-element.91), channel_id=1, source_target_pairs={{0,1},{1,2},{2,3},{3,0},{4,5},{5,6},{6,7},{7,4},{8,9},{9,10},{10,1... | collective-permute-start | bytes 393224 | tf_op jit(solution)/shard_map/ppermute | solution.py:371
  87.0 8.7 %collective-permute-start.21 = (bf16[128,512]{1,0:T(8,128)(2,1)S(1)}, bf16[128,512]{1,0:T(8,128)(2,1)S(1)}, u32[]{:S(2)}, u32[]{:S(2)}) collective-permute-start(bf16[128,512]{1,0:T(8,128)(2,1)S(1)} %get-tuple-element.92), channel_id=1, source_target_pairs={{0,2},{1,3},{2,0},{3,1},{4,6},{5,7},{6,4},{7,5},{8,10},{9,11},{10,... | collective-permute-start | bytes 393224 | tf_op jit(solution)/shard_map/ppermute | solution.py:371
  87.0 8.7 %collective-permute-start.22 = (bf16[128,512]{1,0:T(8,128)(2,1)S(1)}, bf16[128,512]{1,0:T(8,128)(2,1)S(1)}, u32[]{:S(2)}, u32[]{:S(2)}) collective-permute-start(bf16[128,512]{1,0:T(8,128)(2,1)S(1)} %get-tuple-element.93), channel_id=1, source_target_pairs={{0,3},{1,0},{2,1},{3,2},{4,7},{5,4},{6,5},{7,6},{8,11},{9,8},{10,9... | collective-permute-start | bytes 393224 | tf_op jit(solution)/shard_map/ppermute | solution.py:371
  96.0 1.3 %collective-permute-start.23 = (bf16[64,512]{1,0:T(8,128)(2,1)S(1)}, bf16[64,512]{1,0:T(8,128)(2,1)S(1)}, u32[]{:S(2)}, u32[]{:S(2)}) collective-permute-start(bf16[64,512]{1,0:T(8,128)(2,1)S(1)} %get-tuple-element.101), channel_id=1, source_target_pairs={{0,4},{4,0},{8,12},{12,8},{16,20},{20,16},{24,28},{28,24},{1,5},{5... | collective-permute-start | bytes 196616 | tf_op jit(solution)/shard_map/ppermute | solution.py:388
  97.3 5.4 %collective-permute-start.24 = (bf16[32,512]{1,0:T(8,128)(2,1)S(1)}, bf16[32,512]{1,0:T(8,128)(2,1)S(1)}, u32[]{:S(2)}, u32[]{:S(2)}) collective-permute-start(bf16[32,512]{1,0:T(8,128)(2,1)S(1)} %get-tuple-element.103), channel_id=1, source_target_pairs={{0,8},{4,12},{8,16},{12,20},{16,24},{20,28},{24,0},{28,4},{1,9},{5... | collective-permute-start | bytes 98312 | tf_op jit(solution)/shard_map/ppermute | solution.py:371
  99.2 3.9 %collective-permute-start.26 = (bf16[32,512]{1,0:T(8,128)(2,1)S(1)}, bf16[32,512]{1,0:T(8,128)(2,1)S(1)}, u32[]{:S(2)}, u32[]{:S(2)}) collective-permute-start(bf16[32,512]{1,0:T(8,128)(2,1)S(1)} %get-tuple-element.104), channel_id=1, source_target_pairs={{0,24},{4,28},{8,0},{12,4},{16,8},{20,12},{24,16},{28,20},{1,25},{... | collective-permute-start | bytes 98312 | tf_op jit(solution)/shard_map/ppermute | solution.py:371
  100.3 3.9 %collective-permute-start.25 = (bf16[32,512]{1,0:T(8,128)(2,1)S(1)}, bf16[32,512]{1,0:T(8,128)(2,1)S(1)}, u32[]{:S(2)}, u32[]{:S(2)}) collective-permute-start(bf16[32,512]{1,0:T(8,128)(2,1)S(1)} %get-tuple-element.105), channel_id=1, source_target_pairs={{0,16},{4,20},{8,24},{12,28},{16,0},{20,4},{24,8},{28,12},{1,17},{... | collective-permute-start | bytes 98312 | tf_op jit(solution)/shard_map/ppermute | solution.py:371
  (5 other events, 47.5 us)

commit v16 on v15

--- a/solution.py
+++ b/solution.py
@@ -472,8 +472,9 @@
     parts[2:] = [shift(part, "head", step) for step, part in enumerate(parts[2:], 2)]
     kept, parts[1] = lax.optimization_barrier((kept, parts[1]))
     own_heads, other_heads = attend(depth, seq.reshape(1), twin_ids("seq"), global_scale, kept, received, pieces)
-    other_heads, parts[2:] = lax.optimization_barrier((swap_cores(other_heads, "seq"), parts[2:]))
+    other_heads, parts[2] = lax.optimization_barrier((swap_cores(other_heads, "seq"), parts[2]))
     updates = scatter(project(core, slots, own_heads, other_heads, global_out), "head")
+    updates, parts[3:] = lax.optimization_barrier((updates, parts[3:]))
     result, kept, given = finish_result(owner_order(owners, seq, patches), residual, updates)
     global_state = route(kept, given, "seq")
     byte_out = finish_bytes(result, back_proj, [early] + parts)

time: 107 us -> 106 us (level)
  transfers between devices with their start and end apart: 27 -> 27, of which waited for: 12 -> 11; matrix products, arithmetic and copies ran while one was open for 2% -> 2% of each run, Pallas kernels for 15% -> 16%
where the time goes in v16:
time: 106 us; the launch traced here: 105 us
  starting transfers between devices  41.4 us (39%)
  waiting for transfers between devices  30.2 us (28%)
  Pallas kernels  29.8 us (28%)
  local copies, waits for them, and re-layouts  1.75 us (2%)
  other arithmetic  1.12 us (1%)
    ppermute x24, starting transfers between devices, shift(): lax.ppermute(value, axis, [(i, (i + step) % count) for i in range(count)])  41.2 us
    ppermute x24, waiting for transfers between devices, shift(): lax.ppermute(value, axis, [(i, (i + step) % count) for i in range(count)])  27.7 us
    pallas_call x2, Pallas kernels, local_part(): pl.pallas_call(functools.partial(local_kernel, span, ways, piece, last),...  20.2 us
    pallas_call x1, Pallas kernels, fetch(): pl.pallas_call(fetch_kernel, in_specs=[HBM], out_specs=VMEM, out_shape=pl...  2.89 us
    ppermute x3, waiting for transfers between devices, swap_cores(): lax.ppermute(value, axis, [(i, i ^ 1) for i in range(lax.axis_size(axis))])  2.48 us
  transfers between devices with their start and end apart: 27, of which 11 were waited for; matrix products, arithmetic and copies ran while one was open for 2% of the time, Pallas kernels for 16%

profile of v16, /device:TPU:0, one launch (start us, length us, event | category | flops | bytes accessed | tf_op | source)
XLA Modules:
  0.0 105.2 jit_solution(15197300747846583028)
XLA Ops:
  0.6 10.1 %local_part.2 = (bf16[128,1024]{1,0:T(8,128)(2,1)}, bf16[128,1024]{1,0:T(8,128)(2,1)}, bf16[128,1024]{1,0:T(8,128)(2,1)}, bf16[128,1024]{1,0:T(8,128)(2,1)}) custom-call(f32[2]{0:T(128)} %scale_ref.4, f32[1,1024]{1,0:T(1,128)} %bitcast.33, bf16[1024,1024]{1,0:T(8,128)(2,1)} %bitcast.29, bf16[3,1024,256]{2,1,0:T(8,128)(2,1)} %bitcast.31, ...), custom_call_target="tpu_custom_call" | custom-call | flops 4294967296 | bytes 10485760 | tf_op jit(solution)/shard_map/local_part/pallas_call | solution.py:117
  10.7 3.1 %collective-permute-start = (bf16[128,1024]{1,0:T(8,128)(2,1)}, bf16[128,1024]{1,0:T(8,128)(2,1)S(1)}, u32[]{:S(2)}, u32[]{:S(2)}) collective-permute-start(bf16[128,1024]{1,0:T(8,128)(2,1)} %get-tuple-element.61), channel_id=1, source_target_pairs={{0,1},{1,2},{2,3},{3,0},{4,5},{5,6},{6,7},{7,4},{8,9},{9,10},{10,1... | collective-permute-start | bytes 786440 | tf_op jit(solution)/shard_map/ppermute | solution.py:371
  13.8 2.6 %collective-permute-start.1 = (bf16[128,1024]{1,0:T(8,128)(2,1)}, bf16[128,1024]{1,0:T(8,128)(2,1)S(1)}, u32[]{:S(2)}, u32[]{:S(2)}) collective-permute-start(bf16[128,1024]{1,0:T(8,128)(2,1)} %get-tuple-element.63), channel_id=1, source_target_pairs={{0,2},{1,3},{2,0},{3,1},{4,6},{5,7},{6,4},{7,5},{8,10},{9,11},{10,... | collective-permute-start | bytes 786440 | tf_op jit(solution)/shard_map/ppermute | solution.py:371
  16.4 1.3 %collective-permute-start.2 = (bf16[128,1024]{1,0:T(8,128)(2,1)}, bf16[128,1024]{1,0:T(8,128)(2,1)S(1)}, u32[]{:S(2)}, u32[]{:S(2)}) collective-permute-start(bf16[128,1024]{1,0:T(8,128)(2,1)} %get-tuple-element.64), channel_id=1, source_target_pairs={{0,3},{1,0},{2,1},{3,2},{4,7},{5,4},{6,5},{7,6},{8,11},{9,8},{10,9... | collective-permute-start | bytes 786440 | tf_op jit(solution)/shard_map/ppermute | solution.py:371
  17.8 10.1 %local_part.3 = (bf16[128,1024]{1,0:T(8,128)(2,1)}, bf16[128,1024]{1,0:T(8,128)(2,1)}, bf16[128,1024]{1,0:T(8,128)(2,1)}, bf16[128,1024]{1,0:T(8,128)(2,1)}, bf1...) custom-call(f32[2]{0:T(128)} %scale_ref.4, ...), custom_call_target="tpu_custom_call" | custom-call | flops 4294967296 | bytes 10485760 | tf_op jit(solution)/shard_map/local_part/pallas_call | solution.py:117
  28.8 6.2 %collective-permute-start.3 = (bf16[64,512]{1,0:T(8,128)(2,1)S(1)}, bf16[64,512]{1,0:T(8,128)(2,1)S(1)}, u32[]{:S(2)}, u32[]{:S(2)}) collective-permute-start(bf16[64,512]{1,0:T(8,128)(2,1)S(1)} %get-tuple-element.67), channel_id=1, source_target_pairs={{0,1},{1,2},{2,3},{3,0},{4,5},{5,6},{6,7},{7,4},{8,9},{9,10},{10,1... | collective-permute-start | bytes 196616 | tf_op jit(solution)/shard_map/ppermute | solution.py:371
  35.0 2.0 %collective-permute-start.4 = (bf16[64,512]{1,0:T(8,128)(2,1)S(1)}, bf16[64,512]{1,0:T(8,128)(2,1)S(1)}, u32[]{:S(2)}, u32[]{:S(2)}) collective-permute-start(bf16[64,512]{1,0:T(8,128)(2,1)S(1)} %get-tuple-element.68), channel_id=1, source_target_pairs={{0,2},{1,3},{2,0},{3,1},{4,6},{5,7},{6,4},{7,5},{8,10},{9,11},{10,... | collective-permute-start | bytes 196616 | tf_op jit(solution)/shard_map/ppermute | solution.py:371
  36.9 2.9 %collective-permute-start.5 = (bf16[64,512]{1,0:T(8,128)(2,1)S(1)}, bf16[64,512]{1,0:T(8,128)(2,1)S(1)}, u32[]{:S(2)}, u32[]{:S(2)}) collective-permute-start(bf16[64,512]{1,0:T(8,128)(2,1)S(1)} %get-tuple-element.69), channel_id=1, source_target_pairs={{0,3},{1,0},{2,1},{3,2},{4,7},{5,4},{6,5},{7,6},{8,11},{9,8},{10,9... | collective-permute-start | bytes 196616 | tf_op jit(solution)/shard_map/ppermute | solution.py:371
  40.9 3.6 %collective-permute-start.8 = (bf16[64,512]{1,0:T(8,128)(2,1)S(1)}, bf16[64,512]{1,0:T(8,128)(2,1)S(1)}, u32[]{:S(2)}, u32[]{:S(2)}) collective-permute-start(bf16[64,512]{1,0:T(8,128)(2,1)S(1)} %get-tuple-element.73.refs_0_), channel_id=1, source_target_pairs={{0,3},{1,0},{2,1},{3,2},{4,7},{5,4},{6,5},{7,6},{8,11},{9,8},{10,9... | collective-permute-start | bytes 196616 | tf_op jit(solution)/shard_map/ppermute | solution.py:371
  45.2 3.3 %collective-permute-start.11 = (bf16[64,512]{1,0:T(8,128)(2,1)S(1)}, bf16[64,512]{1,0:T(8,128)(2,1)S(1)}, u32[]{:S(2)}, u32[]{:S(2)}) collective-permute-start(bf16[64,512]{1,0:T(8,128)(2,1)S(1)} %add_convert_fusion.refs_4_), channel_id=1, source_target_pairs={{0,3},{1,0},{2,1},{3,2},{4,7},{5,4},{6,5},{7,6},{8,11},{9,8},{10,9... | collective-permute-start | bytes 196616 | tf_op jit(solution)/shard_map/ppermute | solution.py:371
  48.5 1.1 %collective-permute-start.10 = (bf16[64,512]{1,0:T(8,128)(2,1)S(1)}, bf16[64,512]{1,0:T(8,128)(2,1)S(1)}, u32[]{:S(2)}, u32[]{:S(2)}) collective-permute-start(bf16[64,512]{1,0:T(8,128)(2,1)S(1)} %add_convert_fusion.refs_4_), channel_id=1, source_target_pairs={{0,2},{1,3},{2,0},{3,1},{4,6},{5,7},{6,4},{7,5},{8,10},{9,11},{10,... | collective-permute-start | bytes 196616 | tf_op jit(solution)/shard_map/ppermute | solution.py:371
  49.6 2.9 %fetch.1.refs_8_ = bf16[3,2048,512]{2,1,0:T(8,128)(2,1)S(1)} custom-call(bf16[3,2048,512]{2,1,0:T(8,128)(2,1)} %bitcast.27), custom_call_target="tpu_custom_call" | custom-call | tf_op jit(solution)/shard_map/fetch/pallas_call | solution.py:173
  52.5 0.7 collective-permute-done.7.refs_2_
  53.2 2.9 %collective-permute-done.10.refs_6_ = bf16[64,512]{1,0:T(8,128)(2,1)S(1)} collective-permute-done((bf16[64,512]{1,0:T(8,128)(2,1)S(1)}, bf16[64,512]{1,0:T(8,128)(2,1)S(1)}, u32[]{:S(2)}, u32[]{:S(2)}) %collective-permute-start.10) | collective-permute-done | bytes 65568 | tf_op jit(solution)/shard_map/ppermute | solution.py:371
  56.2 1.7 %global_heads.1 = (bf16[128,768]{1,0:T(8,128)(2,1)S(1)}, bf16[128,768]{1,0:T(8,128)(2,1)S(1)}) custom-call(s32[1]{0:T(128)} %bitcast.7.core_ref, s32[4]{0:T(128)S(1)} %and_select_fusion.ids_ref, f32[4,1,512]{2,1,0:T(1,128)S(1)} %bitcast.26, bf16[64,512]{1,0:T(8,128)(2,1)S(1)} %get-tuple-element.73.refs_0_, ...), custom_call_target="tpu_custom_call" | custom-call | tf_op jit(solution)/shard_map/global_heads/pallas_call | solution.py:207
  58.2 1.2 %collective-permute-done.13.given_ref = bf16[128,768]{1,0:T(8,128)(2,1)S(1)} collective-permute-done((bf16[128,768]{1,0:T(8,128)(2,1)S(1)}, bf16[128,768]{1,0:T(8,128)(2,1)S(1)}, u32[]{:S(2)}, u32[]{:S(2)}) %collective-permute-start.13) | collective-permute-done | bytes 196640 | tf_op jit(solution)/shard_map/ppermute | solution.py:388
  59.4 2.5 %collective-permute-start.16 = (bf16[256,512]{1,0:T(8,128)(2,1)S(1)}, bf16[256,512]{1,0:T(8,128)(2,1)S(1)}, u32[]{:S(2)}, u32[]{:S(2)}) collective-permute-start(bf16[256,512]{1,0:T(8,128)(2,1)S(1)} %pad_maximum_fusion), channel_id=1, source_target_pairs={{0,24},{4,28},{8,0},{12,4},{16,8},{20,12},{24,16},{28,20},{1,25},{... | collective-permute-start | bytes 786440 | tf_op jit(solution)/shard_map/ppermute | solution.py:371
  63.7 5.4 %collective-permute-done.12.refs_2_ = bf16[128,1024]{1,0:T(8,128)(2,1)S(1)} collective-permute-done((bf16[128,1024]{1,0:T(8,128)(2,1)S(1)}, bf16[128,1024]{1,0:T(8,128)(2,1)S(1)}, u32[]{:S(2)}, u32[]{:S(2)}) %collective-permute-start.12) | collective-permute-done | bytes 262176 | tf_op jit(solution)/shard_map/ppermute | solution.py:371
  69.1 6.4 %collective-permute-done.15.refs_1_ = bf16[256,512]{1,0:T(8,128)(2,1)S(1)} collective-permute-done((bf16[256,512]{1,0:T(8,128)(2,1)S(1)}, bf16[256,512]{1,0:T(8,128)(2,1)S(1)}, u32[]{:S(2)}, u32[]{:S(2)}) %collective-permute-start.15) | collective-permute-done | bytes 262176 | tf_op jit(solution)/shard_map/ppermute | solution.py:371
  75.6 1.7 %attend.1 = (bf16[128,256]{1,0:T(8,128)(2,1)S(1)}, bf16[128,256]{1,0:T(8,128)(2,1)S(1)}) custom-call(s32[1]{0:T(128)} %bitcast.8.me_ref, s32[4]{0:T(128)S(1)} %and_select_fusion.1.ids_ref, f32[4]{0:T(128)S(1)} %copy-done.6, bf16[128,768]{1,0:T(8,128)(2,1)S(1)} %get-tuple-element.84.kept_ref, bf16[128,768]{1,0:T(8,128)(2,1)S(1)} %collective-permute-done.13.given_ref, ...), custom_call_target="tpu_custom_call" | custom-call | flops 1 | bytes 1 | tf_op jit(solution)/shard_map/attend/pallas_call | solution.py:250
  77.4 2.7 %collective-permute-start.22 = (bf16[128,1024]{1,0:T(8,128)(2,1)S(1)}, bf16[128,1024]{1,0:T(8,128)(2,1)S(1)}, u32[]{:S(2)}, u32[]{:S(2)}) collective-permute-start(bf16[128,1024]{1,0:T(8,128)(2,1)S(1)} %copy-done.7), channel_id=1, source_target_pairs={{0,3},{1,0},{2,1},{3,2},{4,7},{5,4},{6,5},{7,6},{8,11},{9,8},{10,9... | collective-permute-start | bytes 786440 | tf_op jit(solution)/shard_map/ppermute | solution.py:371
  80.2 1.0 project.1
  81.2 1.7 %collective-permute-start.20 = (bf16[128,512]{1,0:T(8,128)(2,1)S(1)}, bf16[128,512]{1,0:T(8,128)(2,1)S(1)}, u32[]{:S(2)}, u32[]{:S(2)}) collective-permute-start(bf16[128,512]{1,0:T(8,128)(2,1)S(1)} %get-tuple-element.95), channel_id=1, source_target_pairs={{0,2},{1,3},{2,0},{3,1},{4,6},{5,7},{6,4},{7,5},{8,10},{9,11},{10,... | collective-permute-start | bytes 393224 | tf_op jit(solution)/shard_map/ppermute | solution.py:371
  82.9 2.1 %collective-permute-start.21 = (bf16[128,512]{1,0:T(8,128)(2,1)S(1)}, bf16[128,512]{1,0:T(8,128)(2,1)S(1)}, u32[]{:S(2)}, u32[]{:S(2)}) collective-permute-start(bf16[128,512]{1,0:T(8,128)(2,1)S(1)} %get-tuple-element.96), channel_id=1, source_target_pairs={{0,3},{1,0},{2,1},{3,2},{4,7},{5,4},{6,5},{7,6},{8,11},{9,8},{10,9... | collective-permute-start | bytes 393224 | tf_op jit(solution)/shard_map/ppermute | solution.py:371
  85.1 5.7 %collective-permute-done.22.refs_4_ = bf16[128,1024]{1,0:T(8,128)(2,1)S(1)} collective-permute-done((bf16[128,1024]{1,0:T(8,128)(2,1)S(1)}, bf16[128,1024]{1,0:T(8,128)(2,1)S(1)}, u32[]{:S(2)}, u32[]{:S(2)}) %collective-permute-start.22) | collective-permute-done | bytes 262176 | tf_op jit(solution)/shard_map/ppermute | solution.py:371
  90.8 3.8 %collective-permute-done.20.refs_2_ = bf16[128,512]{1,0:T(8,128)(2,1)S(1)} collective-permute-done((bf16[128,512]{1,0:T(8,128)(2,1)S(1)}, bf16[128,512]{1,0:T(8,128)(2,1)S(1)}, u32[]{:S(2)}, u32[]{:S(2)}) %collective-permute-start.20) | collective-permute-done | bytes 131104 | tf_op jit(solution)/shard_map/ppermute | solution.py:371
  95.3 1.2 %collective-permute-done.23 = bf16[64,512]{1,0:T(8,128)(2,1)S(1)} collective-permute-done((bf16[64,512]{1,0:T(8,128)(2,1)S(1)}, bf16[64,512]{1,0:T(8,128)(2,1)S(1)}, u32[]{:S(2)}, u32[]{:S(2)}) %collective-permute-start.23) | collective-permute-done | bytes 65568 | tf_op jit(solution)/shard_map/ppermute | solution.py:388
  97.2 2.3 %collective-permute-start.26 = (bf16[32,512]{1,0:T(8,128)(2,1)S(1)}, bf16[32,512]{1,0:T(8,128)(2,1)S(1)}, u32[]{:S(2)}, u32[]{:S(2)}) collective-permute-start(bf16[32,512]{1,0:T(8,128)(2,1)S(1)} %get-tuple-element.112), channel_id=1, source_target_pairs={{0,24},{4,28},{8,0},{12,4},{16,8},{20,12},{24,16},{28,20},{1,25},{... | collective-permute-start | bytes 98312 | tf_op jit(solution)/shard_map/ppermute | solution.py:371
  100.1 0.9 finish_bytes.1
  101.4 2.0 %collective-permute-done.25 = bf16[32,512]{1,0:T(8,128)(2,1)S(1)} collective-permute-done((bf16[32,512]{1,0:T(8,128)(2,1)S(1)}, bf16[32,512]{1,0:T(8,128)(2,1)S(1)}, u32[]{:S(2)}, u32[]{:S(2)}) %collective-permute-start.25) | collective-permute-done | bytes 32800 | tf_op jit(solution)/shard_map/ppermute | solution.py:371
  103.4 1.0 reshape.86
  104.4 0.8 sort_rows.1
  (70 shorter events, 7.2 us)
Async XLA Ops:
  10.7 18.0 %collective-permute-start = (bf16[128,1024]{1,0:T(8,128)(2,1)}, bf16[128,1024]{1,0:T(8,128)(2,1)S(1)}, u32[]{:S(2)}, u32[]{:S(2)}) collective-permute-start(bf16[128,1024]{1,0:T(8,128)(2,1)} %get-tuple-element.61), channel_id=1, source_target_pairs={{0,1},{1,2},{2,3},{3,0},{4,5},{5,6},{6,7},{7,4},{8,9},{9,10},{10,1... | collective-permute-start | bytes 786440 | tf_op jit(solution)/shard_map/ppermute | solution.py:371
  13.8 26.7 %collective-permute-start.1 = (bf16[128,1024]{1,0:T(8,128)(2,1)}, bf16[128,1024]{1,0:T(8,128)(2,1)S(1)}, u32[]{:S(2)}, u32[]{:S(2)}) collective-permute-start(bf16[128,1024]{1,0:T(8,128)(2,1)} %get-tuple-element.63), channel_id=1, source_target_pairs={{0,2},{1,3},{2,0},{3,1},{4,6},{5,7},{6,4},{7,5},{8,10},{9,11},{10,... | collective-permute-start | bytes 786440 | tf_op jit(solution)/shard_map/ppermute | solution.py:371
  16.4 24.2 %copy-start.1 = (bf16[1024,256]{1,0:T(8,128)(2,1)S(1)}, bf16[1024,256]{1,0:T(8,128)(2,1)}, u32[]{:S(2)}) copy-start(bf16[1024,256]{1,0:T(8,128)(2,1)} %proj_ref.3) | copy-start | bytes 1572868
  16.4 24.2 %copy-start.4 = (bf16[128,1024]{1,0:T(8,128)(2,1)S(1)}, bf16[128,1024]{1,0:T(8,128)(2,1)}, u32[]{:S(2)}) copy-start(bf16[128,1024]{1,0:T(8,128)(2,1)} %get-tuple-element.56.refs_0_) | copy-start | bytes 786436
  16.4 24.1 %collective-permute-start.2 = (bf16[128,1024]{1,0:T(8,128)(2,1)}, bf16[128,1024]{1,0:T(8,128)(2,1)S(1)}, u32[]{:S(2)}, u32[]{:S(2)}) collective-permute-start(bf16[128,1024]{1,0:T(8,128)(2,1)} %get-tuple-element.64), channel_id=1, source_target_pairs={{0,3},{1,0},{2,1},{3,2},{4,7},{5,4},{6,5},{7,6},{8,11},{9,8},{10,9... | collective-permute-start | bytes 786440 | tf_op jit(solution)/shard_map/ppermute | solution.py:371
  28.8 15.8 %collective-permute-start.3 = (bf16[64,512]{1,0:T(8,128)(2,1)S(1)}, bf16[64,512]{1,0:T(8,128)(2,1)S(1)}, u32[]{:S(2)}, u32[]{:S(2)}) collective-permute-start(bf16[64,512]{1,0:T(8,128)(2,1)S(1)} %get-tuple-element.67), channel_id=1, source_target_pairs={{0,1},{1,2},{2,3},{3,0},{4,5},{5,6},{6,7},{7,4},{8,9},{9,10},{10,1... | collective-permute-start | bytes 196616 | tf_op jit(solution)/shard_map/ppermute | solution.py:371
  35.0 10.2 %collective-permute-start.4 = (bf16[64,512]{1,0:T(8,128)(2,1)S(1)}, bf16[64,512]{1,0:T(8,128)(2,1)S(1)}, u32[]{:S(2)}, u32[]{:S(2)}) collective-permute-start(bf16[64,512]{1,0:T(8,128)(2,1)S(1)} %get-tuple-element.68), channel_id=1, source_target_pairs={{0,2},{1,3},{2,0},{3,1},{4,6},{5,7},{6,4},{7,5},{8,10},{9,11},{10,... | collective-permute-start | bytes 196616 | tf_op jit(solution)/shard_map/ppermute | solution.py:371
  36.9 8.2 %collective-permute-start.5 = (bf16[64,512]{1,0:T(8,128)(2,1)S(1)}, bf16[64,512]{1,0:T(8,128)(2,1)S(1)}, u32[]{:S(2)}, u32[]{:S(2)}) collective-permute-start(bf16[64,512]{1,0:T(8,128)(2,1)S(1)} %get-tuple-element.69), channel_id=1, source_target_pairs={{0,3},{1,0},{2,1},{3,2},{4,7},{5,4},{6,5},{7,6},{8,11},{9,8},{10,9... | collective-permute-start | bytes 196616 | tf_op jit(solution)/shard_map/ppermute | solution.py:371
  40.9 8.7 %collective-permute-start.8 = (bf16[64,512]{1,0:T(8,128)(2,1)S(1)}, bf16[64,512]{1,0:T(8,128)(2,1)S(1)}, u32[]{:S(2)}, u32[]{:S(2)}) collective-permute-start(bf16[64,512]{1,0:T(8,128)(2,1)S(1)} %get-tuple-element.73.refs_0_), channel_id=1, source_target_pairs={{0,3},{1,0},{2,1},{3,2},{4,7},{5,4},{6,5},{7,6},{8,11},{9,8},{10,9... | collective-permute-start | bytes 196616 | tf_op jit(solution)/shard_map/ppermute | solution.py:371
  44.5 8.7 %collective-permute-start.7 = (bf16[64,512]{1,0:T(8,128)(2,1)S(1)}, bf16[64,512]{1,0:T(8,128)(2,1)S(1)}, u32[]{:S(2)}, u32[]{:S(2)}) collective-permute-start(bf16[64,512]{1,0:T(8,128)(2,1)S(1)} %get-tuple-element.73.refs_0_), channel_id=1, source_target_pairs={{0,2},{1,3},{2,0},{3,1},{4,6},{5,7},{6,4},{7,5},{8,10},{9,11},{10,... | collective-permute-start | bytes 196616 | tf_op jit(solution)/shard_map/ppermute | solution.py:371
  44.6 8.7 %collective-permute-start.6 = (bf16[64,512]{1,0:T(8,128)(2,1)S(1)}, bf16[64,512]{1,0:T(8,128)(2,1)S(1)}, u32[]{:S(2)}, u32[]{:S(2)}) collective-permute-start(bf16[64,512]{1,0:T(8,128)(2,1)S(1)} %get-tuple-element.73.refs_0_), channel_id=1, source_target_pairs={{0,1},{1,2},{2,3},{3,0},{4,5},{5,6},{6,7},{7,4},{8,9},{9,10},{10,1... | collective-permute-start | bytes 196616 | tf_op jit(solution)/shard_map/ppermute | solution.py:371
  45.2 8.0 %collective-permute-start.11 = (bf16[64,512]{1,0:T(8,128)(2,1)S(1)}, bf16[64,512]{1,0:T(8,128)(2,1)S(1)}, u32[]{:S(2)}, u32[]{:S(2)}) collective-permute-start(bf16[64,512]{1,0:T(8,128)(2,1)S(1)} %add_convert_fusion.refs_4_), channel_id=1, source_target_pairs={{0,3},{1,0},{2,1},{3,2},{4,7},{5,4},{6,5},{7,6},{8,11},{9,8},{10,9... | collective-permute-start | bytes 196616 | tf_op jit(solution)/shard_map/ppermute | solution.py:371
  48.5 7.6 %collective-permute-start.10 = (bf16[64,512]{1,0:T(8,128)(2,1)S(1)}, bf16[64,512]{1,0:T(8,128)(2,1)S(1)}, u32[]{:S(2)}, u32[]{:S(2)}) collective-permute-start(bf16[64,512]{1,0:T(8,128)(2,1)S(1)} %add_convert_fusion.refs_4_), channel_id=1, source_target_pairs={{0,2},{1,3},{2,0},{3,1},{4,6},{5,7},{6,4},{7,5},{8,10},{9,11},{10,... | collective-permute-start | bytes 196616 | tf_op jit(solution)/shard_map/ppermute | solution.py:371
  49.6 6.6 %collective-permute-start.9 = (bf16[64,512]{1,0:T(8,128)(2,1)S(1)}, bf16[64,512]{1,0:T(8,128)(2,1)S(1)}, u32[]{:S(2)}, u32[]{:S(2)}) collective-permute-start(bf16[64,512]{1,0:T(8,128)(2,1)S(1)} %add_convert_fusion.refs_4_), channel_id=1, source_target_pairs={{0,1},{1,2},{2,3},{3,0},{4,5},{5,6},{6,7},{7,4},{8,9},{9,10},{10,1... | collective-permute-start | bytes 196616 | tf_op jit(solution)/shard_map/ppermute | solution.py:371
  57.9 22.3 %copy-start = (bf16[512,2048]{1,0:T(8,128)(2,1)S(1)}, bf16[512,2048]{1,0:T(8,128)(2,1)}, u32[]{:S(2)}) copy-start(bf16[512,2048]{1,0:T(8,128)(2,1)} %proj_ref.4) | copy-start | bytes 6291460
  57.9 1.5 %collective-permute-start.13 = (bf16[128,768]{1,0:T(8,128)(2,1)S(1)}, bf16[128,768]{1,0:T(8,128)(2,1)S(1)}, u32[]{:S(2)}, u32[]{:S(2)}) collective-permute-start(bf16[128,768]{1,0:T(8,128)(2,1)S(1)} %get-tuple-element.85), channel_id=1, source_target_pairs={{0,4},{4,0},{8,12},{12,8},{16,20},{20,16},{24,28},{28,24},{1,5},{5... | collective-permute-start | bytes 589832 | tf_op jit(solution)/shard_map/ppermute | solution.py:388
  58.1 11.1 %collective-permute-start.12 = (bf16[128,1024]{1,0:T(8,128)(2,1)S(1)}, bf16[128,1024]{1,0:T(8,128)(2,1)S(1)}, u32[]{:S(2)}, u32[]{:S(2)}) collective-permute-start(bf16[128,1024]{1,0:T(8,128)(2,1)S(1)} %copy-done.9), channel_id=1, source_target_pairs={{0,1},{1,2},{2,3},{3,0},{4,5},{5,6},{6,7},{7,4},{8,9},{9,10},{10,1... | collective-permute-start | bytes 786440 | tf_op jit(solution)/shard_map/ppermute | solution.py:371
  59.4 9.7 %collective-permute-start.16 = (bf16[256,512]{1,0:T(8,128)(2,1)S(1)}, bf16[256,512]{1,0:T(8,128)(2,1)S(1)}, u32[]{:S(2)}, u32[]{:S(2)}) collective-permute-start(bf16[256,512]{1,0:T(8,128)(2,1)S(1)} %pad_maximum_fusion), channel_id=1, source_target_pairs={{0,24},{4,28},{8,0},{12,4},{16,8},{20,12},{24,16},{28,20},{1,25},{... | collective-permute-start | bytes 786440 | tf_op jit(solution)/shard_map/ppermute | solution.py:371
  61.9 13.7 %collective-permute-start.15 = (bf16[256,512]{1,0:T(8,128)(2,1)S(1)}, bf16[256,512]{1,0:T(8,128)(2,1)S(1)}, u32[]{:S(2)}, u32[]{:S(2)}) collective-permute-start(bf16[256,512]{1,0:T(8,128)(2,1)S(1)} %pad_maximum_fusion), channel_id=1, source_target_pairs={{0,16},{4,20},{8,24},{12,28},{16,0},{20,4},{24,8},{28,12},{1,17},{... | collective-permute-start | bytes 786440 | tf_op jit(solution)/shard_map/ppermute | solution.py:371
  62.4 13.2 %collective-permute-start.14 = (bf16[256,512]{1,0:T(8,128)(2,1)S(1)}, bf16[256,512]{1,0:T(8,128)(2,1)S(1)}, u32[]{:S(2)}, u32[]{:S(2)}) collective-permute-start(bf16[256,512]{1,0:T(8,128)(2,1)S(1)} %pad_maximum_fusion), channel_id=1, source_target_pairs={{0,8},{4,12},{8,16},{12,20},{16,24},{20,28},{24,0},{28,4},{1,9},{5... | collective-permute-start | bytes 786440 | tf_op jit(solution)/shard_map/ppermute | solution.py:371
  63.0 17.1 %collective-permute-start.18 = (bf16[128,1024]{1,0:T(8,128)(2,1)S(1)}, bf16[128,1024]{1,0:T(8,128)(2,1)S(1)}, u32[]{:S(2)}, u32[]{:S(2)}) collective-permute-start(bf16[128,1024]{1,0:T(8,128)(2,1)S(1)} %copy-done.8), channel_id=1, source_target_pairs={{0,2},{1,3},{2,0},{3,1},{4,6},{5,7},{6,4},{7,5},{8,10},{9,11},{10,... | collective-permute-start | bytes 786440 | tf_op jit(solution)/shard_map/ppermute | solution.py:371
  75.6 24.5 %copy-start.2 = (bf16[256,1024]{1,0:T(8,128)(2,1)S(1)}, bf16[256,1024]{1,0:T(8,128)(2,1)}, u32[]{:S(2)}) copy-start(bf16[256,1024]{1,0:T(8,128)(2,1)} %proj_ref.5) | copy-start | bytes 1572868
  75.6 24.5 %copy-start.3 = (bf16[128,1024]{1,0:T(8,128)(2,1)S(1)}, bf16[128,1024]{1,0:T(8,128)(2,1)}, u32[]{:S(2)}) copy-start(bf16[128,1024]{1,0:T(8,128)(2,1)} %get-tuple-element.104.refs_1_) | copy-start | bytes 786436
  77.3 2.8 %collective-permute-start.17 = (bf16[128,256]{1,0:T(8,128)(2,1)S(1)}, bf16[128,256]{1,0:T(8,128)(2,1)S(1)}, u32[]{:S(2)}, u32[]{:S(2)}) collective-permute-start(bf16[128,256]{1,0:T(8,128)(2,1)S(1)} %get-tuple-element.90), channel_id=1, source_target_pairs={{0,4},{4,0},{8,12},{12,8},{16,20},{20,16},{24,28},{28,24},{1,5},{5... | collective-permute-start | bytes 196616 | tf_op jit(solution)/shard_map/ppermute | solution.py:388
  77.4 13.3 %collective-permute-start.22 = (bf16[128,1024]{1,0:T(8,128)(2,1)S(1)}, bf16[128,1024]{1,0:T(8,128)(2,1)S(1)}, u32[]{:S(2)}, u32[]{:S(2)}) collective-permute-start(bf16[128,1024]{1,0:T(8,128)(2,1)S(1)} %copy-done.7), channel_id=1, source_target_pairs={{0,3},{1,0},{2,1},{3,2},{4,7},{5,4},{6,5},{7,6},{8,11},{9,8},{10,9... | collective-permute-start | bytes 786440 | tf_op jit(solution)/shard_map/ppermute | solution.py:371
  81.2 9.6 %collective-permute-start.19 = (bf16[128,512]{1,0:T(8,128)(2,1)S(1)}, bf16[128,512]{1,0:T(8,128)(2,1)S(1)}, u32[]{:S(2)}, u32[]{:S(2)}) collective-permute-start(bf16[128,512]{1,0:T(8,128)(2,1)S(1)} %get-tuple-element.94), channel_id=1, source_target_pairs={{0,1},{1,2},{2,3},{3,0},{4,5},{5,6},{6,7},{7,4},{8,9},{9,10},{10,1... | collective-permute-start | bytes 393224 | tf_op jit(solution)/shard_map/ppermute | solution.py:371
  81.2 13.4 %collective-permute-start.20 = (bf16[128,512]{1,0:T(8,128)(2,1)S(1)}, bf16[128,512]{1,0:T(8,128)(2,1)S(1)}, u32[]{:S(2)}, u32[]{:S(2)}) collective-permute-start(bf16[128,512]{1,0:T(8,128)(2,1)S(1)} %get-tuple-element.95), channel_id=1, source_target_pairs={{0,2},{1,3},{2,0},{3,1},{4,6},{5,7},{6,4},{7,5},{8,10},{9,11},{10,... | collective-permute-start | bytes 393224 | tf_op jit(solution)/shard_map/ppermute | solution.py:371
  82.9 12.0 %collective-permute-start.21 = (bf16[128,512]{1,0:T(8,128)(2,1)S(1)}, bf16[128,512]{1,0:T(8,128)(2,1)S(1)}, u32[]{:S(2)}, u32[]{:S(2)}) collective-permute-start(bf16[128,512]{1,0:T(8,128)(2,1)S(1)} %get-tuple-element.96), channel_id=1, source_target_pairs={{0,3},{1,0},{2,1},{3,2},{4,7},{5,4},{6,5},{7,6},{8,11},{9,8},{10,9... | collective-permute-start | bytes 393224 | tf_op jit(solution)/shard_map/ppermute | solution.py:371
  95.2 1.3 %collective-permute-start.23 = (bf16[64,512]{1,0:T(8,128)(2,1)S(1)}, bf16[64,512]{1,0:T(8,128)(2,1)S(1)}, u32[]{:S(2)}, u32[]{:S(2)}) collective-permute-start(bf16[64,512]{1,0:T(8,128)(2,1)S(1)} %get-tuple-element.109), channel_id=1, source_target_pairs={{0,4},{4,0},{8,12},{12,8},{16,20},{20,16},{24,28},{28,24},{1,5},{5... | collective-permute-start | bytes 196616 | tf_op jit(solution)/shard_map/ppermute | solution.py:388
  96.5 4.9 %collective-permute-start.24 = (bf16[32,512]{1,0:T(8,128)(2,1)S(1)}, bf16[32,512]{1,0:T(8,128)(2,1)S(1)}, u32[]{:S(2)}, u32[]{:S(2)}) collective-permute-start(bf16[32,512]{1,0:T(8,128)(2,1)S(1)} %get-tuple-element.111), channel_id=1, source_target_pairs={{0,8},{4,12},{8,16},{12,20},{16,24},{20,28},{24,0},{28,4},{1,9},{5... | collective-permute-start | bytes 98312 | tf_op jit(solution)/shard_map/ppermute | solution.py:371
  97.2 4.2 %collective-permute-start.26 = (bf16[32,512]{1,0:T(8,128)(2,1)S(1)}, bf16[32,512]{1,0:T(8,128)(2,1)S(1)}, u32[]{:S(2)}, u32[]{:S(2)}) collective-permute-start(bf16[32,512]{1,0:T(8,128)(2,1)S(1)} %get-tuple-element.112), channel_id=1, source_target_pairs={{0,24},{4,28},{8,0},{12,4},{16,8},{20,12},{24,16},{28,20},{1,25},{... | collective-permute-start | bytes 98312 | tf_op jit(solution)/shard_map/ppermute | solution.py:371
  99.5 3.9 %collective-permute-start.25 = (bf16[32,512]{1,0:T(8,128)(2,1)S(1)}, bf16[32,512]{1,0:T(8,128)(2,1)S(1)}, u32[]{:S(2)}, u32[]{:S(2)}) collective-permute-start(bf16[32,512]{1,0:T(8,128)(2,1)S(1)} %get-tuple-element.113), channel_id=1, source_target_pairs={{0,16},{4,20},{8,24},{12,28},{16,0},{20,4},{24,8},{28,12},{1,17},{... | collective-permute-start | bytes 98312 | tf_op jit(solution)/shard_map/ppermute | solution.py:371
  (5 other events, 56.0 us)

commit v17 on v16

--- a/solution.py
+++ b/solution.py
@@ -338,7 +338,7 @@
     rows = result_ref.shape[0]
     half = rows // 2
     width = proj_ref.shape[0]
-    own = out_ref.shape[0] // rows
+    own = out_ref.shape[1]
     back = [dot(result_ref[:, b * width : (b + 1) * width], proj_ref[...]) for b in range(own)]
     back = jnp.concatenate([b[:half] for b in back] + [b[half:] for b in back], axis=0)
     at = lax.broadcasted_iota(jnp.int32, (rows * own, rows * own), 0)
@@ -349,7 +349,7 @@
         copy.wait()
     late = sum(held[i].astype(F32) for i in range(1, count)).astype(BF16)
     state = jnp.concatenate([held[0], late], axis=0).astype(F32)
-    out_ref[...] = dot(order, (state + back).astype(BF16)).astype(BF16)
+    out_ref[...] = dot(order, (state + back).astype(BF16)).reshape(out_ref.shape).astype(BF16)
 
 
 def finish_bytes(result, proj, pieces):
@@ -358,7 +358,7 @@
         functools.partial(bytes_kernel, len(pieces)),
         in_specs=[VMEM, VMEM] + [pl.BlockSpec(memory_space=pl.ANY)] * len(pieces),
         out_specs=VMEM,
-        out_shape=jax.ShapeDtypeStruct((2 * rows, width), BF16),
+        out_shape=jax.ShapeDtypeStruct((result.shape[0], 2 * rows // result.shape[0], width), BF16),
         scratch_shapes=[pltpu.VMEM((len(pieces), rows, width), BF16), pltpu.SemaphoreType.DMA((len(pieces),))],
         compiler_params=pltpu.CompilerParams(vmem_limit_bytes=16 * 2**20),
         cost_estimate=BRIEF,
@@ -478,7 +478,7 @@
     result, kept, given = finish_result(owner_order(owners, seq, patches), residual, updates)
     global_state = route(kept, given, "seq")
     byte_out = finish_bytes(result, back_proj, [early] + parts)
-    return byte_out.reshape(patches, own, width), global_state
+    return byte_out, global_state
 
 
 def solution(mesh):

time: 106 us -> 108 us (1.019)
  Pallas kernels: 29.8 us -> 31 us
    pallas_call x1, Pallas kernels: 0.92 us -> 2.06 us  [finish_bytes(): pl.pallas_call(functools.partial(bytes_kernel, len(pieces)), in_specs=[VM...]
  transfers between devices with their start and end apart: 27 -> 27, of which waited for: 11 -> 11; matrix products, arithmetic and copies ran while one was open for 2% -> 2% of each run, Pallas kernels for 16% -> 15%
where the time goes in v17:
time: 108 us; the launch traced here: 106 us
  starting transfers between devices  41.5 us (38%)
  Pallas kernels  31 us (29%)
  waiting for transfers between devices  31 us (29%)
  other arithmetic  1.12 us (1%)
    ppermute x24, starting transfers between devices, shift(): lax.ppermute(value, axis, [(i, (i + step) % count) for i in range(count)])  41.3 us
    ppermute x24, waiting for transfers between devices, shift(): lax.ppermute(value, axis, [(i, (i + step) % count) for i in range(count)])  28.6 us
    pallas_call x2, Pallas kernels, local_part(): pl.pallas_call(functools.partial(local_kernel, span, ways, piece, last),...  20.2 us
    pallas_call x1, Pallas kernels, fetch(): pl.pallas_call(fetch_kernel, in_specs=[HBM], out_specs=VMEM, out_shape=pl...  2.89 us
    ppermute x3, waiting for transfers between devices, swap_cores(): lax.ppermute(value, axis, [(i, i ^ 1) for i in range(lax.axis_size(axis))])  2.48 us
  transfers between devices with their start and end apart: 27, of which 11 were waited for; matrix products, arithmetic and copies ran while one was open for 2% of the time, Pallas kernels for 15%

profile of v17, /device:TPU:0, one launch (start us, length us, event | category | flops | bytes accessed | tf_op | source)
XLA Modules:
  0.0 106.3 jit_solution(10339041734232204007)
XLA Ops:
  0.6 10.1 %local_part.2 = (bf16[128,1024]{1,0:T(8,128)(2,1)}, bf16[128,1024]{1,0:T(8,128)(2,1)}, bf16[128,1024]{1,0:T(8,128)(2,1)}, bf16[128,1024]{1,0:T(8,128)(2,1)}) custom-call(f32[2]{0:T(128)} %scale_ref.4, f32[1,1024]{1,0:T(1,128)} %bitcast.33, bf16[1024,1024]{1,0:T(8,128)(2,1)} %bitcast.29, bf16[3,1024,256]{2,1,0:T(8,128)(2,1)} %bitcast.31, ...), custom_call_target="tpu_custom_call" | custom-call | flops 4294967296 | bytes 10485760 | tf_op jit(solution)/shard_map/local_part/pallas_call | solution.py:117
  10.7 3.1 %collective-permute-start = (bf16[128,1024]{1,0:T(8,128)(2,1)}, bf16[128,1024]{1,0:T(8,128)(2,1)S(1)}, u32[]{:S(2)}, u32[]{:S(2)}) collective-permute-start(bf16[128,1024]{1,0:T(8,128)(2,1)} %get-tuple-element.61), channel_id=1, source_target_pairs={{0,1},{1,2},{2,3},{3,0},{4,5},{5,6},{6,7},{7,4},{8,9},{9,10},{10,1... | collective-permute-start | bytes 786440 | tf_op jit(solution)/shard_map/ppermute | solution.py:371
  13.8 2.6 %collective-permute-start.1 = (bf16[128,1024]{1,0:T(8,128)(2,1)}, bf16[128,1024]{1,0:T(8,128)(2,1)S(1)}, u32[]{:S(2)}, u32[]{:S(2)}) collective-permute-start(bf16[128,1024]{1,0:T(8,128)(2,1)} %get-tuple-element.63), channel_id=1, source_target_pairs={{0,2},{1,3},{2,0},{3,1},{4,6},{5,7},{6,4},{7,5},{8,10},{9,11},{10,... | collective-permute-start | bytes 786440 | tf_op jit(solution)/shard_map/ppermute | solution.py:371
  16.4 1.3 %collective-permute-start.2 = (bf16[128,1024]{1,0:T(8,128)(2,1)}, bf16[128,1024]{1,0:T(8,128)(2,1)S(1)}, u32[]{:S(2)}, u32[]{:S(2)}) collective-permute-start(bf16[128,1024]{1,0:T(8,128)(2,1)} %get-tuple-element.64), channel_id=1, source_target_pairs={{0,3},{1,0},{2,1},{3,2},{4,7},{5,4},{6,5},{7,6},{8,11},{9,8},{10,9... | collective-permute-start | bytes 786440 | tf_op jit(solution)/shard_map/ppermute | solution.py:371
  17.8 10.1 %local_part.3 = (bf16[128,1024]{1,0:T(8,128)(2,1)}, bf16[128,1024]{1,0:T(8,128)(2,1)}, bf16[128,1024]{1,0:T(8,128)(2,1)}, bf16[128,1024]{1,0:T(8,128)(2,1)}, bf1...) custom-call(f32[2]{0:T(128)} %scale_ref.4, ...), custom_call_target="tpu_custom_call" | custom-call | flops 4294967296 | bytes 10485760 | tf_op jit(solution)/shard_map/local_part/pallas_call | solution.py:117
  28.8 6.2 %collective-permute-start.3 = (bf16[64,512]{1,0:T(8,128)(2,1)S(1)}, bf16[64,512]{1,0:T(8,128)(2,1)S(1)}, u32[]{:S(2)}, u32[]{:S(2)}) collective-permute-start(bf16[64,512]{1,0:T(8,128)(2,1)S(1)} %get-tuple-element.67), channel_id=1, source_target_pairs={{0,1},{1,2},{2,3},{3,0},{4,5},{5,6},{6,7},{7,4},{8,9},{9,10},{10,1... | collective-permute-start | bytes 196616 | tf_op jit(solution)/shard_map/ppermute | solution.py:371
  35.0 2.0 %collective-permute-start.4 = (bf16[64,512]{1,0:T(8,128)(2,1)S(1)}, bf16[64,512]{1,0:T(8,128)(2,1)S(1)}, u32[]{:S(2)}, u32[]{:S(2)}) collective-permute-start(bf16[64,512]{1,0:T(8,128)(2,1)S(1)} %get-tuple-element.68), channel_id=1, source_target_pairs={{0,2},{1,3},{2,0},{3,1},{4,6},{5,7},{6,4},{7,5},{8,10},{9,11},{10,... | collective-permute-start | bytes 196616 | tf_op jit(solution)/shard_map/ppermute | solution.py:371
  36.9 2.9 %collective-permute-start.5 = (bf16[64,512]{1,0:T(8,128)(2,1)S(1)}, bf16[64,512]{1,0:T(8,128)(2,1)S(1)}, u32[]{:S(2)}, u32[]{:S(2)}) collective-permute-start(bf16[64,512]{1,0:T(8,128)(2,1)S(1)} %get-tuple-element.69), channel_id=1, source_target_pairs={{0,3},{1,0},{2,1},{3,2},{4,7},{5,4},{6,5},{7,6},{8,11},{9,8},{10,9... | collective-permute-start | bytes 196616 | tf_op jit(solution)/shard_map/ppermute | solution.py:371
  40.9 3.6 %collective-permute-start.8 = (bf16[64,512]{1,0:T(8,128)(2,1)S(1)}, bf16[64,512]{1,0:T(8,128)(2,1)S(1)}, u32[]{:S(2)}, u32[]{:S(2)}) collective-permute-start(bf16[64,512]{1,0:T(8,128)(2,1)S(1)} %get-tuple-element.73.refs_0_), channel_id=1, source_target_pairs={{0,3},{1,0},{2,1},{3,2},{4,7},{5,4},{6,5},{7,6},{8,11},{9,8},{10,9... | collective-permute-start | bytes 196616 | tf_op jit(solution)/shard_map/ppermute | solution.py:371
  45.2 3.3 %collective-permute-start.11 = (bf16[64,512]{1,0:T(8,128)(2,1)S(1)}, bf16[64,512]{1,0:T(8,128)(2,1)S(1)}, u32[]{:S(2)}, u32[]{:S(2)}) collective-permute-start(bf16[64,512]{1,0:T(8,128)(2,1)S(1)} %add_convert_fusion.refs_4_), channel_id=1, source_target_pairs={{0,3},{1,0},{2,1},{3,2},{4,7},{5,4},{6,5},{7,6},{8,11},{9,8},{10,9... | collective-permute-start | bytes 196616 | tf_op jit(solution)/shard_map/ppermute | solution.py:371
  48.5 1.1 collective-permute-start.10
  49.6 2.9 %fetch.1.refs_8_ = bf16[3,2048,512]{2,1,0:T(8,128)(2,1)S(1)} custom-call(bf16[3,2048,512]{2,1,0:T(8,128)(2,1)} %bitcast.27), custom_call_target="tpu_custom_call" | custom-call | tf_op jit(solution)/shard_map/fetch/pallas_call | solution.py:173
  52.5 0.7 collective-permute-done.7.refs_2_
  53.2 2.9 %collective-permute-done.10.refs_6_ = bf16[64,512]{1,0:T(8,128)(2,1)S(1)} collective-permute-done((bf16[64,512]{1,0:T(8,128)(2,1)S(1)}, bf16[64,512]{1,0:T(8,128)(2,1)S(1)}, u32[]{:S(2)}, u32[]{:S(2)}) %collective-permute-start.10) | collective-permute-done | bytes 65568 | tf_op jit(solution)/shard_map/ppermute | solution.py:371
  56.2 1.7 %global_heads.1 = (bf16[128,768]{1,0:T(8,128)(2,1)S(1)}, bf16[128,768]{1,0:T(8,128)(2,1)S(1)}) custom-call(s32[1]{0:T(128)} %bitcast.7.core_ref, s32[4]{0:T(128)S(1)} %and_select_fusion.ids_ref, f32[4,1,512]{2,1,0:T(1,128)S(1)} %bitcast.26, bf16[64,512]{1,0:T(8,128)(2,1)S(1)} %get-tuple-element.73.refs_0_, ...), custom_call_target="tpu_custom_call" | custom-call | tf_op jit(solution)/shard_map/global_heads/pallas_call | solution.py:207
  58.2 1.2 %collective-permute-done.13.given_ref = bf16[128,768]{1,0:T(8,128)(2,1)S(1)} collective-permute-done((bf16[128,768]{1,0:T(8,128)(2,1)S(1)}, bf16[128,768]{1,0:T(8,128)(2,1)S(1)}, u32[]{:S(2)}, u32[]{:S(2)}) %collective-permute-start.13) | collective-permute-done | bytes 196640 | tf_op jit(solution)/shard_map/ppermute | solution.py:388
  59.4 2.5 %collective-permute-start.16 = (bf16[256,512]{1,0:T(8,128)(2,1)S(1)}, bf16[256,512]{1,0:T(8,128)(2,1)S(1)}, u32[]{:S(2)}, u32[]{:S(2)}) collective-permute-start(bf16[256,512]{1,0:T(8,128)(2,1)S(1)} %pad_maximum_fusion), channel_id=1, source_target_pairs={{0,24},{4,28},{8,0},{12,4},{16,8},{20,12},{24,16},{28,20},{1,25},{... | collective-permute-start | bytes 786440 | tf_op jit(solution)/shard_map/ppermute | solution.py:371
  63.7 5.4 %collective-permute-done.12.refs_2_ = bf16[128,1024]{1,0:T(8,128)(2,1)S(1)} collective-permute-done((bf16[128,1024]{1,0:T(8,128)(2,1)S(1)}, bf16[128,1024]{1,0:T(8,128)(2,1)S(1)}, u32[]{:S(2)}, u32[]{:S(2)}) %collective-permute-start.12) | collective-permute-done | bytes 262176 | tf_op jit(solution)/shard_map/ppermute | solution.py:371
  69.1 6.4 %collective-permute-done.15.refs_1_ = bf16[256,512]{1,0:T(8,128)(2,1)S(1)} collective-permute-done((bf16[256,512]{1,0:T(8,128)(2,1)S(1)}, bf16[256,512]{1,0:T(8,128)(2,1)S(1)}, u32[]{:S(2)}, u32[]{:S(2)}) %collective-permute-start.15) | collective-permute-done | bytes 262176 | tf_op jit(solution)/shard_map/ppermute | solution.py:371
  75.6 1.7 %attend.1 = (bf16[128,256]{1,0:T(8,128)(2,1)S(1)}, bf16[128,256]{1,0:T(8,128)(2,1)S(1)}) custom-call(s32[1]{0:T(128)} %bitcast.8.me_ref, s32[4]{0:T(128)S(1)} %and_select_fusion.1.ids_ref, f32[4]{0:T(128)S(1)} %copy-done.6, bf16[128,768]{1,0:T(8,128)(2,1)S(1)} %get-tuple-element.84.kept_ref, bf16[128,768]{1,0:T(8,128)(2,1)S(1)} %collective-permute-done.13.given_ref, ...), custom_call_target="tpu_custom_call" | custom-call | flops 1 | bytes 1 | tf_op jit(solution)/shard_map/attend/pallas_call | solution.py:250
  77.5 2.7 %collective-permute-start.22 = (bf16[128,1024]{1,0:T(8,128)(2,1)S(1)}, bf16[128,1024]{1,0:T(8,128)(2,1)S(1)}, u32[]{:S(2)}, u32[]{:S(2)}) collective-permute-start(bf16[128,1024]{1,0:T(8,128)(2,1)S(1)} %copy-done.7), channel_id=1, source_target_pairs={{0,3},{1,0},{2,1},{3,2},{4,7},{5,4},{6,5},{7,6},{8,11},{9,8},{10,9... | collective-permute-start | bytes 786440 | tf_op jit(solution)/shard_map/ppermute | solution.py:371
  80.2 1.0 project.1
  81.2 1.7 %collective-permute-start.20 = (bf16[128,512]{1,0:T(8,128)(2,1)S(1)}, bf16[128,512]{1,0:T(8,128)(2,1)S(1)}, u32[]{:S(2)}, u32[]{:S(2)}) collective-permute-start(bf16[128,512]{1,0:T(8,128)(2,1)S(1)} %get-tuple-element.95), channel_id=1, source_target_pairs={{0,2},{1,3},{2,0},{3,1},{4,6},{5,7},{6,4},{7,5},{8,10},{9,11},{10,... | collective-permute-start | bytes 393224 | tf_op jit(solution)/shard_map/ppermute | solution.py:371
  82.9 2.1 %collective-permute-start.21 = (bf16[128,512]{1,0:T(8,128)(2,1)S(1)}, bf16[128,512]{1,0:T(8,128)(2,1)S(1)}, u32[]{:S(2)}, u32[]{:S(2)}) collective-permute-start(bf16[128,512]{1,0:T(8,128)(2,1)S(1)} %get-tuple-element.96), channel_id=1, source_target_pairs={{0,3},{1,0},{2,1},{3,2},{4,7},{5,4},{6,5},{7,6},{8,11},{9,8},{10,9... | collective-permute-start | bytes 393224 | tf_op jit(solution)/shard_map/ppermute | solution.py:371
  85.1 5.7 %collective-permute-done.22.refs_4_ = bf16[128,1024]{1,0:T(8,128)(2,1)S(1)} collective-permute-done((bf16[128,1024]{1,0:T(8,128)(2,1)S(1)}, bf16[128,1024]{1,0:T(8,128)(2,1)S(1)}, u32[]{:S(2)}, u32[]{:S(2)}) %collective-permute-start.22) | collective-permute-done | bytes 262176 | tf_op jit(solution)/shard_map/ppermute | solution.py:371
  90.8 3.8 %collective-permute-done.20.refs_2_ = bf16[128,512]{1,0:T(8,128)(2,1)S(1)} collective-permute-done((bf16[128,512]{1,0:T(8,128)(2,1)S(1)}, bf16[128,512]{1,0:T(8,128)(2,1)S(1)}, u32[]{:S(2)}, u32[]{:S(2)}) %collective-permute-start.20) | collective-permute-done | bytes 131104 | tf_op jit(solution)/shard_map/ppermute | solution.py:371
  95.3 1.2 %collective-permute-done.23 = bf16[64,512]{1,0:T(8,128)(2,1)S(1)} collective-permute-done((bf16[64,512]{1,0:T(8,128)(2,1)S(1)}, bf16[64,512]{1,0:T(8,128)(2,1)S(1)}, u32[]{:S(2)}, u32[]{:S(2)}) %collective-permute-start.23) | collective-permute-done | bytes 65568 | tf_op jit(solution)/shard_map/ppermute | solution.py:388
  97.2 2.3 %collective-permute-start.26 = (bf16[32,512]{1,0:T(8,128)(2,1)S(1)}, bf16[32,512]{1,0:T(8,128)(2,1)S(1)}, u32[]{:S(2)}, u32[]{:S(2)}) collective-permute-start(bf16[32,512]{1,0:T(8,128)(2,1)S(1)} %get-tuple-element.112), channel_id=1, source_target_pairs={{0,24},{4,28},{8,0},{12,4},{16,8},{20,12},{24,16},{28,20},{1,25},{... | collective-permute-start | bytes 98312 | tf_op jit(solution)/shard_map/ppermute | solution.py:371
  100.2 1.2 %collective-permute-done.24 = bf16[32,512]{1,0:T(8,128)(2,1)S(1)} collective-permute-done((bf16[32,512]{1,0:T(8,128)(2,1)S(1)}, bf16[32,512]{1,0:T(8,128)(2,1)S(1)}, u32[]{:S(2)}, u32[]{:S(2)}) %collective-permute-start.24) | collective-permute-done | bytes 32800 | tf_op jit(solution)/shard_map/ppermute | solution.py:371
  101.4 2.0 %collective-permute-done.25 = bf16[32,512]{1,0:T(8,128)(2,1)S(1)} collective-permute-done((bf16[32,512]{1,0:T(8,128)(2,1)S(1)}, bf16[32,512]{1,0:T(8,128)(2,1)S(1)}, u32[]{:S(2)}, u32[]{:S(2)}) %collective-permute-start.25) | collective-permute-done | bytes 32800 | tf_op jit(solution)/shard_map/ppermute | solution.py:371
  103.4 2.1 %finish_bytes.1 = bf16[128,2,1024]{2,1,0:T(2,128)(2,1)} custom-call(bf16[128,512]{1,0:T(8,128)(2,1)S(1)} %get-tuple-element.102.result_ref, bf16[256,1024]{1,0:T(8,128)(2,1)S(1)} %copy-done.2, bf16[128,1024]{1,0:T(8,128)(2,1)S(1)} %get-tuple-element.103.refs_0_, bf16[128,1024]{1,0:T(8,128)(2,1)S(1)} %copy-done.3, ...), custom_call_target="tpu_custom_call" | custom-call | flops 1 | bytes 1 | tf_op jit(solution)/shard_map/finish_bytes/pallas_call | solution.py:357
  105.5 0.8 sort_rows.1
  (69 shorter events, 6.9 us)
Async XLA Ops:
  10.7 18.0 %collective-permute-start = (bf16[128,1024]{1,0:T(8,128)(2,1)}, bf16[128,1024]{1,0:T(8,128)(2,1)S(1)}, u32[]{:S(2)}, u32[]{:S(2)}) collective-permute-start(bf16[128,1024]{1,0:T(8,128)(2,1)} %get-tuple-element.61), channel_id=1, source_target_pairs={{0,1},{1,2},{2,3},{3,0},{4,5},{5,6},{6,7},{7,4},{8,9},{9,10},{10,1... | collective-permute-start | bytes 786440 | tf_op jit(solution)/shard_map/ppermute | solution.py:371
  13.8 26.7 %collective-permute-start.1 = (bf16[128,1024]{1,0:T(8,128)(2,1)}, bf16[128,1024]{1,0:T(8,128)(2,1)S(1)}, u32[]{:S(2)}, u32[]{:S(2)}) collective-permute-start(bf16[128,1024]{1,0:T(8,128)(2,1)} %get-tuple-element.63), channel_id=1, source_target_pairs={{0,2},{1,3},{2,0},{3,1},{4,6},{5,7},{6,4},{7,5},{8,10},{9,11},{10,... | collective-permute-start | bytes 786440 | tf_op jit(solution)/shard_map/ppermute | solution.py:371
  16.4 24.2 %copy-start.1 = (bf16[1024,256]{1,0:T(8,128)(2,1)S(1)}, bf16[1024,256]{1,0:T(8,128)(2,1)}, u32[]{:S(2)}) copy-start(bf16[1024,256]{1,0:T(8,128)(2,1)} %proj_ref.3) | copy-start | bytes 1572868
  16.4 24.2 %copy-start.4 = (bf16[128,1024]{1,0:T(8,128)(2,1)S(1)}, bf16[128,1024]{1,0:T(8,128)(2,1)}, u32[]{:S(2)}) copy-start(bf16[128,1024]{1,0:T(8,128)(2,1)} %get-tuple-element.56.refs_0_) | copy-start | bytes 786436
  16.4 24.1 %collective-permute-start.2 = (bf16[128,1024]{1,0:T(8,128)(2,1)}, bf16[128,1024]{1,0:T(8,128)(2,1)S(1)}, u32[]{:S(2)}, u32[]{:S(2)}) collective-permute-start(bf16[128,1024]{1,0:T(8,128)(2,1)} %get-tuple-element.64), channel_id=1, source_target_pairs={{0,3},{1,0},{2,1},{3,2},{4,7},{5,4},{6,5},{7,6},{8,11},{9,8},{10,9... | collective-permute-start | bytes 786440 | tf_op jit(solution)/shard_map/ppermute | solution.py:371
  28.8 15.8 %collective-permute-start.3 = (bf16[64,512]{1,0:T(8,128)(2,1)S(1)}, bf16[64,512]{1,0:T(8,128)(2,1)S(1)}, u32[]{:S(2)}, u32[]{:S(2)}) collective-permute-start(bf16[64,512]{1,0:T(8,128)(2,1)S(1)} %get-tuple-element.67), channel_id=1, source_target_pairs={{0,1},{1,2},{2,3},{3,0},{4,5},{5,6},{6,7},{7,4},{8,9},{9,10},{10,1... | collective-permute-start | bytes 196616 | tf_op jit(solution)/shard_map/ppermute | solution.py:371
  35.0 10.2 %collective-permute-start.4 = (bf16[64,512]{1,0:T(8,128)(2,1)S(1)}, bf16[64,512]{1,0:T(8,128)(2,1)S(1)}, u32[]{:S(2)}, u32[]{:S(2)}) collective-permute-start(bf16[64,512]{1,0:T(8,128)(2,1)S(1)} %get-tuple-element.68), channel_id=1, source_target_pairs={{0,2},{1,3},{2,0},{3,1},{4,6},{5,7},{6,4},{7,5},{8,10},{9,11},{10,... | collective-permute-start | bytes 196616 | tf_op jit(solution)/shard_map/ppermute | solution.py:371
  36.9 8.2 %collective-permute-start.5 = (bf16[64,512]{1,0:T(8,128)(2,1)S(1)}, bf16[64,512]{1,0:T(8,128)(2,1)S(1)}, u32[]{:S(2)}, u32[]{:S(2)}) collective-permute-start(bf16[64,512]{1,0:T(8,128)(2,1)S(1)} %get-tuple-element.69), channel_id=1, source_target_pairs={{0,3},{1,0},{2,1},{3,2},{4,7},{5,4},{6,5},{7,6},{8,11},{9,8},{10,9... | collective-permute-start | bytes 196616 | tf_op jit(solution)/shard_map/ppermute | solution.py:371
  40.9 8.7 %collective-permute-start.8 = (bf16[64,512]{1,0:T(8,128)(2,1)S(1)}, bf16[64,512]{1,0:T(8,128)(2,1)S(1)}, u32[]{:S(2)}, u32[]{:S(2)}) collective-permute-start(bf16[64,512]{1,0:T(8,128)(2,1)S(1)} %get-tuple-element.73.refs_0_), channel_id=1, source_target_pairs={{0,3},{1,0},{2,1},{3,2},{4,7},{5,4},{6,5},{7,6},{8,11},{9,8},{10,9... | collective-permute-start | bytes 196616 | tf_op jit(solution)/shard_map/ppermute | solution.py:371
  44.5 8.7 %collective-permute-start.7 = (bf16[64,512]{1,0:T(8,128)(2,1)S(1)}, bf16[64,512]{1,0:T(8,128)(2,1)S(1)}, u32[]{:S(2)}, u32[]{:S(2)}) collective-permute-start(bf16[64,512]{1,0:T(8,128)(2,1)S(1)} %get-tuple-element.73.refs_0_), channel_id=1, source_target_pairs={{0,2},{1,3},{2,0},{3,1},{4,6},{5,7},{6,4},{7,5},{8,10},{9,11},{10,... | collective-permute-start | bytes 196616 | tf_op jit(solution)/shard_map/ppermute | solution.py:371
  44.6 8.7 %collective-permute-start.6 = (bf16[64,512]{1,0:T(8,128)(2,1)S(1)}, bf16[64,512]{1,0:T(8,128)(2,1)S(1)}, u32[]{:S(2)}, u32[]{:S(2)}) collective-permute-start(bf16[64,512]{1,0:T(8,128)(2,1)S(1)} %get-tuple-element.73.refs_0_), channel_id=1, source_target_pairs={{0,1},{1,2},{2,3},{3,0},{4,5},{5,6},{6,7},{7,4},{8,9},{9,10},{10,1... | collective-permute-start | bytes 196616 | tf_op jit(solution)/shard_map/ppermute | solution.py:371
  45.2 8.0 %collective-permute-start.11 = (bf16[64,512]{1,0:T(8,128)(2,1)S(1)}, bf16[64,512]{1,0:T(8,128)(2,1)S(1)}, u32[]{:S(2)}, u32[]{:S(2)}) collective-permute-start(bf16[64,512]{1,0:T(8,128)(2,1)S(1)} %add_convert_fusion.refs_4_), channel_id=1, source_target_pairs={{0,3},{1,0},{2,1},{3,2},{4,7},{5,4},{6,5},{7,6},{8,11},{9,8},{10,9... | collective-permute-start | bytes 196616 | tf_op jit(solution)/shard_map/ppermute | solution.py:371
  48.5 7.6 %collective-permute-start.10 = (bf16[64,512]{1,0:T(8,128)(2,1)S(1)}, bf16[64,512]{1,0:T(8,128)(2,1)S(1)}, u32[]{:S(2)}, u32[]{:S(2)}) collective-permute-start(bf16[64,512]{1,0:T(8,128)(2,1)S(1)} %add_convert_fusion.refs_4_), channel_id=1, source_target_pairs={{0,2},{1,3},{2,0},{3,1},{4,6},{5,7},{6,4},{7,5},{8,10},{9,11},{10,... | collective-permute-start | bytes 196616 | tf_op jit(solution)/shard_map/ppermute | solution.py:371
  49.6 6.6 %collective-permute-start.9 = (bf16[64,512]{1,0:T(8,128)(2,1)S(1)}, bf16[64,512]{1,0:T(8,128)(2,1)S(1)}, u32[]{:S(2)}, u32[]{:S(2)}) collective-permute-start(bf16[64,512]{1,0:T(8,128)(2,1)S(1)} %add_convert_fusion.refs_4_), channel_id=1, source_target_pairs={{0,1},{1,2},{2,3},{3,0},{4,5},{5,6},{6,7},{7,4},{8,9},{9,10},{10,1... | collective-permute-start | bytes 196616 | tf_op jit(solution)/shard_map/ppermute | solution.py:371
  57.9 22.3 %copy-start = (bf16[512,2048]{1,0:T(8,128)(2,1)S(1)}, bf16[512,2048]{1,0:T(8,128)(2,1)}, u32[]{:S(2)}) copy-start(bf16[512,2048]{1,0:T(8,128)(2,1)} %proj_ref.4) | copy-start | bytes 6291460
  57.9 1.5 %collective-permute-start.13 = (bf16[128,768]{1,0:T(8,128)(2,1)S(1)}, bf16[128,768]{1,0:T(8,128)(2,1)S(1)}, u32[]{:S(2)}, u32[]{:S(2)}) collective-permute-start(bf16[128,768]{1,0:T(8,128)(2,1)S(1)} %get-tuple-element.85), channel_id=1, source_target_pairs={{0,4},{4,0},{8,12},{12,8},{16,20},{20,16},{24,28},{28,24},{1,5},{5... | collective-permute-start | bytes 589832 | tf_op jit(solution)/shard_map/ppermute | solution.py:388
  58.1 11.1 %collective-permute-start.12 = (bf16[128,1024]{1,0:T(8,128)(2,1)S(1)}, bf16[128,1024]{1,0:T(8,128)(2,1)S(1)}, u32[]{:S(2)}, u32[]{:S(2)}) collective-permute-start(bf16[128,1024]{1,0:T(8,128)(2,1)S(1)} %copy-done.9), channel_id=1, source_target_pairs={{0,1},{1,2},{2,3},{3,0},{4,5},{5,6},{6,7},{7,4},{8,9},{9,10},{10,1... | collective-permute-start | bytes 786440 | tf_op jit(solution)/shard_map/ppermute | solution.py:371
  59.4 9.7 %collective-permute-start.16 = (bf16[256,512]{1,0:T(8,128)(2,1)S(1)}, bf16[256,512]{1,0:T(8,128)(2,1)S(1)}, u32[]{:S(2)}, u32[]{:S(2)}) collective-permute-start(bf16[256,512]{1,0:T(8,128)(2,1)S(1)} %pad_maximum_fusion), channel_id=1, source_target_pairs={{0,24},{4,28},{8,0},{12,4},{16,8},{20,12},{24,16},{28,20},{1,25},{... | collective-permute-start | bytes 786440 | tf_op jit(solution)/shard_map/ppermute | solution.py:371
  61.9 13.7 %collective-permute-start.15 = (bf16[256,512]{1,0:T(8,128)(2,1)S(1)}, bf16[256,512]{1,0:T(8,128)(2,1)S(1)}, u32[]{:S(2)}, u32[]{:S(2)}) collective-permute-start(bf16[256,512]{1,0:T(8,128)(2,1)S(1)} %pad_maximum_fusion), channel_id=1, source_target_pairs={{0,16},{4,20},{8,24},{12,28},{16,0},{20,4},{24,8},{28,12},{1,17},{... | collective-permute-start | bytes 786440 | tf_op jit(solution)/shard_map/ppermute | solution.py:371
  62.4 13.2 %collective-permute-start.14 = (bf16[256,512]{1,0:T(8,128)(2,1)S(1)}, bf16[256,512]{1,0:T(8,128)(2,1)S(1)}, u32[]{:S(2)}, u32[]{:S(2)}) collective-permute-start(bf16[256,512]{1,0:T(8,128)(2,1)S(1)} %pad_maximum_fusion), channel_id=1, source_target_pairs={{0,8},{4,12},{8,16},{12,20},{16,24},{20,28},{24,0},{28,4},{1,9},{5... | collective-permute-start | bytes 786440 | tf_op jit(solution)/shard_map/ppermute | solution.py:371
  63.0 17.1 %collective-permute-start.18 = (bf16[128,1024]{1,0:T(8,128)(2,1)S(1)}, bf16[128,1024]{1,0:T(8,128)(2,1)S(1)}, u32[]{:S(2)}, u32[]{:S(2)}) collective-permute-start(bf16[128,1024]{1,0:T(8,128)(2,1)S(1)} %copy-done.8), channel_id=1, source_target_pairs={{0,2},{1,3},{2,0},{3,1},{4,6},{5,7},{6,4},{7,5},{8,10},{9,11},{10,... | collective-permute-start | bytes 786440 | tf_op jit(solution)/shard_map/ppermute | solution.py:371
  77.3 26.1 %copy-start.2 = (bf16[256,1024]{1,0:T(8,128)(2,1)S(1)}, bf16[256,1024]{1,0:T(8,128)(2,1)}, u32[]{:S(2)}) copy-start(bf16[256,1024]{1,0:T(8,128)(2,1)} %proj_ref.5) | copy-start | bytes 1572868
  77.3 26.1 %copy-start.3 = (bf16[128,1024]{1,0:T(8,128)(2,1)S(1)}, bf16[128,1024]{1,0:T(8,128)(2,1)}, u32[]{:S(2)}) copy-start(bf16[128,1024]{1,0:T(8,128)(2,1)} %get-tuple-element.104.refs_1_) | copy-start | bytes 786436
  77.3 2.8 %collective-permute-start.17 = (bf16[128,256]{1,0:T(8,128)(2,1)S(1)}, bf16[128,256]{1,0:T(8,128)(2,1)S(1)}, u32[]{:S(2)}, u32[]{:S(2)}) collective-permute-start(bf16[128,256]{1,0:T(8,128)(2,1)S(1)} %get-tuple-element.90), channel_id=1, source_target_pairs={{0,4},{4,0},{8,12},{12,8},{16,20},{20,16},{24,28},{28,24},{1,5},{5... | collective-permute-start | bytes 196616 | tf_op jit(solution)/shard_map/ppermute | solution.py:388
  77.5 13.3 %collective-permute-start.22 = (bf16[128,1024]{1,0:T(8,128)(2,1)S(1)}, bf16[128,1024]{1,0:T(8,128)(2,1)S(1)}, u32[]{:S(2)}, u32[]{:S(2)}) collective-permute-start(bf16[128,1024]{1,0:T(8,128)(2,1)S(1)} %copy-done.7), channel_id=1, source_target_pairs={{0,3},{1,0},{2,1},{3,2},{4,7},{5,4},{6,5},{7,6},{8,11},{9,8},{10,9... | collective-permute-start | bytes 786440 | tf_op jit(solution)/shard_map/ppermute | solution.py:371
  81.2 9.6 %collective-permute-start.19 = (bf16[128,512]{1,0:T(8,128)(2,1)S(1)}, bf16[128,512]{1,0:T(8,128)(2,1)S(1)}, u32[]{:S(2)}, u32[]{:S(2)}) collective-permute-start(bf16[128,512]{1,0:T(8,128)(2,1)S(1)} %get-tuple-element.94), channel_id=1, source_target_pairs={{0,1},{1,2},{2,3},{3,0},{4,5},{5,6},{6,7},{7,4},{8,9},{9,10},{10,1... | collective-permute-start | bytes 393224 | tf_op jit(solution)/shard_map/ppermute | solution.py:371
  81.2 13.4 %collective-permute-start.20 = (bf16[128,512]{1,0:T(8,128)(2,1)S(1)}, bf16[128,512]{1,0:T(8,128)(2,1)S(1)}, u32[]{:S(2)}, u32[]{:S(2)}) collective-permute-start(bf16[128,512]{1,0:T(8,128)(2,1)S(1)} %get-tuple-element.95), channel_id=1, source_target_pairs={{0,2},{1,3},{2,0},{3,1},{4,6},{5,7},{6,4},{7,5},{8,10},{9,11},{10,... | collective-permute-start | bytes 393224 | tf_op jit(solution)/shard_map/ppermute | solution.py:371
  82.9 12.0 %collective-permute-start.21 = (bf16[128,512]{1,0:T(8,128)(2,1)S(1)}, bf16[128,512]{1,0:T(8,128)(2,1)S(1)}, u32[]{:S(2)}, u32[]{:S(2)}) collective-permute-start(bf16[128,512]{1,0:T(8,128)(2,1)S(1)} %get-tuple-element.96), channel_id=1, source_target_pairs={{0,3},{1,0},{2,1},{3,2},{4,7},{5,4},{6,5},{7,6},{8,11},{9,8},{10,9... | collective-permute-start | bytes 393224 | tf_op jit(solution)/shard_map/ppermute | solution.py:371
  95.2 1.3 %collective-permute-start.23 = (bf16[64,512]{1,0:T(8,128)(2,1)S(1)}, bf16[64,512]{1,0:T(8,128)(2,1)S(1)}, u32[]{:S(2)}, u32[]{:S(2)}) collective-permute-start(bf16[64,512]{1,0:T(8,128)(2,1)S(1)} %get-tuple-element.109), channel_id=1, source_target_pairs={{0,4},{4,0},{8,12},{12,8},{16,20},{20,16},{24,28},{28,24},{1,5},{5... | collective-permute-start | bytes 196616 | tf_op jit(solution)/shard_map/ppermute | solution.py:388
  96.5 4.9 %collective-permute-start.24 = (bf16[32,512]{1,0:T(8,128)(2,1)S(1)}, bf16[32,512]{1,0:T(8,128)(2,1)S(1)}, u32[]{:S(2)}, u32[]{:S(2)}) collective-permute-start(bf16[32,512]{1,0:T(8,128)(2,1)S(1)} %get-tuple-element.111), channel_id=1, source_target_pairs={{0,8},{4,12},{8,16},{12,20},{16,24},{20,28},{24,0},{28,4},{1,9},{5... | collective-permute-start | bytes 98312 | tf_op jit(solution)/shard_map/ppermute | solution.py:371
  97.2 4.2 %collective-permute-start.26 = (bf16[32,512]{1,0:T(8,128)(2,1)S(1)}, bf16[32,512]{1,0:T(8,128)(2,1)S(1)}, u32[]{:S(2)}, u32[]{:S(2)}) collective-permute-start(bf16[32,512]{1,0:T(8,128)(2,1)S(1)} %get-tuple-element.112), channel_id=1, source_target_pairs={{0,24},{4,28},{8,0},{12,4},{16,8},{20,12},{24,16},{28,20},{1,25},{... | collective-permute-start | bytes 98312 | tf_op jit(solution)/shard_map/ppermute | solution.py:371
  99.5 3.9 %collective-permute-start.25 = (bf16[32,512]{1,0:T(8,128)(2,1)S(1)}, bf16[32,512]{1,0:T(8,128)(2,1)S(1)}, u32[]{:S(2)}, u32[]{:S(2)}) collective-permute-start(bf16[32,512]{1,0:T(8,128)(2,1)S(1)} %get-tuple-element.113), channel_id=1, source_target_pairs={{0,16},{4,20},{8,24},{12,28},{16,0},{20,4},{24,8},{28,12},{1,17},{... | collective-permute-start | bytes 98312 | tf_op jit(solution)/shard_map/ppermute | solution.py:371
  (5 other events, 56.0 us)
